TPU v7x, 32 devices: a whole 2x2x4 slice. The times are simulated.
32 devices in a mesh: grp: 2 (over core), ep: 16 (over z, y, x).
Axes of the slice: x: 2, y: 2, z: 4, core: 2. Of those that a mesh axis runs over, the one named last changes fastest.
Arguments:
- tokens: bfloat16 [2, 2048, 1024], P('grp', 'ep'), may hold values from -6 to 6
- queries: bfloat16 [2, 2048, 1024], P('grp', 'ep'), may hold values from -128 to 128
- keys: bfloat16 [2, 2048, 1024], P('grp', 'ep'), may hold values from -4 to 4
- values: bfloat16 [2, 2048, 1024], P('grp', 'ep'), may hold values from -6 to 6
- key_mask: int32 [2, 2048], P('grp', 'ep'), may hold values 0 or 1
- labels: int32 [2, 2048, 1], P('grp', 'ep'), may hold values from 0 to 3; in each aligned block of 128 rows (0 to 127, 128 to 255, ..., all dimensions but the last counted through in order) at most 36 rows name the same one
- cotangent: bfloat16 [2, 2048, 1024], P('grp', 'ep'), may hold values from -0.125 to 0.125
- weight_in: bfloat16 [1024, 16384], P(None, 'ep'), may hold values from -0.1875 to 0.1875
- weight_out: bfloat16 [16, 1024, 1024], P('ep'), may hold values from -0.09375 to 0.09375
Outputs:
- layer_out: bfloat16 [2, 2048, 1024], P('grp', 'ep')
- grad_out: bfloat16 [16, 1024, 1024], P('ep', 'grp')
Inputs may be any that keep to these rules, and one draw needn't show every extreme that they name: `labels`: among the 128 tokens of one aligned block of a sample no label occurs more than 36 times, and some block reaches 36.
All inputs are finite; a program needn't handle non-finite values. No bound on the sum of `key_mask` on one device may be relied on, other than what follows from the above.
Results may differ from a plain program's by a relative error of at most 0.018.
Values may be sent and summed in bfloat16 or wider, within the bound.
No kernel may reach another device: no remote copies, remote signals or barrier semaphores. Data moves between devices by JAX's collectives and lax.ppermute only.
A program may use at most 64 MiB of HBM per device.

v0:
```python
import jax
import jax.numpy as jnp
from jax import lax
from jax.sharding import PartitionSpec as P

HEADS = 8
SPLIT = 4
HALO = 64


NEG_FILL = -1e30


def partner_2(value, axis, apart):
    mask = 2**apart
    pairs = [(source, source ^ mask) for source in range(lax.axis_size(axis))]
    return lax.ppermute(value, axis, pairs)


def with_halo(shard, sides, width):
    for axis, dim in sides:
        size, length = (lax.axis_size(axis), shard.shape[dim])
        up = [(i, (i + 1) % size) for i in range(size - 1)]
        down = [(j, i) for i, j in up]
        last = lax.slice_in_dim(shard, length - width, length, axis=dim)
        first = lax.slice_in_dim(shard, 0, width, axis=dim)
        before = lax.ppermute(last, axis, up)
        after = lax.ppermute(first, axis, down)
        shard = jnp.concatenate([before, shard, after], axis=dim)
    return shard


def window_attention(query_rows, key_rows, value_rows, mask_rows):
    query_count = query_rows.shape[0]
    key_count = key_rows.shape[0]
    head_width = query_rows.shape[1] // HEADS
    query_heads = query_rows.reshape(query_count, HEADS, head_width)
    key_heads = key_rows.reshape(key_count, HEADS, head_width)
    value_heads = value_rows.reshape(key_count, HEADS, head_width)
    scores = jnp.einsum(
        "qhd,khd->hqk", query_heads, key_heads, preferred_element_type=jnp.float32
    ) * head_width ** (-0.5)
    offset = (
        jnp.arange(key_count, dtype=jnp.int32)[None, :]
        - HALO
        - jnp.arange(query_count, dtype=jnp.int32)[:, None]
    )
    usable = (jnp.abs(offset) <= HALO) & ((mask_rows[None, :] == 1) | (offset == 0))
    scores = jnp.where(usable[None], scores, NEG_FILL)
    row_max = jnp.max(scores, axis=-1, keepdims=True)
    raised = jnp.exp(scores - row_max)
    soft_weights = (raised / jnp.sum(raised, axis=-1, keepdims=True)).astype(jnp.bfloat16)
    attended = jnp.einsum(
        "hqk,khd->qhd", soft_weights, value_heads, preferred_element_type=jnp.float32
    )
    return attended.reshape(query_count, HEADS * head_width)


def deliver(outgoing):
    experts, capacity, feature_width = outgoing.shape
    axis_count = lax.axis_size("ep")
    part_width = feature_width // SPLIT
    sliced = (
        outgoing.reshape(experts, capacity, SPLIT, part_width)
        .transpose(0, 2, 1, 3)
        .reshape(axis_count, capacity, part_width)
    )
    gathered = lax.all_to_all(sliced, "ep", split_axis=0, concat_axis=0, tiled=True)
    position = lax.axis_index("ep")
    for bit_level in range(SPLIT.bit_length() - 1):
        partner = partner_2(gathered, "ep", bit_level)
        high_side = jnp.right_shift(position, bit_level) % 2 == 1
        gathered = jnp.where(
            high_side,
            jnp.concatenate([partner, gathered], axis=2),
            jnp.concatenate([gathered, partner], axis=2),
        )
    return gathered


def collect(partial_value, experts, capacity, feature_width):
    returned = lax.all_to_all(partial_value, "ep", split_axis=0, concat_axis=0, tiled=True)
    return (
        returned.reshape(experts, SPLIT, capacity, feature_width)
        .astype(jnp.float32)
        .sum(axis=1)
        .reshape(experts * capacity, feature_width)
    )


def shards(tokens, queries, keys, values, key_mask, labels, cotangent, weight_in, weight_out):
    padded_keys, padded_values, padded_mask = (
        with_halo(keys, (("ep", 1),), HALO),
        with_halo(values, (("ep", 1),), HALO),
        with_halo(key_mask, (("ep", 1),), HALO),
    )
    attended = window_attention(queries[0], padded_keys[0], padded_values[0], padded_mask[0])
    mixed = (tokens[0].astype(jnp.float32) + attended).astype(jnp.bfloat16)
    rows_here, feature_width = mixed.shape
    axis_count = lax.axis_size("ep")
    experts = axis_count // SPLIT
    capacity = rows_here // experts + max(1, rows_here // (8 * experts))
    expert_of = labels[0, :, 0]
    onehot = (expert_of[:, None] == jnp.arange(experts, dtype=jnp.int32)[None, :]).astype(jnp.int32)
    running = jnp.cumsum(onehot, axis=0) - 1
    slot_index = jnp.sum(running * onehot, axis=1)
    target = expert_of * capacity + slot_index
    placing = (jnp.arange(experts * capacity, dtype=jnp.int32)[:, None] == target[None, :]).astype(
        jnp.bfloat16
    )
    outgoing = (
        jnp.dot(placing, mixed, preferred_element_type=jnp.float32)
        .astype(jnp.bfloat16)
        .reshape(experts, capacity, feature_width)
    )
    arrived = deliver(outgoing).reshape(axis_count * capacity, feature_width)
    pre_act = jnp.dot(arrived, weight_in, preferred_element_type=jnp.float32)
    hidden = jax.nn.gelu(pre_act).astype(jnp.bfloat16)
    partial_value = (
        jnp.dot(hidden, weight_out[0], preferred_element_type=jnp.float32)
        .astype(jnp.bfloat16)
        .reshape(axis_count, capacity, feature_width)
    )
    summed = collect(partial_value, experts, capacity, feature_width)
    expert_out = jnp.take(summed, target, axis=0)
    layer_out = (mixed.astype(jnp.float32) + expert_out).astype(jnp.bfloat16)[None]
    grad_outgoing = (
        jnp.dot(placing, cotangent[0], preferred_element_type=jnp.float32)
        .astype(jnp.bfloat16)
        .reshape(experts, capacity, feature_width)
    )
    grad_arrived = deliver(grad_outgoing).reshape(axis_count * capacity, feature_width)
    grad_rows = lax.psum_scatter(
        lax.dot_general(
            hidden, grad_arrived, (((0,), (0,)), ((), ())), preferred_element_type=jnp.float32
        ).astype(jnp.bfloat16),
        "grp",
        scatter_dimension=0,
        tiled=True,
    )
    return (layer_out, grad_rows[None])


def solution(mesh):
    in_specs = (
        P("grp", "ep", None),
        P("grp", "ep", None),
        P("grp", "ep", None),
        P("grp", "ep", None),
        P("grp", "ep"),
        P("grp", "ep", None),
        P("grp", "ep", None),
        P(None, "ep"),
        P("ep", None, None),
    )
    out_specs = (P("grp", "ep", None), P("ep", "grp", None))
    return jax.shard_map(shards, mesh=mesh, in_specs=in_specs, out_specs=out_specs, check_vma=False)
```

profile of v0, /device:TPU:0, one launch (start us, length us, event | category | flops | bytes accessed | tf_op | source)
XLA Modules:
  0.0 167.6 jit_solution(11451398796279604112)
XLA Ops:
  7.2 1.8 %fusion.55 = (bf16[1,64,1024]{2,1,0:T(8,128)(2,1)}, bf16[1,64,1024]{2,1,0:T(8,128)(2,1)}) fusion(bf16[1,128,1024]{2,1,0:T(8,128)(2,1)} %param.12), kind=kLoop, calls=%fused_computation.82 | loop fusion | bytes 524288 | tf_op jit(solution)/shard_map/slice | solution.py:25
  9.0 1.3 collective-permute-start.1
  10.3 6.1 %collective-permute-start = (bf16[1,64,1024]{2,1,0:T(8,128)(2,1)}, bf16[1,64,1024]{2,1,0:T(8,128)(2,1)}, u32[]{:S(2)}, u32[]{:S(2)}) collective-permute-start(bf16[1,64,1024]{2,1,0:T(8,128)(2,1)} %get-tuple-element.6), channel_id=1, source_target_pairs={{0,1},{1,2},{2,3},{3,4},{4,5},{5,6},{6,7},{7,8},{8,9},{9,10},{10,1... | collective-permute-start | bytes 393224 | tf_op jit(solution)/shard_map/ppermute | solution.py:27
  18.5 1.3 collective-permute-start.5
  19.8 1.3 collective-permute-start.3
  21.1 5.4 %collective-permute-start.2 = (s32[1,64]{1,0:T(1,128)S(1)}, s32[1,64]{1,0:T(1,128)S(1)}, u32[]{:S(2)}, u32[]{:S(2)}) collective-permute-start(s32[1,64]{1,0:T(1,128)S(1)} %get-tuple-element.8), channel_id=1, source_target_pairs={{0,1},{1,2},{2,3},{3,4},{4,5},{5,6},{6,7},{7,8},{8,9},{9,10},{10,1... | collective-permute-start | bytes 776 | tf_op jit(solution)/shard_map/ppermute | solution.py:27
  28.2 9.1 %all-to-all-start.2 = ((bf16[16,36,256]{2,1,0:T(8,128)(2,1)}), bf16[16,36,256]{2,1,0:T(8,128)(2,1)S(1)}, u32[]{:S(2)}, u32[]{:S(2)}) async-start(bf16[16,36,256]{2,1,0:T(8,128)(2,1)} %bitcast.21), calls=%async_computation.2 | async-start | bytes 655360 | tf_op jit(solution)/shard_map/all_to_all | solution.py:68
  38.3 3.8 %collective-permute-start.4 = (bf16[1,64,1024]{1,2,0:T(8,128)(2,1)}, bf16[1,64,1024]{1,2,0:T(8,128)(2,1)S(1)}, u32[]{:S(2)}, u32[]{:S(2)}) collective-permute-start(bf16[1,64,1024]{1,2,0:T(8,128)(2,1)} %get-tuple-element.4), channel_id=1, source_target_pairs={{0,1},{1,2},{2,3},{3,4},{4,5},{5,6},{6,7},{7,8},{8,9},{9,10},{10,1... | collective-permute-start | bytes 393224 | tf_op jit(solution)/shard_map/ppermute | solution.py:27
  43.1 5.0 %collective-permute-done.4 = bf16[1,64,1024]{1,2,0:T(8,128)(2,1)S(1)} collective-permute-done((bf16[1,64,1024]{1,2,0:T(8,128)(2,1)}, bf16[1,64,1024]{1,2,0:T(8,128)(2,1)S(1)}, u32[]{:S(2)}, u32[]{:S(2)}) %collective-permute-start.4) | collective-permute-done | bytes 131104 | tf_op jit(solution)/shard_map/ppermute | solution.py:27
  48.1 1.3 pad_maximum_fusion.1
  49.4 1.3 fusion.17
  53.7 2.2 %fusion.36 = f32[8,128,128]{2,1,0:T(8,128)S(1)} fusion(bf16[256,8,128]{0,2,1:T(8,128)(2,1)} %bitcast.78, f32[8,128]{1,0:T(8,128)S(1)} %fusion.57, f32[8,128,256]{1,2,0:T(8,128)} %fusion.17), kind=kOutput, calls=%fused_computation.53 | convolution fusion | flops 67896576 | bytes 2101248 | tf_op jit(solution)/shard_map/hqk,khd->qhd/dot_general | solution.py:53
  56.9 2.0 %convolution_convert_fusion.2 = bf16[144,1024]{1,0:T(8,128)(2,1)} fusion(f32[128,1024]{1,0:T(8,128)} %copy.54, bf16[1,128,1024]{2,1,0:T(8,128)(2,1)S(1)} %copy-done.4, s32[128]{0:T(128)S(1)} %get-tuple-element.3), kind=kOutput, calls=%fused_computation.22 | convolution fusion | flops 38307840 | bytes 1081856 | tf_op jit(solution)/shard_map/dot_general | solution.py:112
  60.8 7.6 %all-to-all-start = ((bf16[16,36,256]{2,1,0:T(8,128)(2,1)}), bf16[16,36,256]{2,1,0:T(8,128)(2,1)S(1)}, u32[]{:S(2)}, u32[]{:S(2)}) async-start(bf16[16,36,256]{2,1,0:T(8,128)(2,1)} %bitcast.12), calls=%async_computation | async-start | bytes 655360 | tf_op jit(solution)/shard_map/all_to_all | solution.py:68
  68.5 2.0 %collective-permute-start.8 = (bf16[16,36,256]{2,1,0:T(8,128)(2,1)S(1)}, bf16[16,36,256]{2,1,0:T(8,128)(2,1)S(1)}, u32[]{:S(2)}, u32[]{:S(2)}) collective-permute-start(bf16[16,36,256]{2,1,0:T(8,128)(2,1)S(1)} %all-to-all-done.2), channel_id=1, source_target_pairs={{0,1},{1,0},{2,3},{3,2},{4,5},{5,4},{6,7},{7,6},{8,9},{9,8},{10,11... | collective-permute-start | bytes 884744 | tf_op jit(solution)/shard_map/ppermute | solution.py:17
  70.5 8.7 %all-to-all-done = bf16[16,36,256]{2,1,0:T(8,128)(2,1)S(1)} async-done(((bf16[16,36,256]{2,1,0:T(8,128)(2,1)}), bf16[16,36,256]{2,1,0:T(8,128)(2,1)S(1)}, u32[]{:S(2)}, u32[]{:S(2)}) %all-to-all-start) | async-done | bytes 294944 | tf_op jit(solution)/shard_map/all_to_all | solution.py:68
  79.8 2.5 %collective-permute-done.8 = bf16[16,36,256]{2,1,0:T(8,128)(2,1)S(1)} collective-permute-done((bf16[16,36,256]{2,1,0:T(8,128)(2,1)S(1)}, bf16[16,36,256]{2,1,0:T(8,128)(2,1)S(1)}, u32[]{:S(2)}, u32[]{:S(2)}) %collective-permute-start.8) | collective-permute-done | bytes 294944 | tf_op jit(solution)/shard_map/ppermute | solution.py:17
  83.4 1.5 collective-permute-start.9
  84.9 2.9 %collective-permute-done.6 = bf16[16,36,256]{2,1,0:T(8,128)(2,1)} collective-permute-done((bf16[16,36,256]{2,1,0:T(8,128)(2,1)S(1)}, bf16[16,36,256]{2,1,0:T(8,128)(2,1)}, u32[]{:S(2)}, u32[]{:S(2)}) %collective-permute-start.6) | collective-permute-done | bytes 294944 | tf_op jit(solution)/shard_map/ppermute | solution.py:17
  87.8 1.2 maximum_select_fusion.6
  90.0 1.5 collective-permute-start.7
  95.3 4.7 %collective-permute-done.9 = bf16[16,36,512]{2,0,1:T(8,128)(2,1)} collective-permute-done((bf16[16,36,512]{2,0,1:T(8,128)(2,1)}, bf16[16,36,512]{2,0,1:T(8,128)(2,1)}, u32[]{:S(2)}, u32[]{:S(2)}) %collective-permute-start.9) | collective-permute-done | bytes 589856 | tf_op jit(solution)/shard_map/ppermute | solution.py:17
  100.0 1.4 copy.62
  102.4 6.2 %collective-permute-done.7 = bf16[16,36,512]{2,0,1:T(8,128)(2,1)} collective-permute-done((bf16[16,36,512]{2,0,1:T(8,128)(2,1)}, bf16[16,36,512]{2,0,1:T(8,128)(2,1)}, u32[]{:S(2)}, u32[]{:S(2)}) %collective-permute-start.7) | collective-permute-done | bytes 589856 | tf_op jit(solution)/shard_map/ppermute | solution.py:17
  108.5 1.4 copy.58
  110.9 3.2 %fusion.8 = bf16[576,1024]{1,0:T(8,128)(2,1)S(1)} fusion(bf16[1024,1024]{1,0:T(8,128)(2,1)S(1)} %copy-done, bf16[576,512]{1,0:T(8,128)(2,1)S(1)} %maximum_select_fusion.8, bf16[576,512]{1,0:T(8,128)(2,1)} %concatenate.80, pred[]{:T(512)S(6)} %eq.67), kind=kOutput, calls=%fused_computation.11 | convolution fusion | flops 1218576384 | bytes 4456449 | tf_op jit(solution)/shard_map/dot_general | solution.py:117
  115.1 3.2 %convolution_convert_fusion = bf16[1024,1024]{1,0:T(8,128)(2,1)} fusion(bf16[576,1024]{1,0:T(8,128)(2,1)S(1)} %fusion.8, bf16[576,512]{1,0:T(8,128)(2,1)S(1)} %copy-done.6, bf16[576,512]{1,0:T(8,128)(2,1)S(1)} %copy-done.7, pred[]{:T(512)S(6)} %eq.67), kind=kOutput, calls=%fused_computation.14 | convolution fusion | flops 1214316544 | bytes 4456449 | tf_op jit(solution)/shard_map/dot_general | solution.py:134
  118.3 3.3 %fusion.11 = bf16[576,1024]{1,0:T(8,128)(2,1)S(1)} fusion(bf16[576,1024]{1,0:T(8,128)(2,1)} %copy-done.12, bf16[1,1024,1024]{2,1,0:T(8,128)(2,1)} %param.17), kind=kOutput, calls=%fused_computation.15 | convolution fusion | flops 1208549376 | bytes 4456448 | tf_op jit(solution)/shard_map/dot_general | solution.py:120
  122.8 6.1 %all-to-all-start.1 = ((bf16[16,36,1024]{2,1,0:T(8,128)(2,1)}), bf16[16,36,1024]{2,1,0:T(8,128)(2,1)S(1)}, u32[]{:S(2)}, u32[]{:S(2)}) async-start(bf16[16,36,1024]{2,1,0:T(8,128)(2,1)} %reshape.187), calls=%async_computation.1 | async-start | bytes 2621440 | tf_op jit(solution)/shard_map/all_to_all | solution.py:82
  128.9 2.0 %copy.53 = f32[1,128,1024]{2,1,0:T(8,128)} copy(f32[1,128,1024]{1,2,0:T(8,128)} %bitcast.73) | data formatting | bytes 1048576 | tf_op jit(solution)/shard_map/reshape | solution.py:56
  131.0 24.8 %all-to-all-done.1 = bf16[16,36,1024]{2,1,0:T(8,128)(2,1)S(1)} async-done(((bf16[16,36,1024]{2,1,0:T(8,128)(2,1)}), bf16[16,36,1024]{2,1,0:T(8,128)(2,1)S(1)}, u32[]{:S(2)}, u32[]{:S(2)}) %all-to-all-start.1) | async-done | bytes 1179680 | tf_op jit(solution)/shard_map/all_to_all | solution.py:82
  158.9 1.9 %fusion.35 = bf16[1,128,1024]{2,1,0:T(8,128)(2,1)} fusion(f32[128,1024]{1,0:T(8,128)S(1)} %gather_fusion, f32[1,128,1024]{2,1,0:T(8,128)} %copy.53, bf16[1,128,1024]{2,1,0:T(8,128)(2,1)S(1)} %copy-done.5, pred[128]{0:T(512)(128)(4,1)S(1)} %get-tuple-element.2), kind=kLoop, calls=%fused_computation.52 | loop fusion | flops 917504 | bytes 1572992 | tf_op jit(solution)/shard_map/convert_element_type | solution.py:126
  (73 shorter events, 25.4 us)
Async XLA Ops:
  7.2 103.7 %copy-start = (bf16[1024,1024]{1,0:T(8,128)(2,1)S(1)}, bf16[1024,1024]{1,0:T(8,128)(2,1)}, u32[]{:S(2)}) copy-start(bf16[1024,1024]{1,0:T(8,128)(2,1)} %param.16) | copy-start | bytes 6291460
  7.2 12.6 %copy-start.11 = (s32[1,128]{1,0:T(1,128)S(1)}, s32[1,128]{1,0:T(1,128)}, u32[]{:S(2)}) copy-start(s32[1,128]{1,0:T(1,128)} %param.13) | copy-start | bytes 1540
  7.2 19.4 %copy-start.10 = (s32[1,128,1]{1,2,0:T(1,128)S(1)}, s32[1,128,1]{1,2,0:T(1,128)}, u32[]{:S(2)}) copy-start(s32[1,128,1]{1,2,0:T(1,128)} %param.14) | copy-start | bytes 1540
  7.2 19.8 %copy-start.9 = (bf16[1,128,1024]{2,1,0:T(8,128)(2,1)S(1)}, bf16[1,128,1024]{2,1,0:T(8,128)(2,1)}, u32[]{:S(2)}) copy-start(bf16[1,128,1024]{2,1,0:T(8,128)(2,1)} %param.15) | copy-start | bytes 786436
  9.0 42.2 %collective-permute-start.1 = (bf16[1,64,1024]{2,1,0:T(8,128)(2,1)}, bf16[1,64,1024]{2,1,0:T(8,128)(2,1)}, u32[]{:S(2)}, u32[]{:S(2)}) collective-permute-start(bf16[1,64,1024]{2,1,0:T(8,128)(2,1)} %get-tuple-element.7), channel_id=1, source_target_pairs={{1,0},{2,1},{3,2},{4,3},{5,4},{6,5},{7,6},{8,7},{9,8},{10,9},{11,1... | collective-permute-start | bytes 393224 | tf_op jit(solution)/shard_map/ppermute | solution.py:28
  10.3 40.9 %collective-permute-start = (bf16[1,64,1024]{2,1,0:T(8,128)(2,1)}, bf16[1,64,1024]{2,1,0:T(8,128)(2,1)}, u32[]{:S(2)}, u32[]{:S(2)}) collective-permute-start(bf16[1,64,1024]{2,1,0:T(8,128)(2,1)} %get-tuple-element.6), channel_id=1, source_target_pairs={{0,1},{1,2},{2,3},{3,4},{4,5},{5,6},{6,7},{7,8},{8,9},{9,10},{10,1... | collective-permute-start | bytes 393224 | tf_op jit(solution)/shard_map/ppermute | solution.py:27
  18.5 24.0 %collective-permute-start.5 = (bf16[1,64,1024]{1,2,0:T(8,128)(2,1)}, bf16[1,64,1024]{1,2,0:T(8,128)(2,1)S(1)}, u32[]{:S(2)}, u32[]{:S(2)}) collective-permute-start(bf16[1,64,1024]{1,2,0:T(8,128)(2,1)} %get-tuple-element.5), channel_id=1, source_target_pairs={{1,0},{2,1},{3,2},{4,3},{5,4},{6,5},{7,6},{8,7},{9,8},{10,9},{11,1... | collective-permute-start | bytes 393224 | tf_op jit(solution)/shard_map/ppermute | solution.py:28
  19.8 18.5 %collective-permute-start.3 = (s32[1,64]{1,0:T(1,128)S(1)}, s32[1,64]{1,0:T(1,128)S(1)}, u32[]{:S(2)}, u32[]{:S(2)}) collective-permute-start(s32[1,64]{1,0:T(1,128)S(1)} %get-tuple-element.9), channel_id=1, source_target_pairs={{1,0},{2,1},{3,2},{4,3},{5,4},{6,5},{7,6},{8,7},{9,8},{10,9},{11,1... | collective-permute-start | bytes 776 | tf_op jit(solution)/shard_map/ppermute | solution.py:28
  21.1 21.1 %collective-permute-start.2 = (s32[1,64]{1,0:T(1,128)S(1)}, s32[1,64]{1,0:T(1,128)S(1)}, u32[]{:S(2)}, u32[]{:S(2)}) collective-permute-start(s32[1,64]{1,0:T(1,128)S(1)} %get-tuple-element.8), channel_id=1, source_target_pairs={{0,1},{1,2},{2,3},{3,4},{4,5},{5,6},{6,7},{7,8},{8,9},{9,10},{10,1... | collective-permute-start | bytes 776 | tf_op jit(solution)/shard_map/ppermute | solution.py:27
  28.2 32.6 %all-to-all-start.2 = ((bf16[16,36,256]{2,1,0:T(8,128)(2,1)}), bf16[16,36,256]{2,1,0:T(8,128)(2,1)S(1)}, u32[]{:S(2)}, u32[]{:S(2)}) async-start(bf16[16,36,256]{2,1,0:T(8,128)(2,1)} %bitcast.21), calls=%async_computation.2 | async-start | bytes 655360 | tf_op jit(solution)/shard_map/all_to_all | solution.py:68
  38.3 9.8 %collective-permute-start.4 = (bf16[1,64,1024]{1,2,0:T(8,128)(2,1)}, bf16[1,64,1024]{1,2,0:T(8,128)(2,1)S(1)}, u32[]{:S(2)}, u32[]{:S(2)}) collective-permute-start(bf16[1,64,1024]{1,2,0:T(8,128)(2,1)} %get-tuple-element.4), channel_id=1, source_target_pairs={{0,1},{1,2},{2,3},{3,4},{4,5},{5,6},{6,7},{7,8},{8,9},{9,10},{10,1... | collective-permute-start | bytes 393224 | tf_op jit(solution)/shard_map/ppermute | solution.py:27
  42.4 0.7 copy-start.8
  50.7 0.9 copy-start.3
  53.7 3.2 %copy-start.4 = (bf16[1,128,1024]{2,1,0:T(8,128)(2,1)S(1)}, bf16[1,128,1024]{2,1,0:T(8,128)(2,1)}, u32[]{:S(2)}) copy-start(bf16[1,128,1024]{2,1,0:T(8,128)(2,1)} %param.9) | copy-start | bytes 786436
  55.9 4.9 %copy-start.1 = (f32[8,128,128]{2,1,0:T(8,128)}, f32[8,128,128]{2,1,0:T(8,128)S(1)}, u32[]{:S(2)}) copy-start(f32[8,128,128]{2,1,0:T(8,128)S(1)} %fusion.36) | copy-start | bytes 1572868
  60.8 18.4 %all-to-all-start = ((bf16[16,36,256]{2,1,0:T(8,128)(2,1)}), bf16[16,36,256]{2,1,0:T(8,128)(2,1)S(1)}, u32[]{:S(2)}, u32[]{:S(2)}) async-start(bf16[16,36,256]{2,1,0:T(8,128)(2,1)} %bitcast.12), calls=%async_computation | async-start | bytes 655360 | tf_op jit(solution)/shard_map/all_to_all | solution.py:68
  68.4 92.3 %reduce-scatter.2.cloned.1.call-start = ((), (), s32[]{:S(2)}) async-start(), calls=%async_computation.4 | async-start | bytes 3145728 | tf_op jit(solution)/shard_map/reduce_scatter | solution.py:133
  68.5 13.8 %collective-permute-start.8 = (bf16[16,36,256]{2,1,0:T(8,128)(2,1)S(1)}, bf16[16,36,256]{2,1,0:T(8,128)(2,1)S(1)}, u32[]{:S(2)}, u32[]{:S(2)}) collective-permute-start(bf16[16,36,256]{2,1,0:T(8,128)(2,1)S(1)} %all-to-all-done.2), channel_id=1, source_target_pairs={{0,1},{1,0},{2,3},{3,2},{4,5},{5,4},{6,7},{7,6},{8,9},{9,8},{10,11... | collective-permute-start | bytes 884744 | tf_op jit(solution)/shard_map/ppermute | solution.py:17
  79.2 8.6 %collective-permute-start.6 = (bf16[16,36,256]{2,1,0:T(8,128)(2,1)S(1)}, bf16[16,36,256]{2,1,0:T(8,128)(2,1)}, u32[]{:S(2)}, u32[]{:S(2)}) collective-permute-start(bf16[16,36,256]{2,1,0:T(8,128)(2,1)S(1)} %all-to-all-done), channel_id=1, source_target_pairs={{0,1},{1,0},{2,3},{3,2},{4,5},{5,4},{6,7},{7,6},{8,9},{9,8},{10,11... | collective-permute-start | bytes 884744 | tf_op jit(solution)/shard_map/ppermute | solution.py:17
  83.4 16.6 %collective-permute-start.9 = (bf16[16,36,512]{2,0,1:T(8,128)(2,1)}, bf16[16,36,512]{2,0,1:T(8,128)(2,1)}, u32[]{:S(2)}, u32[]{:S(2)}) collective-permute-start(bf16[16,36,512]{2,0,1:T(8,128)(2,1)} %copy.61), channel_id=1, source_target_pairs={{0,2},{1,3},{2,0},{3,1},{4,6},{5,7},{6,4},{7,5},{8,10},{9,11},{10,... | collective-permute-start | bytes 1769480 | tf_op jit(solution)/shard_map/ppermute | solution.py:17
  90.0 18.5 %collective-permute-start.7 = (bf16[16,36,512]{2,0,1:T(8,128)(2,1)}, bf16[16,36,512]{2,0,1:T(8,128)(2,1)}, u32[]{:S(2)}, u32[]{:S(2)}) collective-permute-start(bf16[16,36,512]{2,0,1:T(8,128)(2,1)} %copy.57), channel_id=1, source_target_pairs={{0,2},{1,3},{2,0},{3,1},{4,6},{5,7},{6,4},{7,5},{8,10},{9,11},{10,... | collective-permute-start | bytes 1769480 | tf_op jit(solution)/shard_map/ppermute | solution.py:17
  92.3 1.0 copy-start.2
  110.9 4.2 %copy-start.6 = (bf16[576,512]{1,0:T(8,128)(2,1)S(1)}, bf16[576,512]{1,0:T(8,128)(2,1)}, u32[]{:S(2)}) copy-start(bf16[576,512]{1,0:T(8,128)(2,1)} %maximum_select_fusion.9) | copy-start | bytes 1769476
  110.9 4.2 %copy-start.7 = (bf16[576,512]{1,0:T(8,128)(2,1)S(1)}, bf16[576,512]{1,0:T(8,128)(2,1)}, u32[]{:S(2)}) copy-start(bf16[576,512]{1,0:T(8,128)(2,1)} %concatenate.89) | copy-start | bytes 1769476
  114.0 1.0 copy-start.12
  122.8 32.9 %all-to-all-start.1 = ((bf16[16,36,1024]{2,1,0:T(8,128)(2,1)}), bf16[16,36,1024]{2,1,0:T(8,128)(2,1)S(1)}, u32[]{:S(2)}, u32[]{:S(2)}) async-start(bf16[16,36,1024]{2,1,0:T(8,128)(2,1)} %reshape.187), calls=%async_computation.1 | async-start | bytes 2621440 | tf_op jit(solution)/shard_map/all_to_all | solution.py:82
  158.0 1.0 copy-start.5
Sparse Core Ops, SparseCore 0:
  118.4 10.0 reduce-scatter.1
where the time goes:
time: 170 us; the launch traced here: 168 us
  waiting for transfers between devices  54.7 us (32%)
  starting transfers between devices  47.5 us (28%)
  local copies, waits for them, and re-layouts  26.7 us (16%)
  matrix products  16 us (9%)
  between operations  14.4 us (8%)
  other arithmetic  8.35 us (5%)
    all_to_all x1, waiting for transfers between devices, collect(): lax.all_to_all(partial_value, 'ep', split_axis=0, concat_axis=0, tiled=True)  24.8 us
    all_to_all x2, starting transfers between devices, deliver(): lax.all_to_all(sliced, 'ep', split_axis=0, concat_axis=0, tiled=True)  16.7 us
    ppermute x4, waiting for transfers between devices, partner_2(): return lax.ppermute(value, axis, pairs)  16.2 us
    ppermute x3, starting transfers between devices, with_halo(): before = lax.ppermute(last, axis, up)  15.4 us
    all_to_all x2, waiting for transfers between devices, deliver(): lax.all_to_all(sliced, 'ep', split_axis=0, concat_axis=0, tiled=True)  8.74 us
    all_to_all x1, starting transfers between devices, collect(): lax.all_to_all(partial_value, 'ep', split_axis=0, concat_axis=0, tiled=True)  6.06 us
    ppermute x4, starting transfers between devices, partner_2(): return lax.ppermute(value, axis, pairs)  5.48 us
    unnamed x28, local copies, waits for them, and re-layouts  5.24 us
  transfers between devices with their start and end apart: 14, of which 7 were waited for; matrix products, arithmetic and copies ran while one was open for 22% of the time, Pallas kernels for 0%

commit v1 on v0

v1 whole, which is shorter than its diff:
```python
import functools

import jax
import jax.numpy as jnp
from jax import lax
from jax.experimental import pallas as pl
from jax.experimental.pallas import tpu as pltpu
from jax.sharding import PartitionSpec as P

HEADS = 8
SPLIT = 4
HALO = 64
NEG_FILL = -1e30
PARTS = 4
BF16 = jnp.bfloat16
F32 = jnp.float32
VMEM_LIMIT = 48 * 1024 * 1024


def call(body, outs, args, flops=0, **kwargs):
    size = sum(a.size * a.dtype.itemsize for a in args) + sum(o.size * o.dtype.itemsize for o in outs)
    return pl.pallas_call(
        body,
        out_shape=outs,
        compiler_params=pltpu.CompilerParams(vmem_limit_bytes=VMEM_LIMIT),
        cost_estimate=pl.CostEstimate(flops=flops, bytes_accessed=size, transcendentals=0),
        **kwargs,
    )(*args)


def dot(a, b, contract=(1, 0)):
    return lax.dot_general(
        a, b, (((contract[0],), (contract[1],)), ((), ())), preferred_element_type=F32
    )


def out(*shape):
    return jax.ShapeDtypeStruct(shape, BF16)


def iota(shape, dim):
    return lax.broadcasted_iota(jnp.int32, shape, dim)


def one_hot(condition):
    return jnp.where(condition, 1.0, 0.0).astype(BF16)


def halo_body(key_ref, value_ref, mask_ref, up_ref, down_ref):
    rows = key_ref.shape[1]
    width = key_ref.shape[2] // HEADS
    for message, first in ((up_ref, rows - HALO), (down_ref, 0)):
        for head in range(HEADS):
            columns = slice(head * width, (head + 1) * width)
            message[head * HALO : (head + 1) * HALO, :] = key_ref[0, first : first + HALO, columns]
            start = (HEADS + head) * HALO
            message[start : start + HALO, :] = value_ref[0, first : first + HALO, columns]
        mask = mask_ref[:, first : first + HALO].astype(F32)
        mask = jnp.concatenate([mask, jnp.zeros((1, width - HALO), F32)], axis=1)
        message[2 * HEADS * HALO :, :] = jnp.broadcast_to(mask, (16, width)).astype(BF16)


def slots_by_row(labels):
    count = labels.shape[1]
    before = iota((count, count), 0) < iota((count, count), 1)
    as_column = jnp.sum(
        jnp.where(iota((count, count), 0) == iota((count, count), 1), labels, 0), axis=1, keepdims=True
    )
    return jnp.sum(jnp.where(before & (as_column == labels), 1, 0), axis=0, keepdims=True)


def pack(rows, labels, home, message_refs, capacity):
    count, features = rows.shape
    width = features // PARTS
    slot = slots_by_row(labels)
    stacked = jnp.concatenate([rows[:, j * width : (j + 1) * width] for j in range(PARTS)], axis=0)
    height = message_refs[0].shape[0]
    for k, message in enumerate(message_refs):
        mine = labels == (home ^ k)
        places = [
            one_hot(mine & (slot + j * capacity == iota((height, count), 0))) for j in range(PARTS)
        ]
        message[...] = dot(jnp.concatenate(places, axis=1), stacked).astype(BF16)


def pack_body(capacity, rows_ref, label_ref, *message_refs):
    home = lax.axis_index("ep") // SPLIT
    pack(rows_ref[0], label_ref[...], home, message_refs, capacity)


def moving(height, block, count, capacity, which):
    row = iota((height, count * block), 0)
    group = jnp.zeros_like(row)
    for a in range(1, count):
        group += jnp.where(row >= a * capacity, 1, 0)
    inside = row < count * capacity
    return one_hot(inside & (iota(row.shape, 1) == row + group * (block - capacity) + which * capacity))


def assemble_body(capacity, experts, *refs):
    *message_refs, rows_ref = refs
    stacked = jnp.concatenate([m[...] for m in message_refs], axis=0)
    block, width = message_refs[0].shape
    for j in range(PARTS):
        place = moving(rows_ref.shape[0], block, experts, capacity, j)
        rows_ref[:, j * width : (j + 1) * width] = dot(place, stacked).astype(BF16)


def attention_body(
    capacity,
    token_ref,
    query_ref,
    key_ref,
    value_ref,
    mask_ref,
    label_ref,
    before_ref,
    after_ref,
    mixed_ref,
    *message_refs,
):
    rows, features = query_ref.shape[1:]
    width = features // HEADS
    position = lax.axis_index("ep")
    last = lax.axis_size("ep") - 1
    mask_row = 2 * HEADS * HALO
    mask = jnp.concatenate(
        [
            before_ref[mask_row : mask_row + 1, :HALO].astype(F32) * jnp.where(position > 0, 1.0, 0.0),
            mask_ref[...].astype(F32),
            after_ref[mask_row : mask_row + 1, :HALO].astype(F32) * jnp.where(position < last, 1.0, 0.0),
        ],
        axis=1,
    )
    count = rows + 2 * HALO
    offset = iota((rows, count), 1) - HALO - iota((rows, count), 0)
    usable = (jnp.abs(offset) <= HALO) & ((mask > 0.5) | (offset == 0))
    scale = width ** (-0.5)
    for head in range(HEADS):
        columns = slice(head * width, (head + 1) * width)
        at, value_at = head * HALO, (HEADS + head) * HALO
        keys = jnp.concatenate(
            [before_ref[at : at + HALO, :], key_ref[0, :, columns], after_ref[at : at + HALO, :]], axis=0
        )
        values = jnp.concatenate(
            [
                before_ref[value_at : value_at + HALO, :],
                value_ref[0, :, columns],
                after_ref[value_at : value_at + HALO, :],
            ],
            axis=0,
        )
        scores = dot(query_ref[0, :, columns], keys, (1, 1)) * scale
        scores = jnp.where(usable, scores, NEG_FILL)
        raised = jnp.exp(scores - jnp.max(scores, axis=1, keepdims=True))
        soft = (raised * (1.0 / jnp.sum(raised, axis=1, keepdims=True))).astype(BF16)
        mixed_ref[:, columns] = (token_ref[0, :, columns].astype(F32) + dot(soft, values)).astype(BF16)
    home = position // SPLIT
    pack(mixed_ref[...], label_ref[...], home, message_refs, capacity)


def expert_body(*refs):
    row_refs, (in_ref, out_ref), hidden_ref, partial_refs = refs[:SPLIT], refs[SPLIT : SPLIT + 2], refs[SPLIT + 2], refs[SPLIT + 3 :]
    rows = jnp.concatenate([r[...] for r in row_refs], axis=0)
    step = 256
    for at in range(0, in_ref.shape[1], step):
        pre_act = dot(rows, in_ref[:, at : at + step])
        hidden_ref[:, at : at + step] = jax.nn.gelu(pre_act).astype(BF16)
    hidden = hidden_ref[...]
    each = row_refs[0].shape[0]
    for at in range(0, out_ref.shape[2], step):
        partial = dot(hidden, out_ref[0, :, at : at + step]).astype(BF16)
        for k, partial_ref in enumerate(partial_refs):
            partial_ref[:, at : at + step] = partial[k * each : (k + 1) * each]


def combine_body(capacity, experts, *refs):
    partial_refs, message_refs = refs[:SPLIT], refs[SPLIT:]
    total = partial_refs[0][...].astype(F32)
    for p in partial_refs[1:]:
        total += p[...].astype(F32)
    total = total.astype(BF16)
    height, features = total.shape
    width = features // PARTS
    stacked = jnp.concatenate([total[:, j * width : (j + 1) * width] for j in range(PARTS)], axis=0)
    for k, message in enumerate(message_refs):
        place = moving(message.shape[0], height, PARTS, capacity, k)
        message[...] = dot(place, stacked).astype(BF16)


def finish_body(capacity, mixed_ref, label_ref, *refs):
    *message_refs, layer_ref = refs
    home = lax.axis_index("ep") // SPLIT
    labels = label_ref[...]
    count = labels.shape[1]
    slot = slots_by_row(labels)
    block, width = message_refs[0].shape
    stacked = jnp.concatenate([m[...] for m in message_refs], axis=0)
    for j in range(PARTS):
        places = [
            one_hot((labels == (home ^ k)) & (slot + j * capacity == iota((block, count), 0)))
            for k in range(len(message_refs))
        ]
        taken = dot(jnp.concatenate(places, axis=0), stacked, (0, 0))
        columns = slice(j * width, (j + 1) * width)
        layer_ref[0, :, columns] = (mixed_ref[:, columns].astype(F32) + taken).astype(BF16)


def term_body(hidden_ref, *refs):
    *cot_refs, term_ref = refs
    cot = jnp.concatenate([c[...] for c in cot_refs], axis=0)
    step = 256
    for at in range(0, hidden_ref.shape[1], step):
        term_ref[at : at + step, :] = dot(hidden_ref[:, at : at + step], cot, (0, 0)).astype(BF16)


def permute(value, apart):
    return lax.ppermute(value, "ep", [(i, i ^ apart) for i in range(lax.axis_size("ep"))])


def along_line(messages):
    return [messages[0]] + [permute(m, SPLIT * k) for k, m in enumerate(messages) if k > 0]


def in_plane(rows):
    got = {k: permute(rows[k], k) for k in range(SPLIT - 1, 0, -1)}
    return [rows[0]] + [got[k] for k in range(1, SPLIT)]


def shards(tokens, queries, keys, values, key_mask, labels, cotangent, weight_in, weight_out):
    rows_here, features = tokens.shape[1:]
    axis_count = lax.axis_size("ep")
    groups = lax.axis_size("grp")
    experts = axis_count // SPLIT
    capacity = rows_here // experts + max(1, rows_here // (8 * experts))
    width = features // PARTS
    height = -(-PARTS * capacity // 16) * 16
    plane_rows = -(-experts * capacity // 16) * 16
    hidden_units = weight_in.shape[1]
    head_width = features // HEADS
    label_row = labels.reshape(1, rows_here)
    message = out(height, width)

    halo = out(2 * HEADS * HALO + 16, head_width)
    up, down = call(halo_body, (halo, halo), (keys, values, key_mask))
    steps = [(i, i + 1) for i in range(axis_count - 1)]
    before = lax.ppermute(up, "ep", steps)
    after = lax.ppermute(down, "ep", [(j, i) for i, j in steps])

    sent = call(functools.partial(pack_body, capacity), [message] * experts, (cotangent, label_row))
    assemble = functools.partial(assemble_body, capacity, experts)
    (cot_rows,) = call(assemble, [out(plane_rows, features)], along_line(sent))
    cot_all = in_plane([cot_rows] * SPLIT)

    mixed, *sent = call(
        functools.partial(attention_body, capacity),
        [out(rows_here, features)] + [message] * experts,
        (tokens, queries, keys, values, key_mask, label_row, before, after),
        flops=4 * rows_here * (rows_here + 2 * HALO) * features,
    )
    (rows,) = call(assemble, [out(plane_rows, features)], along_line(sent))
    rows_all = in_plane([rows] * SPLIT)

    hidden, *partials = call(
        expert_body,
        [out(SPLIT * plane_rows, hidden_units)] + [out(plane_rows, features)] * SPLIT,
        (*rows_all, weight_in, weight_out),
        flops=4 * SPLIT * plane_rows * features * hidden_units,
    )
    partials = in_plane(partials)
    sent = call(functools.partial(combine_body, capacity, experts), [message] * experts, partials)
    back = along_line(sent)
    (layer_out,) = call(
        functools.partial(finish_body, capacity), [out(1, rows_here, features)], (mixed, label_row, *back)
    )

    (term,) = call(
        term_body,
        [out(hidden_units, features)],
        (hidden, *cot_all),
        flops=2 * SPLIT * plane_rows * features * hidden_units,
    )
    if groups == 2:
        group = lax.axis_index("grp")
        half = hidden_units // 2
        mine = lax.dynamic_slice_in_dim(term, group * half, half, axis=0)
        other = lax.dynamic_slice_in_dim(term, (1 - group) * half, half, axis=0)
        theirs = lax.ppermute(other, "grp", [(0, 1), (1, 0)])
        grad = (mine.astype(F32) + theirs.astype(F32)).astype(BF16)
    else:
        grad = lax.psum_scatter(term, "grp", scatter_dimension=0, tiled=True)
    return (layer_out, grad[None])


def solution(mesh):
    in_specs = (
        P("grp", "ep", None),
        P("grp", "ep", None),
        P("grp", "ep", None),
        P("grp", "ep", None),
        P("grp", "ep"),
        P("grp", "ep", None),
        P("grp", "ep", None),
        P(None, "ep"),
        P("ep", None, None),
    )
    out_specs = (P("grp", "ep", None), P("ep", "grp", None))
    return jax.shard_map(shards, mesh=mesh, in_specs=in_specs, out_specs=out_specs, check_vma=False)
```

time: 170 us -> 97.1 us (0.57); the launches traced: 168 us -> 96.7 us
  local copies, waits for them, and re-layouts: 26.7 us -> 7.75 us
  starting transfers between devices: 47.5 us -> 30.5 us
  matrix products: 16 us -> 0 us
  between operations: 14.4 us -> 0.76 us
  Pallas kernels: 0 us -> 11 us
  waiting for transfers between devices: 54.7 us -> 44.1 us
  other arithmetic: 8.35 us -> 2.59 us
    all_to_all x3 -> x0, waiting for transfers between devices: 33.5 us -> none  [the longest x1 24.8 us: collect(): lax.all_to_all(partial_value, 'ep', split_axis=0, concat_axis=0, tiled=True)]
    ppermute x10 -> x21, waiting for transfers between devices: 21.2 us -> 44.1 us  [the longest x18 32.1 us: permute(): lax.ppermute(value, 'ep', [(i, i ^ apart) for i in range(lax.axis_size('e...]
    all_to_all x3 -> x0, starting transfers between devices: 22.7 us -> none  [the longest x2 16.7 us: deliver(): lax.all_to_all(sliced, 'ep', split_axis=0, concat_axis=0, tiled=True)]
    dot_general x7 -> x0, matrix products: 15.4 us -> none  [the longest x1 3.34 us: shards(): jnp.dot(hidden, weight_out[0], preferred_element_type=jnp.float32)]
    pallas_call x0 -> x9, Pallas kernels: none -> 11 us  [call(): pl.pallas_call(body, out_shape=outs, compiler_params=pltpu.CompilerParams...]
    reshape x6 -> x0, local copies, waits for them, and re-layouts: 6.89 us -> none  [the longest x2 3.03 us: window_attention(): return attended.reshape(query_count, HEADS * head_width)]
    ppermute x10 -> x21, starting transfers between devices: 24.7 us -> 30.5 us  [the longest x18 24.3 us: permute(): lax.ppermute(value, 'ep', [(i, i ^ apart) for i in range(lax.axis_size('e...]
    concatenate x7 -> x0, local copies, waits for them, and re-layouts: 4.78 us -> none  [the longest x6 3.79 us: deliver(): jnp.concatenate([partner, gathered], axis=2)]
  transfers between devices with their start and end apart: 14 -> 21, of which waited for: 7 -> 13; matrix products, arithmetic and copies ran while one was open for 22% -> 0% of each run, Pallas kernels for 0% -> 7%
where the time goes in v1:
time: 97.1 us; the launch traced here: 96.7 us
  waiting for transfers between devices  44.1 us (45%)
  starting transfers between devices  30.5 us (31%)
  Pallas kernels  11 us (11%)
  local copies, waits for them, and re-layouts  7.75 us (8%)
  other arithmetic  2.59 us (3%)
    ppermute x18, waiting for transfers between devices, permute(): lax.ppermute(value, 'ep', [(i, i ^ apart) for i in range(lax.axis_size('e...  32.1 us
    ppermute x18, starting transfers between devices, permute(): lax.ppermute(value, 'ep', [(i, i ^ apart) for i in range(lax.axis_size('e...  24.3 us
    pallas_call x9, Pallas kernels, call(): pl.pallas_call(body, out_shape=outs, compiler_params=pltpu.CompilerParams...  11 us
    ppermute x1, waiting for transfers between devices, shards(): before = lax.ppermute(up, 'ep', steps)  10.1 us
    unnamed x18, local copies, waits for them, and re-layouts  6.7 us
    ppermute x1, starting transfers between devices, shards(): before = lax.ppermute(up, 'ep', steps)  4.85 us
    broadcast_in_dim x1, other arithmetic, shards(): return (layer_out, grad[None])  2.59 us
  transfers between devices with their start and end apart: 21, of which 13 were waited for; matrix products, arithmetic and copies ran while one was open for 0% of the time, Pallas kernels for 7%

profile of v1, /device:TPU:0, one launch (start us, length us, event | category | flops | bytes accessed | tf_op | source)
XLA Modules:
  0.0 96.7 jit_solution(10595836527267390202)
XLA Ops:
  3.3 4.8 %collective-permute-start = (bf16[1040,128]{1,0:T(8,128)(2,1)S(1)}, bf16[1040,128]{1,0:T(8,128)(2,1)S(1)}, u32[]{:S(2)}, u32[]{:S(2)}) collective-permute-start(bf16[1040,128]{1,0:T(8,128)(2,1)S(1)} %get-tuple-element.22), channel_id=1, source_target_pairs={{0,1},{1,2},{2,3},{3,4},{4,5},{5,6},{6,7},{7,8},{8,9},{9,10},{10,1... | collective-permute-start | bytes 798728 | tf_op jit(solution)/shard_map/ppermute | solution.py:247
  8.2 1.3 %collective-permute-start.1 = (bf16[1040,128]{1,0:T(8,128)(2,1)S(1)}, bf16[1040,128]{1,0:T(8,128)(2,1)S(1)}, u32[]{:S(2)}, u32[]{:S(2)}) collective-permute-start(bf16[1040,128]{1,0:T(8,128)(2,1)S(1)} %get-tuple-element.23), channel_id=1, source_target_pairs={{1,0},{2,1},{3,2},{4,3},{5,4},{6,5},{7,6},{8,7},{9,8},{10,9},{11,1... | collective-permute-start | bytes 798728 | tf_op jit(solution)/shard_map/ppermute | solution.py:248
  9.5 10.1 %collective-permute-done.before_ref = bf16[1040,128]{1,0:T(8,128)(2,1)S(1)} collective-permute-done((bf16[1040,128]{1,0:T(8,128)(2,1)S(1)}, bf16[1040,128]{1,0:T(8,128)(2,1)S(1)}, u32[]{:S(2)}, u32[]{:S(2)}) %collective-permute-start) | collective-permute-done | bytes 266272 | tf_op jit(solution)/shard_map/ppermute | solution.py:247
  19.5 1.9 %collective-permute-done.1.after_ref = bf16[1040,128]{1,0:T(8,128)(2,1)S(1)} collective-permute-done((bf16[1040,128]{1,0:T(8,128)(2,1)S(1)}, bf16[1040,128]{1,0:T(8,128)(2,1)S(1)}, u32[]{:S(2)}, u32[]{:S(2)}) %collective-permute-start.1) | collective-permute-done | bytes 266272 | tf_op jit(solution)/shard_map/ppermute | solution.py:248
  24.0 1.5 %shard_map.105 = (bf16[128,1024]{1,0:T(8,128)(2,1)S(1)}, bf16[144,256]{1,0:T(8,128)(2,1)S(1)}, bf16[144,256]{1,0:T(8,128)(2,1)S(1)}, bf16[144,256]{1,0:T(8,128)(2,1)S(1)}, bf16[144,256]{1,0:T(8,128)(2,1)S(1)}) custom-call(bf16[1,128,1024]{2,1,0:T(8,128)(2,1)S(1)} %copy-done.3, bf16[1,128,1024]{2,1,0:T(8,128)(2,1)S(1)} %copy-done.4, ...), custom_call_target="tpu_custom_call" | custom-call | flops 134217728 | bytes 2139136 | tf_op jit(solution)/shard_map/pallas_call | solution.py:22
  25.5 1.6 %collective-permute-start.2 = (bf16[144,256]{1,0:T(8,128)(2,1)S(1)}, bf16[144,256]{1,0:T(8,128)(2,1)S(1)}, u32[]{:S(2)}, u32[]{:S(2)}) collective-permute-start(bf16[144,256]{1,0:T(8,128)(2,1)S(1)} %get-tuple-element.26), channel_id=1, source_target_pairs={{0,4},{1,5},{2,6},{3,7},{4,0},{5,1},{6,2},{7,3},{8,12},{9,13},{10,... | collective-permute-start | bytes 221192 | tf_op jit(solution)/shard_map/ppermute | solution.py:218
  27.1 2.6 %collective-permute-start.3 = (bf16[144,256]{1,0:T(8,128)(2,1)S(1)}, bf16[144,256]{1,0:T(8,128)(2,1)S(1)}, u32[]{:S(2)}, u32[]{:S(2)}) collective-permute-start(bf16[144,256]{1,0:T(8,128)(2,1)S(1)} %get-tuple-element.27), channel_id=1, source_target_pairs={{0,8},{1,9},{2,10},{3,11},{4,12},{5,13},{6,14},{7,15},{8,0},{9,1},... | collective-permute-start | bytes 221192 | tf_op jit(solution)/shard_map/ppermute | solution.py:218
  30.6 3.4 %collective-permute-done.3.refs_2_ = bf16[144,256]{1,0:T(8,128)(2,1)S(1)} collective-permute-done((bf16[144,256]{1,0:T(8,128)(2,1)S(1)}, bf16[144,256]{1,0:T(8,128)(2,1)S(1)}, u32[]{:S(2)}, u32[]{:S(2)}) %collective-permute-start.3) | collective-permute-done | bytes 73760 | tf_op jit(solution)/shard_map/ppermute | solution.py:218
  34.0 1.8 %collective-permute-done.4.refs_3_ = bf16[144,256]{1,0:T(8,128)(2,1)S(1)} collective-permute-done((bf16[144,256]{1,0:T(8,128)(2,1)S(1)}, bf16[144,256]{1,0:T(8,128)(2,1)S(1)}, u32[]{:S(2)}, u32[]{:S(2)}) %collective-permute-start.4) | collective-permute-done | bytes 73760 | tf_op jit(solution)/shard_map/ppermute | solution.py:218
  36.3 1.5 %collective-permute-start.5 = (bf16[144,1024]{1,0:T(8,128)(2,1)S(1)}, bf16[144,1024]{1,0:T(8,128)(2,1)S(1)}, u32[]{:S(2)}, u32[]{:S(2)}) collective-permute-start(bf16[144,1024]{1,0:T(8,128)(2,1)S(1)} %shard_map.106.refs_0_), channel_id=1, source_target_pairs={{0,1},{1,0},{2,3},{3,2},{4,5},{5,4},{6,7},{7,6},{8,9},{9,8},{10,11... | collective-permute-start | bytes 884744 | tf_op jit(solution)/shard_map/ppermute | solution.py:218
  37.9 1.9 %collective-permute-start.7 = (bf16[144,1024]{1,0:T(8,128)(2,1)S(1)}, bf16[144,1024]{1,0:T(8,128)(2,1)S(1)}, u32[]{:S(2)}, u32[]{:S(2)}) collective-permute-start(bf16[144,1024]{1,0:T(8,128)(2,1)S(1)} %shard_map.106.refs_0_), channel_id=1, source_target_pairs={{0,3},{1,2},{2,1},{3,0},{4,7},{5,6},{6,5},{7,4},{8,11},{9,10},{10,... | collective-permute-start | bytes 884744 | tf_op jit(solution)/shard_map/ppermute | solution.py:218
  41.1 1.6 %collective-permute-start.15 = (bf16[144,256]{1,0:T(8,128)(2,1)S(1)}, bf16[144,256]{1,0:T(8,128)(2,1)S(1)}, u32[]{:S(2)}, u32[]{:S(2)}) collective-permute-start(bf16[144,256]{1,0:T(8,128)(2,1)S(1)} %get-tuple-element.40), channel_id=1, source_target_pairs={{0,8},{1,9},{2,10},{3,11},{4,12},{5,13},{6,14},{7,15},{8,0},{9,1},... | collective-permute-start | bytes 221192 | tf_op jit(solution)/shard_map/ppermute | solution.py:218
  42.8 1.9 %collective-permute-done.14.refs_1_ = bf16[144,256]{1,0:T(8,128)(2,1)S(1)} collective-permute-done((bf16[144,256]{1,0:T(8,128)(2,1)S(1)}, bf16[144,256]{1,0:T(8,128)(2,1)S(1)}, u32[]{:S(2)}, u32[]{:S(2)}) %collective-permute-start.14) | collective-permute-done | bytes 73760 | tf_op jit(solution)/shard_map/ppermute | solution.py:218
  44.7 2.3 %collective-permute-start.16 = (bf16[144,256]{1,0:T(8,128)(2,1)S(1)}, bf16[144,256]{1,0:T(8,128)(2,1)S(1)}, u32[]{:S(2)}, u32[]{:S(2)}) collective-permute-start(bf16[144,256]{1,0:T(8,128)(2,1)S(1)} %get-tuple-element.41), channel_id=1, source_target_pairs={{0,12},{1,13},{2,14},{3,15},{4,8},{5,9},{6,10},{7,11},{8,4},{9,5},... | collective-permute-start | bytes 221192 | tf_op jit(solution)/shard_map/ppermute | solution.py:218
  47.8 3.0 %collective-permute-done.16.refs_3_ = bf16[144,256]{1,0:T(8,128)(2,1)S(1)} collective-permute-done((bf16[144,256]{1,0:T(8,128)(2,1)S(1)}, bf16[144,256]{1,0:T(8,128)(2,1)S(1)}, u32[]{:S(2)}, u32[]{:S(2)}) %collective-permute-start.16) | collective-permute-done | bytes 73760 | tf_op jit(solution)/shard_map/ppermute | solution.py:218
  51.3 1.5 %collective-permute-start.17 = (bf16[144,1024]{1,0:T(8,128)(2,1)S(1)}, bf16[144,1024]{1,0:T(8,128)(2,1)S(1)}, u32[]{:S(2)}, u32[]{:S(2)}) collective-permute-start(bf16[144,1024]{1,0:T(8,128)(2,1)S(1)} %shard_map.111.refs_0_), channel_id=1, source_target_pairs={{0,1},{1,0},{2,3},{3,2},{4,5},{5,4},{6,7},{7,6},{8,9},{9,8},{10,11... | collective-permute-start | bytes 884744 | tf_op jit(solution)/shard_map/ppermute | solution.py:218
  52.9 1.9 %collective-permute-start.19 = (bf16[144,1024]{1,0:T(8,128)(2,1)S(1)}, bf16[144,1024]{1,0:T(8,128)(2,1)S(1)}, u32[]{:S(2)}, u32[]{:S(2)}) collective-permute-start(bf16[144,1024]{1,0:T(8,128)(2,1)S(1)} %shard_map.111.refs_0_), channel_id=1, source_target_pairs={{0,3},{1,2},{2,1},{3,0},{4,7},{5,6},{6,5},{7,4},{8,11},{9,10},{10,... | collective-permute-start | bytes 884744 | tf_op jit(solution)/shard_map/ppermute | solution.py:218
  54.8 1.6 %copy-done.8 = bf16[1024,1024]{1,0:T(8,128)(2,1)S(1)} copy-done((bf16[1024,1024]{1,0:T(8,128)(2,1)S(1)}, bf16[1024,1024]{1,0:T(8,128)(2,1)}, u32[]{:S(2)}) %copy-start.8) | copy-done | bytes 2097176
  56.4 4.6 %shard_map.107 = (bf16[576,1024]{1,0:T(8,128)(2,1)S(1)}, bf16[144,1024]{1,0:T(8,128)(2,1)S(1)}, bf16[144,1024]{1,0:T(8,128)(2,1)S(1)}, bf16[144,1024]{1,0:T(8,128)(2,1)S(1)}, bf16[144,1024]{1,0:T(8,128)(2,1)S(1)}) custom-call(bf16[144,1024]{1,0:T(8,128)(2,1)S(1)} %shard_map.106.refs_0_, bf16[144,1024]{1,0:T(8,128)(2,1)S(1)} %collective-permute-done.5.refs_1_, ...), custom_call_target="tpu_custom_call" | custom-call | flops 2415919104 | bytes 7733248 | tf_op jit(solution)/shard_map/pallas_call | solution.py:22
  61.1 2.7 %collective-permute-done.18.refs_2_ = bf16[144,1024]{1,0:T(8,128)(2,1)S(1)} collective-permute-done((bf16[144,1024]{1,0:T(8,128)(2,1)S(1)}, bf16[144,1024]{1,0:T(8,128)(2,1)S(1)}, u32[]{:S(2)}, u32[]{:S(2)}) %collective-permute-start.18) | collective-permute-done | bytes 294944 | tf_op jit(solution)/shard_map/ppermute | solution.py:218
  63.8 1.8 %shard_map.112 = bf16[1024,1024]{1,0:T(8,128)(2,1)S(1)} custom-call(bf16[576,1024]{1,0:T(8,128)(2,1)S(1)} %get-tuple-element.37.hidden_ref, bf16[144,1024]{1,0:T(8,128)(2,1)S(1)} %shard_map.111.refs_0_, bf16[144,1024]{1,0:T(8,128)(2,1)S(1)} %collective-permute-done.17.refs_1_, bf16[144,1024]{1,0:T(8,128)(2,1)S(1)} %collective-permute-done.18.refs_2_, ...), custom_call_target="tpu_custom_call" | custom-call | flops 1207959552 | bytes 4456448 | tf_op jit(solution)/shard_map/pallas_call | solution.py:22
  65.6 1.0 %constant_dynamic-slice_fusion = bf16[512,1024]{1,0:T(8,128)(2,1)} fusion(bf16[1024,1024]{1,0:T(8,128)(2,1)S(1)} %shard_map.112, s32[]{:T(128)S(6)} %select_n.7), kind=kLoop, calls=%fused_computation.2 | loop fusion | bytes 2097156 | tf_op jit(solution)/shard_map/dynamic_slice | solution.py:287
  67.5 1.3 %collective-permute-start.9 = (bf16[144,1024]{1,0:T(8,128)(2,1)S(1)}, bf16[144,1024]{1,0:T(8,128)(2,1)S(1)}, u32[]{:S(2)}, u32[]{:S(2)}) collective-permute-start(bf16[144,1024]{1,0:T(8,128)(2,1)S(1)} %get-tuple-element.31), channel_id=1, source_target_pairs={{0,2},{1,3},{2,0},{3,1},{4,6},{5,7},{6,4},{7,5},{8,10},{9,11},{10,... | collective-permute-start | bytes 884744 | tf_op jit(solution)/shard_map/ppermute | solution.py:218
  68.8 1.4 %collective-permute-start.10 = (bf16[144,1024]{1,0:T(8,128)(2,1)S(1)}, bf16[144,1024]{1,0:T(8,128)(2,1)S(1)}, u32[]{:S(2)}, u32[]{:S(2)}) collective-permute-start(bf16[144,1024]{1,0:T(8,128)(2,1)S(1)} %get-tuple-element.32), channel_id=1, source_target_pairs={{0,3},{1,2},{2,1},{3,0},{4,7},{5,6},{6,5},{7,4},{8,11},{9,10},{10,... | collective-permute-start | bytes 884744 | tf_op jit(solution)/shard_map/ppermute | solution.py:218
  70.2 6.3 %collective-permute-done.8.refs_1_ = bf16[144,1024]{1,0:T(8,128)(2,1)S(1)} collective-permute-done((bf16[144,1024]{1,0:T(8,128)(2,1)S(1)}, bf16[144,1024]{1,0:T(8,128)(2,1)S(1)}, u32[]{:S(2)}, u32[]{:S(2)}) %collective-permute-start.8) | collective-permute-done | bytes 294944 | tf_op jit(solution)/shard_map/ppermute | solution.py:218
  76.5 6.4 %collective-permute-done.9.refs_2_ = bf16[144,1024]{1,0:T(8,128)(2,1)S(1)} collective-permute-done((bf16[144,1024]{1,0:T(8,128)(2,1)S(1)}, bf16[144,1024]{1,0:T(8,128)(2,1)S(1)}, u32[]{:S(2)}, u32[]{:S(2)}) %collective-permute-start.9) | collective-permute-done | bytes 294944 | tf_op jit(solution)/shard_map/ppermute | solution.py:218
  83.5 1.1 %collective-permute-start.11 = (bf16[144,256]{1,0:T(8,128)(2,1)S(1)}, bf16[144,256]{1,0:T(8,128)(2,1)S(1)}, u32[]{:S(2)}, u32[]{:S(2)}) collective-permute-start(bf16[144,256]{1,0:T(8,128)(2,1)S(1)} %get-tuple-element.34), channel_id=1, source_target_pairs={{0,4},{1,5},{2,6},{3,7},{4,0},{5,1},{6,2},{7,3},{8,12},{9,13},{10,... | collective-permute-start | bytes 221192 | tf_op jit(solution)/shard_map/ppermute | solution.py:218
  84.5 1.4 %collective-permute-start.12 = (bf16[144,256]{1,0:T(8,128)(2,1)S(1)}, bf16[144,256]{1,0:T(8,128)(2,1)S(1)}, u32[]{:S(2)}, u32[]{:S(2)}) collective-permute-start(bf16[144,256]{1,0:T(8,128)(2,1)S(1)} %get-tuple-element.35), channel_id=1, source_target_pairs={{0,8},{1,9},{2,10},{3,11},{4,12},{5,13},{6,14},{7,15},{8,0},{9,1},... | collective-permute-start | bytes 221192 | tf_op jit(solution)/shard_map/ppermute | solution.py:218
  86.0 1.9 %collective-permute-start.13 = (bf16[144,256]{1,0:T(8,128)(2,1)S(1)}, bf16[144,256]{1,0:T(8,128)(2,1)S(1)}, u32[]{:S(2)}, u32[]{:S(2)}) collective-permute-start(bf16[144,256]{1,0:T(8,128)(2,1)S(1)} %get-tuple-element.36), channel_id=1, source_target_pairs={{0,12},{1,13},{2,14},{3,15},{4,8},{5,9},{6,10},{7,11},{8,4},{9,5},... | collective-permute-start | bytes 221192 | tf_op jit(solution)/shard_map/ppermute | solution.py:218
  88.6 4.2 %collective-permute-done.12.refs_2_ = bf16[144,256]{1,0:T(8,128)(2,1)S(1)} collective-permute-done((bf16[144,256]{1,0:T(8,128)(2,1)S(1)}, bf16[144,256]{1,0:T(8,128)(2,1)S(1)}, u32[]{:S(2)}, u32[]{:S(2)}) %collective-permute-start.12) | collective-permute-done | bytes 73760 | tf_op jit(solution)/shard_map/ppermute | solution.py:218
  92.8 1.3 %shard_map.109 = bf16[1,128,1024]{2,1,0:T(8,128)(2,1)} custom-call(bf16[128,1024]{1,0:T(8,128)(2,1)S(1)} %get-tuple-element.24.mixed_ref, s32[1,128]{1,0:T(1,128)S(1)} %bitcast.5, bf16[144,256]{1,0:T(8,128)(2,1)S(1)} %get-tuple-element.33.refs_0_, bf16[144,256]{1,0:T(8,128)(2,1)S(1)} %collective-permute-done.11.refs_1_, ...), custom_call_target="tpu_custom_call" | custom-call | bytes 819712 | tf_op jit(solution)/shard_map/pallas_call | solution.py:22
  94.1 2.6 %fusion = bf16[1,512,1024]{2,1,0:T(8,128)(2,1)} fusion(bf16[512,1024]{1,0:T(8,128)(2,1)} %collective-permute-done.20, bf16[1024,1024]{1,0:T(8,128)(2,1)S(1)} %shard_map.112, s32[]{:T(128)S(6)} %select_n.6), kind=kLoop, calls=%fused_computation.1 | loop fusion | flops 2097152 | bytes 3145732 | tf_op jit(solution)/shard_map/broadcast_in_dim | solution.py:292
  (39 shorter events, 11.3 us)
Async XLA Ops:
  0.6 1.0 copy-start
  1.6 0.9 copy-start.1
  2.5 0.7 copy-start.7
  3.2 36.6 %copy-start.2 = (bf16[1,128,1024]{2,1,0:T(8,128)(2,1)S(1)}, bf16[1,128,1024]{2,1,0:T(8,128)(2,1)}, u32[]{:S(2)}) copy-start(bf16[1,128,1024]{2,1,0:T(8,128)(2,1)} %rows_ref.1) | copy-start | bytes 786436
  3.3 16.2 %collective-permute-start = (bf16[1040,128]{1,0:T(8,128)(2,1)S(1)}, bf16[1040,128]{1,0:T(8,128)(2,1)S(1)}, u32[]{:S(2)}, u32[]{:S(2)}) collective-permute-start(bf16[1040,128]{1,0:T(8,128)(2,1)S(1)} %get-tuple-element.22), channel_id=1, source_target_pairs={{0,1},{1,2},{2,3},{3,4},{4,5},{5,6},{6,7},{7,8},{8,9},{9,10},{10,1... | collective-permute-start | bytes 798728 | tf_op jit(solution)/shard_map/ppermute | solution.py:247
  8.2 13.3 %collective-permute-start.1 = (bf16[1040,128]{1,0:T(8,128)(2,1)S(1)}, bf16[1040,128]{1,0:T(8,128)(2,1)S(1)}, u32[]{:S(2)}, u32[]{:S(2)}) collective-permute-start(bf16[1040,128]{1,0:T(8,128)(2,1)S(1)} %get-tuple-element.23), channel_id=1, source_target_pairs={{1,0},{2,1},{3,2},{4,3},{5,4},{6,5},{7,6},{8,7},{9,8},{10,9},{11,1... | collective-permute-start | bytes 798728 | tf_op jit(solution)/shard_map/ppermute | solution.py:248
  21.4 1.0 copy-start.3
  22.4 0.9 copy-start.4
  23.3 0.7 copy-start.5
  25.5 5.1 %collective-permute-start.2 = (bf16[144,256]{1,0:T(8,128)(2,1)S(1)}, bf16[144,256]{1,0:T(8,128)(2,1)S(1)}, u32[]{:S(2)}, u32[]{:S(2)}) collective-permute-start(bf16[144,256]{1,0:T(8,128)(2,1)S(1)} %get-tuple-element.26), channel_id=1, source_target_pairs={{0,4},{1,5},{2,6},{3,7},{4,0},{5,1},{6,2},{7,3},{8,12},{9,13},{10,... | collective-permute-start | bytes 221192 | tf_op jit(solution)/shard_map/ppermute | solution.py:218
  27.1 6.9 %collective-permute-start.3 = (bf16[144,256]{1,0:T(8,128)(2,1)S(1)}, bf16[144,256]{1,0:T(8,128)(2,1)S(1)}, u32[]{:S(2)}, u32[]{:S(2)}) collective-permute-start(bf16[144,256]{1,0:T(8,128)(2,1)S(1)} %get-tuple-element.27), channel_id=1, source_target_pairs={{0,8},{1,9},{2,10},{3,11},{4,12},{5,13},{6,14},{7,15},{8,0},{9,1},... | collective-permute-start | bytes 221192 | tf_op jit(solution)/shard_map/ppermute | solution.py:218
  29.7 6.2 %collective-permute-start.4 = (bf16[144,256]{1,0:T(8,128)(2,1)S(1)}, bf16[144,256]{1,0:T(8,128)(2,1)S(1)}, u32[]{:S(2)}, u32[]{:S(2)}) collective-permute-start(bf16[144,256]{1,0:T(8,128)(2,1)S(1)} %get-tuple-element.28), channel_id=1, source_target_pairs={{0,12},{1,13},{2,14},{3,15},{4,8},{5,9},{6,10},{7,11},{8,4},{9,5},... | collective-permute-start | bytes 221192 | tf_op jit(solution)/shard_map/ppermute | solution.py:218
  36.3 16.6 %collective-permute-start.5 = (bf16[144,1024]{1,0:T(8,128)(2,1)S(1)}, bf16[144,1024]{1,0:T(8,128)(2,1)S(1)}, u32[]{:S(2)}, u32[]{:S(2)}) collective-permute-start(bf16[144,1024]{1,0:T(8,128)(2,1)S(1)} %shard_map.106.refs_0_), channel_id=1, source_target_pairs={{0,1},{1,0},{2,3},{3,2},{4,5},{5,4},{6,7},{7,6},{8,9},{9,8},{10,11... | collective-permute-start | bytes 884744 | tf_op jit(solution)/shard_map/ppermute | solution.py:218
  37.8 17.0 %collective-permute-start.6 = (bf16[144,1024]{1,0:T(8,128)(2,1)S(1)}, bf16[144,1024]{1,0:T(8,128)(2,1)S(1)}, u32[]{:S(2)}, u32[]{:S(2)}) collective-permute-start(bf16[144,1024]{1,0:T(8,128)(2,1)S(1)} %shard_map.106.refs_0_), channel_id=1, source_target_pairs={{0,2},{1,3},{2,0},{3,1},{4,6},{5,7},{6,4},{7,5},{8,10},{9,11},{10,... | collective-permute-start | bytes 884744 | tf_op jit(solution)/shard_map/ppermute | solution.py:218
  37.9 16.9 %collective-permute-start.7 = (bf16[144,1024]{1,0:T(8,128)(2,1)S(1)}, bf16[144,1024]{1,0:T(8,128)(2,1)S(1)}, u32[]{:S(2)}, u32[]{:S(2)}) collective-permute-start(bf16[144,1024]{1,0:T(8,128)(2,1)S(1)} %shard_map.106.refs_0_), channel_id=1, source_target_pairs={{0,3},{1,2},{2,1},{3,0},{4,7},{5,6},{6,5},{7,4},{8,11},{9,10},{10,... | collective-permute-start | bytes 884744 | tf_op jit(solution)/shard_map/ppermute | solution.py:218
  40.3 4.5 %collective-permute-start.14 = (bf16[144,256]{1,0:T(8,128)(2,1)S(1)}, bf16[144,256]{1,0:T(8,128)(2,1)S(1)}, u32[]{:S(2)}, u32[]{:S(2)}) collective-permute-start(bf16[144,256]{1,0:T(8,128)(2,1)S(1)} %get-tuple-element.39), channel_id=1, source_target_pairs={{0,4},{1,5},{2,6},{3,7},{4,0},{5,1},{6,2},{7,3},{8,12},{9,13},{10,... | collective-permute-start | bytes 221192 | tf_op jit(solution)/shard_map/ppermute | solution.py:218
  41.1 6.7 %collective-permute-start.15 = (bf16[144,256]{1,0:T(8,128)(2,1)S(1)}, bf16[144,256]{1,0:T(8,128)(2,1)S(1)}, u32[]{:S(2)}, u32[]{:S(2)}) collective-permute-start(bf16[144,256]{1,0:T(8,128)(2,1)S(1)} %get-tuple-element.40), channel_id=1, source_target_pairs={{0,8},{1,9},{2,10},{3,11},{4,12},{5,13},{6,14},{7,15},{8,0},{9,1},... | collective-permute-start | bytes 221192 | tf_op jit(solution)/shard_map/ppermute | solution.py:218
  44.7 6.2 %collective-permute-start.16 = (bf16[144,256]{1,0:T(8,128)(2,1)S(1)}, bf16[144,256]{1,0:T(8,128)(2,1)S(1)}, u32[]{:S(2)}, u32[]{:S(2)}) collective-permute-start(bf16[144,256]{1,0:T(8,128)(2,1)S(1)} %get-tuple-element.41), channel_id=1, source_target_pairs={{0,12},{1,13},{2,14},{3,15},{4,8},{5,9},{6,10},{7,11},{8,4},{9,5},... | collective-permute-start | bytes 221192 | tf_op jit(solution)/shard_map/ppermute | solution.py:218
  51.3 9.8 %collective-permute-start.17 = (bf16[144,1024]{1,0:T(8,128)(2,1)S(1)}, bf16[144,1024]{1,0:T(8,128)(2,1)S(1)}, u32[]{:S(2)}, u32[]{:S(2)}) collective-permute-start(bf16[144,1024]{1,0:T(8,128)(2,1)S(1)} %shard_map.111.refs_0_), channel_id=1, source_target_pairs={{0,1},{1,0},{2,3},{3,2},{4,5},{5,4},{6,7},{7,6},{8,9},{9,8},{10,11... | collective-permute-start | bytes 884744 | tf_op jit(solution)/shard_map/ppermute | solution.py:218
  52.8 11.0 %collective-permute-start.18 = (bf16[144,1024]{1,0:T(8,128)(2,1)S(1)}, bf16[144,1024]{1,0:T(8,128)(2,1)S(1)}, u32[]{:S(2)}, u32[]{:S(2)}) collective-permute-start(bf16[144,1024]{1,0:T(8,128)(2,1)S(1)} %shard_map.111.refs_0_), channel_id=1, source_target_pairs={{0,2},{1,3},{2,0},{3,1},{4,6},{5,7},{6,4},{7,5},{8,10},{9,11},{10,... | collective-permute-start | bytes 884744 | tf_op jit(solution)/shard_map/ppermute | solution.py:218
  52.9 10.9 %collective-permute-start.19 = (bf16[144,1024]{1,0:T(8,128)(2,1)S(1)}, bf16[144,1024]{1,0:T(8,128)(2,1)S(1)}, u32[]{:S(2)}, u32[]{:S(2)}) collective-permute-start(bf16[144,1024]{1,0:T(8,128)(2,1)S(1)} %shard_map.111.refs_0_), channel_id=1, source_target_pairs={{0,3},{1,2},{2,1},{3,0},{4,7},{5,6},{6,5},{7,4},{8,11},{9,10},{10,... | collective-permute-start | bytes 884744 | tf_op jit(solution)/shard_map/ppermute | solution.py:218
  54.8 1.6 %copy-start.8 = (bf16[1024,1024]{1,0:T(8,128)(2,1)S(1)}, bf16[1024,1024]{1,0:T(8,128)(2,1)}, u32[]{:S(2)}) copy-start(bf16[1024,1024]{1,0:T(8,128)(2,1)} %refs_4_.1) | copy-start | bytes 6291460
  65.6 27.2 %copy-start.6 = (s32[1,128,1]{1,2,0:T(1,128)S(1)}, s32[1,128,1]{1,2,0:T(1,128)}, u32[]{:S(2)}) copy-start(s32[1,128,1]{1,2,0:T(1,128)} %param.14) | copy-start | bytes 1540
  66.7 27.4 %collective-permute-start.20 = (bf16[512,1024]{1,0:T(8,128)(2,1)}, bf16[512,1024]{1,0:T(8,128)(2,1)}, u32[]{:S(2)}, u32[]{:S(2)}) collective-permute-start(bf16[512,1024]{1,0:T(8,128)(2,1)} %constant_dynamic-slice_fusion), channel_id=1, source_target_pairs={{0,16},{16,0},{1,17},{17,1},{2,18},{18,2},{3,19},{19,3},{4,20},{20... | collective-permute-start | bytes 3145736 | tf_op jit(solution)/shard_map/ppermute | solution.py:288
  66.7 9.8 %collective-permute-start.8 = (bf16[144,1024]{1,0:T(8,128)(2,1)S(1)}, bf16[144,1024]{1,0:T(8,128)(2,1)S(1)}, u32[]{:S(2)}, u32[]{:S(2)}) collective-permute-start(bf16[144,1024]{1,0:T(8,128)(2,1)S(1)} %get-tuple-element.30), channel_id=1, source_target_pairs={{0,1},{1,0},{2,3},{3,2},{4,5},{5,4},{6,7},{7,6},{8,9},{9,8},{10,11... | collective-permute-start | bytes 884744 | tf_op jit(solution)/shard_map/ppermute | solution.py:218
  67.5 15.5 %collective-permute-start.9 = (bf16[144,1024]{1,0:T(8,128)(2,1)S(1)}, bf16[144,1024]{1,0:T(8,128)(2,1)S(1)}, u32[]{:S(2)}, u32[]{:S(2)}) collective-permute-start(bf16[144,1024]{1,0:T(8,128)(2,1)S(1)} %get-tuple-element.31), channel_id=1, source_target_pairs={{0,2},{1,3},{2,0},{3,1},{4,6},{5,7},{6,4},{7,5},{8,10},{9,11},{10,... | collective-permute-start | bytes 884744 | tf_op jit(solution)/shard_map/ppermute | solution.py:218
  68.8 14.2 %collective-permute-start.10 = (bf16[144,1024]{1,0:T(8,128)(2,1)S(1)}, bf16[144,1024]{1,0:T(8,128)(2,1)S(1)}, u32[]{:S(2)}, u32[]{:S(2)}) collective-permute-start(bf16[144,1024]{1,0:T(8,128)(2,1)S(1)} %get-tuple-element.32), channel_id=1, source_target_pairs={{0,3},{1,2},{2,1},{3,0},{4,7},{5,6},{6,5},{7,4},{8,11},{9,10},{10,... | collective-permute-start | bytes 884744 | tf_op jit(solution)/shard_map/ppermute | solution.py:218
  83.5 5.2 %collective-permute-start.11 = (bf16[144,256]{1,0:T(8,128)(2,1)S(1)}, bf16[144,256]{1,0:T(8,128)(2,1)S(1)}, u32[]{:S(2)}, u32[]{:S(2)}) collective-permute-start(bf16[144,256]{1,0:T(8,128)(2,1)S(1)} %get-tuple-element.34), channel_id=1, source_target_pairs={{0,4},{1,5},{2,6},{3,7},{4,0},{5,1},{6,2},{7,3},{8,12},{9,13},{10,... | collective-permute-start | bytes 221192 | tf_op jit(solution)/shard_map/ppermute | solution.py:218
  84.5 8.3 %collective-permute-start.12 = (bf16[144,256]{1,0:T(8,128)(2,1)S(1)}, bf16[144,256]{1,0:T(8,128)(2,1)S(1)}, u32[]{:S(2)}, u32[]{:S(2)}) collective-permute-start(bf16[144,256]{1,0:T(8,128)(2,1)S(1)} %get-tuple-element.35), channel_id=1, source_target_pairs={{0,8},{1,9},{2,10},{3,11},{4,12},{5,13},{6,14},{7,15},{8,0},{9,1},... | collective-permute-start | bytes 221192 | tf_op jit(solution)/shard_map/ppermute | solution.py:218
  86.0 6.9 %collective-permute-start.13 = (bf16[144,256]{1,0:T(8,128)(2,1)S(1)}, bf16[144,256]{1,0:T(8,128)(2,1)S(1)}, u32[]{:S(2)}, u32[]{:S(2)}) collective-permute-start(bf16[144,256]{1,0:T(8,128)(2,1)S(1)} %get-tuple-element.36), channel_id=1, source_target_pairs={{0,12},{1,13},{2,14},{3,15},{4,8},{5,9},{6,10},{7,11},{8,4},{9,5},... | collective-permute-start | bytes 221192 | tf_op jit(solution)/shard_map/ppermute | solution.py:218

commit v2 on v1

v2 whole, which is shorter than its diff:
```python
import functools

import jax
import jax.numpy as jnp
from jax import lax
from jax.experimental import pallas as pl
from jax.experimental.pallas import tpu as pltpu
from jax.sharding import PartitionSpec as P

HEADS = 8
SPLIT = 4
HALO = 64
NEG_FILL = -1e30
PARTS = 4
STEP = 256
BF16 = jnp.bfloat16
F32 = jnp.float32
VMEM_LIMIT = 48 * 1024 * 1024
HBM = pl.BlockSpec(memory_space=pltpu.HBM)
VMEM = pl.BlockSpec(memory_space=pltpu.VMEM)
ANY = pl.BlockSpec(memory_space=pl.ANY)


def call(body, outs, vmem=(), hbm=(), after=(), scratch=(), flops=0, size=None):
    args = (*vmem, *(pltpu.with_memory_space_constraint(a, pltpu.HBM) for a in hbm), *after)
    n_in, n_after = len(vmem) + len(hbm), len(after)

    def kernel(*refs):
        body(*refs[:n_in], *refs[n_in + n_after :])

    if size is None:
        size = sum(a.size * a.dtype.itemsize for a in (*vmem, *hbm, *outs))
    return pl.pallas_call(
        kernel,
        out_shape=outs,
        in_specs=[VMEM] * len(vmem) + [HBM] * len(hbm) + [ANY] * n_after,
        out_specs=[VMEM] * len(outs),
        scratch_shapes=scratch,
        compiler_params=pltpu.CompilerParams(vmem_limit_bytes=VMEM_LIMIT),
        cost_estimate=pl.CostEstimate(flops=flops, bytes_accessed=size, transcendentals=0),
    )(*args)


def load(pairs, sems):
    copies = [pltpu.make_async_copy(src, dst, sems.at[i]) for i, (src, dst) in enumerate(pairs)]
    for c in copies:
        c.start()
    return copies


def dot(a, b, contract=(1, 0)):
    return lax.dot_general(
        a, b, (((contract[0],), (contract[1],)), ((), ())), preferred_element_type=F32
    )


def out(*shape, dtype=BF16):
    return jax.ShapeDtypeStruct(shape, dtype)


def iota(shape, dim):
    return lax.broadcasted_iota(jnp.int32, shape, dim)


def one_hot(condition):
    return jnp.where(condition, 1.0, 0.0).astype(BF16)


def column_blocks(rows):
    width = rows.shape[1] // PARTS
    return jnp.concatenate([rows[:, j * width : (j + 1) * width] for j in range(PARTS)], axis=0)


def home_plane():
    return lax.axis_index("ep") // SPLIT


def halo_body(key_hbm, value_hbm, mask_hbm, up_ref, down_ref, key_ref, value_ref, mask_ref, sems):
    copies = load(((key_hbm, key_ref), (value_hbm, value_ref), (mask_hbm, mask_ref)), sems)
    for c in copies:
        c.wait()
    rows = key_ref.shape[1]
    width = key_ref.shape[2] // HEADS
    for message, first in ((up_ref, rows - HALO), (down_ref, 0)):
        for head in range(HEADS):
            columns = slice(head * width, (head + 1) * width)
            message[head * HALO : (head + 1) * HALO, :] = key_ref[0, first : first + HALO, columns]
            start = (HEADS + head) * HALO
            message[start : start + HALO, :] = value_ref[0, first : first + HALO, columns]
        mask = mask_ref[:, first : first + HALO].astype(F32)
        mask = jnp.concatenate([mask, jnp.zeros((1, width - HALO), F32)], axis=1)
        message[2 * HEADS * HALO :, :] = jnp.broadcast_to(mask, (16, width)).astype(BF16)


def slots_of(labels):
    count = labels.shape[1]
    row, column = iota((count, count), 0), iota((count, count), 1)
    as_column = jnp.sum(jnp.where(row == column, labels, 0), axis=1, keepdims=True)
    return jnp.sum(jnp.where((row < column) & (as_column == labels), 1, 0), axis=0, keepdims=True)


def pack(rows, labels, slot, message_refs, capacity):
    home = home_plane()
    count = rows.shape[0]
    stacked = column_blocks(rows)
    height = message_refs[0].shape[0]
    for k, message in enumerate(message_refs):
        mine = labels == (home ^ k)
        places = [one_hot(mine & (slot + j * capacity == iota((height, count), 0))) for j in range(PARTS)]
        message[...] = dot(jnp.concatenate(places, axis=1), stacked).astype(BF16)


def pack_body(capacity, cot_hbm, label_hbm, query_hbm, token_hbm, route_ref, query_ref, token_ref, *refs):
    *message_refs, cot_ref, label_ref, sems = refs
    copies = load(
        ((label_hbm, label_ref), (cot_hbm, cot_ref), (query_hbm, query_ref), (token_hbm, token_ref)), sems
    )
    copies[0].wait()
    labels = label_ref[...]
    slot = slots_of(labels)
    route_ref[0:1, :] = labels
    route_ref[1:2, :] = slot
    copies[1].wait()
    pack(cot_ref[0], labels, slot, message_refs, capacity)
    for c in copies[2:]:
        c.wait()


def group_of(row, capacity, experts):
    group = jnp.zeros_like(row)
    for a in range(1, experts):
        group += jnp.where(row >= a * capacity, 1, 0)
    return group


def gather_body(capacity, experts, first_row, first_group, *refs):
    *message_refs, rows_ref = refs
    stacked = jnp.concatenate([m[...] for m in message_refs], axis=0)
    block, width = message_refs[0].shape
    row = iota((rows_ref.shape[0], stacked.shape[0]), 0) + first_row
    group = group_of(row, capacity, experts)
    source = (group - first_group) * block + row - group * capacity
    source = jnp.where(row < experts * capacity, source, -(1 << 20)) - iota(row.shape, 1)
    for j in range(PARTS):
        place = one_hot(source == -j * capacity)
        rows_ref[:, j * width : (j + 1) * width] = dot(place, stacked).astype(BF16)


def scatter(total, groups, message_refs, capacity):
    stacked = column_blocks(total)
    block = total.shape[0]
    height = message_refs[0].shape[0]
    row = iota((height, stacked.shape[0]), 0)
    part = group_of(row, capacity, PARTS)
    source = part * block + row - part * capacity
    source = jnp.where(row < PARTS * capacity, source, -(1 << 20)) - iota(row.shape, 1)
    for group, message in zip(groups, message_refs, strict=True):
        message[...] = dot(one_hot(source == -group * capacity), stacked).astype(BF16)


def added(refs):
    total = refs[0][...].astype(F32)
    for r in refs[1:]:
        total += r[...].astype(F32)
    return total.astype(BF16)


def combine_body(capacity, experts, *refs):
    scatter(added(refs[:SPLIT]), range(experts), refs[SPLIT:], capacity)


def attention_body(
    capacity, query_ref, token_ref, key_ref, value_ref, mask_ref, route_ref, before_ref, after_ref, mixed_ref, *message_refs
):
    rows, features = query_ref.shape[1:]
    width = features // HEADS
    position = lax.axis_index("ep")
    last = lax.axis_size("ep") - 1
    mask_row = 2 * HEADS * HALO
    mask = jnp.concatenate(
        [
            before_ref[mask_row : mask_row + 1, :HALO].astype(F32) * jnp.where(position > 0, 1.0, 0.0),
            mask_ref[...].astype(F32),
            after_ref[mask_row : mask_row + 1, :HALO].astype(F32) * jnp.where(position < last, 1.0, 0.0),
        ],
        axis=1,
    )
    count = rows + 2 * HALO
    offset = iota((rows, count), 1) - HALO - iota((rows, count), 0)
    usable = (jnp.abs(offset) <= HALO) & ((mask > 0.5) | (offset == 0))
    scale = width ** (-0.5)
    for head in range(HEADS):
        columns = slice(head * width, (head + 1) * width)
        at, value_at = head * HALO, (HEADS + head) * HALO
        keys = jnp.concatenate(
            [before_ref[at : at + HALO, :], key_ref[0, :, columns], after_ref[at : at + HALO, :]], axis=0
        )
        values = jnp.concatenate(
            [
                before_ref[value_at : value_at + HALO, :],
                value_ref[0, :, columns],
                after_ref[value_at : value_at + HALO, :],
            ],
            axis=0,
        )
        scores = dot(query_ref[0, :, columns], keys, (1, 1)) * scale
        scores = jnp.where(usable, scores, NEG_FILL)
        raised = jnp.exp(scores - jnp.max(scores, axis=1, keepdims=True))
        soft = (raised * (1.0 / jnp.sum(raised, axis=1, keepdims=True))).astype(BF16)
        mixed_ref[:, columns] = (token_ref[0, :, columns].astype(F32) + dot(soft, values)).astype(BF16)
    pack(mixed_ref[...], route_ref[0:1, :], route_ref[1:2, :], message_refs, capacity)


def expert_body(rows_ref, in_ref, out_ref, hidden_ref, partial_ref):
    rows = rows_ref[...]
    for at in range(0, in_ref.shape[1], STEP):
        hidden_ref[:, at : at + STEP] = jax.nn.gelu(dot(rows, in_ref[:, at : at + STEP])).astype(BF16)
    hidden = hidden_ref[...]
    for at in range(0, out_ref.shape[1], STEP):
        partial_ref[:, at : at + STEP] = dot(hidden, out_ref[:, at : at + STEP]).astype(BF16)


def finish_body(capacity, order, mixed_ref, route_ref, *refs):
    *message_refs, layer_ref = refs
    home = home_plane()
    labels, slot = route_ref[0:1, :], route_ref[1:2, :]
    count = labels.shape[1]
    block, width = message_refs[0].shape
    stacked = jnp.concatenate([m[...] for m in message_refs], axis=0)
    for j in range(PARTS):
        places = [
            one_hot((labels == (home ^ k)) & (slot + j * capacity == iota((block, count), 0))) for k in order
        ]
        taken = dot(jnp.concatenate(places, axis=0), stacked, (0, 0))
        columns = slice(j * width, (j + 1) * width)
        layer_ref[0, :, columns] = (mixed_ref[:, columns].astype(F32) + taken).astype(BF16)


def term_body(side, *refs):
    hidden_refs, cot_refs, rest = refs[:SPLIT], refs[SPLIT : 2 * SPLIT], refs[2 * SPLIT :]
    grad_ref, done_ref = rest[-2:]
    done_ref[...] = jnp.zeros_like(done_ref)
    cot = jnp.concatenate([c[...] for c in cot_refs], axis=0)
    half = hidden_refs[0].shape[1] // 2
    start = (lax.axis_index("grp") ^ side) * half
    for at in range(0, half, STEP):
        columns = pl.ds(pl.multiple_of(start + at, STEP), STEP)
        hidden = jnp.concatenate([h[:, columns] for h in hidden_refs], axis=0)
        term = dot(hidden, cot, (0, 0)).astype(BF16)
        if side == 1:
            grad_ref[at : at + STEP, :] = term
        else:
            theirs = rest[0][at : at + STEP, :].astype(F32)
            grad_ref[0, at : at + STEP, :] = (term.astype(F32) + theirs).astype(BF16)


def whole_term_body(*refs):
    hidden = jnp.concatenate([h[...] for h in refs[:SPLIT]], axis=0)
    cot = jnp.concatenate([c[...] for c in refs[SPLIT : 2 * SPLIT]], axis=0)
    refs[-1][...] = dot(hidden, cot, (0, 0)).astype(BF16)


def permute(value, apart):
    return lax.ppermute(value, "ep", [(i, i ^ apart) for i in range(lax.axis_size("ep"))])


def along_line(messages):
    return [m if k == 0 else permute(m, SPLIT * k) for k, m in enumerate(messages)]


def shards(tokens, queries, keys, values, key_mask, labels, cotangent, weight_in, weight_out):
    rows_here, features = tokens.shape[1:]
    axis_count = lax.axis_size("ep")
    experts = axis_count // SPLIT
    capacity = rows_here // experts + max(1, rows_here // (8 * experts))
    width = features // PARTS
    height = -(-PARTS * capacity // 16) * 16
    plane_rows = -(-experts * capacity // 16) * 16
    hidden_units = weight_in.shape[1]
    head_width = features // HEADS
    label_row = labels.reshape(1, rows_here)
    message = out(height, width)
    block = out(1, rows_here, features)
    row_ints = pltpu.VMEM((1, rows_here), jnp.int32)
    block_scratch = pltpu.VMEM((1, rows_here, features), BF16)

    halo = out(2 * HEADS * HALO + 16, head_width)
    up, down, key_here, value_here, mask_here = call(
        halo_body,
        (halo, halo, block, block, out(1, rows_here, dtype=jnp.int32)),
        hbm=(keys, values, key_mask),
        scratch=[pltpu.SemaphoreType.DMA((3,))],
    )
    steps = [(i, i + 1) for i in range(axis_count - 1)]
    before = lax.ppermute(up, "ep", steps)
    after = lax.ppermute(down, "ep", [(j, i) for i, j in steps])

    gather = functools.partial(gather_body, capacity, experts, 0, 0)
    route, query_here, token_here, *sent = call(
        functools.partial(pack_body, capacity),
        [out(8, rows_here, dtype=jnp.int32), block, block] + [message] * experts,
        hbm=(cotangent, label_row, queries, tokens),
        after=(up,),
        scratch=[block_scratch, row_ints, pltpu.SemaphoreType.DMA((4,))],
        size=0,
    )
    cot_got = along_line(sent)
    in_here, out_here = weight_in, weight_out.reshape(weight_out.shape[1:])

    mixed, *sent = call(
        functools.partial(attention_body, capacity),
        [out(rows_here, features)] + [message] * experts,
        vmem=(query_here, token_here, key_here, value_here, mask_here, route, before, after),
        after=cot_got,
        flops=4 * rows_here * (rows_here + 2 * HALO) * features,
    )

    (cot_rows,) = call(gather, [out(plane_rows, features)], vmem=cot_got, after=(mixed,), size=0)
    cot_x, cot_y = permute(cot_rows, 1), permute(cot_rows, 2)
    (rows,) = call(gather, [out(plane_rows, features)], vmem=along_line(sent))
    cot_xy = permute(cot_x, 2)

    done = [None] * SPLIT
    for k in (0, 3, 1, 2):
        done[k] = call(
            expert_body,
            [out(plane_rows, hidden_units), out(plane_rows, features)],
            vmem=(permute(rows, k) if k else rows, in_here, out_here),
            after=() if k else (cot_x, cot_y),
            flops=4 * plane_rows * features * hidden_units,
        )
    hidden = [d[0] for d in done]

    sums = [permute(d[1], k) if k else d[1] for k, d in enumerate(done)]
    sent = call(functools.partial(combine_body, capacity, experts), [message] * experts, vmem=sums)
    back = along_line(sent)

    inputs = (*hidden, cot_rows, cot_x, cot_y, cot_xy)
    flops = SPLIT * plane_rows * features * hidden_units
    if lax.axis_size("grp") == 2:
        half = hidden_units // 2
        tick = out(8, 128, dtype=F32)
        other, _ = call(
            functools.partial(term_body, 1), [out(half, features), tick], vmem=inputs, after=(sent[0],), flops=flops
        )
        theirs = lax.ppermute(other, "grp", [(0, 1), (1, 0)])
        grad, done = call(
            functools.partial(term_body, 0), [out(1, half, features), tick], vmem=(*inputs, theirs), flops=flops
        )
        ready = (done,)
    else:
        (term,) = call(whole_term_body, [out(hidden_units, features)], vmem=inputs, flops=2 * flops)
        grad = lax.psum_scatter(term, "grp", scatter_dimension=0, tiled=True)[None]
        ready = ()
    (layer_out,) = call(
        functools.partial(finish_body, capacity, range(experts)), [block], vmem=(mixed, route, *back), after=ready
    )
    return (layer_out, grad)


def solution(mesh):
    in_specs = (
        P("grp", "ep", None),
        P("grp", "ep", None),
        P("grp", "ep", None),
        P("grp", "ep", None),
        P("grp", "ep"),
        P("grp", "ep", None),
        P("grp", "ep", None),
        P(None, "ep"),
        P("ep", None, None),
    )
    out_specs = (P("grp", "ep", None), P("ep", "grp", None))
    return jax.shard_map(shards, mesh=mesh, in_specs=in_specs, out_specs=out_specs, check_vma=False)
```

time: 97.1 us -> 86.1 us (0.89)
  waiting for transfers between devices: 44.1 us -> 35.4 us
  local copies, waits for them, and re-layouts: 7.75 us -> 0.01 us
  starting transfers between devices: 30.5 us -> 35.9 us
  Pallas kernels: 11 us -> 13.9 us
  other arithmetic: 2.59 us -> 0 us
    ppermute x1, waiting for transfers between devices: 10.1 us -> 0.01 us  [shards(): before = lax.ppermute(up, 'ep', steps)]
    unnamed x18 -> x4, local copies, waits for them, and re-layouts: 6.7 us -> 0.01 us
    ppermute x18, starting transfers between devices: 24.3 us -> 29.1 us  [permute(): lax.ppermute(value, 'ep', [(i, i ^ apart) for i in range(lax.axis_size('e...]
    ppermute x18, waiting for transfers between devices: 32.1 us -> 35.4 us  [permute(): lax.ppermute(value, 'ep', [(i, i ^ apart) for i in range(lax.axis_size('e...]
    pallas_call x9 -> x13, Pallas kernels: 11 us -> 13.9 us  [call(): pl.pallas_call(kernel, out_shape=outs, in_specs=[VMEM] * len(vmem) + [HBM...]
    broadcast_in_dim x1 -> x0, other arithmetic: 2.59 us -> none  [shards(): return (layer_out, grad[None])]
    ppermute x1, waiting for transfers between devices: 1.91 us -> 0.01 us  [shards(): after = lax.ppermute(down, 'ep', [(j, i) for i, j in steps])]
    dynamic_slice x1 -> x0, local copies, waits for them, and re-layouts: 1.05 us -> none  [shards(): other = lax.dynamic_slice_in_dim(term, (1 - group) * half, half, axis=0)]
  transfers between devices with their start and end apart: 21 -> 21, of which waited for: 13 -> 14; matrix products, arithmetic and copies ran while one was open for 0% -> 0% of each run, Pallas kernels for 7% -> 10%
where the time goes in v2:
time: 86.1 us; the launch traced here: 86 us
  starting transfers between devices  35.9 us (42%)
  waiting for transfers between devices  35.4 us (41%)
  Pallas kernels  13.9 us (16%)
    ppermute x18, waiting for transfers between devices, permute(): lax.ppermute(value, 'ep', [(i, i ^ apart) for i in range(lax.axis_size('e...  35.4 us
    ppermute x18, starting transfers between devices, permute(): lax.ppermute(value, 'ep', [(i, i ^ apart) for i in range(lax.axis_size('e...  29.1 us
    pallas_call x13, Pallas kernels, call(): pl.pallas_call(kernel, out_shape=outs, in_specs=[VMEM] * len(vmem) + [HBM...  13.9 us
    ppermute x1, starting transfers between devices, shards(): before = lax.ppermute(up, 'ep', steps)  5.49 us
  transfers between devices with their start and end apart: 21, of which 14 were waited for; matrix products, arithmetic and copies ran while one was open for 0% of the time, Pallas kernels for 10%

profile of v2, /device:TPU:0, one launch (start us, length us, event | category | flops | bytes accessed | tf_op | source)
XLA Modules:
  0.0 86.0 jit_solution(5327964053197254950)
XLA Ops:
  0.6 1.2 %shard_map.104 = (bf16[1040,128]{1,0:T(8,128)(2,1)S(1)}, bf16[1040,128]{1,0:T(8,128)(2,1)S(1)}, bf16[1,128,1024]{2,1,0:T(8,128)(2,1)S(1)}, bf16[1,128,1024]{2,1,0:T(8,128)(2,1)S(1)}, s32[1,128]{1,0:T(1,128)S(1)}) custom-call(bf16[1,128,1024]{2,1,0:T(8,128)(2,1)} %refs_0_.2, bf16[1,128,1024]{2,1,0:T(8,128)(2,1)} %refs_1_.5, s32[1,128]{1,0:T(1,128)} %refs_2_.2), custom_call_target="tpu_custom_call" | custom-call | bytes 1582080 | tf_op jit(solution)/shard_map/pallas_call | solution.py:33
  1.8 1.3 %collective-permute-start.1 = (bf16[1040,128]{1,0:T(8,128)(2,1)S(1)}, bf16[1040,128]{1,0:T(8,128)(2,1)S(1)}, u32[]{:S(2)}, u32[]{:S(2)}) collective-permute-start(bf16[1040,128]{1,0:T(8,128)(2,1)S(1)} %get-tuple-element.41), channel_id=1, source_target_pairs={{1,0},{2,1},{3,2},{4,3},{5,4},{6,5},{7,6},{8,7},{9,8},{10,9},{11,1... | collective-permute-start | bytes 798728 | tf_op jit(solution)/shard_map/ppermute | solution.py:296
  3.1 5.5 %collective-permute-start = (bf16[1040,128]{1,0:T(8,128)(2,1)S(1)}, bf16[1040,128]{1,0:T(8,128)(2,1)S(1)}, u32[]{:S(2)}, u32[]{:S(2)}) collective-permute-start(bf16[1040,128]{1,0:T(8,128)(2,1)S(1)} %get-tuple-element.34.refs_4_), channel_id=1, source_target_pairs={{0,1},{1,2},{2,3},{3,4},{4,5},{5,6},{6,7},{7,8},{8,9},{9,10},{10,1... | collective-permute-start | bytes 798728 | tf_op jit(solution)/shard_map/ppermute | solution.py:295
  8.6 1.5 %shard_map.105 = (s32[8,128]{1,0:T(8,128)S(1)}, bf16[1,128,1024]{2,1,0:T(8,128)(2,1)S(1)}, bf16[1,128,1024]{2,1,0:T(8,128)(2,1)S(1)}, bf16[144,256]{1,0:T(8,128)...) custom-call(bf16[1,128,1024]{2,1,0:T(8,128)(2,1)} %refs_0_.3, ...), custom_call_target="tpu_custom_call" | custom-call | tf_op jit(solution)/shard_map/pallas_call | solution.py:33
  10.1 2.5 %collective-permute-start.2 = (bf16[144,256]{1,0:T(8,128)(2,1)S(1)}, bf16[144,256]{1,0:T(8,128)(2,1)S(1)}, u32[]{:S(2)}, u32[]{:S(2)}) collective-permute-start(bf16[144,256]{1,0:T(8,128)(2,1)S(1)} %get-tuple-element.43), channel_id=1, source_target_pairs={{0,4},{1,5},{2,6},{3,7},{4,0},{5,1},{6,2},{7,3},{8,12},{9,13},{10,... | collective-permute-start | bytes 221192 | tf_op jit(solution)/shard_map/ppermute | solution.py:264
  12.6 2.6 %collective-permute-start.3 = (bf16[144,256]{1,0:T(8,128)(2,1)S(1)}, bf16[144,256]{1,0:T(8,128)(2,1)S(1)}, u32[]{:S(2)}, u32[]{:S(2)}) collective-permute-start(bf16[144,256]{1,0:T(8,128)(2,1)S(1)} %get-tuple-element.44), channel_id=1, source_target_pairs={{0,8},{1,9},{2,10},{3,11},{4,12},{5,13},{6,14},{7,15},{8,0},{9,1},... | collective-permute-start | bytes 221192 | tf_op jit(solution)/shard_map/ppermute | solution.py:264
  15.2 2.7 %collective-permute-done.2.refs_9_.refs_1_ = bf16[144,256]{1,0:T(8,128)(2,1)S(1)} collective-permute-done((bf16[144,256]{1,0:T(8,128)(2,1)S(1)}, bf16[144,256]{1,0:T(8,128)(2,1)S(1)}, u32[]{:S(2)}, u32[]{:S(2)}) %collective-permute-start.2) | collective-permute-done | bytes 73760 | tf_op jit(solution)/shard_map/ppermute | solution.py:264
  17.9 1.6 %collective-permute-done.3.refs_10_.refs_2_ = bf16[144,256]{1,0:T(8,128)(2,1)S(1)} collective-permute-done((bf16[144,256]{1,0:T(8,128)(2,1)S(1)}, bf16[144,256]{1,0:T(8,128)(2,1)S(1)}, u32[]{:S(2)}, u32[]{:S(2)}) %collective-permute-start.3) | collective-permute-done | bytes 73760 | tf_op jit(solution)/shard_map/ppermute | solution.py:264
  19.5 2.6 %collective-permute-done.4.refs_11_.refs_3_ = bf16[144,256]{1,0:T(8,128)(2,1)S(1)} collective-permute-done((bf16[144,256]{1,0:T(8,128)(2,1)S(1)}, bf16[144,256]{1,0:T(8,128)(2,1)S(1)}, u32[]{:S(2)}, u32[]{:S(2)}) %collective-permute-start.4) | collective-permute-done | bytes 73760 | tf_op jit(solution)/shard_map/ppermute | solution.py:264
  22.1 1.5 %shard_map.106 = (bf16[128,1024]{1,0:T(8,128)(2,1)S(1)}, bf16[144,256]{1,0:T(8,128)(2,1)S(1)}, bf16[144,256]{1,0:T(8,128)(2,1)S(1)}, bf16[144,256]{1,0:T(8,128)(2,1)S(1)}, bf16[144,256]{1,0:T(8,128)(2,1)S(1)}) custom-call(bf16[1,128,1024]{2,1,0:T(8,128)(2,1)S(1)} %get-tuple-element.35.refs_0_, bf16[1,128,1024]{2,1,0:T(8,128)(2,1)S(1)} %get-tuple-element.36.refs_1_, ...), custom_call_target="tpu_custom_call" | custom-call | flops 134217728 | bytes 2142720 | tf_op jit(solution)/shard_map/pallas_call | solution.py:33
  23.6 1.1 %collective-permute-start.5 = (bf16[144,256]{1,0:T(8,128)(2,1)S(1)}, bf16[144,256]{1,0:T(8,128)(2,1)S(1)}, u32[]{:S(2)}, u32[]{:S(2)}) collective-permute-start(bf16[144,256]{1,0:T(8,128)(2,1)S(1)} %get-tuple-element.48), channel_id=1, source_target_pairs={{0,4},{1,5},{2,6},{3,7},{4,0},{5,1},{6,2},{7,3},{8,12},{9,13},{10,... | collective-permute-start | bytes 221192 | tf_op jit(solution)/shard_map/ppermute | solution.py:264
  24.7 1.8 %collective-permute-start.6 = (bf16[144,256]{1,0:T(8,128)(2,1)S(1)}, bf16[144,256]{1,0:T(8,128)(2,1)S(1)}, u32[]{:S(2)}, u32[]{:S(2)}) collective-permute-start(bf16[144,256]{1,0:T(8,128)(2,1)S(1)} %get-tuple-element.49), channel_id=1, source_target_pairs={{0,8},{1,9},{2,10},{3,11},{4,12},{5,13},{6,14},{7,15},{8,0},{9,1},... | collective-permute-start | bytes 221192 | tf_op jit(solution)/shard_map/ppermute | solution.py:264
  26.5 1.6 %collective-permute-start.7 = (bf16[144,256]{1,0:T(8,128)(2,1)S(1)}, bf16[144,256]{1,0:T(8,128)(2,1)S(1)}, u32[]{:S(2)}, u32[]{:S(2)}) collective-permute-start(bf16[144,256]{1,0:T(8,128)(2,1)S(1)} %get-tuple-element.50), channel_id=1, source_target_pairs={{0,12},{1,13},{2,14},{3,15},{4,8},{5,9},{6,10},{7,11},{8,4},{9,5},... | collective-permute-start | bytes 221192 | tf_op jit(solution)/shard_map/ppermute | solution.py:264
  28.0 2.9 %collective-permute-done.6.refs_2_ = bf16[144,256]{1,0:T(8,128)(2,1)S(1)} collective-permute-done((bf16[144,256]{1,0:T(8,128)(2,1)S(1)}, bf16[144,256]{1,0:T(8,128)(2,1)S(1)}, u32[]{:S(2)}, u32[]{:S(2)}) %collective-permute-start.6) | collective-permute-done | bytes 73760 | tf_op jit(solution)/shard_map/ppermute | solution.py:264
  31.0 1.7 %collective-permute-done.7.refs_3_ = bf16[144,256]{1,0:T(8,128)(2,1)S(1)} collective-permute-done((bf16[144,256]{1,0:T(8,128)(2,1)S(1)}, bf16[144,256]{1,0:T(8,128)(2,1)S(1)}, u32[]{:S(2)}, u32[]{:S(2)}) %collective-permute-start.7) | collective-permute-done | bytes 73760 | tf_op jit(solution)/shard_map/ppermute | solution.py:264
  33.1 4.4 %collective-permute-start.14 = (bf16[144,1024]{1,0:T(8,128)(2,1)S(1)}, bf16[144,1024]{1,0:T(8,128)(2,1)S(1)}, u32[]{:S(2)}, u32[]{:S(2)}) collective-permute-start(bf16[144,1024]{1,0:T(8,128)(2,1)S(1)} %shard_map.107.refs_0_), channel_id=1, source_target_pairs={{0,3},{1,2},{2,1},{3,0},{4,7},{5,6},{6,5},{7,4},{8,11},{9,10},{10,... | collective-permute-start | bytes 884744 | tf_op jit(solution)/shard_map/ppermute | solution.py:264
  38.5 1.5 %collective-permute-start.8 = (bf16[144,1024]{1,0:T(8,128)(2,1)S(1)}, bf16[144,1024]{1,0:T(8,128)(2,1)S(1)}, u32[]{:S(2)}, u32[]{:S(2)}) collective-permute-start(bf16[144,1024]{1,0:T(8,128)(2,1)S(1)} %shard_map.108.refs_4_), channel_id=1, source_target_pairs={{0,1},{1,0},{2,3},{3,2},{4,5},{5,4},{6,7},{7,6},{8,9},{9,8},{10,11... | collective-permute-start | bytes 884744 | tf_op jit(solution)/shard_map/ppermute | solution.py:264
  39.9 2.0 %collective-permute-start.9 = (bf16[144,1024]{1,0:T(8,128)(2,1)S(1)}, bf16[144,1024]{1,0:T(8,128)(2,1)S(1)}, u32[]{:S(2)}, u32[]{:S(2)}) collective-permute-start(bf16[144,1024]{1,0:T(8,128)(2,1)S(1)} %shard_map.108.refs_4_), channel_id=1, source_target_pairs={{0,2},{1,3},{2,0},{3,1},{4,6},{5,7},{6,4},{7,5},{8,10},{9,11},{10,... | collective-permute-start | bytes 884744 | tf_op jit(solution)/shard_map/ppermute | solution.py:264
  42.0 3.4 %collective-permute-done.14.refs_0_ = bf16[144,1024]{1,0:T(8,128)(2,1)S(1)} collective-permute-done((bf16[144,1024]{1,0:T(8,128)(2,1)S(1)}, bf16[144,1024]{1,0:T(8,128)(2,1)S(1)}, u32[]{:S(2)}, u32[]{:S(2)}) %collective-permute-start.14) | collective-permute-done | bytes 294944 | tf_op jit(solution)/shard_map/ppermute | solution.py:264
  46.3 3.0 %collective-permute-start.15 = (bf16[144,1024]{1,0:T(8,128)(2,1)S(1)}, bf16[144,1024]{1,0:T(8,128)(2,1)S(1)}, u32[]{:S(2)}, u32[]{:S(2)}) collective-permute-start(bf16[144,1024]{1,0:T(8,128)(2,1)S(1)} %get-tuple-element.54), channel_id=1, source_target_pairs={{0,3},{1,2},{2,1},{3,0},{4,7},{5,6},{6,5},{7,4},{8,11},{9,10},{10,... | collective-permute-start | bytes 884744 | tf_op jit(solution)/shard_map/ppermute | solution.py:264
  52.2 2.5 %collective-permute-start.11 = (bf16[144,1024]{1,0:T(8,128)(2,1)S(1)}, bf16[144,1024]{1,0:T(8,128)(2,1)S(1)}, u32[]{:S(2)}, u32[]{:S(2)}) collective-permute-start(bf16[144,1024]{1,0:T(8,128)(2,1)S(1)} %get-tuple-element.52), channel_id=1, source_target_pairs={{0,1},{1,0},{2,3},{3,2},{4,5},{5,4},{6,7},{7,6},{8,9},{9,8},{10,11... | collective-permute-start | bytes 884744 | tf_op jit(solution)/shard_map/ppermute | solution.py:264
  54.7 2.8 %collective-permute-done.8.refs_3_.refs_5_ = bf16[144,1024]{1,0:T(8,128)(2,1)S(1)} collective-permute-done((bf16[144,1024]{1,0:T(8,128)(2,1)S(1)}, bf16[144,1024]{1,0:T(8,128)(2,1)S(1)}, u32[]{:S(2)}, u32[]{:S(2)}) %collective-permute-start.8) | collective-permute-done | bytes 294944 | tf_op jit(solution)/shard_map/ppermute | solution.py:264
  58.6 1.5 %collective-permute-done.9.refs_4_.refs_6_ = bf16[144,1024]{1,0:T(8,128)(2,1)S(1)} collective-permute-done((bf16[144,1024]{1,0:T(8,128)(2,1)S(1)}, bf16[144,1024]{1,0:T(8,128)(2,1)S(1)}, u32[]{:S(2)}, u32[]{:S(2)}) %collective-permute-start.9) | collective-permute-done | bytes 294944 | tf_op jit(solution)/shard_map/ppermute | solution.py:264
  61.1 2.6 %collective-permute-done.15.refs_3_ = bf16[144,1024]{1,0:T(8,128)(2,1)S(1)} collective-permute-done((bf16[144,1024]{1,0:T(8,128)(2,1)S(1)}, bf16[144,1024]{1,0:T(8,128)(2,1)S(1)}, u32[]{:S(2)}, u32[]{:S(2)}) %collective-permute-start.15) | collective-permute-done | bytes 294944 | tf_op jit(solution)/shard_map/ppermute | solution.py:264
  63.7 4.8 %collective-permute-done.13.refs_2_ = bf16[144,1024]{1,0:T(8,128)(2,1)S(1)} collective-permute-done((bf16[144,1024]{1,0:T(8,128)(2,1)S(1)}, bf16[144,1024]{1,0:T(8,128)(2,1)S(1)}, u32[]{:S(2)}, u32[]{:S(2)}) %collective-permute-start.13) | collective-permute-done | bytes 294944 | tf_op jit(solution)/shard_map/ppermute | solution.py:264
  69.0 4.0 %collective-permute-done.19.refs_7_ = bf16[144,1024]{1,0:T(8,128)(2,1)S(1)} collective-permute-done((bf16[144,1024]{1,0:T(8,128)(2,1)S(1)}, bf16[144,1024]{1,0:T(8,128)(2,1)S(1)}, u32[]{:S(2)}, u32[]{:S(2)}) %collective-permute-start.19) | collective-permute-done | bytes 294944 | tf_op jit(solution)/shard_map/ppermute | solution.py:264
  73.0 1.4 %shard_map.114 = (bf16[512,1024]{1,0:T(8,128)(2,1)S(1)}, f32[8,128]{1,0:T(8,128)}) custom-call(bf16[144,1024]{1,0:T(8,128)(2,1)S(1)} %get-tuple-element.59.refs_0_, bf16[144,1024]{1,0:T(8,128)(2,1)S(1)} %get-tuple-element.60.refs_1_, bf16[144,1024]{1,0:T(8,128)(2,1)S(1)} %get-tuple-element.61.refs_2_, bf16[144,1024]{1,0:T(8,128)(2,1)S(1)} %get-tuple-element.62.refs_3_, ...), custom_call_target="tpu_custom_call" | custom-call | flops 603979776 | bytes 3411968 | tf_op jit(solution)/shard_map/pallas_call | solution.py:33
  75.1 2.4 %collective-permute-start.17 = (bf16[144,256]{1,0:T(8,128)(2,1)S(1)}, bf16[144,256]{1,0:T(8,128)(2,1)S(1)}, u32[]{:S(2)}, u32[]{:S(2)}) collective-permute-start(bf16[144,256]{1,0:T(8,128)(2,1)S(1)} %get-tuple-element.57), channel_id=1, source_target_pairs={{0,8},{1,9},{2,10},{3,11},{4,12},{5,13},{6,14},{7,15},{8,0},{9,1},... | collective-permute-start | bytes 221192 | tf_op jit(solution)/shard_map/ppermute | solution.py:264
  77.4 1.5 %collective-permute-start.18 = (bf16[144,256]{1,0:T(8,128)(2,1)S(1)}, bf16[144,256]{1,0:T(8,128)(2,1)S(1)}, u32[]{:S(2)}, u32[]{:S(2)}) collective-permute-start(bf16[144,256]{1,0:T(8,128)(2,1)S(1)} %get-tuple-element.58), channel_id=1, source_target_pairs={{0,12},{1,13},{2,14},{3,15},{4,8},{5,9},{6,10},{7,11},{8,4},{9,5},... | collective-permute-start | bytes 221192 | tf_op jit(solution)/shard_map/ppermute | solution.py:264
  78.9 2.0 %shard_map.115 = (bf16[1,512,1024]{2,1,0:T(8,128)(2,1)}, f32[8,128]{1,0:T(8,128)S(1)}) custom-call(bf16[144,1024]{1,0:T(8,128)(2,1)S(1)} %get-tuple-element.59.refs_0_, bf16[144,1024]{1,0:T(8,128)(2,1)S(1)} %get-tuple-element.60.refs_1_, bf16[144,1024]{1,0:T(8,128)(2,1)S(1)} %get-tuple-element.61.refs_2_, bf16[144,1024]{1,0:T(8,128)(2,1)S(1)} %get-tuple-element.62.refs_3_, ...), custom_call_target="tpu_custom_call" | custom-call | flops 603979776 | bytes 4460544 | tf_op jit(solution)/shard_map/pallas_call | solution.py:33
  80.9 3.9 %collective-permute-done.18.refs_5_ = bf16[144,256]{1,0:T(8,128)(2,1)S(1)} collective-permute-done((bf16[144,256]{1,0:T(8,128)(2,1)S(1)}, bf16[144,256]{1,0:T(8,128)(2,1)S(1)}, u32[]{:S(2)}, u32[]{:S(2)}) %collective-permute-start.18) | collective-permute-done | bytes 73760 | tf_op jit(solution)/shard_map/ppermute | solution.py:264
  84.8 1.1 %shard_map.116 = bf16[1,128,1024]{2,1,0:T(8,128)(2,1)} custom-call(bf16[128,1024]{1,0:T(8,128)(2,1)S(1)} %get-tuple-element.46.refs_4_.refs_0_, s32[8,128]{1,0:T(8,128)S(1)} %get-tuple-element.40.refs_5_.refs_1_, bf16[144,256]{1,0:T(8,128)(2,1)S(1)} %get-tuple-element.55.refs_8_.refs_2_, bf16[144,256]{1,0:T(8,128)(2,1)S(1)} %collective-permute-done.16.refs_3_, ...), custom_call_target="tpu_custom_call" | custom-call | bytes 823296 | tf_op jit(solution)/shard_map/pallas_call | solution.py:33
  (27 shorter events, 8.4 us)
Async XLA Ops:
  1.8 20.3 %collective-permute-start.1 = (bf16[1040,128]{1,0:T(8,128)(2,1)S(1)}, bf16[1040,128]{1,0:T(8,128)(2,1)S(1)}, u32[]{:S(2)}, u32[]{:S(2)}) collective-permute-start(bf16[1040,128]{1,0:T(8,128)(2,1)S(1)} %get-tuple-element.41), channel_id=1, source_target_pairs={{1,0},{2,1},{3,2},{4,3},{5,4},{6,5},{7,6},{8,7},{9,8},{10,9},{11,1... | collective-permute-start | bytes 798728 | tf_op jit(solution)/shard_map/ppermute | solution.py:296
  3.1 19.0 %collective-permute-start = (bf16[1040,128]{1,0:T(8,128)(2,1)S(1)}, bf16[1040,128]{1,0:T(8,128)(2,1)S(1)}, u32[]{:S(2)}, u32[]{:S(2)}) collective-permute-start(bf16[1040,128]{1,0:T(8,128)(2,1)S(1)} %get-tuple-element.34.refs_4_), channel_id=1, source_target_pairs={{0,1},{1,2},{2,3},{3,4},{4,5},{5,6},{6,7},{7,8},{8,9},{9,10},{10,1... | collective-permute-start | bytes 798728 | tf_op jit(solution)/shard_map/ppermute | solution.py:295
  8.6 36.8 %copy-start = (bf16[1024,1024]{1,0:T(8,128)(2,1)S(1)}, bf16[1024,1024]{1,0:T(8,128)(2,1)}, u32[]{:S(2)}) copy-start(bf16[1024,1024]{1,0:T(8,128)(2,1)} %refs_1_.9) | copy-start | bytes 6291460
  8.6 36.8 %copy-start.1 = (bf16[1,1024,1024]{2,1,0:T(8,128)(2,1)S(1)}, bf16[1,1024,1024]{2,1,0:T(8,128)(2,1)}, u32[]{:S(2)}) copy-start(bf16[1,1024,1024]{2,1,0:T(8,128)(2,1)} %param.17) | copy-start | bytes 6291460
  10.1 7.8 %collective-permute-start.2 = (bf16[144,256]{1,0:T(8,128)(2,1)S(1)}, bf16[144,256]{1,0:T(8,128)(2,1)S(1)}, u32[]{:S(2)}, u32[]{:S(2)}) collective-permute-start(bf16[144,256]{1,0:T(8,128)(2,1)S(1)} %get-tuple-element.43), channel_id=1, source_target_pairs={{0,4},{1,5},{2,6},{3,7},{4,0},{5,1},{6,2},{7,3},{8,12},{9,13},{10,... | collective-permute-start | bytes 221192 | tf_op jit(solution)/shard_map/ppermute | solution.py:264
  12.6 6.9 %collective-permute-start.3 = (bf16[144,256]{1,0:T(8,128)(2,1)S(1)}, bf16[144,256]{1,0:T(8,128)(2,1)S(1)}, u32[]{:S(2)}, u32[]{:S(2)}) collective-permute-start(bf16[144,256]{1,0:T(8,128)(2,1)S(1)} %get-tuple-element.44), channel_id=1, source_target_pairs={{0,8},{1,9},{2,10},{3,11},{4,12},{5,13},{6,14},{7,15},{8,0},{9,1},... | collective-permute-start | bytes 221192 | tf_op jit(solution)/shard_map/ppermute | solution.py:264
  15.2 6.9 %collective-permute-start.4 = (bf16[144,256]{1,0:T(8,128)(2,1)S(1)}, bf16[144,256]{1,0:T(8,128)(2,1)S(1)}, u32[]{:S(2)}, u32[]{:S(2)}) collective-permute-start(bf16[144,256]{1,0:T(8,128)(2,1)S(1)} %get-tuple-element.45), channel_id=1, source_target_pairs={{0,12},{1,13},{2,14},{3,15},{4,8},{5,9},{6,10},{7,11},{8,4},{9,5},... | collective-permute-start | bytes 221192 | tf_op jit(solution)/shard_map/ppermute | solution.py:264
  23.6 4.5 %collective-permute-start.5 = (bf16[144,256]{1,0:T(8,128)(2,1)S(1)}, bf16[144,256]{1,0:T(8,128)(2,1)S(1)}, u32[]{:S(2)}, u32[]{:S(2)}) collective-permute-start(bf16[144,256]{1,0:T(8,128)(2,1)S(1)} %get-tuple-element.48), channel_id=1, source_target_pairs={{0,4},{1,5},{2,6},{3,7},{4,0},{5,1},{6,2},{7,3},{8,12},{9,13},{10,... | collective-permute-start | bytes 221192 | tf_op jit(solution)/shard_map/ppermute | solution.py:264
  24.7 6.3 %collective-permute-start.6 = (bf16[144,256]{1,0:T(8,128)(2,1)S(1)}, bf16[144,256]{1,0:T(8,128)(2,1)S(1)}, u32[]{:S(2)}, u32[]{:S(2)}) collective-permute-start(bf16[144,256]{1,0:T(8,128)(2,1)S(1)} %get-tuple-element.49), channel_id=1, source_target_pairs={{0,8},{1,9},{2,10},{3,11},{4,12},{5,13},{6,14},{7,15},{8,0},{9,1},... | collective-permute-start | bytes 221192 | tf_op jit(solution)/shard_map/ppermute | solution.py:264
  26.5 6.2 %collective-permute-start.7 = (bf16[144,256]{1,0:T(8,128)(2,1)S(1)}, bf16[144,256]{1,0:T(8,128)(2,1)S(1)}, u32[]{:S(2)}, u32[]{:S(2)}) collective-permute-start(bf16[144,256]{1,0:T(8,128)(2,1)S(1)} %get-tuple-element.50), channel_id=1, source_target_pairs={{0,12},{1,13},{2,14},{3,15},{4,8},{5,9},{6,10},{7,11},{8,4},{9,5},... | collective-permute-start | bytes 221192 | tf_op jit(solution)/shard_map/ppermute | solution.py:264
  33.1 12.3 %collective-permute-start.14 = (bf16[144,1024]{1,0:T(8,128)(2,1)S(1)}, bf16[144,1024]{1,0:T(8,128)(2,1)S(1)}, u32[]{:S(2)}, u32[]{:S(2)}) collective-permute-start(bf16[144,1024]{1,0:T(8,128)(2,1)S(1)} %shard_map.107.refs_0_), channel_id=1, source_target_pairs={{0,3},{1,2},{2,1},{3,0},{4,7},{5,6},{6,5},{7,4},{8,11},{9,10},{10,... | collective-permute-start | bytes 884744 | tf_op jit(solution)/shard_map/ppermute | solution.py:264
  37.4 12.1 %collective-permute-start.12 = (bf16[144,1024]{1,0:T(8,128)(2,1)S(1)}, bf16[144,1024]{1,0:T(8,128)(2,1)S(1)}, u32[]{:S(2)}, u32[]{:S(2)}) collective-permute-start(bf16[144,1024]{1,0:T(8,128)(2,1)S(1)} %shard_map.107.refs_0_), channel_id=1, source_target_pairs={{0,2},{1,3},{2,0},{3,1},{4,6},{5,7},{6,4},{7,5},{8,10},{9,11},{10,... | collective-permute-start | bytes 884744 | tf_op jit(solution)/shard_map/ppermute | solution.py:264
  37.4 13.8 %collective-permute-start.10 = (bf16[144,1024]{1,0:T(8,128)(2,1)S(1)}, bf16[144,1024]{1,0:T(8,128)(2,1)S(1)}, u32[]{:S(2)}, u32[]{:S(2)}) collective-permute-start(bf16[144,1024]{1,0:T(8,128)(2,1)S(1)} %shard_map.107.refs_0_), channel_id=1, source_target_pairs={{0,1},{1,0},{2,3},{3,2},{4,5},{5,4},{6,7},{7,6},{8,9},{9,8},{10,11... | collective-permute-start | bytes 884744 | tf_op jit(solution)/shard_map/ppermute | solution.py:264
  38.5 19.1 %collective-permute-start.8 = (bf16[144,1024]{1,0:T(8,128)(2,1)S(1)}, bf16[144,1024]{1,0:T(8,128)(2,1)S(1)}, u32[]{:S(2)}, u32[]{:S(2)}) collective-permute-start(bf16[144,1024]{1,0:T(8,128)(2,1)S(1)} %shard_map.108.refs_4_), channel_id=1, source_target_pairs={{0,1},{1,0},{2,3},{3,2},{4,5},{5,4},{6,7},{7,6},{8,9},{9,8},{10,11... | collective-permute-start | bytes 884744 | tf_op jit(solution)/shard_map/ppermute | solution.py:264
  39.9 20.1 %collective-permute-start.9 = (bf16[144,1024]{1,0:T(8,128)(2,1)S(1)}, bf16[144,1024]{1,0:T(8,128)(2,1)S(1)}, u32[]{:S(2)}, u32[]{:S(2)}) collective-permute-start(bf16[144,1024]{1,0:T(8,128)(2,1)S(1)} %shard_map.108.refs_4_), channel_id=1, source_target_pairs={{0,2},{1,3},{2,0},{3,1},{4,6},{5,7},{6,4},{7,5},{8,10},{9,11},{10,... | collective-permute-start | bytes 884744 | tf_op jit(solution)/shard_map/ppermute | solution.py:264
  46.3 17.3 %collective-permute-start.15 = (bf16[144,1024]{1,0:T(8,128)(2,1)S(1)}, bf16[144,1024]{1,0:T(8,128)(2,1)S(1)}, u32[]{:S(2)}, u32[]{:S(2)}) collective-permute-start(bf16[144,1024]{1,0:T(8,128)(2,1)S(1)} %get-tuple-element.54), channel_id=1, source_target_pairs={{0,3},{1,2},{2,1},{3,0},{4,7},{5,6},{6,5},{7,4},{8,11},{9,10},{10,... | collective-permute-start | bytes 884744 | tf_op jit(solution)/shard_map/ppermute | solution.py:264
  50.5 18.0 %collective-permute-start.13 = (bf16[144,1024]{1,0:T(8,128)(2,1)S(1)}, bf16[144,1024]{1,0:T(8,128)(2,1)S(1)}, u32[]{:S(2)}, u32[]{:S(2)}) collective-permute-start(bf16[144,1024]{1,0:T(8,128)(2,1)S(1)} %get-tuple-element.53), channel_id=1, source_target_pairs={{0,2},{1,3},{2,0},{3,1},{4,6},{5,7},{6,4},{7,5},{8,10},{9,11},{10,... | collective-permute-start | bytes 884744 | tf_op jit(solution)/shard_map/ppermute | solution.py:264
  52.2 16.3 %collective-permute-start.11 = (bf16[144,1024]{1,0:T(8,128)(2,1)S(1)}, bf16[144,1024]{1,0:T(8,128)(2,1)S(1)}, u32[]{:S(2)}, u32[]{:S(2)}) collective-permute-start(bf16[144,1024]{1,0:T(8,128)(2,1)S(1)} %get-tuple-element.52), channel_id=1, source_target_pairs={{0,1},{1,0},{2,3},{3,2},{4,5},{5,4},{6,7},{7,6},{8,9},{9,8},{10,11... | collective-permute-start | bytes 884744 | tf_op jit(solution)/shard_map/ppermute | solution.py:264
  57.5 15.5 %collective-permute-start.19 = (bf16[144,1024]{1,0:T(8,128)(2,1)S(1)}, bf16[144,1024]{1,0:T(8,128)(2,1)S(1)}, u32[]{:S(2)}, u32[]{:S(2)}) collective-permute-start(bf16[144,1024]{1,0:T(8,128)(2,1)S(1)} %collective-permute-done.8.refs_3_.refs_5_), channel_id=1, source_target_pairs={{0,2},{1,3},{2,0},{3,1},{4,6},{5,7},{6,4},{7,5},{8,10},{9,11},{10,... | collective-permute-start | bytes 884744 | tf_op jit(solution)/shard_map/ppermute | solution.py:264
  74.4 4.5 %collective-permute-start.20 = (bf16[512,1024]{1,0:T(8,128)(2,1)S(1)}, bf16[512,1024]{1,0:T(8,128)(2,1)S(1)}, u32[]{:S(2)}, u32[]{:S(2)}) collective-permute-start(bf16[512,1024]{1,0:T(8,128)(2,1)S(1)} %get-tuple-element.63), channel_id=1, source_target_pairs={{0,16},{16,0},{1,17},{17,1},{2,18},{18,2},{3,19},{19,3},{4,20},{20... | collective-permute-start | bytes 3145736 | tf_op jit(solution)/shard_map/ppermute | solution.py:346
  74.5 6.5 %collective-permute-start.16 = (bf16[144,256]{1,0:T(8,128)(2,1)S(1)}, bf16[144,256]{1,0:T(8,128)(2,1)S(1)}, u32[]{:S(2)}, u32[]{:S(2)}) collective-permute-start(bf16[144,256]{1,0:T(8,128)(2,1)S(1)} %get-tuple-element.56), channel_id=1, source_target_pairs={{0,4},{1,5},{2,6},{3,7},{4,0},{5,1},{6,2},{7,3},{8,12},{9,13},{10,... | collective-permute-start | bytes 221192 | tf_op jit(solution)/shard_map/ppermute | solution.py:264
  75.1 5.9 %collective-permute-start.17 = (bf16[144,256]{1,0:T(8,128)(2,1)S(1)}, bf16[144,256]{1,0:T(8,128)(2,1)S(1)}, u32[]{:S(2)}, u32[]{:S(2)}) collective-permute-start(bf16[144,256]{1,0:T(8,128)(2,1)S(1)} %get-tuple-element.57), channel_id=1, source_target_pairs={{0,8},{1,9},{2,10},{3,11},{4,12},{5,13},{6,14},{7,15},{8,0},{9,1},... | collective-permute-start | bytes 221192 | tf_op jit(solution)/shard_map/ppermute | solution.py:264
  77.4 7.4 %collective-permute-start.18 = (bf16[144,256]{1,0:T(8,128)(2,1)S(1)}, bf16[144,256]{1,0:T(8,128)(2,1)S(1)}, u32[]{:S(2)}, u32[]{:S(2)}) collective-permute-start(bf16[144,256]{1,0:T(8,128)(2,1)S(1)} %get-tuple-element.58), channel_id=1, source_target_pairs={{0,12},{1,13},{2,14},{3,15},{4,8},{5,9},{6,10},{7,11},{8,4},{9,5},... | collective-permute-start | bytes 221192 | tf_op jit(solution)/shard_map/ppermute | solution.py:264

commit v3 on v2

--- a/solution.py
+++ b/solution.py
@@ -13,6 +13,7 @@
 NEG_FILL = -1e30
 PARTS = 4
 STEP = 256
+PIECES = 4
 BF16 = jnp.bfloat16
 F32 = jnp.float32
 VMEM_LIMIT = 48 * 1024 * 1024
@@ -158,15 +159,13 @@
         message[...] = dot(one_hot(source == -group * capacity), stacked).astype(BF16)
 
 
-def added(refs):
-    total = refs[0][...].astype(F32)
-    for r in refs[1:]:
-        total += r[...].astype(F32)
-    return total.astype(BF16)
-
-
-def combine_body(capacity, experts, *refs):
-    scatter(added(refs[:SPLIT]), range(experts), refs[SPLIT:], capacity)
+def add_body(first_ref, second_ref, sum_ref):
+    sum_ref[...] = first_ref[...].astype(F32) + second_ref[...].astype(F32)
+
+
+def combine_body(capacity, experts, sum_ref, last_ref, *message_refs):
+    total = (sum_ref[...] + last_ref[...].astype(F32)).astype(BF16)
+    scatter(total, range(experts), message_refs, capacity)
 
 
 def attention_body(
@@ -236,22 +235,33 @@
         layer_ref[0, :, columns] = (mixed_ref[:, columns].astype(F32) + taken).astype(BF16)
 
 
-def term_body(side, *refs):
-    hidden_refs, cot_refs, rest = refs[:SPLIT], refs[SPLIT : 2 * SPLIT], refs[2 * SPLIT :]
-    grad_ref, done_ref = rest[-2:]
-    done_ref[...] = jnp.zeros_like(done_ref)
+def half_terms(refs, side):
+    hidden_refs, cot_refs = refs[:SPLIT], refs[SPLIT : 2 * SPLIT]
     cot = jnp.concatenate([c[...] for c in cot_refs], axis=0)
     half = hidden_refs[0].shape[1] // 2
     start = (lax.axis_index("grp") ^ side) * half
     for at in range(0, half, STEP):
         columns = pl.ds(pl.multiple_of(start + at, STEP), STEP)
         hidden = jnp.concatenate([h[:, columns] for h in hidden_refs], axis=0)
-        term = dot(hidden, cot, (0, 0)).astype(BF16)
-        if side == 1:
-            grad_ref[at : at + STEP, :] = term
-        else:
-            theirs = rest[0][at : at + STEP, :].astype(F32)
-            grad_ref[0, at : at + STEP, :] = (term.astype(F32) + theirs).astype(BF16)
+        yield at, dot(hidden, cot, (0, 0)).astype(BF16)
+
+
+def other_half_body(*refs):
+    piece_refs = refs[2 * SPLIT :]
+    rows = piece_refs[0].shape[0]
+    for at, term in half_terms(refs, 1):
+        for r in range(0, STEP, rows):
+            piece_refs[(at + r) // rows][...] = term[r : r + rows, :]
+
+
+def own_half_body(*refs):
+    *piece_refs, grad_ref, done_ref = refs[2 * SPLIT :]
+    rows = piece_refs[0].shape[0]
+    done_ref[...] = jnp.zeros_like(done_ref)
+    for at, term in half_terms(refs, 0):
+        for r in range(0, STEP, rows):
+            theirs = piece_refs[(at + r) // rows][...].astype(F32)
+            grad_ref[0, at + r : at + r + rows, :] = (term[r : r + rows, :].astype(F32) + theirs).astype(BF16)
 
 
 def whole_term_body(*refs):
@@ -311,7 +321,6 @@
         functools.partial(attention_body, capacity),
         [out(rows_here, features)] + [message] * experts,
         vmem=(query_here, token_here, key_here, value_here, mask_here, route, before, after),
-        after=cot_got,
         flops=4 * rows_here * (rows_here + 2 * HALO) * features,
     )
 
@@ -320,38 +329,54 @@
     (rows,) = call(gather, [out(plane_rows, features)], vmem=along_line(sent))
     cot_xy = permute(cot_x, 2)
 
-    done = [None] * SPLIT
-    for k in (0, 3, 1, 2):
-        done[k] = call(
+    own_hidden, own_partial = call(
+        expert_body,
+        [out(plane_rows, hidden_units), out(plane_rows, features)],
+        vmem=(rows, in_here, out_here),
+        after=(cot_x, cot_y),
+        flops=4 * plane_rows * features * hidden_units,
+    )
+    hiddens, partials = [own_hidden], []
+    for k in (3, 1, 2):
+        hidden, partial = call(
             expert_body,
             [out(plane_rows, hidden_units), out(plane_rows, features)],
-            vmem=(permute(rows, k) if k else rows, in_here, out_here),
-            after=() if k else (cot_x, cot_y),
+            vmem=(permute(rows, k), in_here, out_here),
+            after=(own_hidden,),
             flops=4 * plane_rows * features * hidden_units,
         )
-    hidden = [d[0] for d in done]
-
-    sums = [permute(d[1], k) if k else d[1] for k, d in enumerate(done)]
-    sent = call(functools.partial(combine_body, capacity, experts), [message] * experts, vmem=sums)
-    back = along_line(sent)
-
-    inputs = (*hidden, cot_rows, cot_x, cot_y, cot_xy)
+        hiddens.append(hidden)
+        partials.append(partial)
+
+    total = own_partial
+    totals = []
+    for partial, k in zip(partials[:-1], (3, 1)):
+        (total,) = call(
+            add_body, [out(plane_rows, features, dtype=F32)], vmem=(total, permute(partial, k)), size=0
+        )
+        totals.append(total)
+    last = permute(partials[-1], 2)
+    inputs = (*hiddens, cot_rows, cot_xy, cot_x, cot_y)
     flops = SPLIT * plane_rows * features * hidden_units
     if lax.axis_size("grp") == 2:
         half = hidden_units // 2
-        tick = out(8, 128, dtype=F32)
-        other, _ = call(
-            functools.partial(term_body, 1), [out(half, features), tick], vmem=inputs, after=(sent[0],), flops=flops
-        )
-        theirs = lax.ppermute(other, "grp", [(0, 1), (1, 0)])
+        pieces = call(
+            other_half_body, [out(half // PIECES, features)] * PIECES, vmem=inputs, after=totals[:1], flops=flops
+        )
+        theirs = [lax.ppermute(piece, "grp", [(0, 1), (1, 0)]) for piece in pieces]
         grad, done = call(
-            functools.partial(term_body, 0), [out(1, half, features), tick], vmem=(*inputs, theirs), flops=flops
+            own_half_body,
+            [out(1, half, features), out(8, 128, dtype=F32)],
+            vmem=(*inputs, *theirs),
+            flops=flops,
         )
         ready = (done,)
     else:
         (term,) = call(whole_term_body, [out(hidden_units, features)], vmem=inputs, flops=2 * flops)
         grad = lax.psum_scatter(term, "grp", scatter_dimension=0, tiled=True)[None]
         ready = ()
+    sent = call(functools.partial(combine_body, capacity, experts), [message] * experts, vmem=(total, last))
+    back = along_line(sent)
     (layer_out,) = call(
         functools.partial(finish_body, capacity, range(experts)), [block], vmem=(mixed, route, *back), after=ready
     )

time: 86.1 us -> 78.5 us (0.912)
  waiting for transfers between devices: 35.4 us -> 29.6 us
  starting transfers between devices: 35.9 us -> 33.9 us
    ppermute x18, waiting for transfers between devices: 35.4 us -> 24.8 us  [permute(): lax.ppermute(value, 'ep', [(i, i ^ apart) for i in range(lax.axis_size('e...]
    ppermute x1, waiting for transfers between devices: 0.01 us -> 4.84 us  [shards(): before = lax.ppermute(up, 'ep', steps)]
    ppermute x18, starting transfers between devices: 29.1 us -> 25.9 us  [permute(): lax.ppermute(value, 'ep', [(i, i ^ apart) for i in range(lax.axis_size('e...]
    ppermute x1 -> x4, starting transfers between devices: 0.01 us -> 1.08 us  [shards(): theirs = [lax.ppermute(piece, 'grp', [(0, 1), (1, 0)]) for piece in pieces]]
    pallas_call x13 -> x15, Pallas kernels: 13.9 us -> 13.5 us  [call(): pl.pallas_call(kernel, out_shape=outs, in_specs=[VMEM] * len(vmem) + [HBM...]
  transfers between devices with their start and end apart: 21 -> 24, of which waited for: 14 -> 11; matrix products, arithmetic and copies ran while one was open for 0% -> 0% of each run, Pallas kernels for 10% -> 14%
where the time goes in v3:
time: 78.5 us; the launch traced here: 77.9 us
  starting transfers between devices  33.9 us (43%)
  waiting for transfers between devices  29.6 us (38%)
  Pallas kernels  13.5 us (17%)
  between operations  0.8 us (1%)
    ppermute x18, starting transfers between devices, permute(): lax.ppermute(value, 'ep', [(i, i ^ apart) for i in range(lax.axis_size('e...  25.9 us
    ppermute x18, waiting for transfers between devices, permute(): lax.ppermute(value, 'ep', [(i, i ^ apart) for i in range(lax.axis_size('e...  24.8 us
    pallas_call x15, Pallas kernels, call(): pl.pallas_call(kernel, out_shape=outs, in_specs=[VMEM] * len(vmem) + [HBM...  13.5 us
    ppermute x1, starting transfers between devices, shards(): before = lax.ppermute(up, 'ep', steps)  5.49 us
    ppermute x1, waiting for transfers between devices, shards(): before = lax.ppermute(up, 'ep', steps)  4.84 us
  transfers between devices with their start and end apart: 24, of which 11 were waited for; matrix products, arithmetic and copies ran while one was open for 0% of the time, Pallas kernels for 14%

profile of v3, /device:TPU:0, one launch (start us, length us, event | category | flops | bytes accessed | tf_op | source)
XLA Modules:
  0.0 77.9 jit_solution(2617780118776290070)
XLA Ops:
  0.6 1.3 %shard_map.104 = (bf16[1040,128]{1,0:T(8,128)(2,1)S(1)}, bf16[1040,128]{1,0:T(8,128)(2,1)S(1)}, bf16[1,128,1024]{2,1,0:T(8,128)(2,1)S(1)}, bf16[1,128,1024]{2,1,0:T(8,128)(2,1)S(1)}, s32[1,128]{1,0:T(1,128)S(1)}) custom-call(bf16[1,128,1024]{2,1,0:T(8,128)(2,1)} %refs_0_.2, bf16[1,128,1024]{2,1,0:T(8,128)(2,1)} %refs_1_.5, s32[1,128]{1,0:T(1,128)} %refs_2_.2), custom_call_target="tpu_custom_call" | custom-call | bytes 1582080 | tf_op jit(solution)/shard_map/pallas_call | solution.py:34
  2.0 1.4 %collective-permute-start.1 = (bf16[1040,128]{1,0:T(8,128)(2,1)S(1)}, bf16[1040,128]{1,0:T(8,128)(2,1)S(1)}, u32[]{:S(2)}, u32[]{:S(2)}) collective-permute-start(bf16[1040,128]{1,0:T(8,128)(2,1)S(1)} %get-tuple-element.44), channel_id=1, source_target_pairs={{1,0},{2,1},{3,2},{4,3},{5,4},{6,5},{7,6},{8,7},{9,8},{10,9},{11,1... | collective-permute-start | bytes 798728 | tf_op jit(solution)/shard_map/ppermute | solution.py:306
  3.4 5.5 %collective-permute-start = (bf16[1040,128]{1,0:T(8,128)(2,1)S(1)}, bf16[1040,128]{1,0:T(8,128)(2,1)S(1)}, u32[]{:S(2)}, u32[]{:S(2)}) collective-permute-start(bf16[1040,128]{1,0:T(8,128)(2,1)S(1)} %get-tuple-element.37.refs_4_), channel_id=1, source_target_pairs={{0,1},{1,2},{2,3},{3,4},{4,5},{5,6},{6,7},{7,8},{8,9},{9,10},{10,1... | collective-permute-start | bytes 798728 | tf_op jit(solution)/shard_map/ppermute | solution.py:305
  8.9 1.3 %shard_map.105 = (s32[8,128]{1,0:T(8,128)S(1)}, bf16[1,128,1024]{2,1,0:T(8,128)(2,1)S(1)}, bf16[1,128,1024]{2,1,0:T(8,128)(2,1)S(1)}, bf16[144,256]{1,0:T(8,128)...) custom-call(bf16[1,128,1024]{2,1,0:T(8,128)(2,1)} %refs_0_.3, ...), custom_call_target="tpu_custom_call" | custom-call | tf_op jit(solution)/shard_map/pallas_call | solution.py:34
  10.3 2.5 %collective-permute-start.5 = (bf16[144,256]{1,0:T(8,128)(2,1)S(1)}, bf16[144,256]{1,0:T(8,128)(2,1)S(1)}, u32[]{:S(2)}, u32[]{:S(2)}) collective-permute-start(bf16[144,256]{1,0:T(8,128)(2,1)S(1)} %get-tuple-element.51), channel_id=1, source_target_pairs={{0,4},{1,5},{2,6},{3,7},{4,0},{5,1},{6,2},{7,3},{8,12},{9,13},{10,... | collective-permute-start | bytes 221192 | tf_op jit(solution)/shard_map/ppermute | solution.py:274
  12.7 2.6 %collective-permute-start.6 = (bf16[144,256]{1,0:T(8,128)(2,1)S(1)}, bf16[144,256]{1,0:T(8,128)(2,1)S(1)}, u32[]{:S(2)}, u32[]{:S(2)}) collective-permute-start(bf16[144,256]{1,0:T(8,128)(2,1)S(1)} %get-tuple-element.52), channel_id=1, source_target_pairs={{0,8},{1,9},{2,10},{3,11},{4,12},{5,13},{6,14},{7,15},{8,0},{9,1},... | collective-permute-start | bytes 221192 | tf_op jit(solution)/shard_map/ppermute | solution.py:274
  15.3 4.8 %collective-permute-done.refs_6_ = bf16[1040,128]{1,0:T(8,128)(2,1)S(1)} collective-permute-done((bf16[1040,128]{1,0:T(8,128)(2,1)S(1)}, bf16[1040,128]{1,0:T(8,128)(2,1)S(1)}, u32[]{:S(2)}, u32[]{:S(2)}) %collective-permute-start) | collective-permute-done | bytes 266272 | tf_op jit(solution)/shard_map/ppermute | solution.py:305
  20.2 1.5 %shard_map.106 = (bf16[128,1024]{1,0:T(8,128)(2,1)S(1)}, bf16[144,256]{1,0:T(8,128)(2,1)S(1)}, bf16[144,256]{1,0:T(8,128)(2,1)S(1)}, bf16[144,256]{1,0:T(8,128)(2,1)S(1)}, bf16[144,256]{1,0:T(8,128)(2,1)S(1)}) custom-call(bf16[1,128,1024]{2,1,0:T(8,128)(2,1)S(1)} %get-tuple-element.38.refs_0_, bf16[1,128,1024]{2,1,0:T(8,128)(2,1)S(1)} %get-tuple-element.39.refs_1_, ...), custom_call_target="tpu_custom_call" | custom-call | flops 134217728 | bytes 2142720 | tf_op jit(solution)/shard_map/pallas_call | solution.py:34
  21.6 2.3 %collective-permute-start.2 = (bf16[144,256]{1,0:T(8,128)(2,1)S(1)}, bf16[144,256]{1,0:T(8,128)(2,1)S(1)}, u32[]{:S(2)}, u32[]{:S(2)}) collective-permute-start(bf16[144,256]{1,0:T(8,128)(2,1)S(1)} %get-tuple-element.47), channel_id=1, source_target_pairs={{0,4},{1,5},{2,6},{3,7},{4,0},{5,1},{6,2},{7,3},{8,12},{9,13},{10,... | collective-permute-start | bytes 221192 | tf_op jit(solution)/shard_map/ppermute | solution.py:274
  24.0 2.8 %collective-permute-start.3 = (bf16[144,256]{1,0:T(8,128)(2,1)S(1)}, bf16[144,256]{1,0:T(8,128)(2,1)S(1)}, u32[]{:S(2)}, u32[]{:S(2)}) collective-permute-start(bf16[144,256]{1,0:T(8,128)(2,1)S(1)} %get-tuple-element.48), channel_id=1, source_target_pairs={{0,8},{1,9},{2,10},{3,11},{4,12},{5,13},{6,14},{7,15},{8,0},{9,1},... | collective-permute-start | bytes 221192 | tf_op jit(solution)/shard_map/ppermute | solution.py:274
  26.8 1.0 %collective-permute-start.4 = (bf16[144,256]{1,0:T(8,128)(2,1)S(1)}, bf16[144,256]{1,0:T(8,128)(2,1)S(1)}, u32[]{:S(2)}, u32[]{:S(2)}) collective-permute-start(bf16[144,256]{1,0:T(8,128)(2,1)S(1)} %get-tuple-element.49), channel_id=1, source_target_pairs={{0,12},{1,13},{2,14},{3,15},{4,8},{5,9},{6,10},{7,11},{8,4},{9,5},... | collective-permute-start | bytes 221192 | tf_op jit(solution)/shard_map/ppermute | solution.py:274
  29.1 2.1 %collective-permute-done.3.refs_2_ = bf16[144,256]{1,0:T(8,128)(2,1)S(1)} collective-permute-done((bf16[144,256]{1,0:T(8,128)(2,1)S(1)}, bf16[144,256]{1,0:T(8,128)(2,1)S(1)}, u32[]{:S(2)}, u32[]{:S(2)}) %collective-permute-start.3) | collective-permute-done | bytes 73760 | tf_op jit(solution)/shard_map/ppermute | solution.py:274
  31.3 1.7 %collective-permute-done.4.refs_3_ = bf16[144,256]{1,0:T(8,128)(2,1)S(1)} collective-permute-done((bf16[144,256]{1,0:T(8,128)(2,1)S(1)}, bf16[144,256]{1,0:T(8,128)(2,1)S(1)}, u32[]{:S(2)}, u32[]{:S(2)}) %collective-permute-start.4) | collective-permute-done | bytes 73760 | tf_op jit(solution)/shard_map/ppermute | solution.py:274
  34.0 1.1 %collective-permute-start.12 = (bf16[144,1024]{1,0:T(8,128)(2,1)S(1)}, bf16[144,1024]{1,0:T(8,128)(2,1)S(1)}, u32[]{:S(2)}, u32[]{:S(2)}) collective-permute-start(bf16[144,1024]{1,0:T(8,128)(2,1)S(1)} %shard_map.107.refs_0_), channel_id=1, source_target_pairs={{0,1},{1,0},{2,3},{3,2},{4,5},{5,4},{6,7},{7,6},{8,9},{9,8},{10,11... | collective-permute-start | bytes 884744 | tf_op jit(solution)/shard_map/ppermute | solution.py:274
  35.1 1.8 %collective-permute-start.14 = (bf16[144,1024]{1,0:T(8,128)(2,1)S(1)}, bf16[144,1024]{1,0:T(8,128)(2,1)S(1)}, u32[]{:S(2)}, u32[]{:S(2)}) collective-permute-start(bf16[144,1024]{1,0:T(8,128)(2,1)S(1)} %shard_map.107.refs_0_), channel_id=1, source_target_pairs={{0,2},{1,3},{2,0},{3,1},{4,6},{5,7},{6,4},{7,5},{8,10},{9,11},{10,... | collective-permute-start | bytes 884744 | tf_op jit(solution)/shard_map/ppermute | solution.py:274
  37.7 1.0 %shard_map.109 = (bf16[144,1024]{1,0:T(8,128)(2,1)S(1)}, bf16[144,1024]{1,0:T(8,128)(2,1)S(1)}) custom-call(bf16[144,1024]{1,0:T(8,128)(2,1)S(1)} %shard_map.107.refs_0_, bf16[1024,1024]{1,0:T(8,128)(2,1)S(1)} %copy-done, bf16[1024,1024]{1,0:T(8,128)(2,1)S(1)} %bitcast.2, bf16[144,1024]{1,0:T(8,128)(2,1)S(1)} %collective-permute-done.8.refs_3_.refs_6_, ...), custom_call_target="tpu_custom_call" | custom-call | flops 603979776 | bytes 5079040 | tf_op jit(solution)/shard_map/pallas_call | solution.py:34
  38.6 7.4 %collective-permute-done.10.refs_0_ = bf16[144,1024]{1,0:T(8,128)(2,1)S(1)} collective-permute-done((bf16[144,1024]{1,0:T(8,128)(2,1)S(1)}, bf16[144,1024]{1,0:T(8,128)(2,1)S(1)}, u32[]{:S(2)}, u32[]{:S(2)}) %collective-permute-start.10) | collective-permute-done | bytes 294944 | tf_op jit(solution)/shard_map/ppermute | solution.py:274
  47.4 1.7 %collective-permute-start.19 = (bf16[144,1024]{1,0:T(8,128)(2,1)S(1)}, bf16[144,1024]{1,0:T(8,128)(2,1)S(1)}, u32[]{:S(2)}, u32[]{:S(2)}) collective-permute-start(bf16[144,1024]{1,0:T(8,128)(2,1)S(1)} %collective-permute-done.8.refs_3_.refs_6_), channel_id=1, source_target_pairs={{0,2},{1,3},{2,0},{3,1},{4,6},{5,7},{6,4},{7,5},{8,10},{9,11},{10,... | collective-permute-start | bytes 884744 | tf_op jit(solution)/shard_map/ppermute | solution.py:274
  50.8 2.0 %collective-permute-start.13 = (bf16[144,1024]{1,0:T(8,128)(2,1)S(1)}, bf16[144,1024]{1,0:T(8,128)(2,1)S(1)}, u32[]{:S(2)}, u32[]{:S(2)}) collective-permute-start(bf16[144,1024]{1,0:T(8,128)(2,1)S(1)} %get-tuple-element.57), channel_id=1, source_target_pairs={{0,1},{1,0},{2,3},{3,2},{4,5},{5,4},{6,7},{7,6},{8,9},{9,8},{10,11... | collective-permute-start | bytes 884744 | tf_op jit(solution)/shard_map/ppermute | solution.py:274
  52.8 1.0 %shard_map.114 = (bf16[144,1024]{1,0:T(8,128)(2,1)S(1)}, bf16[144,1024]{1,0:T(8,128)(2,1)S(1)}) custom-call(bf16[144,1024]{1,0:T(8,128)(2,1)S(1)} %collective-permute-done.14.refs_0_, bf16[1024,1024]{1,0:T(8,128)(2,1)S(1)} %copy-done, bf16[1024,1024]{1,0:T(8,128)(2,1)S(1)} %bitcast.5, bf16[144,1024]{1,0:T(8,128)(2,1)S(1)} %get-tuple-element.55.refs_3_.refs_0_), custom_call_target="tpu_custom_call" | custom-call | flops 603979776 | bytes 5079040 | tf_op jit(solution)/shard_map/pallas_call | solution.py:34
  53.8 1.7 %collective-permute-start.15 = (bf16[144,1024]{1,0:T(8,128)(2,1)S(1)}, bf16[144,1024]{1,0:T(8,128)(2,1)S(1)}, u32[]{:S(2)}, u32[]{:S(2)}) collective-permute-start(bf16[144,1024]{1,0:T(8,128)(2,1)S(1)} %get-tuple-element.58), channel_id=1, source_target_pairs={{0,2},{1,3},{2,0},{3,1},{4,6},{5,7},{6,4},{7,5},{8,10},{9,11},{10,... | collective-permute-start | bytes 884744 | tf_op jit(solution)/shard_map/ppermute | solution.py:274
  55.5 3.2 %collective-permute-done.11.refs_1_ = bf16[144,1024]{1,0:T(8,128)(2,1)S(1)} collective-permute-done((bf16[144,1024]{1,0:T(8,128)(2,1)S(1)}, bf16[144,1024]{1,0:T(8,128)(2,1)S(1)}, u32[]{:S(2)}, u32[]{:S(2)}) %collective-permute-start.11) | collective-permute-done | bytes 294944 | tf_op jit(solution)/shard_map/ppermute | solution.py:274
  58.7 2.7 %collective-permute-done.19.refs_5_ = bf16[144,1024]{1,0:T(8,128)(2,1)S(1)} collective-permute-done((bf16[144,1024]{1,0:T(8,128)(2,1)S(1)}, bf16[144,1024]{1,0:T(8,128)(2,1)S(1)}, u32[]{:S(2)}, u32[]{:S(2)}) %collective-permute-start.19) | collective-permute-done | bytes 294944 | tf_op jit(solution)/shard_map/ppermute | solution.py:274
  61.4 1.0 %shard_map.116 = (bf16[128,1024]{1,0:T(8,128)(2,1)S(1)}, bf16[128,1024]{1,0:T(8,128)(2,1)S(1)}, bf16[128,1024]{1,0:T(8,128)(2,1)S(1)}, bf16[128,1024]{1,0:T(8,128)(2,1)S(1)}) custom-call(bf16[144,1024]{1,0:T(8,128)(2,1)S(1)} %get-tuple-element.55.refs_3_.refs_0_, bf16[144,1024]{1,0:T(8,128)(2,1)S(1)} %get-tuple-element.63.refs_1_, ...), custom_call_target="tpu_custom_call" | custom-call | flops 603979776 | bytes 3407872 | tf_op jit(solution)/shard_map/pallas_call | solution.py:34
  63.6 3.0 %collective-permute-done.15.refs_1_ = bf16[144,1024]{1,0:T(8,128)(2,1)S(1)} collective-permute-done((bf16[144,1024]{1,0:T(8,128)(2,1)S(1)}, bf16[144,1024]{1,0:T(8,128)(2,1)S(1)}, u32[]{:S(2)}, u32[]{:S(2)}) %collective-permute-start.15) | collective-permute-done | bytes 294944 | tf_op jit(solution)/shard_map/ppermute | solution.py:274
  67.0 1.3 %collective-permute-start.16 = (bf16[144,256]{1,0:T(8,128)(2,1)S(1)}, bf16[144,256]{1,0:T(8,128)(2,1)S(1)}, u32[]{:S(2)}, u32[]{:S(2)}) collective-permute-start(bf16[144,256]{1,0:T(8,128)(2,1)S(1)} %get-tuple-element.60), channel_id=1, source_target_pairs={{0,4},{1,5},{2,6},{3,7},{4,0},{5,1},{6,2},{7,3},{8,12},{9,13},{10,... | collective-permute-start | bytes 221192 | tf_op jit(solution)/shard_map/ppermute | solution.py:274
  68.4 2.1 %collective-permute-start.17 = (bf16[144,256]{1,0:T(8,128)(2,1)S(1)}, bf16[144,256]{1,0:T(8,128)(2,1)S(1)}, u32[]{:S(2)}, u32[]{:S(2)}) collective-permute-start(bf16[144,256]{1,0:T(8,128)(2,1)S(1)} %get-tuple-element.61), channel_id=1, source_target_pairs={{0,8},{1,9},{2,10},{3,11},{4,12},{5,13},{6,14},{7,15},{8,0},{9,1},... | collective-permute-start | bytes 221192 | tf_op jit(solution)/shard_map/ppermute | solution.py:274
  70.5 1.0 %collective-permute-start.18 = (bf16[144,256]{1,0:T(8,128)(2,1)S(1)}, bf16[144,256]{1,0:T(8,128)(2,1)S(1)}, u32[]{:S(2)}, u32[]{:S(2)}) collective-permute-start(bf16[144,256]{1,0:T(8,128)(2,1)S(1)} %get-tuple-element.62), channel_id=1, source_target_pairs={{0,12},{1,13},{2,14},{3,15},{4,8},{5,9},{6,10},{7,11},{8,4},{9,5},... | collective-permute-start | bytes 221192 | tf_op jit(solution)/shard_map/ppermute | solution.py:274
  71.5 2.0 %shard_map.117 = (bf16[1,512,1024]{2,1,0:T(8,128)(2,1)}, f32[8,128]{1,0:T(8,128)S(1)}) custom-call(bf16[144,1024]{1,0:T(8,128)(2,1)S(1)} %get-tuple-element.55.refs_3_.refs_0_, bf16[144,1024]{1,0:T(8,128)(2,1)S(1)} %get-tuple-element.63.refs_1_, bf16[144,1024]{1,0:T(8,128)(2,1)S(1)} %get-tuple-element.64.refs_2_, ...), custom_call_target="tpu_custom_call" | custom-call | flops 603979776 | bytes 4460544 | tf_op jit(solution)/shard_map/pallas_call | solution.py:34
  73.5 2.0 %collective-permute-done.17.refs_4_ = bf16[144,256]{1,0:T(8,128)(2,1)S(1)} collective-permute-done((bf16[144,256]{1,0:T(8,128)(2,1)S(1)}, bf16[144,256]{1,0:T(8,128)(2,1)S(1)}, u32[]{:S(2)}, u32[]{:S(2)}) %collective-permute-start.17) | collective-permute-done | bytes 73760 | tf_op jit(solution)/shard_map/ppermute | solution.py:274
  75.6 1.2 %collective-permute-done.18.refs_5_ = bf16[144,256]{1,0:T(8,128)(2,1)S(1)} collective-permute-done((bf16[144,256]{1,0:T(8,128)(2,1)S(1)}, bf16[144,256]{1,0:T(8,128)(2,1)S(1)}, u32[]{:S(2)}, u32[]{:S(2)}) %collective-permute-start.18) | collective-permute-done | bytes 73760 | tf_op jit(solution)/shard_map/ppermute | solution.py:274
  76.7 1.1 %shard_map.118 = bf16[1,128,1024]{2,1,0:T(8,128)(2,1)} custom-call(bf16[128,1024]{1,0:T(8,128)(2,1)S(1)} %get-tuple-element.45.refs_4_.refs_0_, s32[8,128]{1,0:T(8,128)S(1)} %get-tuple-element.43.refs_5_.refs_1_, bf16[144,256]{1,0:T(8,128)(2,1)S(1)} %get-tuple-element.59.refs_2_, bf16[144,256]{1,0:T(8,128)(2,1)S(1)} %collective-permute-done.16.refs_3_, ...), custom_call_target="tpu_custom_call" | custom-call | bytes 823296 | tf_op jit(solution)/shard_map/pallas_call | solution.py:34
  (35 shorter events, 7.9 us)
Async XLA Ops:
  0.6 37.0 %copy-start.1 = (bf16[1,1024,1024]{2,1,0:T(8,128)(2,1)S(1)}, bf16[1,1024,1024]{2,1,0:T(8,128)(2,1)}, u32[]{:S(2)}) copy-start(bf16[1,1024,1024]{2,1,0:T(8,128)(2,1)} %param.17) | copy-start | bytes 6291460
  2.0 35.7 %copy-start = (bf16[1024,1024]{1,0:T(8,128)(2,1)S(1)}, bf16[1024,1024]{1,0:T(8,128)(2,1)}, u32[]{:S(2)}) copy-start(bf16[1024,1024]{1,0:T(8,128)(2,1)} %refs_1_.9) | copy-start | bytes 6291460
  2.0 13.3 %collective-permute-start.1 = (bf16[1040,128]{1,0:T(8,128)(2,1)S(1)}, bf16[1040,128]{1,0:T(8,128)(2,1)S(1)}, u32[]{:S(2)}, u32[]{:S(2)}) collective-permute-start(bf16[1040,128]{1,0:T(8,128)(2,1)S(1)} %get-tuple-element.44), channel_id=1, source_target_pairs={{1,0},{2,1},{3,2},{4,3},{5,4},{6,5},{7,6},{8,7},{9,8},{10,9},{11,1... | collective-permute-start | bytes 798728 | tf_op jit(solution)/shard_map/ppermute | solution.py:306
  3.4 16.7 %collective-permute-start = (bf16[1040,128]{1,0:T(8,128)(2,1)S(1)}, bf16[1040,128]{1,0:T(8,128)(2,1)S(1)}, u32[]{:S(2)}, u32[]{:S(2)}) collective-permute-start(bf16[1040,128]{1,0:T(8,128)(2,1)S(1)} %get-tuple-element.37.refs_4_), channel_id=1, source_target_pairs={{0,1},{1,2},{2,3},{3,4},{4,5},{5,6},{6,7},{7,8},{8,9},{9,10},{10,1... | collective-permute-start | bytes 798728 | tf_op jit(solution)/shard_map/ppermute | solution.py:305
  10.3 16.5 %collective-permute-start.5 = (bf16[144,256]{1,0:T(8,128)(2,1)S(1)}, bf16[144,256]{1,0:T(8,128)(2,1)S(1)}, u32[]{:S(2)}, u32[]{:S(2)}) collective-permute-start(bf16[144,256]{1,0:T(8,128)(2,1)S(1)} %get-tuple-element.51), channel_id=1, source_target_pairs={{0,4},{1,5},{2,6},{3,7},{4,0},{5,1},{6,2},{7,3},{8,12},{9,13},{10,... | collective-permute-start | bytes 221192 | tf_op jit(solution)/shard_map/ppermute | solution.py:274
  12.7 15.1 %collective-permute-start.6 = (bf16[144,256]{1,0:T(8,128)(2,1)S(1)}, bf16[144,256]{1,0:T(8,128)(2,1)S(1)}, u32[]{:S(2)}, u32[]{:S(2)}) collective-permute-start(bf16[144,256]{1,0:T(8,128)(2,1)S(1)} %get-tuple-element.52), channel_id=1, source_target_pairs={{0,8},{1,9},{2,10},{3,11},{4,12},{5,13},{6,14},{7,15},{8,0},{9,1},... | collective-permute-start | bytes 221192 | tf_op jit(solution)/shard_map/ppermute | solution.py:274
  15.3 12.5 %collective-permute-start.7 = (bf16[144,256]{1,0:T(8,128)(2,1)S(1)}, bf16[144,256]{1,0:T(8,128)(2,1)S(1)}, u32[]{:S(2)}, u32[]{:S(2)}) collective-permute-start(bf16[144,256]{1,0:T(8,128)(2,1)S(1)} %get-tuple-element.53), channel_id=1, source_target_pairs={{0,12},{1,13},{2,14},{3,15},{4,8},{5,9},{6,10},{7,11},{8,4},{9,5},... | collective-permute-start | bytes 221192 | tf_op jit(solution)/shard_map/ppermute | solution.py:274
  21.6 7.5 %collective-permute-start.2 = (bf16[144,256]{1,0:T(8,128)(2,1)S(1)}, bf16[144,256]{1,0:T(8,128)(2,1)S(1)}, u32[]{:S(2)}, u32[]{:S(2)}) collective-permute-start(bf16[144,256]{1,0:T(8,128)(2,1)S(1)} %get-tuple-element.47), channel_id=1, source_target_pairs={{0,4},{1,5},{2,6},{3,7},{4,0},{5,1},{6,2},{7,3},{8,12},{9,13},{10,... | collective-permute-start | bytes 221192 | tf_op jit(solution)/shard_map/ppermute | solution.py:274
  24.0 7.3 %collective-permute-start.3 = (bf16[144,256]{1,0:T(8,128)(2,1)S(1)}, bf16[144,256]{1,0:T(8,128)(2,1)S(1)}, u32[]{:S(2)}, u32[]{:S(2)}) collective-permute-start(bf16[144,256]{1,0:T(8,128)(2,1)S(1)} %get-tuple-element.48), channel_id=1, source_target_pairs={{0,8},{1,9},{2,10},{3,11},{4,12},{5,13},{6,14},{7,15},{8,0},{9,1},... | collective-permute-start | bytes 221192 | tf_op jit(solution)/shard_map/ppermute | solution.py:274
  26.8 6.2 %collective-permute-start.4 = (bf16[144,256]{1,0:T(8,128)(2,1)S(1)}, bf16[144,256]{1,0:T(8,128)(2,1)S(1)}, u32[]{:S(2)}, u32[]{:S(2)}) collective-permute-start(bf16[144,256]{1,0:T(8,128)(2,1)S(1)} %get-tuple-element.49), channel_id=1, source_target_pairs={{0,12},{1,13},{2,14},{3,15},{4,8},{5,9},{6,10},{7,11},{8,4},{9,5},... | collective-permute-start | bytes 221192 | tf_op jit(solution)/shard_map/ppermute | solution.py:274
  28.2 9.4 %collective-permute-start.9 = (bf16[144,1024]{1,0:T(8,128)(2,1)S(1)}, bf16[144,1024]{1,0:T(8,128)(2,1)S(1)}, u32[]{:S(2)}, u32[]{:S(2)}) collective-permute-start(bf16[144,1024]{1,0:T(8,128)(2,1)S(1)} %shard_map.108.refs_4_), channel_id=1, source_target_pairs={{0,2},{1,3},{2,0},{3,1},{4,6},{5,7},{6,4},{7,5},{8,10},{9,11},{10,... | collective-permute-start | bytes 884744 | tf_op jit(solution)/shard_map/ppermute | solution.py:274
  28.3 9.4 %collective-permute-start.8 = (bf16[144,1024]{1,0:T(8,128)(2,1)S(1)}, bf16[144,1024]{1,0:T(8,128)(2,1)S(1)}, u32[]{:S(2)}, u32[]{:S(2)}) collective-permute-start(bf16[144,1024]{1,0:T(8,128)(2,1)S(1)} %shard_map.108.refs_4_), channel_id=1, source_target_pairs={{0,1},{1,0},{2,3},{3,2},{4,5},{5,4},{6,7},{7,6},{8,9},{9,8},{10,11... | collective-permute-start | bytes 884744 | tf_op jit(solution)/shard_map/ppermute | solution.py:274
  33.4 12.7 %collective-permute-start.10 = (bf16[144,1024]{1,0:T(8,128)(2,1)S(1)}, bf16[144,1024]{1,0:T(8,128)(2,1)S(1)}, u32[]{:S(2)}, u32[]{:S(2)}) collective-permute-start(bf16[144,1024]{1,0:T(8,128)(2,1)S(1)} %shard_map.107.refs_0_), channel_id=1, source_target_pairs={{0,3},{1,2},{2,1},{3,0},{4,7},{5,6},{6,5},{7,4},{8,11},{9,10},{10,... | collective-permute-start | bytes 884744 | tf_op jit(solution)/shard_map/ppermute | solution.py:274
  34.0 15.8 %collective-permute-start.12 = (bf16[144,1024]{1,0:T(8,128)(2,1)S(1)}, bf16[144,1024]{1,0:T(8,128)(2,1)S(1)}, u32[]{:S(2)}, u32[]{:S(2)}) collective-permute-start(bf16[144,1024]{1,0:T(8,128)(2,1)S(1)} %shard_map.107.refs_0_), channel_id=1, source_target_pairs={{0,1},{1,0},{2,3},{3,2},{4,5},{5,4},{6,7},{7,6},{8,9},{9,8},{10,11... | collective-permute-start | bytes 884744 | tf_op jit(solution)/shard_map/ppermute | solution.py:274
  35.1 17.7 %collective-permute-start.14 = (bf16[144,1024]{1,0:T(8,128)(2,1)S(1)}, bf16[144,1024]{1,0:T(8,128)(2,1)S(1)}, u32[]{:S(2)}, u32[]{:S(2)}) collective-permute-start(bf16[144,1024]{1,0:T(8,128)(2,1)S(1)} %shard_map.107.refs_0_), channel_id=1, source_target_pairs={{0,2},{1,3},{2,0},{3,1},{4,6},{5,7},{6,4},{7,5},{8,10},{9,11},{10,... | collective-permute-start | bytes 884744 | tf_op jit(solution)/shard_map/ppermute | solution.py:274
  47.0 11.7 %collective-permute-start.11 = (bf16[144,1024]{1,0:T(8,128)(2,1)S(1)}, bf16[144,1024]{1,0:T(8,128)(2,1)S(1)}, u32[]{:S(2)}, u32[]{:S(2)}) collective-permute-start(bf16[144,1024]{1,0:T(8,128)(2,1)S(1)} %get-tuple-element.56), channel_id=1, source_target_pairs={{0,3},{1,2},{2,1},{3,0},{4,7},{5,6},{6,5},{7,4},{8,11},{9,10},{10,... | collective-permute-start | bytes 884744 | tf_op jit(solution)/shard_map/ppermute | solution.py:274
  47.4 14.0 %collective-permute-start.19 = (bf16[144,1024]{1,0:T(8,128)(2,1)S(1)}, bf16[144,1024]{1,0:T(8,128)(2,1)S(1)}, u32[]{:S(2)}, u32[]{:S(2)}) collective-permute-start(bf16[144,1024]{1,0:T(8,128)(2,1)S(1)} %collective-permute-done.8.refs_3_.refs_6_), channel_id=1, source_target_pairs={{0,2},{1,3},{2,0},{3,1},{4,6},{5,7},{6,4},{7,5},{8,10},{9,11},{10,... | collective-permute-start | bytes 884744 | tf_op jit(solution)/shard_map/ppermute | solution.py:274
  50.8 12.3 %collective-permute-start.13 = (bf16[144,1024]{1,0:T(8,128)(2,1)S(1)}, bf16[144,1024]{1,0:T(8,128)(2,1)S(1)}, u32[]{:S(2)}, u32[]{:S(2)}) collective-permute-start(bf16[144,1024]{1,0:T(8,128)(2,1)S(1)} %get-tuple-element.57), channel_id=1, source_target_pairs={{0,1},{1,0},{2,3},{3,2},{4,5},{5,4},{6,7},{7,6},{8,9},{9,8},{10,11... | collective-permute-start | bytes 884744 | tf_op jit(solution)/shard_map/ppermute | solution.py:274
  53.8 12.8 %collective-permute-start.15 = (bf16[144,1024]{1,0:T(8,128)(2,1)S(1)}, bf16[144,1024]{1,0:T(8,128)(2,1)S(1)}, u32[]{:S(2)}, u32[]{:S(2)}) collective-permute-start(bf16[144,1024]{1,0:T(8,128)(2,1)S(1)} %get-tuple-element.58), channel_id=1, source_target_pairs={{0,2},{1,3},{2,0},{3,1},{4,6},{5,7},{6,4},{7,5},{8,10},{9,11},{10,... | collective-permute-start | bytes 884744 | tf_op jit(solution)/shard_map/ppermute | solution.py:274
  62.5 5.9 %collective-permute-start.20 = (bf16[128,1024]{1,0:T(8,128)(2,1)S(1)}, bf16[128,1024]{1,0:T(8,128)(2,1)S(1)}, u32[]{:S(2)}, u32[]{:S(2)}) collective-permute-start(bf16[128,1024]{1,0:T(8,128)(2,1)S(1)} %get-tuple-element.66), channel_id=1, source_target_pairs={{0,16},{16,0},{1,17},{17,1},{2,18},{18,2},{3,19},{19,3},{4,20},{20... | collective-permute-start | bytes 786440 | tf_op jit(solution)/shard_map/ppermute | solution.py:366
  62.5 7.9 %collective-permute-start.21 = (bf16[128,1024]{1,0:T(8,128)(2,1)S(1)}, bf16[128,1024]{1,0:T(8,128)(2,1)S(1)}, u32[]{:S(2)}, u32[]{:S(2)}) collective-permute-start(bf16[128,1024]{1,0:T(8,128)(2,1)S(1)} %get-tuple-element.67), channel_id=1, source_target_pairs={{0,16},{16,0},{1,17},{17,1},{2,18},{18,2},{3,19},{19,3},{4,20},{20... | collective-permute-start | bytes 786440 | tf_op jit(solution)/shard_map/ppermute | solution.py:366
  63.0 8.5 %collective-permute-start.22 = (bf16[128,1024]{1,0:T(8,128)(2,1)S(1)}, bf16[128,1024]{1,0:T(8,128)(2,1)S(1)}, u32[]{:S(2)}, u32[]{:S(2)}) collective-permute-start(bf16[128,1024]{1,0:T(8,128)(2,1)S(1)} %get-tuple-element.68), channel_id=1, source_target_pairs={{0,16},{16,0},{1,17},{17,1},{2,18},{18,2},{3,19},{19,3},{4,20},{20... | collective-permute-start | bytes 786440 | tf_op jit(solution)/shard_map/ppermute | solution.py:366
  63.1 8.4 %collective-permute-start.23 = (bf16[128,1024]{1,0:T(8,128)(2,1)S(1)}, bf16[128,1024]{1,0:T(8,128)(2,1)S(1)}, u32[]{:S(2)}, u32[]{:S(2)}) collective-permute-start(bf16[128,1024]{1,0:T(8,128)(2,1)S(1)} %get-tuple-element.69), channel_id=1, source_target_pairs={{0,16},{16,0},{1,17},{17,1},{2,18},{18,2},{3,19},{19,3},{4,20},{20... | collective-permute-start | bytes 786440 | tf_op jit(solution)/shard_map/ppermute | solution.py:366
  67.0 6.5 %collective-permute-start.16 = (bf16[144,256]{1,0:T(8,128)(2,1)S(1)}, bf16[144,256]{1,0:T(8,128)(2,1)S(1)}, u32[]{:S(2)}, u32[]{:S(2)}) collective-permute-start(bf16[144,256]{1,0:T(8,128)(2,1)S(1)} %get-tuple-element.60), channel_id=1, source_target_pairs={{0,4},{1,5},{2,6},{3,7},{4,0},{5,1},{6,2},{7,3},{8,12},{9,13},{10,... | collective-permute-start | bytes 221192 | tf_op jit(solution)/shard_map/ppermute | solution.py:274
  68.4 7.2 %collective-permute-start.17 = (bf16[144,256]{1,0:T(8,128)(2,1)S(1)}, bf16[144,256]{1,0:T(8,128)(2,1)S(1)}, u32[]{:S(2)}, u32[]{:S(2)}) collective-permute-start(bf16[144,256]{1,0:T(8,128)(2,1)S(1)} %get-tuple-element.61), channel_id=1, source_target_pairs={{0,8},{1,9},{2,10},{3,11},{4,12},{5,13},{6,14},{7,15},{8,0},{9,1},... | collective-permute-start | bytes 221192 | tf_op jit(solution)/shard_map/ppermute | solution.py:274
  70.5 6.3 %collective-permute-start.18 = (bf16[144,256]{1,0:T(8,128)(2,1)S(1)}, bf16[144,256]{1,0:T(8,128)(2,1)S(1)}, u32[]{:S(2)}, u32[]{:S(2)}) collective-permute-start(bf16[144,256]{1,0:T(8,128)(2,1)S(1)} %get-tuple-element.62), channel_id=1, source_target_pairs={{0,12},{1,13},{2,14},{3,15},{4,8},{5,9},{6,10},{7,11},{8,4},{9,5},... | collective-permute-start | bytes 221192 | tf_op jit(solution)/shard_map/ppermute | solution.py:274

commit v4 on v3

--- a/solution.py
+++ b/solution.py
@@ -76,19 +76,21 @@
     return lax.axis_index("ep") // SPLIT
 
 
-def halo_body(key_hbm, value_hbm, mask_hbm, up_ref, down_ref, key_ref, value_ref, mask_ref, sems):
+def halo_body(key_hbm, value_hbm, mask_hbm, near_out, far_out, key_ref, value_ref, mask_ref, sems):
     copies = load(((key_hbm, key_ref), (value_hbm, value_ref), (mask_hbm, mask_ref)), sems)
     for c in copies:
         c.wait()
     rows = key_ref.shape[1]
     width = key_ref.shape[2] // HEADS
-    for message, first in ((up_ref, rows - HALO), (down_ref, 0)):
+    odd = lax.axis_index("ep") % 2
+    for message, last in ((near_out, 1 - odd), (far_out, odd)):
+        mine = pl.ds(pl.multiple_of(last * (rows - HALO), HALO), HALO)
         for head in range(HEADS):
             columns = slice(head * width, (head + 1) * width)
-            message[head * HALO : (head + 1) * HALO, :] = key_ref[0, first : first + HALO, columns]
+            message[head * HALO : (head + 1) * HALO, :] = key_ref[0, mine, columns]
             start = (HEADS + head) * HALO
-            message[start : start + HALO, :] = value_ref[0, first : first + HALO, columns]
-        mask = mask_ref[:, first : first + HALO].astype(F32)
+            message[start : start + HALO, :] = value_ref[0, mine, columns]
+        mask = jnp.where(last == 1, mask_ref[:, rows - HALO :], mask_ref[:, :HALO]).astype(F32)
         mask = jnp.concatenate([mask, jnp.zeros((1, width - HALO), F32)], axis=1)
         message[2 * HEADS * HALO :, :] = jnp.broadcast_to(mask, (16, width)).astype(BF16)
 
@@ -105,8 +107,8 @@
     count = rows.shape[0]
     stacked = column_blocks(rows)
     height = message_refs[0].shape[0]
-    for k, message in enumerate(message_refs):
-        mine = labels == (home ^ k)
+    for p, message in enumerate(message_refs):
+        mine = labels == (home ^ (-p % len(message_refs)))
         places = [one_hot(mine & (slot + j * capacity == iota((height, count), 0))) for j in range(PARTS)]
         message[...] = dot(jnp.concatenate(places, axis=1), stacked).astype(BF16)
 
@@ -169,36 +171,41 @@
 
 
 def attention_body(
-    capacity, query_ref, token_ref, key_ref, value_ref, mask_ref, route_ref, before_ref, after_ref, mixed_ref, *message_refs
+    capacity, query_ref, token_ref, key_ref, value_ref, mask_ref, route_ref, near_ref, far_ref, mixed_ref, *message_refs
 ):
     rows, features = query_ref.shape[1:]
     width = features // HEADS
     position = lax.axis_index("ep")
-    last = lax.axis_size("ep") - 1
+    odd = position % 2
+    inside = (position > 0) & (position < lax.axis_size("ep") - 1)
     mask_row = 2 * HEADS * HALO
     mask = jnp.concatenate(
         [
-            before_ref[mask_row : mask_row + 1, :HALO].astype(F32) * jnp.where(position > 0, 1.0, 0.0),
+            near_ref[mask_row : mask_row + 1, :HALO].astype(F32),
             mask_ref[...].astype(F32),
-            after_ref[mask_row : mask_row + 1, :HALO].astype(F32) * jnp.where(position < last, 1.0, 0.0),
+            far_ref[mask_row : mask_row + 1, :HALO].astype(F32) * jnp.where(inside, 1.0, 0.0),
         ],
         axis=1,
     )
     count = rows + 2 * HALO
-    offset = iota((rows, count), 1) - HALO - iota((rows, count), 0)
+    column = iota((rows, count), 1)
+    near_first = jnp.where(odd == 1, -HALO, rows)
+    far_first = jnp.where(odd == 1, rows, -HALO) - HALO - rows
+    first = jnp.where(column < HALO, near_first, jnp.where(column < HALO + rows, -HALO, far_first))
+    offset = column + first - iota((rows, count), 0)
     usable = (jnp.abs(offset) <= HALO) & ((mask > 0.5) | (offset == 0))
     scale = width ** (-0.5)
     for head in range(HEADS):
         columns = slice(head * width, (head + 1) * width)
         at, value_at = head * HALO, (HEADS + head) * HALO
         keys = jnp.concatenate(
-            [before_ref[at : at + HALO, :], key_ref[0, :, columns], after_ref[at : at + HALO, :]], axis=0
+            [near_ref[at : at + HALO, :], key_ref[0, :, columns], far_ref[at : at + HALO, :]], axis=0
         )
         values = jnp.concatenate(
             [
-                before_ref[value_at : value_at + HALO, :],
+                near_ref[value_at : value_at + HALO, :],
                 value_ref[0, :, columns],
-                after_ref[value_at : value_at + HALO, :],
+                far_ref[value_at : value_at + HALO, :],
             ],
             axis=0,
         )
@@ -210,8 +217,9 @@
     pack(mixed_ref[...], route_ref[0:1, :], route_ref[1:2, :], message_refs, capacity)
 
 
-def expert_body(rows_ref, in_ref, out_ref, hidden_ref, partial_ref):
-    rows = rows_ref[...]
+def expert_body(*refs):
+    *row_refs, in_ref, out_ref, hidden_ref, partial_ref = refs
+    rows = jnp.concatenate([r[...] for r in row_refs], axis=0)
     for at in range(0, in_ref.shape[1], STEP):
         hidden_ref[:, at : at + STEP] = jax.nn.gelu(dot(rows, in_ref[:, at : at + STEP])).astype(BF16)
     hidden = hidden_ref[...]
@@ -219,7 +227,7 @@
         partial_ref[:, at : at + STEP] = dot(hidden, out_ref[:, at : at + STEP]).astype(BF16)
 
 
-def finish_body(capacity, order, mixed_ref, route_ref, *refs):
+def finish_body(capacity, mixed_ref, route_ref, *refs):
     *message_refs, layer_ref = refs
     home = home_plane()
     labels, slot = route_ref[0:1, :], route_ref[1:2, :]
@@ -228,7 +236,8 @@
     stacked = jnp.concatenate([m[...] for m in message_refs], axis=0)
     for j in range(PARTS):
         places = [
-            one_hot((labels == (home ^ k)) & (slot + j * capacity == iota((block, count), 0))) for k in order
+            one_hot((labels == (home ^ (-p % len(message_refs)))) & (slot + j * capacity == iota((block, count), 0)))
+            for p in range(len(message_refs))
         ]
         taken = dot(jnp.concatenate(places, axis=0), stacked, (0, 0))
         columns = slice(j * width, (j + 1) * width)
@@ -236,7 +245,7 @@
 
 
 def half_terms(refs, side):
-    hidden_refs, cot_refs = refs[:SPLIT], refs[SPLIT : 2 * SPLIT]
+    hidden_refs, cot_refs = refs[:SPLIT], refs[SPLIT : 2 * SPLIT + 1]
     cot = jnp.concatenate([c[...] for c in cot_refs], axis=0)
     half = hidden_refs[0].shape[1] // 2
     start = (lax.axis_index("grp") ^ side) * half
@@ -247,7 +256,7 @@
 
 
 def other_half_body(*refs):
-    piece_refs = refs[2 * SPLIT :]
+    piece_refs = refs[2 * SPLIT + 1 :]
     rows = piece_refs[0].shape[0]
     for at, term in half_terms(refs, 1):
         for r in range(0, STEP, rows):
@@ -255,7 +264,7 @@
 
 
 def own_half_body(*refs):
-    *piece_refs, grad_ref, done_ref = refs[2 * SPLIT :]
+    *piece_refs, grad_ref, done_ref = refs[2 * SPLIT + 1 :]
     rows = piece_refs[0].shape[0]
     done_ref[...] = jnp.zeros_like(done_ref)
     for at, term in half_terms(refs, 0):
@@ -266,7 +275,7 @@
 
 def whole_term_body(*refs):
     hidden = jnp.concatenate([h[...] for h in refs[:SPLIT]], axis=0)
-    cot = jnp.concatenate([c[...] for c in refs[SPLIT : 2 * SPLIT]], axis=0)
+    cot = jnp.concatenate([c[...] for c in refs[SPLIT : 2 * SPLIT + 1]], axis=0)
     refs[-1][...] = dot(hidden, cot, (0, 0)).astype(BF16)
 
 
@@ -274,8 +283,14 @@
     return lax.ppermute(value, "ep", [(i, i ^ apart) for i in range(lax.axis_size("ep"))])
 
 
+def forwarded(along_x, along_y):
+    half = along_x.shape[0] // 32 * 16
+    return permute(along_x[:half], 2), permute(along_y[half:], 1)
+
+
 def along_line(messages):
-    return [m if k == 0 else permute(m, SPLIT * k) for k, m in enumerate(messages)]
+    count = len(messages)
+    return [m if p == 0 else permute(m, SPLIT * (count - p)) for p, m in enumerate(messages)]
 
 
 def shards(tokens, queries, keys, values, key_mask, labels, cotangent, weight_in, weight_out):
@@ -295,22 +310,22 @@
     block_scratch = pltpu.VMEM((1, rows_here, features), BF16)
 
     halo = out(2 * HEADS * HALO + 16, head_width)
-    up, down, key_here, value_here, mask_here = call(
+    near, far, key_here, value_here, mask_here = call(
         halo_body,
         (halo, halo, block, block, out(1, rows_here, dtype=jnp.int32)),
         hbm=(keys, values, key_mask),
         scratch=[pltpu.SemaphoreType.DMA((3,))],
     )
-    steps = [(i, i + 1) for i in range(axis_count - 1)]
-    before = lax.ppermute(up, "ep", steps)
-    after = lax.ppermute(down, "ep", [(j, i) for i, j in steps])
+    near = permute(near, 1)
+    steps = [(i, i + 1) for i in range(1, axis_count - 1, 2)]
+    far = lax.ppermute(far, "ep", steps + [(j, i) for i, j in steps])
 
     gather = functools.partial(gather_body, capacity, experts, 0, 0)
     route, query_here, token_here, *sent = call(
         functools.partial(pack_body, capacity),
         [out(8, rows_here, dtype=jnp.int32), block, block] + [message] * experts,
         hbm=(cotangent, label_row, queries, tokens),
-        after=(up,),
+        after=(key_here,),
         scratch=[block_scratch, row_ints, pltpu.SemaphoreType.DMA((4,))],
         size=0,
     )
@@ -320,43 +335,37 @@
     mixed, *sent = call(
         functools.partial(attention_body, capacity),
         [out(rows_here, features)] + [message] * experts,
-        vmem=(query_here, token_here, key_here, value_here, mask_here, route, before, after),
+        vmem=(query_here, token_here, key_here, value_here, mask_here, route, near, far),
         flops=4 * rows_here * (rows_here + 2 * HALO) * features,
     )
 
     (cot_rows,) = call(gather, [out(plane_rows, features)], vmem=cot_got, after=(mixed,), size=0)
     cot_x, cot_y = permute(cot_rows, 1), permute(cot_rows, 2)
     (rows,) = call(gather, [out(plane_rows, features)], vmem=along_line(sent))
-    cot_xy = permute(cot_x, 2)
-
-    own_hidden, own_partial = call(
-        expert_body,
-        [out(plane_rows, hidden_units), out(plane_rows, features)],
-        vmem=(rows, in_here, out_here),
-        after=(cot_x, cot_y),
-        flops=4 * plane_rows * features * hidden_units,
-    )
-    hiddens, partials = [own_hidden], []
-    for k in (3, 1, 2):
+    cot_far = forwarded(cot_x, cot_y)
+
+    row_x, row_y = permute(rows, 1), permute(rows, 2)
+    hiddens, partials = [], []
+    for pieces, first in (((rows,), (cot_x, cot_y)), ((row_x,), ()), ((row_y,), ()), (forwarded(row_x, row_y), ())):
         hidden, partial = call(
             expert_body,
             [out(plane_rows, hidden_units), out(plane_rows, features)],
-            vmem=(permute(rows, k), in_here, out_here),
-            after=(own_hidden,),
+            vmem=(*pieces, in_here, out_here),
+            after=(*first, *hiddens[:1]),
             flops=4 * plane_rows * features * hidden_units,
         )
         hiddens.append(hidden)
         partials.append(partial)
 
-    total = own_partial
+    total = partials[0]
     totals = []
-    for partial, k in zip(partials[:-1], (3, 1)):
+    for k in (1, 2):
         (total,) = call(
-            add_body, [out(plane_rows, features, dtype=F32)], vmem=(total, permute(partial, k)), size=0
+            add_body, [out(plane_rows, features, dtype=F32)], vmem=(total, permute(partials[k], k)), size=0
         )
         totals.append(total)
-    last = permute(partials[-1], 2)
-    inputs = (*hiddens, cot_rows, cot_xy, cot_x, cot_y)
+    last = permute(partials[3], 3)
+    inputs = (*hiddens, cot_rows, cot_x, cot_y, *cot_far)
     flops = SPLIT * plane_rows * features * hidden_units
     if lax.axis_size("grp") == 2:
         half = hidden_units // 2
@@ -378,7 +387,7 @@
     sent = call(functools.partial(combine_body, capacity, experts), [message] * experts, vmem=(total, last))
     back = along_line(sent)
     (layer_out,) = call(
-        functools.partial(finish_body, capacity, range(experts)), [block], vmem=(mixed, route, *back), after=ready
+        functools.partial(finish_body, capacity), [block], vmem=(mixed, route, *back), after=ready
     )
     return (layer_out, grad)
 

time: 78.5 us -> 72.2 us (0.920)
  waiting for transfers between devices: 29.6 us -> 25.3 us
  starting transfers between devices: 33.9 us -> 32.3 us
    ppermute x2 -> x1, starting transfers between devices: 6.91 us -> 0.67 us  [shards(): far = lax.ppermute(far, 'ep', steps + [(j, i) for i, j in steps])]
    ppermute x2 -> x1, waiting for transfers between devices: 4.84 us -> 0.01 us  [shards(): far = lax.ppermute(far, 'ep', steps + [(j, i) for i, j in steps])]
    ppermute x18 -> x21, starting transfers between devices: 25.9 us -> 30.6 us  [permute(): lax.ppermute(value, 'ep', [(i, i ^ apart) for i in range(lax.axis_size('e...]
    ppermute x18 -> x21, waiting for transfers between devices: 24.8 us -> 25.3 us  [permute(): lax.ppermute(value, 'ep', [(i, i ^ apart) for i in range(lax.axis_size('e...]
  transfers between devices with their start and end apart: 24 -> 26, of which waited for: 11 -> 13; matrix products, arithmetic and copies ran while one was open for 0% -> 0% of each run, Pallas kernels for 14% -> 15%
where the time goes in v4:
time: 72.2 us; the launch traced here: 72.1 us
  starting transfers between devices  32.3 us (45%)
  waiting for transfers between devices  25.3 us (35%)
  Pallas kernels  13.5 us (19%)
  between operations  0.83 us (1%)
    ppermute x21, starting transfers between devices, permute(): lax.ppermute(value, 'ep', [(i, i ^ apart) for i in range(lax.axis_size('e...  30.6 us
    ppermute x21, waiting for transfers between devices, permute(): lax.ppermute(value, 'ep', [(i, i ^ apart) for i in range(lax.axis_size('e...  25.3 us
    pallas_call x15, Pallas kernels, call(): pl.pallas_call(kernel, out_shape=outs, in_specs=[VMEM] * len(vmem) + [HBM...  13.5 us
  transfers between devices with their start and end apart: 26, of which 13 were waited for; matrix products, arithmetic and copies ran while one was open for 0% of the time, Pallas kernels for 15%

profile of v4, /device:TPU:0, one launch (start us, length us, event | category | flops | bytes accessed | tf_op | source)
XLA Modules:
  0.0 72.1 jit_solution(12075828116726963927)
XLA Ops:
  0.6 1.3 %shard_map.104 = (bf16[1040,128]{1,0:T(8,128)(2,1)S(1)}, bf16[1040,128]{1,0:T(8,128)(2,1)S(1)}, bf16[1,128,1024]{2,1,0:T(8,128)(2,1)S(1)}, bf16[1,128,1024]{2,1,0:T(8,128)(2,1)S(1)}, s32[1,128]{1,0:T(1,128)S(1)}) custom-call(bf16[1,128,1024]{2,1,0:T(8,128)(2,1)} %refs_0_.2, bf16[1,128,1024]{2,1,0:T(8,128)(2,1)} %refs_1_.4, s32[1,128]{1,0:T(1,128)} %refs_2_.3), custom_call_target="tpu_custom_call" | custom-call | bytes 1582080 | tf_op jit(solution)/shard_map/pallas_call | solution.py:34
  2.0 3.0 %collective-permute-start = (bf16[1040,128]{1,0:T(8,128)(2,1)S(1)}, bf16[1040,128]{1,0:T(8,128)(2,1)S(1)}, u32[]{:S(2)}, u32[]{:S(2)}) collective-permute-start(bf16[1040,128]{1,0:T(8,128)(2,1)S(1)} %get-tuple-element.43), channel_id=1, source_target_pairs={{0,1},{1,0},{2,3},{3,2},{4,5},{5,4},{6,7},{7,6},{8,9},{9,8},{10,11... | collective-permute-start | bytes 798728 | tf_op jit(solution)/shard_map/ppermute | solution.py:283
  5.7 1.3 %shard_map.105 = (s32[8,128]{1,0:T(8,128)S(1)}, bf16[1,128,1024]{2,1,0:T(8,128)(2,1)S(1)}, bf16[1,128,1024]{2,1,0:T(8,128)(2,1)S(1)}, bf16[144,256]{1,0:T(8,128)...) custom-call(bf16[1,128,1024]{2,1,0:T(8,128)(2,1)} %refs_0_.3, ...), custom_call_target="tpu_custom_call" | custom-call | tf_op jit(solution)/shard_map/pallas_call | solution.py:34
  7.0 6.4 %collective-permute-start.5 = (bf16[144,256]{1,0:T(8,128)(2,1)S(1)}, bf16[144,256]{1,0:T(8,128)(2,1)S(1)}, u32[]{:S(2)}, u32[]{:S(2)}) collective-permute-start(bf16[144,256]{1,0:T(8,128)(2,1)S(1)} %get-tuple-element.51), channel_id=1, source_target_pairs={{0,12},{1,13},{2,14},{3,15},{4,8},{5,9},{6,10},{7,11},{8,4},{9,5},... | collective-permute-start | bytes 221192 | tf_op jit(solution)/shard_map/ppermute | solution.py:283
  14.1 2.3 %collective-permute-done.refs_6_ = bf16[1040,128]{1,0:T(8,128)(2,1)S(1)} collective-permute-done((bf16[1040,128]{1,0:T(8,128)(2,1)S(1)}, bf16[1040,128]{1,0:T(8,128)(2,1)S(1)}, u32[]{:S(2)}, u32[]{:S(2)}) %collective-permute-start) | collective-permute-done | bytes 266272 | tf_op jit(solution)/shard_map/ppermute | solution.py:283
  16.4 1.5 %shard_map.106 = (bf16[128,1024]{1,0:T(8,128)(2,1)S(1)}, bf16[144,256]{1,0:T(8,128)(2,1)S(1)}, bf16[144,256]{1,0:T(8,128)(2,1)S(1)}, bf16[144,256]{1,0:T(8,128)(2,1)S(1)}, bf16[144,256]{1,0:T(8,128)(2,1)S(1)}) custom-call(bf16[1,128,1024]{2,1,0:T(8,128)(2,1)S(1)} %get-tuple-element.38.refs_0_, bf16[1,128,1024]{2,1,0:T(8,128)(2,1)S(1)} %get-tuple-element.39.refs_1_, ...), custom_call_target="tpu_custom_call" | custom-call | flops 134217728 | bytes 2142720 | tf_op jit(solution)/shard_map/pallas_call | solution.py:34
  17.9 5.8 %collective-permute-start.2 = (bf16[144,256]{1,0:T(8,128)(2,1)S(1)}, bf16[144,256]{1,0:T(8,128)(2,1)S(1)}, u32[]{:S(2)}, u32[]{:S(2)}) collective-permute-start(bf16[144,256]{1,0:T(8,128)(2,1)S(1)} %get-tuple-element.47), channel_id=1, source_target_pairs={{0,12},{1,13},{2,14},{3,15},{4,8},{5,9},{6,10},{7,11},{8,4},{9,5},... | collective-permute-start | bytes 221192 | tf_op jit(solution)/shard_map/ppermute | solution.py:283
  23.7 2.0 %collective-permute-start.3 = (bf16[144,256]{1,0:T(8,128)(2,1)S(1)}, bf16[144,256]{1,0:T(8,128)(2,1)S(1)}, u32[]{:S(2)}, u32[]{:S(2)}) collective-permute-start(bf16[144,256]{1,0:T(8,128)(2,1)S(1)} %get-tuple-element.48), channel_id=1, source_target_pairs={{0,8},{1,9},{2,10},{3,11},{4,12},{5,13},{6,14},{7,15},{8,0},{9,1},... | collective-permute-start | bytes 221192 | tf_op jit(solution)/shard_map/ppermute | solution.py:283
  27.6 1.4 %collective-permute-done.3.refs_2_ = bf16[144,256]{1,0:T(8,128)(2,1)S(1)} collective-permute-done((bf16[144,256]{1,0:T(8,128)(2,1)S(1)}, bf16[144,256]{1,0:T(8,128)(2,1)S(1)}, u32[]{:S(2)}, u32[]{:S(2)}) %collective-permute-start.3) | collective-permute-done | bytes 73760 | tf_op jit(solution)/shard_map/ppermute | solution.py:283
  29.0 1.1 %collective-permute-done.4.refs_3_ = bf16[144,256]{1,0:T(8,128)(2,1)S(1)} collective-permute-done((bf16[144,256]{1,0:T(8,128)(2,1)S(1)}, bf16[144,256]{1,0:T(8,128)(2,1)S(1)}, u32[]{:S(2)}, u32[]{:S(2)}) %collective-permute-start.4) | collective-permute-done | bytes 73760 | tf_op jit(solution)/shard_map/ppermute | solution.py:283
  31.2 0.9 %collective-permute-start.12 = (bf16[144,1024]{1,0:T(8,128)(2,1)S(1)}, bf16[144,1024]{1,0:T(8,128)(2,1)S(1)}, u32[]{:S(2)}, u32[]{:S(2)}) collective-permute-start(bf16[144,1024]{1,0:T(8,128)(2,1)S(1)} %shard_map.107.refs_0_), channel_id=1, source_target_pairs={{0,2},{1,3},{2,0},{3,1},{4,6},{5,7},{6,4},{7,5},{8,10},{9,11},{10,... | collective-permute-start | bytes 884744 | tf_op jit(solution)/shard_map/ppermute | solution.py:283
  32.1 3.3 %collective-permute-done.9.refs_4_.refs_6_ = bf16[144,1024]{1,0:T(8,128)(2,1)S(1)} collective-permute-done((bf16[144,1024]{1,0:T(8,128)(2,1)S(1)}, bf16[144,1024]{1,0:T(8,128)(2,1)S(1)}, u32[]{:S(2)}, u32[]{:S(2)}) %collective-permute-start.9) | collective-permute-done | bytes 294944 | tf_op jit(solution)/shard_map/ppermute | solution.py:283
  35.4 1.7 %collective-permute-done.8.refs_3_.refs_5_ = bf16[144,1024]{1,0:T(8,128)(2,1)S(1)} collective-permute-done((bf16[144,1024]{1,0:T(8,128)(2,1)S(1)}, bf16[144,1024]{1,0:T(8,128)(2,1)S(1)}, u32[]{:S(2)}, u32[]{:S(2)}) %collective-permute-start.8) | collective-permute-done | bytes 294944 | tf_op jit(solution)/shard_map/ppermute | solution.py:283
  37.1 1.0 %shard_map.109 = (bf16[144,1024]{1,0:T(8,128)(2,1)S(1)}, bf16[144,1024]{1,0:T(8,128)(2,1)S(1)}) custom-call(bf16[144,1024]{1,0:T(8,128)(2,1)S(1)} %shard_map.107.refs_0_, bf16[1024,1024]{1,0:T(8,128)(2,1)S(1)} %copy-done, bf16[1024,1024]{1,0:T(8,128)(2,1)S(1)} %bitcast.2, bf16[144,1024]{1,0:T(8,128)(2,1)S(1)} %collective-permute-done.8.refs_3_.refs_5_, ...), custom_call_target="tpu_custom_call" | custom-call | flops 603979776 | bytes 5079040 | tf_op jit(solution)/shard_map/pallas_call | solution.py:34
  38.1 2.5 %collective-permute-done.10.refs_0_ = bf16[144,1024]{1,0:T(8,128)(2,1)S(1)} collective-permute-done((bf16[144,1024]{1,0:T(8,128)(2,1)S(1)}, bf16[144,1024]{1,0:T(8,128)(2,1)S(1)}, u32[]{:S(2)}, u32[]{:S(2)}) %collective-permute-start.10) | collective-permute-done | bytes 294944 | tf_op jit(solution)/shard_map/ppermute | solution.py:283
  40.6 1.0 %shard_map.110 = (bf16[144,1024]{1,0:T(8,128)(2,1)S(1)}, bf16[144,1024]{1,0:T(8,128)(2,1)S(1)}) custom-call(bf16[144,1024]{1,0:T(8,128)(2,1)S(1)} %collective-permute-done.10.refs_0_, bf16[1024,1024]{1,0:T(8,128)(2,1)S(1)} %copy-done, bf16[1024,1024]{1,0:T(8,128)(2,1)S(1)} %bitcast.3, bf16[144,1024]{1,0:T(8,128)(2,1)S(1)} %get-tuple-element.55.refs_3_.refs_4_.refs_0_), custom_call_target="tpu_custom_call" | custom-call | flops 603979776 | bytes 5079040 | tf_op jit(solution)/shard_map/pallas_call | solution.py:34
  41.6 1.6 %collective-permute-start.14 = (bf16[64,1024]{1,0:T(8,128)(2,1)S(1)}, bf16[64,1024]{1,0:T(8,128)(2,1)S(1)}, u32[]{:S(2)}, u32[]{:S(2)}) collective-permute-start(bf16[64,1024]{1,0:T(8,128)(2,1)S(1)} %slice.16), channel_id=1, source_target_pairs={{0,2},{1,3},{2,0},{3,1},{4,6},{5,7},{6,4},{7,5},{8,10},{9,11},{10,... | collective-permute-start | bytes 393224 | tf_op jit(solution)/shard_map/ppermute | solution.py:283
  43.3 1.0 %shard_map.112 = (bf16[144,1024]{1,0:T(8,128)(2,1)S(1)}, bf16[144,1024]{1,0:T(8,128)(2,1)S(1)}) custom-call(bf16[144,1024]{1,0:T(8,128)(2,1)S(1)} %collective-permute-done.12.refs_0_, bf16[1024,1024]{1,0:T(8,128)(2,1)S(1)} %copy-done, bf16[1024,1024]{1,0:T(8,128)(2,1)S(1)} %bitcast.4, bf16[144,1024]{1,0:T(8,128)(2,1)S(1)} %get-tuple-element.55.refs_3_.refs_4_.refs_0_), custom_call_target="tpu_custom_call" | custom-call | flops 603979776 | bytes 5079040 | tf_op jit(solution)/shard_map/pallas_call | solution.py:34
  44.8 2.1 %collective-permute-start.15 = (bf16[80,1024]{1,0:T(8,128)(2,1)S(1)}, bf16[80,1024]{1,0:T(8,128)(2,1)S(1)}, u32[]{:S(2)}, u32[]{:S(2)}) collective-permute-start(bf16[80,1024]{1,0:T(8,128)(2,1)S(1)} %slice.17), channel_id=1, source_target_pairs={{0,1},{1,0},{2,3},{3,2},{4,5},{5,4},{6,7},{7,6},{8,9},{9,8},{10,11... | collective-permute-start | bytes 491528 | tf_op jit(solution)/shard_map/ppermute | solution.py:283
  47.0 1.2 %collective-permute-done.14.refs_0_ = bf16[64,1024]{1,0:T(8,128)(2,1)S(1)} collective-permute-done((bf16[64,1024]{1,0:T(8,128)(2,1)S(1)}, bf16[64,1024]{1,0:T(8,128)(2,1)S(1)}, u32[]{:S(2)}, u32[]{:S(2)}) %collective-permute-start.14) | collective-permute-done | bytes 131104 | tf_op jit(solution)/shard_map/ppermute | solution.py:283
  48.1 1.5 %collective-permute-start.20 = (bf16[64,1024]{1,0:T(8,128)(2,1)S(1)}, bf16[64,1024]{1,0:T(8,128)(2,1)S(1)}, u32[]{:S(2)}, u32[]{:S(2)}) collective-permute-start(bf16[64,1024]{1,0:T(8,128)(2,1)S(1)} %slice.18), channel_id=1, source_target_pairs={{0,2},{1,3},{2,0},{3,1},{4,6},{5,7},{6,4},{7,5},{8,10},{9,11},{10,... | collective-permute-start | bytes 393224 | tf_op jit(solution)/shard_map/ppermute | solution.py:283
  49.6 4.4 %collective-permute-done.15.refs_1_ = bf16[80,1024]{1,0:T(8,128)(2,1)S(1)} collective-permute-done((bf16[80,1024]{1,0:T(8,128)(2,1)S(1)}, bf16[80,1024]{1,0:T(8,128)(2,1)S(1)}, u32[]{:S(2)}, u32[]{:S(2)}) %collective-permute-start.15) | collective-permute-done | bytes 163872 | tf_op jit(solution)/shard_map/ppermute | solution.py:283
  54.0 1.0 %shard_map.114 = (bf16[144,1024]{1,0:T(8,128)(2,1)S(1)}, bf16[144,1024]{1,0:T(8,128)(2,1)S(1)}) custom-call(bf16[64,1024]{1,0:T(8,128)(2,1)S(1)} %collective-permute-done.14.refs_0_, bf16[80,1024]{1,0:T(8,128)(2,1)S(1)} %collective-permute-done.15.refs_1_, bf16[1024,1024]{1,0:T(8,128)(2,1)S(1)} %copy-done, bf16[1024,1024]{1,0:T(8,128)(2,1)S(1)} %bitcast.5, ...), custom_call_target="tpu_custom_call" | custom-call | flops 603979776 | bytes 5079040 | tf_op jit(solution)/shard_map/pallas_call | solution.py:34
  55.2 1.0 %collective-permute-done.20.refs_7_ = bf16[64,1024]{1,0:T(8,128)(2,1)S(1)} collective-permute-done((bf16[64,1024]{1,0:T(8,128)(2,1)S(1)}, bf16[64,1024]{1,0:T(8,128)(2,1)S(1)}, u32[]{:S(2)}, u32[]{:S(2)}) %collective-permute-start.20) | collective-permute-done | bytes 131104 | tf_op jit(solution)/shard_map/ppermute | solution.py:283
  56.2 1.3 %collective-permute-done.21.refs_8_ = bf16[80,1024]{1,0:T(8,128)(2,1)S(1)} collective-permute-done((bf16[80,1024]{1,0:T(8,128)(2,1)S(1)}, bf16[80,1024]{1,0:T(8,128)(2,1)S(1)}, u32[]{:S(2)}, u32[]{:S(2)}) %collective-permute-start.21) | collective-permute-done | bytes 163872 | tf_op jit(solution)/shard_map/ppermute | solution.py:283
  57.6 1.0 %shard_map.116 = (bf16[128,1024]{1,0:T(8,128)(2,1)S(1)}, bf16[128,1024]{1,0:T(8,128)(2,1)S(1)}, bf16[128,1024]{1,0:T(8,128)(2,1)S(1)}, bf16[128,1024]{1,0:T(8,128)(2,1)S(1)}) custom-call(bf16[144,1024]{1,0:T(8,128)(2,1)S(1)} %get-tuple-element.55.refs_3_.refs_4_.refs_0_, bf16[144,1024]{1,0:T(8,128)(2,1)S(1)} %get-tuple-element.63.refs_1_, ...), custom_call_target="tpu_custom_call" | custom-call | flops 603979776 | bytes 3407872 | tf_op jit(solution)/shard_map/pallas_call | solution.py:34
  59.7 3.0 %collective-permute-done.16.refs_1_ = bf16[144,1024]{1,0:T(8,128)(2,1)S(1)} collective-permute-done((bf16[144,1024]{1,0:T(8,128)(2,1)S(1)}, bf16[144,1024]{1,0:T(8,128)(2,1)S(1)}, u32[]{:S(2)}, u32[]{:S(2)}) %collective-permute-start.16) | collective-permute-done | bytes 294944 | tf_op jit(solution)/shard_map/ppermute | solution.py:283
  63.1 1.2 %collective-permute-start.17 = (bf16[144,256]{1,0:T(8,128)(2,1)S(1)}, bf16[144,256]{1,0:T(8,128)(2,1)S(1)}, u32[]{:S(2)}, u32[]{:S(2)}) collective-permute-start(bf16[144,256]{1,0:T(8,128)(2,1)S(1)} %get-tuple-element.60), channel_id=1, source_target_pairs={{0,12},{1,13},{2,14},{3,15},{4,8},{5,9},{6,10},{7,11},{8,4},{9,5},... | collective-permute-start | bytes 221192 | tf_op jit(solution)/shard_map/ppermute | solution.py:283
  64.6 3.0 %collective-permute-start.19 = (bf16[144,256]{1,0:T(8,128)(2,1)S(1)}, bf16[144,256]{1,0:T(8,128)(2,1)S(1)}, u32[]{:S(2)}, u32[]{:S(2)}) collective-permute-start(bf16[144,256]{1,0:T(8,128)(2,1)S(1)} %get-tuple-element.62), channel_id=1, source_target_pairs={{0,4},{1,5},{2,6},{3,7},{4,0},{5,1},{6,2},{7,3},{8,12},{9,13},{10,... | collective-permute-start | bytes 221192 | tf_op jit(solution)/shard_map/ppermute | solution.py:283
  67.6 2.0 %shard_map.117 = (bf16[1,512,1024]{2,1,0:T(8,128)(2,1)}, f32[8,128]{1,0:T(8,128)S(1)}) custom-call(bf16[144,1024]{1,0:T(8,128)(2,1)S(1)} %get-tuple-element.55.refs_3_.refs_4_.refs_0_, bf16[144,1024]{1,0:T(8,128)(2,1)S(1)} %get-tuple-element.63.refs_1_, bf16[144,1024]{1,0:T(8,128)(2,1)S(1)} %get-tuple-element.64.refs_2_, ...), custom_call_target="tpu_custom_call" | custom-call | flops 603979776 | bytes 4460544 | tf_op jit(solution)/shard_map/pallas_call | solution.py:34
  69.6 1.3 %collective-permute-done.18.refs_4_ = bf16[144,256]{1,0:T(8,128)(2,1)S(1)} collective-permute-done((bf16[144,256]{1,0:T(8,128)(2,1)S(1)}, bf16[144,256]{1,0:T(8,128)(2,1)S(1)}, u32[]{:S(2)}, u32[]{:S(2)}) %collective-permute-start.18) | collective-permute-done | bytes 73760 | tf_op jit(solution)/shard_map/ppermute | solution.py:283
  70.9 1.1 %shard_map.118 = bf16[1,128,1024]{2,1,0:T(8,128)(2,1)} custom-call(bf16[128,1024]{1,0:T(8,128)(2,1)S(1)} %get-tuple-element.45.refs_4_.refs_0_, s32[8,128]{1,0:T(8,128)S(1)} %get-tuple-element.42.refs_5_.refs_1_, bf16[144,256]{1,0:T(8,128)(2,1)S(1)} %get-tuple-element.59.refs_2_, bf16[144,256]{1,0:T(8,128)(2,1)S(1)} %collective-permute-done.17.refs_3_, ...), custom_call_target="tpu_custom_call" | custom-call | bytes 823296 | tf_op jit(solution)/shard_map/pallas_call | solution.py:34
  (43 shorter events, 6.9 us)
Async XLA Ops:
  0.6 36.5 %copy-start.1 = (bf16[1,1024,1024]{2,1,0:T(8,128)(2,1)S(1)}, bf16[1,1024,1024]{2,1,0:T(8,128)(2,1)}, u32[]{:S(2)}) copy-start(bf16[1,1024,1024]{2,1,0:T(8,128)(2,1)} %param.17) | copy-start | bytes 6291460
  2.0 35.1 %copy-start = (bf16[1024,1024]{1,0:T(8,128)(2,1)S(1)}, bf16[1024,1024]{1,0:T(8,128)(2,1)}, u32[]{:S(2)}) copy-start(bf16[1024,1024]{1,0:T(8,128)(2,1)} %refs_2_.5) | copy-start | bytes 6291460
  2.0 14.4 %collective-permute-start = (bf16[1040,128]{1,0:T(8,128)(2,1)S(1)}, bf16[1040,128]{1,0:T(8,128)(2,1)S(1)}, u32[]{:S(2)}, u32[]{:S(2)}) collective-permute-start(bf16[1040,128]{1,0:T(8,128)(2,1)S(1)} %get-tuple-element.43), channel_id=1, source_target_pairs={{0,1},{1,0},{2,3},{3,2},{4,5},{5,4},{6,7},{7,6},{8,9},{9,8},{10,11... | collective-permute-start | bytes 798728 | tf_op jit(solution)/shard_map/ppermute | solution.py:283
  5.0 11.4 %collective-permute-start.1 = (bf16[1040,128]{1,0:T(8,128)(2,1)S(1)}, bf16[1040,128]{1,0:T(8,128)(2,1)S(1)}, u32[]{:S(2)}, u32[]{:S(2)}) collective-permute-start(bf16[1040,128]{1,0:T(8,128)(2,1)S(1)} %get-tuple-element.44), channel_id=1, source_target_pairs={{1,2},{3,4},{5,6},{7,8},{9,10},{11,12},{13,14},{2,1},{4,3},{6,5},{... | collective-permute-start | bytes 798728 | tf_op jit(solution)/shard_map/ppermute | solution.py:321
  7.0 18.7 %collective-permute-start.5 = (bf16[144,256]{1,0:T(8,128)(2,1)S(1)}, bf16[144,256]{1,0:T(8,128)(2,1)S(1)}, u32[]{:S(2)}, u32[]{:S(2)}) collective-permute-start(bf16[144,256]{1,0:T(8,128)(2,1)S(1)} %get-tuple-element.51), channel_id=1, source_target_pairs={{0,12},{1,13},{2,14},{3,15},{4,8},{5,9},{6,10},{7,11},{8,4},{9,5},... | collective-permute-start | bytes 221192 | tf_op jit(solution)/shard_map/ppermute | solution.py:283
  13.4 13.5 %collective-permute-start.6 = (bf16[144,256]{1,0:T(8,128)(2,1)S(1)}, bf16[144,256]{1,0:T(8,128)(2,1)S(1)}, u32[]{:S(2)}, u32[]{:S(2)}) collective-permute-start(bf16[144,256]{1,0:T(8,128)(2,1)S(1)} %get-tuple-element.52), channel_id=1, source_target_pairs={{0,8},{1,9},{2,10},{3,11},{4,12},{5,13},{6,14},{7,15},{8,0},{9,1},... | collective-permute-start | bytes 221192 | tf_op jit(solution)/shard_map/ppermute | solution.py:283
  13.4 13.5 %collective-permute-start.7 = (bf16[144,256]{1,0:T(8,128)(2,1)S(1)}, bf16[144,256]{1,0:T(8,128)(2,1)S(1)}, u32[]{:S(2)}, u32[]{:S(2)}) collective-permute-start(bf16[144,256]{1,0:T(8,128)(2,1)S(1)} %get-tuple-element.53), channel_id=1, source_target_pairs={{0,4},{1,5},{2,6},{3,7},{4,0},{5,1},{6,2},{7,3},{8,12},{9,13},{10,... | collective-permute-start | bytes 221192 | tf_op jit(solution)/shard_map/ppermute | solution.py:283
  17.9 9.7 %collective-permute-start.2 = (bf16[144,256]{1,0:T(8,128)(2,1)S(1)}, bf16[144,256]{1,0:T(8,128)(2,1)S(1)}, u32[]{:S(2)}, u32[]{:S(2)}) collective-permute-start(bf16[144,256]{1,0:T(8,128)(2,1)S(1)} %get-tuple-element.47), channel_id=1, source_target_pairs={{0,12},{1,13},{2,14},{3,15},{4,8},{5,9},{6,10},{7,11},{8,4},{9,5},... | collective-permute-start | bytes 221192 | tf_op jit(solution)/shard_map/ppermute | solution.py:283
  23.7 5.3 %collective-permute-start.3 = (bf16[144,256]{1,0:T(8,128)(2,1)S(1)}, bf16[144,256]{1,0:T(8,128)(2,1)S(1)}, u32[]{:S(2)}, u32[]{:S(2)}) collective-permute-start(bf16[144,256]{1,0:T(8,128)(2,1)S(1)} %get-tuple-element.48), channel_id=1, source_target_pairs={{0,8},{1,9},{2,10},{3,11},{4,12},{5,13},{6,14},{7,15},{8,0},{9,1},... | collective-permute-start | bytes 221192 | tf_op jit(solution)/shard_map/ppermute | solution.py:283
  25.7 4.4 %collective-permute-start.4 = (bf16[144,256]{1,0:T(8,128)(2,1)S(1)}, bf16[144,256]{1,0:T(8,128)(2,1)S(1)}, u32[]{:S(2)}, u32[]{:S(2)}) collective-permute-start(bf16[144,256]{1,0:T(8,128)(2,1)S(1)} %get-tuple-element.49), channel_id=1, source_target_pairs={{0,4},{1,5},{2,6},{3,7},{4,0},{5,1},{6,2},{7,3},{8,12},{9,13},{10,... | collective-permute-start | bytes 221192 | tf_op jit(solution)/shard_map/ppermute | solution.py:283
  27.4 8.1 %collective-permute-start.9 = (bf16[144,1024]{1,0:T(8,128)(2,1)S(1)}, bf16[144,1024]{1,0:T(8,128)(2,1)S(1)}, u32[]{:S(2)}, u32[]{:S(2)}) collective-permute-start(bf16[144,1024]{1,0:T(8,128)(2,1)S(1)} %shard_map.108.refs_4_), channel_id=1, source_target_pairs={{0,2},{1,3},{2,0},{3,1},{4,6},{5,7},{6,4},{7,5},{8,10},{9,11},{10,... | collective-permute-start | bytes 884744 | tf_op jit(solution)/shard_map/ppermute | solution.py:283
  27.5 9.7 %collective-permute-start.8 = (bf16[144,1024]{1,0:T(8,128)(2,1)S(1)}, bf16[144,1024]{1,0:T(8,128)(2,1)S(1)}, u32[]{:S(2)}, u32[]{:S(2)}) collective-permute-start(bf16[144,1024]{1,0:T(8,128)(2,1)S(1)} %shard_map.108.refs_4_), channel_id=1, source_target_pairs={{0,1},{1,0},{2,3},{3,2},{4,5},{5,4},{6,7},{7,6},{8,9},{9,8},{10,11... | collective-permute-start | bytes 884744 | tf_op jit(solution)/shard_map/ppermute | solution.py:283
  30.5 10.1 %collective-permute-start.10 = (bf16[144,1024]{1,0:T(8,128)(2,1)S(1)}, bf16[144,1024]{1,0:T(8,128)(2,1)S(1)}, u32[]{:S(2)}, u32[]{:S(2)}) collective-permute-start(bf16[144,1024]{1,0:T(8,128)(2,1)S(1)} %shard_map.107.refs_0_), channel_id=1, source_target_pairs={{0,1},{1,0},{2,3},{3,2},{4,5},{5,4},{6,7},{7,6},{8,9},{9,8},{10,11... | collective-permute-start | bytes 884744 | tf_op jit(solution)/shard_map/ppermute | solution.py:283
  31.2 12.1 %collective-permute-start.12 = (bf16[144,1024]{1,0:T(8,128)(2,1)S(1)}, bf16[144,1024]{1,0:T(8,128)(2,1)S(1)}, u32[]{:S(2)}, u32[]{:S(2)}) collective-permute-start(bf16[144,1024]{1,0:T(8,128)(2,1)S(1)} %shard_map.107.refs_0_), channel_id=1, source_target_pairs={{0,2},{1,3},{2,0},{3,1},{4,6},{5,7},{6,4},{7,5},{8,10},{9,11},{10,... | collective-permute-start | bytes 884744 | tf_op jit(solution)/shard_map/ppermute | solution.py:283
  41.5 13.6 %collective-permute-start.11 = (bf16[144,1024]{1,0:T(8,128)(2,1)S(1)}, bf16[144,1024]{1,0:T(8,128)(2,1)S(1)}, u32[]{:S(2)}, u32[]{:S(2)}) collective-permute-start(bf16[144,1024]{1,0:T(8,128)(2,1)S(1)} %get-tuple-element.56), channel_id=1, source_target_pairs={{0,1},{1,0},{2,3},{3,2},{4,5},{5,4},{6,7},{7,6},{8,9},{9,8},{10,11... | collective-permute-start | bytes 884744 | tf_op jit(solution)/shard_map/ppermute | solution.py:283
  41.6 6.5 %collective-permute-start.14 = (bf16[64,1024]{1,0:T(8,128)(2,1)S(1)}, bf16[64,1024]{1,0:T(8,128)(2,1)S(1)}, u32[]{:S(2)}, u32[]{:S(2)}) collective-permute-start(bf16[64,1024]{1,0:T(8,128)(2,1)S(1)} %slice.16), channel_id=1, source_target_pairs={{0,2},{1,3},{2,0},{3,1},{4,6},{5,7},{6,4},{7,5},{8,10},{9,11},{10,... | collective-permute-start | bytes 393224 | tf_op jit(solution)/shard_map/ppermute | solution.py:283
  44.2 15.0 %collective-permute-start.13 = (bf16[144,1024]{1,0:T(8,128)(2,1)S(1)}, bf16[144,1024]{1,0:T(8,128)(2,1)S(1)}, u32[]{:S(2)}, u32[]{:S(2)}) collective-permute-start(bf16[144,1024]{1,0:T(8,128)(2,1)S(1)} %get-tuple-element.57), channel_id=1, source_target_pairs={{0,2},{1,3},{2,0},{3,1},{4,6},{5,7},{6,4},{7,5},{8,10},{9,11},{10,... | collective-permute-start | bytes 884744 | tf_op jit(solution)/shard_map/ppermute | solution.py:283
  44.8 9.2 %collective-permute-start.15 = (bf16[80,1024]{1,0:T(8,128)(2,1)S(1)}, bf16[80,1024]{1,0:T(8,128)(2,1)S(1)}, u32[]{:S(2)}, u32[]{:S(2)}) collective-permute-start(bf16[80,1024]{1,0:T(8,128)(2,1)S(1)} %slice.17), channel_id=1, source_target_pairs={{0,1},{1,0},{2,3},{3,2},{4,5},{5,4},{6,7},{7,6},{8,9},{9,8},{10,11... | collective-permute-start | bytes 491528 | tf_op jit(solution)/shard_map/ppermute | solution.py:283
  46.9 10.7 %collective-permute-start.21 = (bf16[80,1024]{1,0:T(8,128)(2,1)S(1)}, bf16[80,1024]{1,0:T(8,128)(2,1)S(1)}, u32[]{:S(2)}, u32[]{:S(2)}) collective-permute-start(bf16[80,1024]{1,0:T(8,128)(2,1)S(1)} %slice.19), channel_id=1, source_target_pairs={{0,1},{1,0},{2,3},{3,2},{4,5},{5,4},{6,7},{7,6},{8,9},{9,8},{10,11... | collective-permute-start | bytes 491528 | tf_op jit(solution)/shard_map/ppermute | solution.py:283
  48.1 8.1 %collective-permute-start.20 = (bf16[64,1024]{1,0:T(8,128)(2,1)S(1)}, bf16[64,1024]{1,0:T(8,128)(2,1)S(1)}, u32[]{:S(2)}, u32[]{:S(2)}) collective-permute-start(bf16[64,1024]{1,0:T(8,128)(2,1)S(1)} %slice.18), channel_id=1, source_target_pairs={{0,2},{1,3},{2,0},{3,1},{4,6},{5,7},{6,4},{7,5},{8,10},{9,11},{10,... | collective-permute-start | bytes 393224 | tf_op jit(solution)/shard_map/ppermute | solution.py:283
  55.0 7.7 %collective-permute-start.16 = (bf16[144,1024]{1,0:T(8,128)(2,1)S(1)}, bf16[144,1024]{1,0:T(8,128)(2,1)S(1)}, u32[]{:S(2)}, u32[]{:S(2)}) collective-permute-start(bf16[144,1024]{1,0:T(8,128)(2,1)S(1)} %get-tuple-element.58), channel_id=1, source_target_pairs={{0,3},{1,2},{2,1},{3,0},{4,7},{5,6},{6,5},{7,4},{8,11},{9,10},{10,... | collective-permute-start | bytes 884744 | tf_op jit(solution)/shard_map/ppermute | solution.py:283
  58.6 5.8 %collective-permute-start.22 = (bf16[128,1024]{1,0:T(8,128)(2,1)S(1)}, bf16[128,1024]{1,0:T(8,128)(2,1)S(1)}, u32[]{:S(2)}, u32[]{:S(2)}) collective-permute-start(bf16[128,1024]{1,0:T(8,128)(2,1)S(1)} %get-tuple-element.66), channel_id=1, source_target_pairs={{0,16},{16,0},{1,17},{17,1},{2,18},{18,2},{3,19},{19,3},{4,20},{20... | collective-permute-start | bytes 786440 | tf_op jit(solution)/shard_map/ppermute | solution.py:375
  58.7 5.9 %collective-permute-start.23 = (bf16[128,1024]{1,0:T(8,128)(2,1)S(1)}, bf16[128,1024]{1,0:T(8,128)(2,1)S(1)}, u32[]{:S(2)}, u32[]{:S(2)}) collective-permute-start(bf16[128,1024]{1,0:T(8,128)(2,1)S(1)} %get-tuple-element.67), channel_id=1, source_target_pairs={{0,16},{16,0},{1,17},{17,1},{2,18},{18,2},{3,19},{19,3},{4,20},{20... | collective-permute-start | bytes 786440 | tf_op jit(solution)/shard_map/ppermute | solution.py:375
  59.2 8.4 %collective-permute-start.24 = (bf16[128,1024]{1,0:T(8,128)(2,1)S(1)}, bf16[128,1024]{1,0:T(8,128)(2,1)S(1)}, u32[]{:S(2)}, u32[]{:S(2)}) collective-permute-start(bf16[128,1024]{1,0:T(8,128)(2,1)S(1)} %get-tuple-element.68), channel_id=1, source_target_pairs={{0,16},{16,0},{1,17},{17,1},{2,18},{18,2},{3,19},{19,3},{4,20},{20... | collective-permute-start | bytes 786440 | tf_op jit(solution)/shard_map/ppermute | solution.py:375
  59.2 8.3 %collective-permute-start.25 = (bf16[128,1024]{1,0:T(8,128)(2,1)S(1)}, bf16[128,1024]{1,0:T(8,128)(2,1)S(1)}, u32[]{:S(2)}, u32[]{:S(2)}) collective-permute-start(bf16[128,1024]{1,0:T(8,128)(2,1)S(1)} %get-tuple-element.69), channel_id=1, source_target_pairs={{0,16},{16,0},{1,17},{17,1},{2,18},{18,2},{3,19},{19,3},{4,20},{20... | collective-permute-start | bytes 786440 | tf_op jit(solution)/shard_map/ppermute | solution.py:375
  63.1 6.5 %collective-permute-start.17 = (bf16[144,256]{1,0:T(8,128)(2,1)S(1)}, bf16[144,256]{1,0:T(8,128)(2,1)S(1)}, u32[]{:S(2)}, u32[]{:S(2)}) collective-permute-start(bf16[144,256]{1,0:T(8,128)(2,1)S(1)} %get-tuple-element.60), channel_id=1, source_target_pairs={{0,12},{1,13},{2,14},{3,15},{4,8},{5,9},{6,10},{7,11},{8,4},{9,5},... | collective-permute-start | bytes 221192 | tf_op jit(solution)/shard_map/ppermute | solution.py:283
  64.3 6.6 %collective-permute-start.18 = (bf16[144,256]{1,0:T(8,128)(2,1)S(1)}, bf16[144,256]{1,0:T(8,128)(2,1)S(1)}, u32[]{:S(2)}, u32[]{:S(2)}) collective-permute-start(bf16[144,256]{1,0:T(8,128)(2,1)S(1)} %get-tuple-element.61), channel_id=1, source_target_pairs={{0,8},{1,9},{2,10},{3,11},{4,12},{5,13},{6,14},{7,15},{8,0},{9,1},... | collective-permute-start | bytes 221192 | tf_op jit(solution)/shard_map/ppermute | solution.py:283
  64.6 6.3 %collective-permute-start.19 = (bf16[144,256]{1,0:T(8,128)(2,1)S(1)}, bf16[144,256]{1,0:T(8,128)(2,1)S(1)}, u32[]{:S(2)}, u32[]{:S(2)}) collective-permute-start(bf16[144,256]{1,0:T(8,128)(2,1)S(1)} %get-tuple-element.62), channel_id=1, source_target_pairs={{0,4},{1,5},{2,6},{3,7},{4,0},{5,1},{6,2},{7,3},{8,12},{9,13},{10,... | collective-permute-start | bytes 221192 | tf_op jit(solution)/shard_map/ppermute | solution.py:283

commit v5 on v4

--- a/solution.py
+++ b/solution.py
@@ -108,7 +108,7 @@
     stacked = column_blocks(rows)
     height = message_refs[0].shape[0]
     for p, message in enumerate(message_refs):
-        mine = labels == (home ^ (-p % len(message_refs)))
+        mine = labels == (home ^ p)
         places = [one_hot(mine & (slot + j * capacity == iota((height, count), 0))) for j in range(PARTS)]
         message[...] = dot(jnp.concatenate(places, axis=1), stacked).astype(BF16)
 
@@ -136,13 +136,14 @@
     return group
 
 
-def gather_body(capacity, experts, first_row, first_group, *refs):
+def gather_body(capacity, experts, order, *refs):
     *message_refs, rows_ref = refs
+    message_refs = [message_refs[order.index(k)] for k in range(experts)]
     stacked = jnp.concatenate([m[...] for m in message_refs], axis=0)
     block, width = message_refs[0].shape
-    row = iota((rows_ref.shape[0], stacked.shape[0]), 0) + first_row
+    row = iota((rows_ref.shape[0], stacked.shape[0]), 0)
     group = group_of(row, capacity, experts)
-    source = (group - first_group) * block + row - group * capacity
+    source = group * block + row - group * capacity
     source = jnp.where(row < experts * capacity, source, -(1 << 20)) - iota(row.shape, 1)
     for j in range(PARTS):
         place = one_hot(source == -j * capacity)
@@ -227,8 +228,9 @@
         partial_ref[:, at : at + STEP] = dot(hidden, out_ref[:, at : at + STEP]).astype(BF16)
 
 
-def finish_body(capacity, mixed_ref, route_ref, *refs):
+def finish_body(capacity, order, mixed_ref, route_ref, *refs):
     *message_refs, layer_ref = refs
+    message_refs = [message_refs[order.index(k)] for k in range(len(message_refs))]
     home = home_plane()
     labels, slot = route_ref[0:1, :], route_ref[1:2, :]
     count = labels.shape[1]
@@ -236,7 +238,7 @@
     stacked = jnp.concatenate([m[...] for m in message_refs], axis=0)
     for j in range(PARTS):
         places = [
-            one_hot((labels == (home ^ (-p % len(message_refs)))) & (slot + j * capacity == iota((block, count), 0)))
+            one_hot((labels == (home ^ p)) & (slot + j * capacity == iota((block, count), 0)))
             for p in range(len(message_refs))
         ]
         taken = dot(jnp.concatenate(places, axis=0), stacked, (0, 0))
@@ -289,8 +291,7 @@
 
 
 def along_line(messages):
-    count = len(messages)
-    return [m if p == 0 else permute(m, SPLIT * (count - p)) for p, m in enumerate(messages)]
+    return [m if k == 0 else permute(m, SPLIT * k) for k, m in enumerate(messages)]
 
 
 def shards(tokens, queries, keys, values, key_mask, labels, cotangent, weight_in, weight_out):
@@ -320,7 +321,7 @@
     steps = [(i, i + 1) for i in range(1, axis_count - 1, 2)]
     far = lax.ppermute(far, "ep", steps + [(j, i) for i, j in steps])
 
-    gather = functools.partial(gather_body, capacity, experts, 0, 0)
+    gather = functools.partial(gather_body, capacity, experts)
     route, query_here, token_here, *sent = call(
         functools.partial(pack_body, capacity),
         [out(8, rows_here, dtype=jnp.int32), block, block] + [message] * experts,
@@ -339,9 +340,15 @@
         flops=4 * rows_here * (rows_here + 2 * HALO) * features,
     )
 
-    (cot_rows,) = call(gather, [out(plane_rows, features)], vmem=cot_got, after=(mixed,), size=0)
+    (cot_rows,) = call(
+        functools.partial(gather, range(experts)), [out(plane_rows, features)], vmem=cot_got, after=(mixed,), size=0
+    )
     cot_x, cot_y = permute(cot_rows, 1), permute(cot_rows, 2)
-    (rows,) = call(gather, [out(plane_rows, features)], vmem=along_line(sent))
+    mixed_got = along_line(sent)
+    order = [0, *range(2, experts), 1]
+    (rows,) = call(
+        functools.partial(gather, order), [out(plane_rows, features)], vmem=[mixed_got[k] for k in order]
+    )
     cot_far = forwarded(cot_x, cot_y)
 
     row_x, row_y = permute(rows, 1), permute(rows, 2)
@@ -386,8 +393,9 @@
         ready = ()
     sent = call(functools.partial(combine_body, capacity, experts), [message] * experts, vmem=(total, last))
     back = along_line(sent)
+    order = [0, *range(experts - 1, 0, -1)]
     (layer_out,) = call(
-        functools.partial(finish_body, capacity), [block], vmem=(mixed, route, *back), after=ready
+        functools.partial(finish_body, capacity, order), [block], vmem=(mixed, route, *[back[k] for k in order]), after=ready
     )
     return (layer_out, grad)
 

time: 72.2 us -> 71.1 us (0.985)
  waiting for transfers between devices: 25.3 us -> 20.6 us
  starting transfers between devices: 32.3 us -> 35.9 us
    ppermute x21, waiting for transfers between devices: 25.3 us -> 20.6 us  [permute(): lax.ppermute(value, 'ep', [(i, i ^ apart) for i in range(lax.axis_size('e...]
    ppermute x21, starting transfers between devices: 30.6 us -> 34.2 us  [permute(): lax.ppermute(value, 'ep', [(i, i ^ apart) for i in range(lax.axis_size('e...]
  transfers between devices with their start and end apart: 26 -> 26, of which waited for: 13 -> 12; matrix products, arithmetic and copies ran while one was open for 0% -> 0% of each run, Pallas kernels for 15% -> 16%
where the time goes in v5:
time: 71.1 us; the launch traced here: 70.9 us
  starting transfers between devices  35.9 us (50%)
  waiting for transfers between devices  20.6 us (29%)
  Pallas kernels  13.5 us (19%)
  between operations  0.8 us (1%)
    ppermute x21, starting transfers between devices, permute(): lax.ppermute(value, 'ep', [(i, i ^ apart) for i in range(lax.axis_size('e...  34.2 us
    ppermute x21, waiting for transfers between devices, permute(): lax.ppermute(value, 'ep', [(i, i ^ apart) for i in range(lax.axis_size('e...  20.6 us
    pallas_call x15, Pallas kernels, call(): pl.pallas_call(kernel, out_shape=outs, in_specs=[VMEM] * len(vmem) + [HBM...  13.5 us
  transfers between devices with their start and end apart: 26, of which 12 were waited for; matrix products, arithmetic and copies ran while one was open for 0% of the time, Pallas kernels for 16%

profile of v5, /device:TPU:0, one launch (start us, length us, event | category | flops | bytes accessed | tf_op | source)
XLA Modules:
  0.0 70.9 jit_solution(18000389627814853533)
XLA Ops:
  0.6 1.3 %shard_map.104 = (bf16[1040,128]{1,0:T(8,128)(2,1)S(1)}, bf16[1040,128]{1,0:T(8,128)(2,1)S(1)}, bf16[1,128,1024]{2,1,0:T(8,128)(2,1)S(1)}, bf16[1,128,1024]{2,1,0:T(8,128)(2,1)S(1)}, s32[1,128]{1,0:T(1,128)S(1)}) custom-call(bf16[1,128,1024]{2,1,0:T(8,128)(2,1)} %refs_0_.2, bf16[1,128,1024]{2,1,0:T(8,128)(2,1)} %refs_1_.4, s32[1,128]{1,0:T(1,128)} %refs_2_.3), custom_call_target="tpu_custom_call" | custom-call | bytes 1582080 | tf_op jit(solution)/shard_map/pallas_call | solution.py:34
  2.0 3.0 %collective-permute-start = (bf16[1040,128]{1,0:T(8,128)(2,1)S(1)}, bf16[1040,128]{1,0:T(8,128)(2,1)S(1)}, u32[]{:S(2)}, u32[]{:S(2)}) collective-permute-start(bf16[1040,128]{1,0:T(8,128)(2,1)S(1)} %get-tuple-element.43), channel_id=1, source_target_pairs={{0,1},{1,0},{2,3},{3,2},{4,5},{5,4},{6,7},{7,6},{8,9},{9,8},{10,11... | collective-permute-start | bytes 798728 | tf_op jit(solution)/shard_map/ppermute | solution.py:285
  5.7 1.3 %shard_map.105 = (s32[8,128]{1,0:T(8,128)S(1)}, bf16[1,128,1024]{2,1,0:T(8,128)(2,1)S(1)}, bf16[1,128,1024]{2,1,0:T(8,128)(2,1)S(1)}, bf16[144,256]{1,0:T(8,128)...) custom-call(bf16[1,128,1024]{2,1,0:T(8,128)(2,1)} %refs_0_.3, ...), custom_call_target="tpu_custom_call" | custom-call | tf_op jit(solution)/shard_map/pallas_call | solution.py:34
  7.0 4.4 %collective-permute-start.5 = (bf16[144,256]{1,0:T(8,128)(2,1)S(1)}, bf16[144,256]{1,0:T(8,128)(2,1)S(1)}, u32[]{:S(2)}, u32[]{:S(2)}) collective-permute-start(bf16[144,256]{1,0:T(8,128)(2,1)S(1)} %get-tuple-element.51), channel_id=1, source_target_pairs={{0,4},{1,5},{2,6},{3,7},{4,0},{5,1},{6,2},{7,3},{8,12},{9,13},{10,... | collective-permute-start | bytes 221192 | tf_op jit(solution)/shard_map/ppermute | solution.py:285
  11.4 2.6 %collective-permute-start.6 = (bf16[144,256]{1,0:T(8,128)(2,1)S(1)}, bf16[144,256]{1,0:T(8,128)(2,1)S(1)}, u32[]{:S(2)}, u32[]{:S(2)}) collective-permute-start(bf16[144,256]{1,0:T(8,128)(2,1)S(1)} %get-tuple-element.52), channel_id=1, source_target_pairs={{0,8},{1,9},{2,10},{3,11},{4,12},{5,13},{6,14},{7,15},{8,0},{9,1},... | collective-permute-start | bytes 221192 | tf_op jit(solution)/shard_map/ppermute | solution.py:285
  14.0 1.8 %collective-permute-done.refs_6_ = bf16[1040,128]{1,0:T(8,128)(2,1)S(1)} collective-permute-done((bf16[1040,128]{1,0:T(8,128)(2,1)S(1)}, bf16[1040,128]{1,0:T(8,128)(2,1)S(1)}, u32[]{:S(2)}, u32[]{:S(2)}) %collective-permute-start) | collective-permute-done | bytes 266272 | tf_op jit(solution)/shard_map/ppermute | solution.py:285
  15.8 1.5 %shard_map.106 = (bf16[128,1024]{1,0:T(8,128)(2,1)S(1)}, bf16[144,256]{1,0:T(8,128)(2,1)S(1)}, bf16[144,256]{1,0:T(8,128)(2,1)S(1)}, bf16[144,256]{1,0:T(8,128)(2,1)S(1)}, bf16[144,256]{1,0:T(8,128)(2,1)S(1)}) custom-call(bf16[1,128,1024]{2,1,0:T(8,128)(2,1)S(1)} %get-tuple-element.38.refs_0_, bf16[1,128,1024]{2,1,0:T(8,128)(2,1)S(1)} %get-tuple-element.39.refs_1_, ...), custom_call_target="tpu_custom_call" | custom-call | flops 134217728 | bytes 2142720 | tf_op jit(solution)/shard_map/pallas_call | solution.py:34
  17.3 6.3 %collective-permute-start.2 = (bf16[144,256]{1,0:T(8,128)(2,1)S(1)}, bf16[144,256]{1,0:T(8,128)(2,1)S(1)}, u32[]{:S(2)}, u32[]{:S(2)}) collective-permute-start(bf16[144,256]{1,0:T(8,128)(2,1)S(1)} %get-tuple-element.47), channel_id=1, source_target_pairs={{0,8},{1,9},{2,10},{3,11},{4,12},{5,13},{6,14},{7,15},{8,0},{9,1},... | collective-permute-start | bytes 221192 | tf_op jit(solution)/shard_map/ppermute | solution.py:285
  25.1 1.3 %collective-permute-start.8 = (bf16[144,1024]{1,0:T(8,128)(2,1)S(1)}, bf16[144,1024]{1,0:T(8,128)(2,1)S(1)}, u32[]{:S(2)}, u32[]{:S(2)}) collective-permute-start(bf16[144,1024]{1,0:T(8,128)(2,1)S(1)} %shard_map.108.refs_4_), channel_id=1, source_target_pairs={{0,1},{1,0},{2,3},{3,2},{4,5},{5,4},{6,7},{7,6},{8,9},{9,8},{10,11... | collective-permute-start | bytes 884744 | tf_op jit(solution)/shard_map/ppermute | solution.py:285
  26.4 1.6 %collective-permute-done.2.refs_1_ = bf16[144,256]{1,0:T(8,128)(2,1)S(1)} collective-permute-done((bf16[144,256]{1,0:T(8,128)(2,1)S(1)}, bf16[144,256]{1,0:T(8,128)(2,1)S(1)}, u32[]{:S(2)}, u32[]{:S(2)}) %collective-permute-start.2) | collective-permute-done | bytes 73760 | tf_op jit(solution)/shard_map/ppermute | solution.py:285
  28.1 1.6 %collective-permute-done.3.refs_2_ = bf16[144,256]{1,0:T(8,128)(2,1)S(1)} collective-permute-done((bf16[144,256]{1,0:T(8,128)(2,1)S(1)}, bf16[144,256]{1,0:T(8,128)(2,1)S(1)}, u32[]{:S(2)}, u32[]{:S(2)}) %collective-permute-start.3) | collective-permute-done | bytes 73760 | tf_op jit(solution)/shard_map/ppermute | solution.py:285
  30.1 0.8 %collective-permute-start.10 = (bf16[144,1024]{1,0:T(8,128)(2,1)S(1)}, bf16[144,1024]{1,0:T(8,128)(2,1)S(1)}, u32[]{:S(2)}, u32[]{:S(2)}) collective-permute-start(bf16[144,1024]{1,0:T(8,128)(2,1)S(1)} %shard_map.107.refs_0_), channel_id=1, source_target_pairs={{0,1},{1,0},{2,3},{3,2},{4,5},{5,4},{6,7},{7,6},{8,9},{9,8},{10,11... | collective-permute-start | bytes 884744 | tf_op jit(solution)/shard_map/ppermute | solution.py:285
  31.6 2.9 %collective-permute-done.8.refs_3_.refs_5_ = bf16[144,1024]{1,0:T(8,128)(2,1)S(1)} collective-permute-done((bf16[144,1024]{1,0:T(8,128)(2,1)S(1)}, bf16[144,1024]{1,0:T(8,128)(2,1)S(1)}, u32[]{:S(2)}, u32[]{:S(2)}) %collective-permute-start.8) | collective-permute-done | bytes 294944 | tf_op jit(solution)/shard_map/ppermute | solution.py:285
  34.5 1.0 %shard_map.109 = (bf16[144,1024]{1,0:T(8,128)(2,1)S(1)}, bf16[144,1024]{1,0:T(8,128)(2,1)S(1)}) custom-call(bf16[144,1024]{1,0:T(8,128)(2,1)S(1)} %shard_map.107.refs_0_, bf16[1024,1024]{1,0:T(8,128)(2,1)S(1)} %copy-done, bf16[1024,1024]{1,0:T(8,128)(2,1)S(1)} %bitcast.2, bf16[144,1024]{1,0:T(8,128)(2,1)S(1)} %collective-permute-done.8.refs_3_.refs_5_, ...), custom_call_target="tpu_custom_call" | custom-call | flops 603979776 | bytes 5079040 | tf_op jit(solution)/shard_map/pallas_call | solution.py:34
  35.4 2.9 %collective-permute-done.10.refs_0_ = bf16[144,1024]{1,0:T(8,128)(2,1)S(1)} collective-permute-done((bf16[144,1024]{1,0:T(8,128)(2,1)S(1)}, bf16[144,1024]{1,0:T(8,128)(2,1)S(1)}, u32[]{:S(2)}, u32[]{:S(2)}) %collective-permute-start.10) | collective-permute-done | bytes 294944 | tf_op jit(solution)/shard_map/ppermute | solution.py:285
  38.4 1.0 %shard_map.110 = (bf16[144,1024]{1,0:T(8,128)(2,1)S(1)}, bf16[144,1024]{1,0:T(8,128)(2,1)S(1)}) custom-call(bf16[144,1024]{1,0:T(8,128)(2,1)S(1)} %collective-permute-done.10.refs_0_, bf16[1024,1024]{1,0:T(8,128)(2,1)S(1)} %copy-done, bf16[1024,1024]{1,0:T(8,128)(2,1)S(1)} %bitcast.3, bf16[144,1024]{1,0:T(8,128)(2,1)S(1)} %get-tuple-element.55.refs_3_.refs_4_.refs_0_), custom_call_target="tpu_custom_call" | custom-call | flops 603979776 | bytes 5079040 | tf_op jit(solution)/shard_map/pallas_call | solution.py:34
  39.4 1.4 %collective-permute-start.11 = (bf16[144,1024]{1,0:T(8,128)(2,1)S(1)}, bf16[144,1024]{1,0:T(8,128)(2,1)S(1)}, u32[]{:S(2)}, u32[]{:S(2)}) collective-permute-start(bf16[144,1024]{1,0:T(8,128)(2,1)S(1)} %get-tuple-element.56), channel_id=1, source_target_pairs={{0,1},{1,0},{2,3},{3,2},{4,5},{5,4},{6,7},{7,6},{8,9},{9,8},{10,11... | collective-permute-start | bytes 884744 | tf_op jit(solution)/shard_map/ppermute | solution.py:285
  40.8 1.7 %collective-permute-start.14 = (bf16[64,1024]{1,0:T(8,128)(2,1)S(1)}, bf16[64,1024]{1,0:T(8,128)(2,1)S(1)}, u32[]{:S(2)}, u32[]{:S(2)}) collective-permute-start(bf16[64,1024]{1,0:T(8,128)(2,1)S(1)} %slice.16), channel_id=1, source_target_pairs={{0,2},{1,3},{2,0},{3,1},{4,6},{5,7},{6,4},{7,5},{8,10},{9,11},{10,... | collective-permute-start | bytes 393224 | tf_op jit(solution)/shard_map/ppermute | solution.py:285
  42.5 1.0 %shard_map.112 = (bf16[144,1024]{1,0:T(8,128)(2,1)S(1)}, bf16[144,1024]{1,0:T(8,128)(2,1)S(1)}) custom-call(bf16[144,1024]{1,0:T(8,128)(2,1)S(1)} %collective-permute-done.12.refs_0_, bf16[1024,1024]{1,0:T(8,128)(2,1)S(1)} %copy-done, bf16[1024,1024]{1,0:T(8,128)(2,1)S(1)} %bitcast.4, bf16[144,1024]{1,0:T(8,128)(2,1)S(1)} %get-tuple-element.55.refs_3_.refs_4_.refs_0_), custom_call_target="tpu_custom_call" | custom-call | flops 603979776 | bytes 5079040 | tf_op jit(solution)/shard_map/pallas_call | solution.py:34
  44.7 1.4 %collective-permute-start.21 = (bf16[80,1024]{1,0:T(8,128)(2,1)S(1)}, bf16[80,1024]{1,0:T(8,128)(2,1)S(1)}, u32[]{:S(2)}, u32[]{:S(2)}) collective-permute-start(bf16[80,1024]{1,0:T(8,128)(2,1)S(1)} %slice.19), channel_id=1, source_target_pairs={{0,1},{1,0},{2,3},{3,2},{4,5},{5,4},{6,7},{7,6},{8,9},{9,8},{10,11... | collective-permute-start | bytes 491528 | tf_op jit(solution)/shard_map/ppermute | solution.py:285
  46.1 1.2 %collective-permute-done.14.refs_0_ = bf16[64,1024]{1,0:T(8,128)(2,1)S(1)} collective-permute-done((bf16[64,1024]{1,0:T(8,128)(2,1)S(1)}, bf16[64,1024]{1,0:T(8,128)(2,1)S(1)}, u32[]{:S(2)}, u32[]{:S(2)}) %collective-permute-start.14) | collective-permute-done | bytes 131104 | tf_op jit(solution)/shard_map/ppermute | solution.py:285
  47.3 1.7 %collective-permute-start.20 = (bf16[64,1024]{1,0:T(8,128)(2,1)S(1)}, bf16[64,1024]{1,0:T(8,128)(2,1)S(1)}, u32[]{:S(2)}, u32[]{:S(2)}) collective-permute-start(bf16[64,1024]{1,0:T(8,128)(2,1)S(1)} %slice.18), channel_id=1, source_target_pairs={{0,2},{1,3},{2,0},{3,1},{4,6},{5,7},{6,4},{7,5},{8,10},{9,11},{10,... | collective-permute-start | bytes 393224 | tf_op jit(solution)/shard_map/ppermute | solution.py:285
  49.0 2.8 %collective-permute-done.15.refs_1_ = bf16[80,1024]{1,0:T(8,128)(2,1)S(1)} collective-permute-done((bf16[80,1024]{1,0:T(8,128)(2,1)S(1)}, bf16[80,1024]{1,0:T(8,128)(2,1)S(1)}, u32[]{:S(2)}, u32[]{:S(2)}) %collective-permute-start.15) | collective-permute-done | bytes 163872 | tf_op jit(solution)/shard_map/ppermute | solution.py:285
  51.8 1.0 %shard_map.114 = (bf16[144,1024]{1,0:T(8,128)(2,1)S(1)}, bf16[144,1024]{1,0:T(8,128)(2,1)S(1)}) custom-call(bf16[64,1024]{1,0:T(8,128)(2,1)S(1)} %collective-permute-done.14.refs_0_, bf16[80,1024]{1,0:T(8,128)(2,1)S(1)} %collective-permute-done.15.refs_1_, bf16[1024,1024]{1,0:T(8,128)(2,1)S(1)} %copy-done, bf16[1024,1024]{1,0:T(8,128)(2,1)S(1)} %bitcast.5, ...), custom_call_target="tpu_custom_call" | custom-call | flops 603979776 | bytes 5079040 | tf_op jit(solution)/shard_map/pallas_call | solution.py:34
  52.7 1.7 %collective-permute-start.16 = (bf16[144,1024]{1,0:T(8,128)(2,1)S(1)}, bf16[144,1024]{1,0:T(8,128)(2,1)S(1)}, u32[]{:S(2)}, u32[]{:S(2)}) collective-permute-start(bf16[144,1024]{1,0:T(8,128)(2,1)S(1)} %get-tuple-element.58), channel_id=1, source_target_pairs={{0,3},{1,2},{2,1},{3,0},{4,7},{5,6},{6,5},{7,4},{8,11},{9,10},{10,... | collective-permute-start | bytes 884744 | tf_op jit(solution)/shard_map/ppermute | solution.py:285
  55.3 1.0 %shard_map.116 = (bf16[128,1024]{1,0:T(8,128)(2,1)S(1)}, bf16[128,1024]{1,0:T(8,128)(2,1)S(1)}, bf16[128,1024]{1,0:T(8,128)(2,1)S(1)}, bf16[128,1024]{1,0:T(8,128)(2,1)S(1)}) custom-call(bf16[144,1024]{1,0:T(8,128)(2,1)S(1)} %get-tuple-element.55.refs_3_.refs_4_.refs_0_, bf16[144,1024]{1,0:T(8,128)(2,1)S(1)} %get-tuple-element.63.refs_1_, ...), custom_call_target="tpu_custom_call" | custom-call | flops 603979776 | bytes 3407872 | tf_op jit(solution)/shard_map/pallas_call | solution.py:34
  57.4 3.0 %collective-permute-done.16.refs_1_ = bf16[144,1024]{1,0:T(8,128)(2,1)S(1)} collective-permute-done((bf16[144,1024]{1,0:T(8,128)(2,1)S(1)}, bf16[144,1024]{1,0:T(8,128)(2,1)S(1)}, u32[]{:S(2)}, u32[]{:S(2)}) %collective-permute-start.16) | collective-permute-done | bytes 294944 | tf_op jit(solution)/shard_map/ppermute | solution.py:285
  60.8 2.9 %collective-permute-start.17 = (bf16[144,256]{1,0:T(8,128)(2,1)S(1)}, bf16[144,256]{1,0:T(8,128)(2,1)S(1)}, u32[]{:S(2)}, u32[]{:S(2)}) collective-permute-start(bf16[144,256]{1,0:T(8,128)(2,1)S(1)} %get-tuple-element.60), channel_id=1, source_target_pairs={{0,12},{1,13},{2,14},{3,15},{4,8},{5,9},{6,10},{7,11},{8,4},{9,5},... | collective-permute-start | bytes 221192 | tf_op jit(solution)/shard_map/ppermute | solution.py:285
  63.7 1.5 %collective-permute-start.18 = (bf16[144,256]{1,0:T(8,128)(2,1)S(1)}, bf16[144,256]{1,0:T(8,128)(2,1)S(1)}, u32[]{:S(2)}, u32[]{:S(2)}) collective-permute-start(bf16[144,256]{1,0:T(8,128)(2,1)S(1)} %get-tuple-element.61), channel_id=1, source_target_pairs={{0,8},{1,9},{2,10},{3,11},{4,12},{5,13},{6,14},{7,15},{8,0},{9,1},... | collective-permute-start | bytes 221192 | tf_op jit(solution)/shard_map/ppermute | solution.py:285
  65.8 2.0 %shard_map.117 = (bf16[1,512,1024]{2,1,0:T(8,128)(2,1)}, f32[8,128]{1,0:T(8,128)S(1)}) custom-call(bf16[144,1024]{1,0:T(8,128)(2,1)S(1)} %get-tuple-element.55.refs_3_.refs_4_.refs_0_, bf16[144,1024]{1,0:T(8,128)(2,1)S(1)} %get-tuple-element.63.refs_1_, bf16[144,1024]{1,0:T(8,128)(2,1)S(1)} %get-tuple-element.64.refs_2_, ...), custom_call_target="tpu_custom_call" | custom-call | flops 603979776 | bytes 4460544 | tf_op jit(solution)/shard_map/pallas_call | solution.py:34
  67.8 1.2 %collective-permute-done.18.refs_4_ = bf16[144,256]{1,0:T(8,128)(2,1)S(1)} collective-permute-done((bf16[144,256]{1,0:T(8,128)(2,1)S(1)}, bf16[144,256]{1,0:T(8,128)(2,1)S(1)}, u32[]{:S(2)}, u32[]{:S(2)}) %collective-permute-start.18) | collective-permute-done | bytes 73760 | tf_op jit(solution)/shard_map/ppermute | solution.py:285
  69.8 1.1 %shard_map.118 = bf16[1,128,1024]{2,1,0:T(8,128)(2,1)} custom-call(bf16[128,1024]{1,0:T(8,128)(2,1)S(1)} %get-tuple-element.45.refs_4_.refs_0_, s32[8,128]{1,0:T(8,128)S(1)} %get-tuple-element.42.refs_5_.refs_1_, bf16[144,256]{1,0:T(8,128)(2,1)S(1)} %get-tuple-element.59.refs_2_, bf16[144,256]{1,0:T(8,128)(2,1)S(1)} %collective-permute-done.17.refs_3_, ...), custom_call_target="tpu_custom_call" | custom-call | bytes 823296 | tf_op jit(solution)/shard_map/pallas_call | solution.py:34
  (43 shorter events, 8.3 us)
Async XLA Ops:
  0.6 33.8 %copy-start.1 = (bf16[1,1024,1024]{2,1,0:T(8,128)(2,1)S(1)}, bf16[1,1024,1024]{2,1,0:T(8,128)(2,1)}, u32[]{:S(2)}) copy-start(bf16[1,1024,1024]{2,1,0:T(8,128)(2,1)} %param.17) | copy-start | bytes 6291460
  2.0 32.5 %copy-start = (bf16[1024,1024]{1,0:T(8,128)(2,1)S(1)}, bf16[1024,1024]{1,0:T(8,128)(2,1)}, u32[]{:S(2)}) copy-start(bf16[1024,1024]{1,0:T(8,128)(2,1)} %refs_2_.5) | copy-start | bytes 6291460
  2.0 13.8 %collective-permute-start = (bf16[1040,128]{1,0:T(8,128)(2,1)S(1)}, bf16[1040,128]{1,0:T(8,128)(2,1)S(1)}, u32[]{:S(2)}, u32[]{:S(2)}) collective-permute-start(bf16[1040,128]{1,0:T(8,128)(2,1)S(1)} %get-tuple-element.43), channel_id=1, source_target_pairs={{0,1},{1,0},{2,3},{3,2},{4,5},{5,4},{6,7},{7,6},{8,9},{9,8},{10,11... | collective-permute-start | bytes 798728 | tf_op jit(solution)/shard_map/ppermute | solution.py:285
  5.0 10.8 %collective-permute-start.1 = (bf16[1040,128]{1,0:T(8,128)(2,1)S(1)}, bf16[1040,128]{1,0:T(8,128)(2,1)S(1)}, u32[]{:S(2)}, u32[]{:S(2)}) collective-permute-start(bf16[1040,128]{1,0:T(8,128)(2,1)S(1)} %get-tuple-element.44), channel_id=1, source_target_pairs={{1,2},{3,4},{5,6},{7,8},{9,10},{11,12},{13,14},{2,1},{4,3},{6,5},{... | collective-permute-start | bytes 798728 | tf_op jit(solution)/shard_map/ppermute | solution.py:322
  7.0 16.5 %collective-permute-start.5 = (bf16[144,256]{1,0:T(8,128)(2,1)S(1)}, bf16[144,256]{1,0:T(8,128)(2,1)S(1)}, u32[]{:S(2)}, u32[]{:S(2)}) collective-permute-start(bf16[144,256]{1,0:T(8,128)(2,1)S(1)} %get-tuple-element.51), channel_id=1, source_target_pairs={{0,4},{1,5},{2,6},{3,7},{4,0},{5,1},{6,2},{7,3},{8,12},{9,13},{10,... | collective-permute-start | bytes 221192 | tf_op jit(solution)/shard_map/ppermute | solution.py:285
  11.4 12.8 %collective-permute-start.6 = (bf16[144,256]{1,0:T(8,128)(2,1)S(1)}, bf16[144,256]{1,0:T(8,128)(2,1)S(1)}, u32[]{:S(2)}, u32[]{:S(2)}) collective-permute-start(bf16[144,256]{1,0:T(8,128)(2,1)S(1)} %get-tuple-element.52), channel_id=1, source_target_pairs={{0,8},{1,9},{2,10},{3,11},{4,12},{5,13},{6,14},{7,15},{8,0},{9,1},... | collective-permute-start | bytes 221192 | tf_op jit(solution)/shard_map/ppermute | solution.py:285
  14.0 10.2 %collective-permute-start.7 = (bf16[144,256]{1,0:T(8,128)(2,1)S(1)}, bf16[144,256]{1,0:T(8,128)(2,1)S(1)}, u32[]{:S(2)}, u32[]{:S(2)}) collective-permute-start(bf16[144,256]{1,0:T(8,128)(2,1)S(1)} %get-tuple-element.53), channel_id=1, source_target_pairs={{0,12},{1,13},{2,14},{3,15},{4,8},{5,9},{6,10},{7,11},{8,4},{9,5},... | collective-permute-start | bytes 221192 | tf_op jit(solution)/shard_map/ppermute | solution.py:285
  17.3 10.8 %collective-permute-start.2 = (bf16[144,256]{1,0:T(8,128)(2,1)S(1)}, bf16[144,256]{1,0:T(8,128)(2,1)S(1)}, u32[]{:S(2)}, u32[]{:S(2)}) collective-permute-start(bf16[144,256]{1,0:T(8,128)(2,1)S(1)} %get-tuple-element.47), channel_id=1, source_target_pairs={{0,8},{1,9},{2,10},{3,11},{4,12},{5,13},{6,14},{7,15},{8,0},{9,1},... | collective-permute-start | bytes 221192 | tf_op jit(solution)/shard_map/ppermute | solution.py:285
  23.5 6.2 %collective-permute-start.3 = (bf16[144,256]{1,0:T(8,128)(2,1)S(1)}, bf16[144,256]{1,0:T(8,128)(2,1)S(1)}, u32[]{:S(2)}, u32[]{:S(2)}) collective-permute-start(bf16[144,256]{1,0:T(8,128)(2,1)S(1)} %get-tuple-element.48), channel_id=1, source_target_pairs={{0,12},{1,13},{2,14},{3,15},{4,8},{5,9},{6,10},{7,11},{8,4},{9,5},... | collective-permute-start | bytes 221192 | tf_op jit(solution)/shard_map/ppermute | solution.py:285
  23.5 6.1 %collective-permute-start.4 = (bf16[144,256]{1,0:T(8,128)(2,1)S(1)}, bf16[144,256]{1,0:T(8,128)(2,1)S(1)}, u32[]{:S(2)}, u32[]{:S(2)}) collective-permute-start(bf16[144,256]{1,0:T(8,128)(2,1)S(1)} %get-tuple-element.49), channel_id=1, source_target_pairs={{0,4},{1,5},{2,6},{3,7},{4,0},{5,1},{6,2},{7,3},{8,12},{9,13},{10,... | collective-permute-start | bytes 221192 | tf_op jit(solution)/shard_map/ppermute | solution.py:285
  24.6 7.0 %collective-permute-start.9 = (bf16[144,1024]{1,0:T(8,128)(2,1)S(1)}, bf16[144,1024]{1,0:T(8,128)(2,1)S(1)}, u32[]{:S(2)}, u32[]{:S(2)}) collective-permute-start(bf16[144,1024]{1,0:T(8,128)(2,1)S(1)} %shard_map.108.refs_4_), channel_id=1, source_target_pairs={{0,2},{1,3},{2,0},{3,1},{4,6},{5,7},{6,4},{7,5},{8,10},{9,11},{10,... | collective-permute-start | bytes 884744 | tf_op jit(solution)/shard_map/ppermute | solution.py:285
  25.1 9.4 %collective-permute-start.8 = (bf16[144,1024]{1,0:T(8,128)(2,1)S(1)}, bf16[144,1024]{1,0:T(8,128)(2,1)S(1)}, u32[]{:S(2)}, u32[]{:S(2)}) collective-permute-start(bf16[144,1024]{1,0:T(8,128)(2,1)S(1)} %shard_map.108.refs_4_), channel_id=1, source_target_pairs={{0,1},{1,0},{2,3},{3,2},{4,5},{5,4},{6,7},{7,6},{8,9},{9,8},{10,11... | collective-permute-start | bytes 884744 | tf_op jit(solution)/shard_map/ppermute | solution.py:285
  30.1 8.3 %collective-permute-start.10 = (bf16[144,1024]{1,0:T(8,128)(2,1)S(1)}, bf16[144,1024]{1,0:T(8,128)(2,1)S(1)}, u32[]{:S(2)}, u32[]{:S(2)}) collective-permute-start(bf16[144,1024]{1,0:T(8,128)(2,1)S(1)} %shard_map.107.refs_0_), channel_id=1, source_target_pairs={{0,1},{1,0},{2,3},{3,2},{4,5},{5,4},{6,7},{7,6},{8,9},{9,8},{10,11... | collective-permute-start | bytes 884744 | tf_op jit(solution)/shard_map/ppermute | solution.py:285
  30.9 11.6 %collective-permute-start.12 = (bf16[144,1024]{1,0:T(8,128)(2,1)S(1)}, bf16[144,1024]{1,0:T(8,128)(2,1)S(1)}, u32[]{:S(2)}, u32[]{:S(2)}) collective-permute-start(bf16[144,1024]{1,0:T(8,128)(2,1)S(1)} %shard_map.107.refs_0_), channel_id=1, source_target_pairs={{0,2},{1,3},{2,0},{3,1},{4,6},{5,7},{6,4},{7,5},{8,10},{9,11},{10,... | collective-permute-start | bytes 884744 | tf_op jit(solution)/shard_map/ppermute | solution.py:285
  39.4 15.0 %collective-permute-start.11 = (bf16[144,1024]{1,0:T(8,128)(2,1)S(1)}, bf16[144,1024]{1,0:T(8,128)(2,1)S(1)}, u32[]{:S(2)}, u32[]{:S(2)}) collective-permute-start(bf16[144,1024]{1,0:T(8,128)(2,1)S(1)} %get-tuple-element.56), channel_id=1, source_target_pairs={{0,1},{1,0},{2,3},{3,2},{4,5},{5,4},{6,7},{7,6},{8,9},{9,8},{10,11... | collective-permute-start | bytes 884744 | tf_op jit(solution)/shard_map/ppermute | solution.py:285
  40.8 6.5 %collective-permute-start.14 = (bf16[64,1024]{1,0:T(8,128)(2,1)S(1)}, bf16[64,1024]{1,0:T(8,128)(2,1)S(1)}, u32[]{:S(2)}, u32[]{:S(2)}) collective-permute-start(bf16[64,1024]{1,0:T(8,128)(2,1)S(1)} %slice.16), channel_id=1, source_target_pairs={{0,2},{1,3},{2,0},{3,1},{4,6},{5,7},{6,4},{7,5},{8,10},{9,11},{10,... | collective-permute-start | bytes 393224 | tf_op jit(solution)/shard_map/ppermute | solution.py:285
  43.5 13.4 %collective-permute-start.13 = (bf16[144,1024]{1,0:T(8,128)(2,1)S(1)}, bf16[144,1024]{1,0:T(8,128)(2,1)S(1)}, u32[]{:S(2)}, u32[]{:S(2)}) collective-permute-start(bf16[144,1024]{1,0:T(8,128)(2,1)S(1)} %get-tuple-element.57), channel_id=1, source_target_pairs={{0,2},{1,3},{2,0},{3,1},{4,6},{5,7},{6,4},{7,5},{8,10},{9,11},{10,... | collective-permute-start | bytes 884744 | tf_op jit(solution)/shard_map/ppermute | solution.py:285
  43.9 7.8 %collective-permute-start.15 = (bf16[80,1024]{1,0:T(8,128)(2,1)S(1)}, bf16[80,1024]{1,0:T(8,128)(2,1)S(1)}, u32[]{:S(2)}, u32[]{:S(2)}) collective-permute-start(bf16[80,1024]{1,0:T(8,128)(2,1)S(1)} %slice.17), channel_id=1, source_target_pairs={{0,1},{1,0},{2,3},{3,2},{4,5},{5,4},{6,7},{7,6},{8,9},{9,8},{10,11... | collective-permute-start | bytes 491528 | tf_op jit(solution)/shard_map/ppermute | solution.py:285
  44.7 10.6 %collective-permute-start.21 = (bf16[80,1024]{1,0:T(8,128)(2,1)S(1)}, bf16[80,1024]{1,0:T(8,128)(2,1)S(1)}, u32[]{:S(2)}, u32[]{:S(2)}) collective-permute-start(bf16[80,1024]{1,0:T(8,128)(2,1)S(1)} %slice.19), channel_id=1, source_target_pairs={{0,1},{1,0},{2,3},{3,2},{4,5},{5,4},{6,7},{7,6},{8,9},{9,8},{10,11... | collective-permute-start | bytes 491528 | tf_op jit(solution)/shard_map/ppermute | solution.py:285
  47.3 7.3 %collective-permute-start.20 = (bf16[64,1024]{1,0:T(8,128)(2,1)S(1)}, bf16[64,1024]{1,0:T(8,128)(2,1)S(1)}, u32[]{:S(2)}, u32[]{:S(2)}) collective-permute-start(bf16[64,1024]{1,0:T(8,128)(2,1)S(1)} %slice.18), channel_id=1, source_target_pairs={{0,2},{1,3},{2,0},{3,1},{4,6},{5,7},{6,4},{7,5},{8,10},{9,11},{10,... | collective-permute-start | bytes 393224 | tf_op jit(solution)/shard_map/ppermute | solution.py:285
  52.7 7.7 %collective-permute-start.16 = (bf16[144,1024]{1,0:T(8,128)(2,1)S(1)}, bf16[144,1024]{1,0:T(8,128)(2,1)S(1)}, u32[]{:S(2)}, u32[]{:S(2)}) collective-permute-start(bf16[144,1024]{1,0:T(8,128)(2,1)S(1)} %get-tuple-element.58), channel_id=1, source_target_pairs={{0,3},{1,2},{2,1},{3,0},{4,7},{5,6},{6,5},{7,4},{8,11},{9,10},{10,... | collective-permute-start | bytes 884744 | tf_op jit(solution)/shard_map/ppermute | solution.py:285
  56.3 7.4 %collective-permute-start.22 = (bf16[128,1024]{1,0:T(8,128)(2,1)S(1)}, bf16[128,1024]{1,0:T(8,128)(2,1)S(1)}, u32[]{:S(2)}, u32[]{:S(2)}) collective-permute-start(bf16[128,1024]{1,0:T(8,128)(2,1)S(1)} %get-tuple-element.66), channel_id=1, source_target_pairs={{0,16},{16,0},{1,17},{17,1},{2,18},{18,2},{3,19},{19,3},{4,20},{20... | collective-permute-start | bytes 786440 | tf_op jit(solution)/shard_map/ppermute | solution.py:382
  56.4 8.8 %collective-permute-start.23 = (bf16[128,1024]{1,0:T(8,128)(2,1)S(1)}, bf16[128,1024]{1,0:T(8,128)(2,1)S(1)}, u32[]{:S(2)}, u32[]{:S(2)}) collective-permute-start(bf16[128,1024]{1,0:T(8,128)(2,1)S(1)} %get-tuple-element.67), channel_id=1, source_target_pairs={{0,16},{16,0},{1,17},{17,1},{2,18},{18,2},{3,19},{19,3},{4,20},{20... | collective-permute-start | bytes 786440 | tf_op jit(solution)/shard_map/ppermute | solution.py:382
  56.9 8.9 %collective-permute-start.24 = (bf16[128,1024]{1,0:T(8,128)(2,1)S(1)}, bf16[128,1024]{1,0:T(8,128)(2,1)S(1)}, u32[]{:S(2)}, u32[]{:S(2)}) collective-permute-start(bf16[128,1024]{1,0:T(8,128)(2,1)S(1)} %get-tuple-element.68), channel_id=1, source_target_pairs={{0,16},{16,0},{1,17},{17,1},{2,18},{18,2},{3,19},{19,3},{4,20},{20... | collective-permute-start | bytes 786440 | tf_op jit(solution)/shard_map/ppermute | solution.py:382
  56.9 8.8 %collective-permute-start.25 = (bf16[128,1024]{1,0:T(8,128)(2,1)S(1)}, bf16[128,1024]{1,0:T(8,128)(2,1)S(1)}, u32[]{:S(2)}, u32[]{:S(2)}) collective-permute-start(bf16[128,1024]{1,0:T(8,128)(2,1)S(1)} %get-tuple-element.69), channel_id=1, source_target_pairs={{0,16},{16,0},{1,17},{17,1},{2,18},{18,2},{3,19},{19,3},{4,20},{20... | collective-permute-start | bytes 786440 | tf_op jit(solution)/shard_map/ppermute | solution.py:382
  60.8 7.0 %collective-permute-start.17 = (bf16[144,256]{1,0:T(8,128)(2,1)S(1)}, bf16[144,256]{1,0:T(8,128)(2,1)S(1)}, u32[]{:S(2)}, u32[]{:S(2)}) collective-permute-start(bf16[144,256]{1,0:T(8,128)(2,1)S(1)} %get-tuple-element.60), channel_id=1, source_target_pairs={{0,12},{1,13},{2,14},{3,15},{4,8},{5,9},{6,10},{7,11},{8,4},{9,5},... | collective-permute-start | bytes 221192 | tf_op jit(solution)/shard_map/ppermute | solution.py:285
  63.7 5.3 %collective-permute-start.18 = (bf16[144,256]{1,0:T(8,128)(2,1)S(1)}, bf16[144,256]{1,0:T(8,128)(2,1)S(1)}, u32[]{:S(2)}, u32[]{:S(2)}) collective-permute-start(bf16[144,256]{1,0:T(8,128)(2,1)S(1)} %get-tuple-element.61), channel_id=1, source_target_pairs={{0,8},{1,9},{2,10},{3,11},{4,12},{5,13},{6,14},{7,15},{8,0},{9,1},... | collective-permute-start | bytes 221192 | tf_op jit(solution)/shard_map/ppermute | solution.py:285
  65.2 4.6 %collective-permute-start.19 = (bf16[144,256]{1,0:T(8,128)(2,1)S(1)}, bf16[144,256]{1,0:T(8,128)(2,1)S(1)}, u32[]{:S(2)}, u32[]{:S(2)}) collective-permute-start(bf16[144,256]{1,0:T(8,128)(2,1)S(1)} %get-tuple-element.62), channel_id=1, source_target_pairs={{0,4},{1,5},{2,6},{3,7},{4,0},{5,1},{6,2},{7,3},{8,12},{9,13},{10,... | collective-permute-start | bytes 221192 | tf_op jit(solution)/shard_map/ppermute | solution.py:285

commit v6 on v5

--- a/solution.py
+++ b/solution.py
@@ -95,84 +95,72 @@
         message[2 * HEADS * HALO :, :] = jnp.broadcast_to(mask, (16, width)).astype(BF16)
 
 
-def slots_of(labels):
+def routed(labels):
     count = labels.shape[1]
     row, column = iota((count, count), 0), iota((count, count), 1)
     as_column = jnp.sum(jnp.where(row == column, labels, 0), axis=1, keepdims=True)
-    return jnp.sum(jnp.where((row < column) & (as_column == labels), 1, 0), axis=0, keepdims=True)
-
-
-def pack(rows, labels, slot, message_refs, capacity):
-    home = home_plane()
-    count = rows.shape[0]
-    stacked = column_blocks(rows)
-    height = message_refs[0].shape[0]
+    same = as_column == labels
+    slot = jnp.sum(jnp.where((row < column) & same, 1, 0), axis=0, keepdims=True)
+    return as_column, slot, jnp.sum(jnp.where((column < row) & same, 1, 0), axis=1, keepdims=True)
+
+
+def to_messages(rows, message_refs, pitch):
+    height, width = message_refs[0].shape
     for p, message in enumerate(message_refs):
-        mine = labels == (home ^ p)
-        places = [one_hot(mine & (slot + j * capacity == iota((height, count), 0))) for j in range(PARTS)]
-        message[...] = dot(jnp.concatenate(places, axis=1), stacked).astype(BF16)
-
-
-def pack_body(capacity, cot_hbm, label_hbm, query_hbm, token_hbm, route_ref, query_ref, token_ref, *refs):
+        for j in range(PARTS):
+            start = j * (height // PARTS)
+            message[start : start + pitch, :] = rows[p * pitch : (p + 1) * pitch, j * width : (j + 1) * width]
+
+
+def from_messages(message_refs, pitch, height):
+    step, width = message_refs[0].shape[0] // PARTS, message_refs[0].shape[1]
+    columns = []
+    for j in range(PARTS):
+        blocks = [m[j * step : j * step + pitch, :] for m in message_refs]
+        spare = height - pitch * len(blocks)
+        columns.append(jnp.concatenate(blocks + [jnp.zeros((spare, width), BF16)] * (spare > 0), axis=0))
+    return columns
+
+
+def pack(rows, place_ref, message_refs, pitch):
+    to_messages(dot(place_ref[...], rows).astype(BF16), message_refs, pitch)
+
+
+def pack_body(pitch, cot_hbm, label_hbm, query_hbm, token_hbm, place_ref, back_ref, query_ref, token_ref, *refs):
     *message_refs, cot_ref, label_ref, sems = refs
     copies = load(
         ((label_hbm, label_ref), (cot_hbm, cot_ref), (query_hbm, query_ref), (token_hbm, token_ref)), sems
     )
     copies[0].wait()
     labels = label_ref[...]
-    slot = slots_of(labels)
-    route_ref[0:1, :] = labels
-    route_ref[1:2, :] = slot
+    label_column, slot, slot_column = routed(labels)
+    home = home_plane()
+    place_ref[...] = one_hot((labels ^ home) * pitch + slot == iota(place_ref.shape, 0))
+    back_ref[...] = one_hot((label_column ^ home) * pitch + slot_column == iota(back_ref.shape, 1))
     copies[1].wait()
-    pack(cot_ref[0], labels, slot, message_refs, capacity)
+    pack(cot_ref[0], place_ref, message_refs, pitch)
     for c in copies[2:]:
         c.wait()
 
 
-def group_of(row, capacity, experts):
-    group = jnp.zeros_like(row)
-    for a in range(1, experts):
-        group += jnp.where(row >= a * capacity, 1, 0)
-    return group
-
-
-def gather_body(capacity, experts, order, *refs):
+def gather_body(order, pitch, *refs):
     *message_refs, rows_ref = refs
-    message_refs = [message_refs[order.index(k)] for k in range(experts)]
-    stacked = jnp.concatenate([m[...] for m in message_refs], axis=0)
-    block, width = message_refs[0].shape
-    row = iota((rows_ref.shape[0], stacked.shape[0]), 0)
-    group = group_of(row, capacity, experts)
-    source = group * block + row - group * capacity
-    source = jnp.where(row < experts * capacity, source, -(1 << 20)) - iota(row.shape, 1)
-    for j in range(PARTS):
-        place = one_hot(source == -j * capacity)
-        rows_ref[:, j * width : (j + 1) * width] = dot(place, stacked).astype(BF16)
-
-
-def scatter(total, groups, message_refs, capacity):
-    stacked = column_blocks(total)
-    block = total.shape[0]
-    height = message_refs[0].shape[0]
-    row = iota((height, stacked.shape[0]), 0)
-    part = group_of(row, capacity, PARTS)
-    source = part * block + row - part * capacity
-    source = jnp.where(row < PARTS * capacity, source, -(1 << 20)) - iota(row.shape, 1)
-    for group, message in zip(groups, message_refs, strict=True):
-        message[...] = dot(one_hot(source == -group * capacity), stacked).astype(BF16)
-
-
-def add_body(first_ref, second_ref, sum_ref):
-    sum_ref[...] = first_ref[...].astype(F32) + second_ref[...].astype(F32)
-
-
-def combine_body(capacity, experts, sum_ref, last_ref, *message_refs):
-    total = (sum_ref[...] + last_ref[...].astype(F32)).astype(BF16)
-    scatter(total, range(experts), message_refs, capacity)
+    width = message_refs[0].shape[1]
+    ordered = [message_refs[order.index(k)] for k in range(len(order))]
+    for j, column in enumerate(from_messages(ordered, pitch, rows_ref.shape[0])):
+        rows_ref[:, j * width : (j + 1) * width] = column
+
+
+def combine_body(pitch, *refs):
+    partial_refs, message_refs = refs[:SPLIT], refs[SPLIT:]
+    total = partial_refs[0][...].astype(F32)
+    for partial_ref in partial_refs[1:]:
+        total += partial_ref[...].astype(F32)
+    to_messages(total.astype(BF16), message_refs, pitch)
 
 
 def attention_body(
-    capacity, query_ref, token_ref, key_ref, value_ref, mask_ref, route_ref, near_ref, far_ref, mixed_ref, *message_refs
+    pitch, query_ref, token_ref, key_ref, value_ref, mask_ref, near_ref, far_ref, place_ref, mixed_ref, *message_refs
 ):
     rows, features = query_ref.shape[1:]
     width = features // HEADS
@@ -215,12 +203,17 @@
         raised = jnp.exp(scores - jnp.max(scores, axis=1, keepdims=True))
         soft = (raised * (1.0 / jnp.sum(raised, axis=1, keepdims=True))).astype(BF16)
         mixed_ref[:, columns] = (token_ref[0, :, columns].astype(F32) + dot(soft, values)).astype(BF16)
-    pack(mixed_ref[...], route_ref[0:1, :], route_ref[1:2, :], message_refs, capacity)
+    pack(mixed_ref[...], place_ref, message_refs, pitch)
+
+
+def far_part(refs, which):
+    halves = [r.shape[0] // 2 for r in refs]
+    return jnp.concatenate([r[which * n : (which + 1) * n, :] for r, n in zip(refs, halves, strict=True)], axis=0)
 
 
 def expert_body(*refs):
     *row_refs, in_ref, out_ref, hidden_ref, partial_ref = refs
-    rows = jnp.concatenate([r[...] for r in row_refs], axis=0)
+    rows = row_refs[0][...] if len(row_refs) == 1 else far_part(row_refs, 0)
     for at in range(0, in_ref.shape[1], STEP):
         hidden_ref[:, at : at + STEP] = jax.nn.gelu(dot(rows, in_ref[:, at : at + STEP])).astype(BF16)
     hidden = hidden_ref[...]
@@ -228,27 +221,19 @@
         partial_ref[:, at : at + STEP] = dot(hidden, out_ref[:, at : at + STEP]).astype(BF16)
 
 
-def finish_body(capacity, order, mixed_ref, route_ref, *refs):
+def finish_body(order, pitch, mixed_ref, back_ref, *refs):
     *message_refs, layer_ref = refs
-    message_refs = [message_refs[order.index(k)] for k in range(len(message_refs))]
-    home = home_plane()
-    labels, slot = route_ref[0:1, :], route_ref[1:2, :]
-    count = labels.shape[1]
-    block, width = message_refs[0].shape
-    stacked = jnp.concatenate([m[...] for m in message_refs], axis=0)
-    for j in range(PARTS):
-        places = [
-            one_hot((labels == (home ^ p)) & (slot + j * capacity == iota((block, count), 0)))
-            for p in range(len(message_refs))
-        ]
-        taken = dot(jnp.concatenate(places, axis=0), stacked, (0, 0))
+    width = message_refs[0].shape[1]
+    ordered = [message_refs[order.index(k)] for k in range(len(order))]
+    for j, column in enumerate(from_messages(ordered, pitch, back_ref.shape[1])):
         columns = slice(j * width, (j + 1) * width)
+        taken = dot(back_ref[...], column)
         layer_ref[0, :, columns] = (mixed_ref[:, columns].astype(F32) + taken).astype(BF16)
 
 
 def half_terms(refs, side):
-    hidden_refs, cot_refs = refs[:SPLIT], refs[SPLIT : 2 * SPLIT + 1]
-    cot = jnp.concatenate([c[...] for c in cot_refs], axis=0)
+    hidden_refs, cot_refs = refs[:SPLIT], refs[SPLIT : 2 * SPLIT - 1]
+    cot = jnp.concatenate([c[...] for c in cot_refs] + [far_part(refs[2 * SPLIT - 1 : 2 * SPLIT + 1], 1)], axis=0)
     half = hidden_refs[0].shape[1] // 2
     start = (lax.axis_index("grp") ^ side) * half
     for at in range(0, half, STEP):
@@ -277,7 +262,7 @@
 
 def whole_term_body(*refs):
     hidden = jnp.concatenate([h[...] for h in refs[:SPLIT]], axis=0)
-    cot = jnp.concatenate([c[...] for c in refs[SPLIT : 2 * SPLIT + 1]], axis=0)
+    cot = jnp.concatenate([c[...] for c in refs[SPLIT : 2 * SPLIT - 1]] + [far_part(refs[-3:-1], 1)], axis=0)
     refs[-1][...] = dot(hidden, cot, (0, 0)).astype(BF16)
 
 
@@ -285,9 +270,15 @@
     return lax.ppermute(value, "ep", [(i, i ^ apart) for i in range(lax.axis_size("ep"))])
 
 
-def forwarded(along_x, along_y):
-    half = along_x.shape[0] // 32 * 16
-    return permute(along_x[:half], 2), permute(along_y[half:], 1)
+def forward_body(first_row, rows_ref, cot_ref, both_ref):
+    count = both_ref.shape[0] // 2
+    both_ref[:count, :] = rows_ref[first_row : first_row + count, :]
+    both_ref[count:, :] = cot_ref[first_row : first_row + count, :]
+
+
+def forwarded(rows, cot, first_row, count, apart):
+    (both,) = call(functools.partial(forward_body, first_row), [out(2 * count, rows.shape[1])], vmem=(rows, cot))
+    return permute(both, apart)
 
 
 def along_line(messages):
@@ -300,8 +291,9 @@
     experts = axis_count // SPLIT
     capacity = rows_here // experts + max(1, rows_here // (8 * experts))
     width = features // PARTS
-    height = -(-PARTS * capacity // 16) * 16
-    plane_rows = -(-experts * capacity // 16) * 16
+    pitch = capacity + capacity % 2
+    height = -(-PARTS * pitch // 16) * 16
+    plane_rows = -(-experts * pitch // 16) * 16
     hidden_units = weight_in.shape[1]
     head_width = features // HEADS
     label_row = labels.reshape(1, rows_here)
@@ -321,10 +313,10 @@
     steps = [(i, i + 1) for i in range(1, axis_count - 1, 2)]
     far = lax.ppermute(far, "ep", steps + [(j, i) for i, j in steps])
 
-    gather = functools.partial(gather_body, capacity, experts)
-    route, query_here, token_here, *sent = call(
-        functools.partial(pack_body, capacity),
-        [out(8, rows_here, dtype=jnp.int32), block, block] + [message] * experts,
+    place, place_back, query_here, token_here, *sent = call(
+        functools.partial(pack_body, pitch),
+        [out(plane_rows, rows_here), out(rows_here, plane_rows), block, block]
+        + [message] * experts,
         hbm=(cotangent, label_row, queries, tokens),
         after=(key_here,),
         scratch=[block_scratch, row_ints, pltpu.SemaphoreType.DMA((4,))],
@@ -334,26 +326,33 @@
     in_here, out_here = weight_in, weight_out.reshape(weight_out.shape[1:])
 
     mixed, *sent = call(
-        functools.partial(attention_body, capacity),
+        functools.partial(attention_body, pitch),
         [out(rows_here, features)] + [message] * experts,
-        vmem=(query_here, token_here, key_here, value_here, mask_here, route, near, far),
+        vmem=(query_here, token_here, key_here, value_here, mask_here, near, far, place),
         flops=4 * rows_here * (rows_here + 2 * HALO) * features,
     )
 
     (cot_rows,) = call(
-        functools.partial(gather, range(experts)), [out(plane_rows, features)], vmem=cot_got, after=(mixed,), size=0
+        functools.partial(gather_body, range(experts), pitch),
+        [out(plane_rows, features)],
+        vmem=cot_got,
+        after=(mixed,),
+        size=0,
     )
     cot_x, cot_y = permute(cot_rows, 1), permute(cot_rows, 2)
     mixed_got = along_line(sent)
     order = [0, *range(2, experts), 1]
     (rows,) = call(
-        functools.partial(gather, order), [out(plane_rows, features)], vmem=[mixed_got[k] for k in order]
-    )
-    cot_far = forwarded(cot_x, cot_y)
+        functools.partial(gather_body, order, pitch),
+        [out(plane_rows, features)],
+        vmem=[mixed_got[k] for k in order],
+    )
 
     row_x, row_y = permute(rows, 1), permute(rows, 2)
+    part = plane_rows // 32 * 16
+    far = (forwarded(row_x, cot_x, 0, part, 2), forwarded(row_y, cot_y, part, plane_rows - part, 1))
     hiddens, partials = [], []
-    for pieces, first in (((rows,), (cot_x, cot_y)), ((row_x,), ()), ((row_y,), ()), (forwarded(row_x, row_y), ())):
+    for pieces, first in (((rows,), (cot_x, cot_y)), ((row_x,), ()), ((row_y,), ()), (far, ())):
         hidden, partial = call(
             expert_body,
             [out(plane_rows, hidden_units), out(plane_rows, features)],
@@ -364,20 +363,14 @@
         hiddens.append(hidden)
         partials.append(partial)
 
-    total = partials[0]
-    totals = []
-    for k in (1, 2):
-        (total,) = call(
-            add_body, [out(plane_rows, features, dtype=F32)], vmem=(total, permute(partials[k], k)), size=0
-        )
-        totals.append(total)
-    last = permute(partials[3], 3)
-    inputs = (*hiddens, cot_rows, cot_x, cot_y, *cot_far)
+    sums = [p if k == 0 else permute(p, k) for k, p in enumerate(partials)]
+
+    inputs = (*hiddens, cot_rows, cot_x, cot_y, *far)
     flops = SPLIT * plane_rows * features * hidden_units
     if lax.axis_size("grp") == 2:
         half = hidden_units // 2
         pieces = call(
-            other_half_body, [out(half // PIECES, features)] * PIECES, vmem=inputs, after=totals[:1], flops=flops
+            other_half_body, [out(half // PIECES, features)] * PIECES, vmem=inputs, after=sums[1:3], flops=flops
         )
         theirs = [lax.ppermute(piece, "grp", [(0, 1), (1, 0)]) for piece in pieces]
         grad, done = call(
@@ -391,11 +384,11 @@
         (term,) = call(whole_term_body, [out(hidden_units, features)], vmem=inputs, flops=2 * flops)
         grad = lax.psum_scatter(term, "grp", scatter_dimension=0, tiled=True)[None]
         ready = ()
-    sent = call(functools.partial(combine_body, capacity, experts), [message] * experts, vmem=(total, last))
+    sent = call(functools.partial(combine_body, pitch), [message] * experts, vmem=sums)
     back = along_line(sent)
     order = [0, *range(experts - 1, 0, -1)]
     (layer_out,) = call(
-        functools.partial(finish_body, capacity, order), [block], vmem=(mixed, route, *[back[k] for k in order]), after=ready
+        functools.partial(finish_body, order, pitch), [block], vmem=(mixed, place_back, *[back[k] for k in order]), after=ready
     )
     return (layer_out, grad)
 

time: 71.1 us -> 69.9 us (0.983)
  waiting for transfers between devices: 20.6 us -> 24.5 us
  starting transfers between devices: 35.9 us -> 32.3 us
  Pallas kernels: 13.5 us -> 12.1 us
    ppermute x21 -> x19, waiting for transfers between devices: 20.6 us -> 24.5 us  [permute(): lax.ppermute(value, 'ep', [(i, i ^ apart) for i in range(lax.axis_size('e...]
    ppermute x21 -> x19, starting transfers between devices: 34.2 us -> 30.6 us  [permute(): lax.ppermute(value, 'ep', [(i, i ^ apart) for i in range(lax.axis_size('e...]
    pallas_call x15, Pallas kernels: 13.5 us -> 12.1 us  [call(): pl.pallas_call(kernel, out_shape=outs, in_specs=[VMEM] * len(vmem) + [HBM...]
  transfers between devices with their start and end apart: 26 -> 24, of which waited for: 12 -> 11; matrix products, arithmetic and copies ran while one was open for 0% -> 0% of each run, Pallas kernels for 16% -> 14%
where the time goes in v6:
time: 69.9 us; the launch traced here: 69.7 us
  starting transfers between devices  32.3 us (46%)
  waiting for transfers between devices  24.5 us (35%)
  Pallas kernels  12.1 us (17%)
  between operations  0.78 us (1%)
    ppermute x19, starting transfers between devices, permute(): lax.ppermute(value, 'ep', [(i, i ^ apart) for i in range(lax.axis_size('e...  30.6 us
    ppermute x19, waiting for transfers between devices, permute(): lax.ppermute(value, 'ep', [(i, i ^ apart) for i in range(lax.axis_size('e...  24.5 us
    pallas_call x15, Pallas kernels, call(): pl.pallas_call(kernel, out_shape=outs, in_specs=[VMEM] * len(vmem) + [HBM...  12.1 us
  transfers between devices with their start and end apart: 24, of which 11 were waited for; matrix products, arithmetic and copies ran while one was open for 0% of the time, Pallas kernels for 14%

profile of v6, /device:TPU:0, one launch (start us, length us, event | category | flops | bytes accessed | tf_op | source)
XLA Modules:
  0.0 69.7 jit_solution(5292168255153646991)
XLA Ops:
  0.6 1.3 %shard_map.104 = (bf16[1040,128]{1,0:T(8,128)(2,1)S(1)}, bf16[1040,128]{1,0:T(8,128)(2,1)S(1)}, bf16[1,128,1024]{2,1,0:T(8,128)(2,1)S(1)}, bf16[1,128,1024]{2,1,0:T(8,128)(2,1)S(1)}, s32[1,128]{1,0:T(1,128)S(1)}) custom-call(bf16[1,128,1024]{2,1,0:T(8,128)(2,1)} %refs_0_.2, bf16[1,128,1024]{2,1,0:T(8,128)(2,1)} %refs_1_.4, s32[1,128]{1,0:T(1,128)} %refs_2_.3), custom_call_target="tpu_custom_call" | custom-call | bytes 1582080 | tf_op jit(solution)/shard_map/pallas_call | solution.py:34
  2.0 3.0 %collective-permute-start = (bf16[1040,128]{1,0:T(8,128)(2,1)S(1)}, bf16[1040,128]{1,0:T(8,128)(2,1)S(1)}, u32[]{:S(2)}, u32[]{:S(2)}) collective-permute-start(bf16[1040,128]{1,0:T(8,128)(2,1)S(1)} %get-tuple-element.43), channel_id=1, source_target_pairs={{0,1},{1,0},{2,3},{3,2},{4,5},{5,4},{6,7},{7,6},{8,9},{9,8},{10,11... | collective-permute-start | bytes 798728 | tf_op jit(solution)/shard_map/ppermute | solution.py:270
  5.7 1.2 %shard_map.105 = (bf16[144,128]{1,0:T(8,128)(2,1)S(1)}, bf16[128,144]{1,0:T(8,128)(2,1)S(1)}, bf16[1,128,1024]{2,1,0:T(8,128)(2,1)S(1)}, bf16[1,128,1024]{2,1,0:...) custom-call(bf16[1,128,1024]{2,1,0:T(8,128)(2,1)} %refs_0_.3, ...), custom_call_target="tpu_custom_call" | custom-call | tf_op jit(solution)/shard_map/pallas_call | solution.py:34
  6.9 4.4 %collective-permute-start.5 = (bf16[144,256]{1,0:T(8,128)(2,1)S(1)}, bf16[144,256]{1,0:T(8,128)(2,1)S(1)}, u32[]{:S(2)}, u32[]{:S(2)}) collective-permute-start(bf16[144,256]{1,0:T(8,128)(2,1)S(1)} %get-tuple-element.53), channel_id=1, source_target_pairs={{0,4},{1,5},{2,6},{3,7},{4,0},{5,1},{6,2},{7,3},{8,12},{9,13},{10,... | collective-permute-start | bytes 221192 | tf_op jit(solution)/shard_map/ppermute | solution.py:270
  11.3 2.6 %collective-permute-start.6 = (bf16[144,256]{1,0:T(8,128)(2,1)S(1)}, bf16[144,256]{1,0:T(8,128)(2,1)S(1)}, u32[]{:S(2)}, u32[]{:S(2)}) collective-permute-start(bf16[144,256]{1,0:T(8,128)(2,1)S(1)} %get-tuple-element.54), channel_id=1, source_target_pairs={{0,8},{1,9},{2,10},{3,11},{4,12},{5,13},{6,14},{7,15},{8,0},{9,1},... | collective-permute-start | bytes 221192 | tf_op jit(solution)/shard_map/ppermute | solution.py:270
  13.9 1.9 %collective-permute-done.refs_5_ = bf16[1040,128]{1,0:T(8,128)(2,1)S(1)} collective-permute-done((bf16[1040,128]{1,0:T(8,128)(2,1)S(1)}, bf16[1040,128]{1,0:T(8,128)(2,1)S(1)}, u32[]{:S(2)}, u32[]{:S(2)}) %collective-permute-start) | collective-permute-done | bytes 266272 | tf_op jit(solution)/shard_map/ppermute | solution.py:270
  15.8 1.4 %shard_map.106 = (bf16[128,1024]{1,0:T(8,128)(2,1)S(1)}, bf16[144,256]{1,0:T(8,128)(2,1)S(1)}, bf16[144,256]{1,0:T(8,128)(2,1)S(1)}, bf16[144,256]{1,0:T(8,128)(2,1)S(1)}, bf16[144,256]{1,0:T(8,128)(2,1)S(1)}) custom-call(bf16[1,128,1024]{2,1,0:T(8,128)(2,1)S(1)} %get-tuple-element.39.refs_0_, bf16[1,128,1024]{2,1,0:T(8,128)(2,1)S(1)} %get-tuple-element.40.refs_1_, ...), custom_call_target="tpu_custom_call" | custom-call | flops 134217728 | bytes 2175488 | tf_op jit(solution)/shard_map/pallas_call | solution.py:34
  17.2 6.3 %collective-permute-start.2 = (bf16[144,256]{1,0:T(8,128)(2,1)S(1)}, bf16[144,256]{1,0:T(8,128)(2,1)S(1)}, u32[]{:S(2)}, u32[]{:S(2)}) collective-permute-start(bf16[144,256]{1,0:T(8,128)(2,1)S(1)} %get-tuple-element.49), channel_id=1, source_target_pairs={{0,8},{1,9},{2,10},{3,11},{4,12},{5,13},{6,14},{7,15},{8,0},{9,1},... | collective-permute-start | bytes 221192 | tf_op jit(solution)/shard_map/ppermute | solution.py:270
  24.6 1.3 %collective-permute-start.8 = (bf16[144,1024]{1,0:T(8,128)(2,1)S(1)}, bf16[144,1024]{1,0:T(8,128)(2,1)S(1)}, u32[]{:S(2)}, u32[]{:S(2)}) collective-permute-start(bf16[144,1024]{1,0:T(8,128)(2,1)S(1)} %shard_map.108.refs_4_), channel_id=1, source_target_pairs={{0,1},{1,0},{2,3},{3,2},{4,5},{5,4},{6,7},{7,6},{8,9},{9,8},{10,11... | collective-permute-start | bytes 884744 | tf_op jit(solution)/shard_map/ppermute | solution.py:270
  26.0 2.1 %collective-permute-done.2.refs_1_ = bf16[144,256]{1,0:T(8,128)(2,1)S(1)} collective-permute-done((bf16[144,256]{1,0:T(8,128)(2,1)S(1)}, bf16[144,256]{1,0:T(8,128)(2,1)S(1)}, u32[]{:S(2)}, u32[]{:S(2)}) %collective-permute-start.2) | collective-permute-done | bytes 73760 | tf_op jit(solution)/shard_map/ppermute | solution.py:270
  28.1 1.5 %collective-permute-done.3.refs_2_ = bf16[144,256]{1,0:T(8,128)(2,1)S(1)} collective-permute-done((bf16[144,256]{1,0:T(8,128)(2,1)S(1)}, bf16[144,256]{1,0:T(8,128)(2,1)S(1)}, u32[]{:S(2)}, u32[]{:S(2)}) %collective-permute-start.3) | collective-permute-done | bytes 73760 | tf_op jit(solution)/shard_map/ppermute | solution.py:270
  29.6 0.8 %collective-permute-start.10 = (bf16[144,1024]{1,0:T(8,128)(2,1)S(1)}, bf16[144,1024]{1,0:T(8,128)(2,1)S(1)}, u32[]{:S(2)}, u32[]{:S(2)}) collective-permute-start(bf16[144,1024]{1,0:T(8,128)(2,1)S(1)} %shard_map.107.refs_0_), channel_id=1, source_target_pairs={{0,1},{1,0},{2,3},{3,2},{4,5},{5,4},{6,7},{7,6},{8,9},{9,8},{10,11... | collective-permute-start | bytes 884744 | tf_op jit(solution)/shard_map/ppermute | solution.py:270
  31.1 2.9 %collective-permute-done.8.refs_3_.refs_1_.refs_5_ = bf16[144,1024]{1,0:T(8,128)(2,1)S(1)} collective-permute-done((bf16[144,1024]{1,0:T(8,128)(2,1)S(1)}, bf16[144,1024]{1,0:T(8,128)(2,1)S(1)}, u32[]{:S(2)}, u32[]{:S(2)}) %collective-permute-start.8) | collective-permute-done | bytes 294944 | tf_op jit(solution)/shard_map/ppermute | solution.py:270
  34.0 1.0 %shard_map.109 = (bf16[144,1024]{1,0:T(8,128)(2,1)S(1)}, bf16[144,1024]{1,0:T(8,128)(2,1)S(1)}) custom-call(bf16[144,1024]{1,0:T(8,128)(2,1)S(1)} %shard_map.107.refs_0_, bf16[1024,1024]{1,0:T(8,128)(2,1)S(1)} %copy-done, bf16[1024,1024]{1,0:T(8,128)(2,1)S(1)} %bitcast.2, bf16[144,1024]{1,0:T(8,128)(2,1)S(1)} %collective-permute-done.8.refs_3_.refs_1_.refs_5_, ...), custom_call_target="tpu_custom_call" | custom-call | flops 603979776 | bytes 5079040 | tf_op jit(solution)/shard_map/pallas_call | solution.py:34
  35.0 2.9 %collective-permute-done.10.refs_0_ = bf16[144,1024]{1,0:T(8,128)(2,1)S(1)} collective-permute-done((bf16[144,1024]{1,0:T(8,128)(2,1)S(1)}, bf16[144,1024]{1,0:T(8,128)(2,1)S(1)}, u32[]{:S(2)}, u32[]{:S(2)}) %collective-permute-start.10) | collective-permute-done | bytes 294944 | tf_op jit(solution)/shard_map/ppermute | solution.py:270
  37.9 1.4 %collective-permute-start.14 = (bf16[128,1024]{1,0:T(8,128)(2,1)S(1)}, bf16[128,1024]{1,0:T(8,128)(2,1)S(1)}, u32[]{:S(2)}, u32[]{:S(2)}) collective-permute-start(bf16[128,1024]{1,0:T(8,128)(2,1)S(1)} %shard_map.112), channel_id=1, source_target_pairs={{0,2},{1,3},{2,0},{3,1},{4,6},{5,7},{6,4},{7,5},{8,10},{9,11},{10,... | collective-permute-start | bytes 786440 | tf_op jit(solution)/shard_map/ppermute | solution.py:270
  39.4 1.7 %collective-permute-start.15 = (bf16[160,1024]{1,0:T(8,128)(2,1)S(1)}, bf16[160,1024]{1,0:T(8,128)(2,1)S(1)}, u32[]{:S(2)}, u32[]{:S(2)}) collective-permute-start(bf16[160,1024]{1,0:T(8,128)(2,1)S(1)} %shard_map.113), channel_id=1, source_target_pairs={{0,1},{1,0},{2,3},{3,2},{4,5},{5,4},{6,7},{7,6},{8,9},{9,8},{10,11... | collective-permute-start | bytes 983048 | tf_op jit(solution)/shard_map/ppermute | solution.py:270
  41.1 1.0 %shard_map.110 = (bf16[144,1024]{1,0:T(8,128)(2,1)S(1)}, bf16[144,1024]{1,0:T(8,128)(2,1)S(1)}) custom-call(bf16[144,1024]{1,0:T(8,128)(2,1)S(1)} %collective-permute-done.10.refs_0_, bf16[1024,1024]{1,0:T(8,128)(2,1)S(1)} %copy-done, bf16[1024,1024]{1,0:T(8,128)(2,1)S(1)} %bitcast.3, bf16[144,1024]{1,0:T(8,128)(2,1)S(1)} %get-tuple-element.57.refs_3_.refs_4_.refs_0_), custom_call_target="tpu_custom_call" | custom-call | flops 603979776 | bytes 5079040 | tf_op jit(solution)/shard_map/pallas_call | solution.py:34
  42.5 1.0 %shard_map.111 = (bf16[144,1024]{1,0:T(8,128)(2,1)S(1)}, bf16[144,1024]{1,0:T(8,128)(2,1)S(1)}) custom-call(bf16[144,1024]{1,0:T(8,128)(2,1)S(1)} %collective-permute-done.12.refs_0_, bf16[1024,1024]{1,0:T(8,128)(2,1)S(1)} %copy-done, bf16[1024,1024]{1,0:T(8,128)(2,1)S(1)} %bitcast.4, bf16[144,1024]{1,0:T(8,128)(2,1)S(1)} %get-tuple-element.57.refs_3_.refs_4_.refs_0_), custom_call_target="tpu_custom_call" | custom-call | flops 603979776 | bytes 5079040 | tf_op jit(solution)/shard_map/pallas_call | solution.py:34
  43.5 0.7 %collective-permute-start.13 = (bf16[144,1024]{1,0:T(8,128)(2,1)S(1)}, bf16[144,1024]{1,0:T(8,128)(2,1)S(1)}, u32[]{:S(2)}, u32[]{:S(2)}) collective-permute-start(bf16[144,1024]{1,0:T(8,128)(2,1)S(1)} %get-tuple-element.59), channel_id=1, source_target_pairs={{0,2},{1,3},{2,0},{3,1},{4,6},{5,7},{6,4},{7,5},{8,10},{9,11},{10,... | collective-permute-start | bytes 884744 | tf_op jit(solution)/shard_map/ppermute | solution.py:270
  44.2 2.0 %collective-permute-done.14.refs_0_.refs_7_ = bf16[128,1024]{1,0:T(8,128)(2,1)S(1)} collective-permute-done((bf16[128,1024]{1,0:T(8,128)(2,1)S(1)}, bf16[128,1024]{1,0:T(8,128)(2,1)S(1)}, u32[]{:S(2)}, u32[]{:S(2)}) %collective-permute-start.14) | collective-permute-done | bytes 262176 | tf_op jit(solution)/shard_map/ppermute | solution.py:270
  46.2 3.8 %collective-permute-done.15.refs_1_.refs_8_ = bf16[160,1024]{1,0:T(8,128)(2,1)S(1)} collective-permute-done((bf16[160,1024]{1,0:T(8,128)(2,1)S(1)}, bf16[160,1024]{1,0:T(8,128)(2,1)S(1)}, u32[]{:S(2)}, u32[]{:S(2)}) %collective-permute-start.15) | collective-permute-done | bytes 327712 | tf_op jit(solution)/shard_map/ppermute | solution.py:270
  50.1 1.0 %shard_map.114 = (bf16[144,1024]{1,0:T(8,128)(2,1)S(1)}, bf16[144,1024]{1,0:T(8,128)(2,1)S(1)}) custom-call(bf16[128,1024]{1,0:T(8,128)(2,1)S(1)} %collective-permute-done.14.refs_0_.refs_7_, bf16[160,1024]{1,0:T(8,128)(2,1)S(1)} %collective-permute-done.15.refs_1_.refs_8_, bf16[1024,1024]{1,0:T(8,128)(2,1)S(1)} %copy-done, bf16[1024,1024]{1,0:T(8,128)(2,1)S(1)} %bitcast.5, ...), custom_call_target="tpu_custom_call" | custom-call | flops 603979776 | bytes 5373952 | tf_op jit(solution)/shard_map/pallas_call | solution.py:34
  51.1 1.5 %collective-permute-start.16 = (bf16[144,1024]{1,0:T(8,128)(2,1)S(1)}, bf16[144,1024]{1,0:T(8,128)(2,1)S(1)}, u32[]{:S(2)}, u32[]{:S(2)}) collective-permute-start(bf16[144,1024]{1,0:T(8,128)(2,1)S(1)} %get-tuple-element.60), channel_id=1, source_target_pairs={{0,3},{1,2},{2,1},{3,0},{4,7},{5,6},{6,5},{7,4},{8,11},{9,10},{10,... | collective-permute-start | bytes 884744 | tf_op jit(solution)/shard_map/ppermute | solution.py:270
  52.6 2.9 %collective-permute-done.11.refs_1_.refs_9_ = bf16[144,1024]{1,0:T(8,128)(2,1)S(1)} collective-permute-done((bf16[144,1024]{1,0:T(8,128)(2,1)S(1)}, bf16[144,1024]{1,0:T(8,128)(2,1)S(1)}, u32[]{:S(2)}, u32[]{:S(2)}) %collective-permute-start.11) | collective-permute-done | bytes 294944 | tf_op jit(solution)/shard_map/ppermute | solution.py:270
  55.5 1.0 %shard_map.116 = (bf16[128,1024]{1,0:T(8,128)(2,1)S(1)}, bf16[128,1024]{1,0:T(8,128)(2,1)S(1)}, bf16[128,1024]{1,0:T(8,128)(2,1)S(1)}, bf16[128,1024]{1,0:T(8,128)(2,1)S(1)}) custom-call(bf16[144,1024]{1,0:T(8,128)(2,1)S(1)} %get-tuple-element.57.refs_3_.refs_4_.refs_0_, bf16[144,1024]{1,0:T(8,128)(2,1)S(1)} %get-tuple-element.65.refs_1_, ...), custom_call_target="tpu_custom_call" | custom-call | flops 603979776 | bytes 3702784 | tf_op jit(solution)/shard_map/pallas_call | solution.py:34
  57.6 1.7 %collective-permute-done.16.refs_3_ = bf16[144,1024]{1,0:T(8,128)(2,1)S(1)} collective-permute-done((bf16[144,1024]{1,0:T(8,128)(2,1)S(1)}, bf16[144,1024]{1,0:T(8,128)(2,1)S(1)}, u32[]{:S(2)}, u32[]{:S(2)}) %collective-permute-start.16) | collective-permute-done | bytes 294944 | tf_op jit(solution)/shard_map/ppermute | solution.py:270
  59.5 2.5 %collective-permute-start.17 = (bf16[144,256]{1,0:T(8,128)(2,1)S(1)}, bf16[144,256]{1,0:T(8,128)(2,1)S(1)}, u32[]{:S(2)}, u32[]{:S(2)}) collective-permute-start(bf16[144,256]{1,0:T(8,128)(2,1)S(1)} %get-tuple-element.62), channel_id=1, source_target_pairs={{0,12},{1,13},{2,14},{3,15},{4,8},{5,9},{6,10},{7,11},{8,4},{9,5},... | collective-permute-start | bytes 221192 | tf_op jit(solution)/shard_map/ppermute | solution.py:270
  62.0 1.6 %collective-permute-start.18 = (bf16[144,256]{1,0:T(8,128)(2,1)S(1)}, bf16[144,256]{1,0:T(8,128)(2,1)S(1)}, u32[]{:S(2)}, u32[]{:S(2)}) collective-permute-start(bf16[144,256]{1,0:T(8,128)(2,1)S(1)} %get-tuple-element.63), channel_id=1, source_target_pairs={{0,8},{1,9},{2,10},{3,11},{4,12},{5,13},{6,14},{7,15},{8,0},{9,1},... | collective-permute-start | bytes 221192 | tf_op jit(solution)/shard_map/ppermute | solution.py:270
  64.1 2.0 %shard_map.117 = (bf16[1,512,1024]{2,1,0:T(8,128)(2,1)}, f32[8,128]{1,0:T(8,128)S(1)}) custom-call(bf16[144,1024]{1,0:T(8,128)(2,1)S(1)} %get-tuple-element.57.refs_3_.refs_4_.refs_0_, bf16[144,1024]{1,0:T(8,128)(2,1)S(1)} %get-tuple-element.65.refs_1_, bf16[144,1024]{1,0:T(8,128)(2,1)S(1)} %get-tuple-element.66.refs_2_, ...), custom_call_target="tpu_custom_call" | custom-call | flops 603979776 | bytes 4755456 | tf_op jit(solution)/shard_map/pallas_call | solution.py:34
  66.6 2.3 %collective-permute-done.18.refs_4_ = bf16[144,256]{1,0:T(8,128)(2,1)S(1)} collective-permute-done((bf16[144,256]{1,0:T(8,128)(2,1)S(1)}, bf16[144,256]{1,0:T(8,128)(2,1)S(1)}, u32[]{:S(2)}, u32[]{:S(2)}) %collective-permute-start.18) | collective-permute-done | bytes 73760 | tf_op jit(solution)/shard_map/ppermute | solution.py:270
  68.8 0.9 %shard_map.118 = bf16[1,128,1024]{2,1,0:T(8,128)(2,1)} custom-call(bf16[128,1024]{1,0:T(8,128)(2,1)S(1)} %get-tuple-element.46.refs_4_.refs_0_, bf16[128,144]{1,0:T(8,128)(2,1)S(1)} %get-tuple-element.47.refs_1_, bf16[144,256]{1,0:T(8,128)(2,1)S(1)} %get-tuple-element.61.refs_2_, bf16[144,256]{1,0:T(8,128)(2,1)S(1)} %collective-permute-done.17.refs_3_, ...), custom_call_target="tpu_custom_call" | custom-call | bytes 856064 | tf_op jit(solution)/shard_map/pallas_call | solution.py:34
  (35 shorter events, 5.2 us)
Async XLA Ops:
  0.6 33.4 %copy-start.1 = (bf16[1,1024,1024]{2,1,0:T(8,128)(2,1)S(1)}, bf16[1,1024,1024]{2,1,0:T(8,128)(2,1)}, u32[]{:S(2)}) copy-start(bf16[1,1024,1024]{2,1,0:T(8,128)(2,1)} %param.17) | copy-start | bytes 6291460
  2.0 32.0 %copy-start = (bf16[1024,1024]{1,0:T(8,128)(2,1)S(1)}, bf16[1024,1024]{1,0:T(8,128)(2,1)}, u32[]{:S(2)}) copy-start(bf16[1024,1024]{1,0:T(8,128)(2,1)} %refs_2_.5) | copy-start | bytes 6291460
  2.0 13.8 %collective-permute-start = (bf16[1040,128]{1,0:T(8,128)(2,1)S(1)}, bf16[1040,128]{1,0:T(8,128)(2,1)S(1)}, u32[]{:S(2)}, u32[]{:S(2)}) collective-permute-start(bf16[1040,128]{1,0:T(8,128)(2,1)S(1)} %get-tuple-element.43), channel_id=1, source_target_pairs={{0,1},{1,0},{2,3},{3,2},{4,5},{5,4},{6,7},{7,6},{8,9},{9,8},{10,11... | collective-permute-start | bytes 798728 | tf_op jit(solution)/shard_map/ppermute | solution.py:270
  5.0 10.8 %collective-permute-start.1 = (bf16[1040,128]{1,0:T(8,128)(2,1)S(1)}, bf16[1040,128]{1,0:T(8,128)(2,1)S(1)}, u32[]{:S(2)}, u32[]{:S(2)}) collective-permute-start(bf16[1040,128]{1,0:T(8,128)(2,1)S(1)} %get-tuple-element.44), channel_id=1, source_target_pairs={{1,2},{3,4},{5,6},{7,8},{9,10},{11,12},{13,14},{2,1},{4,3},{6,5},{... | collective-permute-start | bytes 798728 | tf_op jit(solution)/shard_map/ppermute | solution.py:314
  6.9 16.5 %collective-permute-start.5 = (bf16[144,256]{1,0:T(8,128)(2,1)S(1)}, bf16[144,256]{1,0:T(8,128)(2,1)S(1)}, u32[]{:S(2)}, u32[]{:S(2)}) collective-permute-start(bf16[144,256]{1,0:T(8,128)(2,1)S(1)} %get-tuple-element.53), channel_id=1, source_target_pairs={{0,4},{1,5},{2,6},{3,7},{4,0},{5,1},{6,2},{7,3},{8,12},{9,13},{10,... | collective-permute-start | bytes 221192 | tf_op jit(solution)/shard_map/ppermute | solution.py:270
  11.3 12.8 %collective-permute-start.6 = (bf16[144,256]{1,0:T(8,128)(2,1)S(1)}, bf16[144,256]{1,0:T(8,128)(2,1)S(1)}, u32[]{:S(2)}, u32[]{:S(2)}) collective-permute-start(bf16[144,256]{1,0:T(8,128)(2,1)S(1)} %get-tuple-element.54), channel_id=1, source_target_pairs={{0,8},{1,9},{2,10},{3,11},{4,12},{5,13},{6,14},{7,15},{8,0},{9,1},... | collective-permute-start | bytes 221192 | tf_op jit(solution)/shard_map/ppermute | solution.py:270
  13.9 10.2 %collective-permute-start.7 = (bf16[144,256]{1,0:T(8,128)(2,1)S(1)}, bf16[144,256]{1,0:T(8,128)(2,1)S(1)}, u32[]{:S(2)}, u32[]{:S(2)}) collective-permute-start(bf16[144,256]{1,0:T(8,128)(2,1)S(1)} %get-tuple-element.55), channel_id=1, source_target_pairs={{0,12},{1,13},{2,14},{3,15},{4,8},{5,9},{6,10},{7,11},{8,4},{9,5},... | collective-permute-start | bytes 221192 | tf_op jit(solution)/shard_map/ppermute | solution.py:270
  17.2 10.9 %collective-permute-start.2 = (bf16[144,256]{1,0:T(8,128)(2,1)S(1)}, bf16[144,256]{1,0:T(8,128)(2,1)S(1)}, u32[]{:S(2)}, u32[]{:S(2)}) collective-permute-start(bf16[144,256]{1,0:T(8,128)(2,1)S(1)} %get-tuple-element.49), channel_id=1, source_target_pairs={{0,8},{1,9},{2,10},{3,11},{4,12},{5,13},{6,14},{7,15},{8,0},{9,1},... | collective-permute-start | bytes 221192 | tf_op jit(solution)/shard_map/ppermute | solution.py:270
  23.4 6.2 %collective-permute-start.3 = (bf16[144,256]{1,0:T(8,128)(2,1)S(1)}, bf16[144,256]{1,0:T(8,128)(2,1)S(1)}, u32[]{:S(2)}, u32[]{:S(2)}) collective-permute-start(bf16[144,256]{1,0:T(8,128)(2,1)S(1)} %get-tuple-element.50), channel_id=1, source_target_pairs={{0,12},{1,13},{2,14},{3,15},{4,8},{5,9},{6,10},{7,11},{8,4},{9,5},... | collective-permute-start | bytes 221192 | tf_op jit(solution)/shard_map/ppermute | solution.py:270
  23.4 6.1 %collective-permute-start.4 = (bf16[144,256]{1,0:T(8,128)(2,1)S(1)}, bf16[144,256]{1,0:T(8,128)(2,1)S(1)}, u32[]{:S(2)}, u32[]{:S(2)}) collective-permute-start(bf16[144,256]{1,0:T(8,128)(2,1)S(1)} %get-tuple-element.51), channel_id=1, source_target_pairs={{0,4},{1,5},{2,6},{3,7},{4,0},{5,1},{6,2},{7,3},{8,12},{9,13},{10,... | collective-permute-start | bytes 221192 | tf_op jit(solution)/shard_map/ppermute | solution.py:270
  24.1 7.0 %collective-permute-start.9 = (bf16[144,1024]{1,0:T(8,128)(2,1)S(1)}, bf16[144,1024]{1,0:T(8,128)(2,1)S(1)}, u32[]{:S(2)}, u32[]{:S(2)}) collective-permute-start(bf16[144,1024]{1,0:T(8,128)(2,1)S(1)} %shard_map.108.refs_4_), channel_id=1, source_target_pairs={{0,2},{1,3},{2,0},{3,1},{4,6},{5,7},{6,4},{7,5},{8,10},{9,11},{10,... | collective-permute-start | bytes 884744 | tf_op jit(solution)/shard_map/ppermute | solution.py:270
  24.6 9.4 %collective-permute-start.8 = (bf16[144,1024]{1,0:T(8,128)(2,1)S(1)}, bf16[144,1024]{1,0:T(8,128)(2,1)S(1)}, u32[]{:S(2)}, u32[]{:S(2)}) collective-permute-start(bf16[144,1024]{1,0:T(8,128)(2,1)S(1)} %shard_map.108.refs_4_), channel_id=1, source_target_pairs={{0,1},{1,0},{2,3},{3,2},{4,5},{5,4},{6,7},{7,6},{8,9},{9,8},{10,11... | collective-permute-start | bytes 884744 | tf_op jit(solution)/shard_map/ppermute | solution.py:270
  29.6 8.3 %collective-permute-start.10 = (bf16[144,1024]{1,0:T(8,128)(2,1)S(1)}, bf16[144,1024]{1,0:T(8,128)(2,1)S(1)}, u32[]{:S(2)}, u32[]{:S(2)}) collective-permute-start(bf16[144,1024]{1,0:T(8,128)(2,1)S(1)} %shard_map.107.refs_0_), channel_id=1, source_target_pairs={{0,1},{1,0},{2,3},{3,2},{4,5},{5,4},{6,7},{7,6},{8,9},{9,8},{10,11... | collective-permute-start | bytes 884744 | tf_op jit(solution)/shard_map/ppermute | solution.py:270
  30.4 8.9 %collective-permute-start.12 = (bf16[144,1024]{1,0:T(8,128)(2,1)S(1)}, bf16[144,1024]{1,0:T(8,128)(2,1)S(1)}, u32[]{:S(2)}, u32[]{:S(2)}) collective-permute-start(bf16[144,1024]{1,0:T(8,128)(2,1)S(1)} %shard_map.107.refs_0_), channel_id=1, source_target_pairs={{0,2},{1,3},{2,0},{3,1},{4,6},{5,7},{6,4},{7,5},{8,10},{9,11},{10,... | collective-permute-start | bytes 884744 | tf_op jit(solution)/shard_map/ppermute | solution.py:270
  37.9 8.3 %collective-permute-start.14 = (bf16[128,1024]{1,0:T(8,128)(2,1)S(1)}, bf16[128,1024]{1,0:T(8,128)(2,1)S(1)}, u32[]{:S(2)}, u32[]{:S(2)}) collective-permute-start(bf16[128,1024]{1,0:T(8,128)(2,1)S(1)} %shard_map.112), channel_id=1, source_target_pairs={{0,2},{1,3},{2,0},{3,1},{4,6},{5,7},{6,4},{7,5},{8,10},{9,11},{10,... | collective-permute-start | bytes 786440 | tf_op jit(solution)/shard_map/ppermute | solution.py:270
  39.4 10.7 %collective-permute-start.15 = (bf16[160,1024]{1,0:T(8,128)(2,1)S(1)}, bf16[160,1024]{1,0:T(8,128)(2,1)S(1)}, u32[]{:S(2)}, u32[]{:S(2)}) collective-permute-start(bf16[160,1024]{1,0:T(8,128)(2,1)S(1)} %shard_map.113), channel_id=1, source_target_pairs={{0,1},{1,0},{2,3},{3,2},{4,5},{5,4},{6,7},{7,6},{8,9},{9,8},{10,11... | collective-permute-start | bytes 983048 | tf_op jit(solution)/shard_map/ppermute | solution.py:270
  42.1 13.3 %collective-permute-start.11 = (bf16[144,1024]{1,0:T(8,128)(2,1)S(1)}, bf16[144,1024]{1,0:T(8,128)(2,1)S(1)}, u32[]{:S(2)}, u32[]{:S(2)}) collective-permute-start(bf16[144,1024]{1,0:T(8,128)(2,1)S(1)} %get-tuple-element.58), channel_id=1, source_target_pairs={{0,1},{1,0},{2,3},{3,2},{4,5},{5,4},{6,7},{7,6},{8,9},{9,8},{10,11... | collective-permute-start | bytes 884744 | tf_op jit(solution)/shard_map/ppermute | solution.py:270
  43.5 12.0 %collective-permute-start.13 = (bf16[144,1024]{1,0:T(8,128)(2,1)S(1)}, bf16[144,1024]{1,0:T(8,128)(2,1)S(1)}, u32[]{:S(2)}, u32[]{:S(2)}) collective-permute-start(bf16[144,1024]{1,0:T(8,128)(2,1)S(1)} %get-tuple-element.59), channel_id=1, source_target_pairs={{0,2},{1,3},{2,0},{3,1},{4,6},{5,7},{6,4},{7,5},{8,10},{9,11},{10,... | collective-permute-start | bytes 884744 | tf_op jit(solution)/shard_map/ppermute | solution.py:270
  51.1 8.2 %collective-permute-start.16 = (bf16[144,1024]{1,0:T(8,128)(2,1)S(1)}, bf16[144,1024]{1,0:T(8,128)(2,1)S(1)}, u32[]{:S(2)}, u32[]{:S(2)}) collective-permute-start(bf16[144,1024]{1,0:T(8,128)(2,1)S(1)} %get-tuple-element.60), channel_id=1, source_target_pairs={{0,3},{1,2},{2,1},{3,0},{4,7},{5,6},{6,5},{7,4},{8,11},{9,10},{10,... | collective-permute-start | bytes 884744 | tf_op jit(solution)/shard_map/ppermute | solution.py:270
  56.5 5.5 %collective-permute-start.20 = (bf16[128,1024]{1,0:T(8,128)(2,1)S(1)}, bf16[128,1024]{1,0:T(8,128)(2,1)S(1)}, u32[]{:S(2)}, u32[]{:S(2)}) collective-permute-start(bf16[128,1024]{1,0:T(8,128)(2,1)S(1)} %get-tuple-element.68), channel_id=1, source_target_pairs={{0,16},{16,0},{1,17},{17,1},{2,18},{18,2},{3,19},{19,3},{4,20},{20... | collective-permute-start | bytes 786440 | tf_op jit(solution)/shard_map/ppermute | solution.py:375
  56.6 7.0 %collective-permute-start.21 = (bf16[128,1024]{1,0:T(8,128)(2,1)S(1)}, bf16[128,1024]{1,0:T(8,128)(2,1)S(1)}, u32[]{:S(2)}, u32[]{:S(2)}) collective-permute-start(bf16[128,1024]{1,0:T(8,128)(2,1)S(1)} %get-tuple-element.69), channel_id=1, source_target_pairs={{0,16},{16,0},{1,17},{17,1},{2,18},{18,2},{3,19},{19,3},{4,20},{20... | collective-permute-start | bytes 786440 | tf_op jit(solution)/shard_map/ppermute | solution.py:375
  57.1 7.0 %collective-permute-start.22 = (bf16[128,1024]{1,0:T(8,128)(2,1)S(1)}, bf16[128,1024]{1,0:T(8,128)(2,1)S(1)}, u32[]{:S(2)}, u32[]{:S(2)}) collective-permute-start(bf16[128,1024]{1,0:T(8,128)(2,1)S(1)} %get-tuple-element.70), channel_id=1, source_target_pairs={{0,16},{16,0},{1,17},{17,1},{2,18},{18,2},{3,19},{19,3},{4,20},{20... | collective-permute-start | bytes 786440 | tf_op jit(solution)/shard_map/ppermute | solution.py:375
  57.1 7.0 %collective-permute-start.23 = (bf16[128,1024]{1,0:T(8,128)(2,1)S(1)}, bf16[128,1024]{1,0:T(8,128)(2,1)S(1)}, u32[]{:S(2)}, u32[]{:S(2)}) collective-permute-start(bf16[128,1024]{1,0:T(8,128)(2,1)S(1)} %get-tuple-element.71), channel_id=1, source_target_pairs={{0,16},{16,0},{1,17},{17,1},{2,18},{18,2},{3,19},{19,3},{4,20},{20... | collective-permute-start | bytes 786440 | tf_op jit(solution)/shard_map/ppermute | solution.py:375
  59.5 7.1 %collective-permute-start.17 = (bf16[144,256]{1,0:T(8,128)(2,1)S(1)}, bf16[144,256]{1,0:T(8,128)(2,1)S(1)}, u32[]{:S(2)}, u32[]{:S(2)}) collective-permute-start(bf16[144,256]{1,0:T(8,128)(2,1)S(1)} %get-tuple-element.62), channel_id=1, source_target_pairs={{0,12},{1,13},{2,14},{3,15},{4,8},{5,9},{6,10},{7,11},{8,4},{9,5},... | collective-permute-start | bytes 221192 | tf_op jit(solution)/shard_map/ppermute | solution.py:270
  62.0 6.9 %collective-permute-start.18 = (bf16[144,256]{1,0:T(8,128)(2,1)S(1)}, bf16[144,256]{1,0:T(8,128)(2,1)S(1)}, u32[]{:S(2)}, u32[]{:S(2)}) collective-permute-start(bf16[144,256]{1,0:T(8,128)(2,1)S(1)} %get-tuple-element.63), channel_id=1, source_target_pairs={{0,8},{1,9},{2,10},{3,11},{4,12},{5,13},{6,14},{7,15},{8,0},{9,1},... | collective-permute-start | bytes 221192 | tf_op jit(solution)/shard_map/ppermute | solution.py:270
  63.5 5.3 %collective-permute-start.19 = (bf16[144,256]{1,0:T(8,128)(2,1)S(1)}, bf16[144,256]{1,0:T(8,128)(2,1)S(1)}, u32[]{:S(2)}, u32[]{:S(2)}) collective-permute-start(bf16[144,256]{1,0:T(8,128)(2,1)S(1)} %get-tuple-element.64), channel_id=1, source_target_pairs={{0,4},{1,5},{2,6},{3,7},{4,0},{5,1},{6,2},{7,3},{8,12},{9,13},{10,... | collective-permute-start | bytes 221192 | tf_op jit(solution)/shard_map/ppermute | solution.py:270

commit v7 on v6

--- a/solution.py
+++ b/solution.py
@@ -143,11 +143,10 @@
         c.wait()
 
 
-def gather_body(order, pitch, *refs):
+def gather_body(pitch, *refs):
     *message_refs, rows_ref = refs
     width = message_refs[0].shape[1]
-    ordered = [message_refs[order.index(k)] for k in range(len(order))]
-    for j, column in enumerate(from_messages(ordered, pitch, rows_ref.shape[0])):
+    for j, column in enumerate(from_messages(message_refs, pitch, rows_ref.shape[0])):
         rows_ref[:, j * width : (j + 1) * width] = column
 
 
@@ -281,6 +280,11 @@
     return permute(both, apart)
 
 
+def of_other_core(value):
+    size = lax.axis_size("grp")
+    return lax.ppermute(value[:16, :128], "grp", [(i, i ^ 1) for i in range(size)])
+
+
 def along_line(messages):
     return [m if k == 0 else permute(m, SPLIT * k) for k, m in enumerate(messages)]
 
@@ -333,20 +337,14 @@
     )
 
     (cot_rows,) = call(
-        functools.partial(gather_body, range(experts), pitch),
+        functools.partial(gather_body, pitch),
         [out(plane_rows, features)],
         vmem=cot_got,
         after=(mixed,),
         size=0,
     )
     cot_x, cot_y = permute(cot_rows, 1), permute(cot_rows, 2)
-    mixed_got = along_line(sent)
-    order = [0, *range(2, experts), 1]
-    (rows,) = call(
-        functools.partial(gather_body, order, pitch),
-        [out(plane_rows, features)],
-        vmem=[mixed_got[k] for k in order],
-    )
+    (rows,) = call(functools.partial(gather_body, pitch), [out(plane_rows, features)], vmem=along_line(sent))
 
     row_x, row_y = permute(rows, 1), permute(rows, 2)
     part = plane_rows // 32 * 16
@@ -357,7 +355,7 @@
             expert_body,
             [out(plane_rows, hidden_units), out(plane_rows, features)],
             vmem=(*pieces, in_here, out_here),
-            after=(*first, *hiddens[:1]),
+            after=(*first, *hiddens[:1], *[of_other_core(h) for h in hiddens[2:]]),
             flops=4 * plane_rows * features * hidden_units,
         )
         hiddens.append(hidden)

time: 69.9 us -> 69 us (0.987)
  waiting for transfers between devices: 24.5 us -> 23.2 us
    ppermute x19, waiting for transfers between devices: 24.5 us -> 22.1 us  [permute(): lax.ppermute(value, 'ep', [(i, i ^ apart) for i in range(lax.axis_size('e...]
    ppermute x0 -> x1, waiting for transfers between devices: none -> 1.15 us  [of_other_core(): lax.ppermute(value[:16, :128], 'grp', [(i, i ^ 1) for i in range(size)])]
  transfers between devices with their start and end apart: 24 -> 25, of which waited for: 11 -> 12; matrix products, arithmetic and copies ran while one was open for 0% -> 0% of each run, Pallas kernels for 14% -> 14%
where the time goes in v7:
time: 69 us; the launch traced here: 68.8 us
  starting transfers between devices  32.6 us (47%)
  waiting for transfers between devices  23.2 us (34%)
  Pallas kernels  12.1 us (18%)
  between operations  0.79 us (1%)
    ppermute x19, starting transfers between devices, permute(): lax.ppermute(value, 'ep', [(i, i ^ apart) for i in range(lax.axis_size('e...  30.9 us
    ppermute x19, waiting for transfers between devices, permute(): lax.ppermute(value, 'ep', [(i, i ^ apart) for i in range(lax.axis_size('e...  22.1 us
    pallas_call x15, Pallas kernels, call(): pl.pallas_call(kernel, out_shape=outs, in_specs=[VMEM] * len(vmem) + [HBM...  12.1 us
  transfers between devices with their start and end apart: 25, of which 12 were waited for; matrix products, arithmetic and copies ran while one was open for 0% of the time, Pallas kernels for 14%

profile of v7, /device:TPU:0, one launch (start us, length us, event | category | flops | bytes accessed | tf_op | source)
XLA Modules:
  0.0 68.8 jit_solution(6128253313948729212)
XLA Ops:
  0.6 1.3 %shard_map.104 = (bf16[1040,128]{1,0:T(8,128)(2,1)S(1)}, bf16[1040,128]{1,0:T(8,128)(2,1)S(1)}, bf16[1,128,1024]{2,1,0:T(8,128)(2,1)S(1)}, bf16[1,128,1024]{2,1,0:T(8,128)(2,1)S(1)}, s32[1,128]{1,0:T(1,128)S(1)}) custom-call(bf16[1,128,1024]{2,1,0:T(8,128)(2,1)} %refs_0_.2, bf16[1,128,1024]{2,1,0:T(8,128)(2,1)} %refs_1_.4, s32[1,128]{1,0:T(1,128)} %refs_2_.3), custom_call_target="tpu_custom_call" | custom-call | bytes 1582080 | tf_op jit(solution)/shard_map/pallas_call | solution.py:34
  2.0 3.0 %collective-permute-start = (bf16[1040,128]{1,0:T(8,128)(2,1)S(1)}, bf16[1040,128]{1,0:T(8,128)(2,1)S(1)}, u32[]{:S(2)}, u32[]{:S(2)}) collective-permute-start(bf16[1040,128]{1,0:T(8,128)(2,1)S(1)} %get-tuple-element.43), channel_id=1, source_target_pairs={{0,1},{1,0},{2,3},{3,2},{4,5},{5,4},{6,7},{7,6},{8,9},{9,8},{10,11... | collective-permute-start | bytes 798728 | tf_op jit(solution)/shard_map/ppermute | solution.py:269
  5.7 1.2 %shard_map.105 = (bf16[144,128]{1,0:T(8,128)(2,1)S(1)}, bf16[128,144]{1,0:T(8,128)(2,1)S(1)}, bf16[1,128,1024]{2,1,0:T(8,128)(2,1)S(1)}, bf16[1,128,1024]{2,1,0:...) custom-call(bf16[1,128,1024]{2,1,0:T(8,128)(2,1)} %refs_0_.3, ...), custom_call_target="tpu_custom_call" | custom-call | tf_op jit(solution)/shard_map/pallas_call | solution.py:34
  6.9 4.4 %collective-permute-start.5 = (bf16[144,256]{1,0:T(8,128)(2,1)S(1)}, bf16[144,256]{1,0:T(8,128)(2,1)S(1)}, u32[]{:S(2)}, u32[]{:S(2)}) collective-permute-start(bf16[144,256]{1,0:T(8,128)(2,1)S(1)} %get-tuple-element.53), channel_id=1, source_target_pairs={{0,4},{1,5},{2,6},{3,7},{4,0},{5,1},{6,2},{7,3},{8,12},{9,13},{10,... | collective-permute-start | bytes 221192 | tf_op jit(solution)/shard_map/ppermute | solution.py:269
  11.3 2.6 %collective-permute-start.6 = (bf16[144,256]{1,0:T(8,128)(2,1)S(1)}, bf16[144,256]{1,0:T(8,128)(2,1)S(1)}, u32[]{:S(2)}, u32[]{:S(2)}) collective-permute-start(bf16[144,256]{1,0:T(8,128)(2,1)S(1)} %get-tuple-element.54), channel_id=1, source_target_pairs={{0,8},{1,9},{2,10},{3,11},{4,12},{5,13},{6,14},{7,15},{8,0},{9,1},... | collective-permute-start | bytes 221192 | tf_op jit(solution)/shard_map/ppermute | solution.py:269
  13.9 1.9 %collective-permute-done.refs_5_ = bf16[1040,128]{1,0:T(8,128)(2,1)S(1)} collective-permute-done((bf16[1040,128]{1,0:T(8,128)(2,1)S(1)}, bf16[1040,128]{1,0:T(8,128)(2,1)S(1)}, u32[]{:S(2)}, u32[]{:S(2)}) %collective-permute-start) | collective-permute-done | bytes 266272 | tf_op jit(solution)/shard_map/ppermute | solution.py:269
  15.8 1.4 %shard_map.106 = (bf16[128,1024]{1,0:T(8,128)(2,1)S(1)}, bf16[144,256]{1,0:T(8,128)(2,1)S(1)}, bf16[144,256]{1,0:T(8,128)(2,1)S(1)}, bf16[144,256]{1,0:T(8,128)(2,1)S(1)}, bf16[144,256]{1,0:T(8,128)(2,1)S(1)}) custom-call(bf16[1,128,1024]{2,1,0:T(8,128)(2,1)S(1)} %get-tuple-element.39.refs_0_, bf16[1,128,1024]{2,1,0:T(8,128)(2,1)S(1)} %get-tuple-element.40.refs_1_, ...), custom_call_target="tpu_custom_call" | custom-call | flops 134217728 | bytes 2175488 | tf_op jit(solution)/shard_map/pallas_call | solution.py:34
  17.2 3.9 %collective-permute-start.2 = (bf16[144,256]{1,0:T(8,128)(2,1)S(1)}, bf16[144,256]{1,0:T(8,128)(2,1)S(1)}, u32[]{:S(2)}, u32[]{:S(2)}) collective-permute-start(bf16[144,256]{1,0:T(8,128)(2,1)S(1)} %get-tuple-element.49), channel_id=1, source_target_pairs={{0,4},{1,5},{2,6},{3,7},{4,0},{5,1},{6,2},{7,3},{8,12},{9,13},{10,... | collective-permute-start | bytes 221192 | tf_op jit(solution)/shard_map/ppermute | solution.py:269
  21.0 2.8 %collective-permute-start.3 = (bf16[144,256]{1,0:T(8,128)(2,1)S(1)}, bf16[144,256]{1,0:T(8,128)(2,1)S(1)}, u32[]{:S(2)}, u32[]{:S(2)}) collective-permute-start(bf16[144,256]{1,0:T(8,128)(2,1)S(1)} %get-tuple-element.50), channel_id=1, source_target_pairs={{0,8},{1,9},{2,10},{3,11},{4,12},{5,13},{6,14},{7,15},{8,0},{9,1},... | collective-permute-start | bytes 221192 | tf_op jit(solution)/shard_map/ppermute | solution.py:269
  23.8 1.0 %collective-permute-start.4 = (bf16[144,256]{1,0:T(8,128)(2,1)S(1)}, bf16[144,256]{1,0:T(8,128)(2,1)S(1)}, u32[]{:S(2)}, u32[]{:S(2)}) collective-permute-start(bf16[144,256]{1,0:T(8,128)(2,1)S(1)} %get-tuple-element.51), channel_id=1, source_target_pairs={{0,12},{1,13},{2,14},{3,15},{4,8},{5,9},{6,10},{7,11},{8,4},{9,5},... | collective-permute-start | bytes 221192 | tf_op jit(solution)/shard_map/ppermute | solution.py:269
  25.0 1.3 %collective-permute-start.8 = (bf16[144,1024]{1,0:T(8,128)(2,1)S(1)}, bf16[144,1024]{1,0:T(8,128)(2,1)S(1)}, u32[]{:S(2)}, u32[]{:S(2)}) collective-permute-start(bf16[144,1024]{1,0:T(8,128)(2,1)S(1)} %shard_map.108.refs_4_), channel_id=1, source_target_pairs={{0,1},{1,0},{2,3},{3,2},{4,5},{5,4},{6,7},{7,6},{8,9},{9,8},{10,11... | collective-permute-start | bytes 884744 | tf_op jit(solution)/shard_map/ppermute | solution.py:269
  27.1 2.9 %collective-permute-done.4.refs_3_ = bf16[144,256]{1,0:T(8,128)(2,1)S(1)} collective-permute-done((bf16[144,256]{1,0:T(8,128)(2,1)S(1)}, bf16[144,256]{1,0:T(8,128)(2,1)S(1)}, u32[]{:S(2)}, u32[]{:S(2)}) %collective-permute-start.4) | collective-permute-done | bytes 73760 | tf_op jit(solution)/shard_map/ppermute | solution.py:269
  30.1 1.6 %collective-permute-start.10 = (bf16[144,1024]{1,0:T(8,128)(2,1)S(1)}, bf16[144,1024]{1,0:T(8,128)(2,1)S(1)}, u32[]{:S(2)}, u32[]{:S(2)}) collective-permute-start(bf16[144,1024]{1,0:T(8,128)(2,1)S(1)} %shard_map.107.refs_0_), channel_id=1, source_target_pairs={{0,1},{1,0},{2,3},{3,2},{4,5},{5,4},{6,7},{7,6},{8,9},{9,8},{10,11... | collective-permute-start | bytes 884744 | tf_op jit(solution)/shard_map/ppermute | solution.py:269
  31.8 1.6 %collective-permute-done.8.refs_3_.refs_1_.refs_5_ = bf16[144,1024]{1,0:T(8,128)(2,1)S(1)} collective-permute-done((bf16[144,1024]{1,0:T(8,128)(2,1)S(1)}, bf16[144,1024]{1,0:T(8,128)(2,1)S(1)}, u32[]{:S(2)}, u32[]{:S(2)}) %collective-permute-start.8) | collective-permute-done | bytes 294944 | tf_op jit(solution)/shard_map/ppermute | solution.py:269
  33.5 1.0 %shard_map.109 = (bf16[144,1024]{1,0:T(8,128)(2,1)S(1)}, bf16[144,1024]{1,0:T(8,128)(2,1)S(1)}) custom-call(bf16[144,1024]{1,0:T(8,128)(2,1)S(1)} %shard_map.107.refs_0_, bf16[1024,1024]{1,0:T(8,128)(2,1)S(1)} %copy-done, bf16[1024,1024]{1,0:T(8,128)(2,1)S(1)} %bitcast.2, bf16[144,1024]{1,0:T(8,128)(2,1)S(1)} %collective-permute-done.8.refs_3_.refs_1_.refs_5_, ...), custom_call_target="tpu_custom_call" | custom-call | flops 603979776 | bytes 5079040 | tf_op jit(solution)/shard_map/pallas_call | solution.py:34
  34.4 3.7 %collective-permute-done.10.refs_0_ = bf16[144,1024]{1,0:T(8,128)(2,1)S(1)} collective-permute-done((bf16[144,1024]{1,0:T(8,128)(2,1)S(1)}, bf16[144,1024]{1,0:T(8,128)(2,1)S(1)}, u32[]{:S(2)}, u32[]{:S(2)}) %collective-permute-start.10) | collective-permute-done | bytes 294944 | tf_op jit(solution)/shard_map/ppermute | solution.py:269
  38.1 2.0 %collective-permute-start.14 = (bf16[128,1024]{1,0:T(8,128)(2,1)S(1)}, bf16[128,1024]{1,0:T(8,128)(2,1)S(1)}, u32[]{:S(2)}, u32[]{:S(2)}) collective-permute-start(bf16[128,1024]{1,0:T(8,128)(2,1)S(1)} %shard_map.112), channel_id=1, source_target_pairs={{0,2},{1,3},{2,0},{3,1},{4,6},{5,7},{6,4},{7,5},{8,10},{9,11},{10,... | collective-permute-start | bytes 786440 | tf_op jit(solution)/shard_map/ppermute | solution.py:269
  41.1 1.0 %shard_map.110 = (bf16[144,1024]{1,0:T(8,128)(2,1)S(1)}, bf16[144,1024]{1,0:T(8,128)(2,1)S(1)}) custom-call(bf16[144,1024]{1,0:T(8,128)(2,1)S(1)} %collective-permute-done.10.refs_0_, bf16[1024,1024]{1,0:T(8,128)(2,1)S(1)} %copy-done, bf16[1024,1024]{1,0:T(8,128)(2,1)S(1)} %bitcast.3, bf16[144,1024]{1,0:T(8,128)(2,1)S(1)} %get-tuple-element.57.refs_3_.refs_4_.refs_0_), custom_call_target="tpu_custom_call" | custom-call | flops 603979776 | bytes 5079040 | tf_op jit(solution)/shard_map/pallas_call | solution.py:34
  42.1 1.2 %collective-permute-start.11 = (bf16[144,1024]{1,0:T(8,128)(2,1)S(1)}, bf16[144,1024]{1,0:T(8,128)(2,1)S(1)}, u32[]{:S(2)}, u32[]{:S(2)}) collective-permute-start(bf16[144,1024]{1,0:T(8,128)(2,1)S(1)} %get-tuple-element.58), channel_id=1, source_target_pairs={{0,1},{1,0},{2,3},{3,2},{4,5},{5,4},{6,7},{7,6},{8,9},{9,8},{10,11... | collective-permute-start | bytes 884744 | tf_op jit(solution)/shard_map/ppermute | solution.py:269
  43.3 1.0 %shard_map.111 = (bf16[144,1024]{1,0:T(8,128)(2,1)S(1)}, bf16[144,1024]{1,0:T(8,128)(2,1)S(1)}) custom-call(bf16[144,1024]{1,0:T(8,128)(2,1)S(1)} %collective-permute-done.12.refs_0_, bf16[1024,1024]{1,0:T(8,128)(2,1)S(1)} %copy-done, bf16[1024,1024]{1,0:T(8,128)(2,1)S(1)} %bitcast.4, bf16[144,1024]{1,0:T(8,128)(2,1)S(1)} %get-tuple-element.57.refs_3_.refs_4_.refs_0_), custom_call_target="tpu_custom_call" | custom-call | flops 603979776 | bytes 5079040 | tf_op jit(solution)/shard_map/pallas_call | solution.py:34
  44.5 1.2 %collective-permute-done.16.refs_5_ = bf16[16,128]{1,0:T(8,128)(2,1)S(1)} collective-permute-done((bf16[16,128]{1,0:T(8,128)(2,1)S(1)}, bf16[16,128]{1,0:T(8,128)(2,1)S(1)}, u32[]{:S(2)}, u32[]{:S(2)}) %collective-permute-start.16) | collective-permute-done | bytes 4128 | tf_op jit(solution)/shard_map/ppermute | solution.py:285
  46.2 3.7 %collective-permute-done.15.refs_1_.refs_8_ = bf16[160,1024]{1,0:T(8,128)(2,1)S(1)} collective-permute-done((bf16[160,1024]{1,0:T(8,128)(2,1)S(1)}, bf16[160,1024]{1,0:T(8,128)(2,1)S(1)}, u32[]{:S(2)}, u32[]{:S(2)}) %collective-permute-start.15) | collective-permute-done | bytes 327712 | tf_op jit(solution)/shard_map/ppermute | solution.py:269
  50.0 1.0 %shard_map.114 = (bf16[144,1024]{1,0:T(8,128)(2,1)S(1)}, bf16[144,1024]{1,0:T(8,128)(2,1)S(1)}) custom-call(bf16[128,1024]{1,0:T(8,128)(2,1)S(1)} %collective-permute-done.14.refs_0_.refs_7_, bf16[160,1024]{1,0:T(8,128)(2,1)S(1)} %collective-permute-done.15.refs_1_.refs_8_, bf16[1024,1024]{1,0:T(8,128)(2,1)S(1)} %copy-done, bf16[1024,1024]{1,0:T(8,128)(2,1)S(1)} %bitcast.5, ...), custom_call_target="tpu_custom_call" | custom-call | flops 603979776 | bytes 5373952 | tf_op jit(solution)/shard_map/pallas_call | solution.py:34
  50.9 1.4 %collective-permute-start.17 = (bf16[144,1024]{1,0:T(8,128)(2,1)S(1)}, bf16[144,1024]{1,0:T(8,128)(2,1)S(1)}, u32[]{:S(2)}, u32[]{:S(2)}) collective-permute-start(bf16[144,1024]{1,0:T(8,128)(2,1)S(1)} %get-tuple-element.61), channel_id=1, source_target_pairs={{0,3},{1,2},{2,1},{3,0},{4,7},{5,6},{6,5},{7,4},{8,11},{9,10},{10,... | collective-permute-start | bytes 884744 | tf_op jit(solution)/shard_map/ppermute | solution.py:269
  52.4 2.9 %collective-permute-done.11.refs_1_.refs_9_ = bf16[144,1024]{1,0:T(8,128)(2,1)S(1)} collective-permute-done((bf16[144,1024]{1,0:T(8,128)(2,1)S(1)}, bf16[144,1024]{1,0:T(8,128)(2,1)S(1)}, u32[]{:S(2)}, u32[]{:S(2)}) %collective-permute-start.11) | collective-permute-done | bytes 294944 | tf_op jit(solution)/shard_map/ppermute | solution.py:269
  55.3 1.0 %shard_map.116 = (bf16[128,1024]{1,0:T(8,128)(2,1)S(1)}, bf16[128,1024]{1,0:T(8,128)(2,1)S(1)}, bf16[128,1024]{1,0:T(8,128)(2,1)S(1)}, bf16[128,1024]{1,0:T(8,128)(2,1)S(1)}) custom-call(bf16[144,1024]{1,0:T(8,128)(2,1)S(1)} %get-tuple-element.57.refs_3_.refs_4_.refs_0_, bf16[144,1024]{1,0:T(8,128)(2,1)S(1)} %get-tuple-element.66.refs_1_, ...), custom_call_target="tpu_custom_call" | custom-call | flops 603979776 | bytes 3702784 | tf_op jit(solution)/shard_map/pallas_call | solution.py:34
  57.4 2.5 %collective-permute-done.17.refs_3_ = bf16[144,1024]{1,0:T(8,128)(2,1)S(1)} collective-permute-done((bf16[144,1024]{1,0:T(8,128)(2,1)S(1)}, bf16[144,1024]{1,0:T(8,128)(2,1)S(1)}, u32[]{:S(2)}, u32[]{:S(2)}) %collective-permute-start.17) | collective-permute-done | bytes 294944 | tf_op jit(solution)/shard_map/ppermute | solution.py:269
  60.1 2.1 %collective-permute-start.18 = (bf16[144,256]{1,0:T(8,128)(2,1)S(1)}, bf16[144,256]{1,0:T(8,128)(2,1)S(1)}, u32[]{:S(2)}, u32[]{:S(2)}) collective-permute-start(bf16[144,256]{1,0:T(8,128)(2,1)S(1)} %get-tuple-element.63), channel_id=1, source_target_pairs={{0,12},{1,13},{2,14},{3,15},{4,8},{5,9},{6,10},{7,11},{8,4},{9,5},... | collective-permute-start | bytes 221192 | tf_op jit(solution)/shard_map/ppermute | solution.py:269
  62.2 2.3 %collective-permute-start.20 = (bf16[144,256]{1,0:T(8,128)(2,1)S(1)}, bf16[144,256]{1,0:T(8,128)(2,1)S(1)}, u32[]{:S(2)}, u32[]{:S(2)}) collective-permute-start(bf16[144,256]{1,0:T(8,128)(2,1)S(1)} %get-tuple-element.65), channel_id=1, source_target_pairs={{0,4},{1,5},{2,6},{3,7},{4,0},{5,1},{6,2},{7,3},{8,12},{9,13},{10,... | collective-permute-start | bytes 221192 | tf_op jit(solution)/shard_map/ppermute | solution.py:269
  64.5 2.0 %shard_map.117 = (bf16[1,512,1024]{2,1,0:T(8,128)(2,1)}, f32[8,128]{1,0:T(8,128)S(1)}) custom-call(bf16[144,1024]{1,0:T(8,128)(2,1)S(1)} %get-tuple-element.57.refs_3_.refs_4_.refs_0_, bf16[144,1024]{1,0:T(8,128)(2,1)S(1)} %get-tuple-element.66.refs_1_, bf16[144,1024]{1,0:T(8,128)(2,1)S(1)} %get-tuple-element.60.refs_2_, ...), custom_call_target="tpu_custom_call" | custom-call | flops 603979776 | bytes 4755456 | tf_op jit(solution)/shard_map/pallas_call | solution.py:34
  66.5 1.3 %collective-permute-done.19.refs_4_ = bf16[144,256]{1,0:T(8,128)(2,1)S(1)} collective-permute-done((bf16[144,256]{1,0:T(8,128)(2,1)S(1)}, bf16[144,256]{1,0:T(8,128)(2,1)S(1)}, u32[]{:S(2)}, u32[]{:S(2)}) %collective-permute-start.19) | collective-permute-done | bytes 73760 | tf_op jit(solution)/shard_map/ppermute | solution.py:269
  67.9 0.9 %shard_map.118 = bf16[1,128,1024]{2,1,0:T(8,128)(2,1)} custom-call(bf16[128,1024]{1,0:T(8,128)(2,1)S(1)} %get-tuple-element.46.refs_4_.refs_0_, bf16[128,144]{1,0:T(8,128)(2,1)S(1)} %get-tuple-element.47.refs_1_, bf16[144,256]{1,0:T(8,128)(2,1)S(1)} %get-tuple-element.62.refs_2_, bf16[144,256]{1,0:T(8,128)(2,1)S(1)} %collective-permute-done.18.refs_3_, ...), custom_call_target="tpu_custom_call" | custom-call | bytes 856064 | tf_op jit(solution)/shard_map/pallas_call | solution.py:34
  (38 shorter events, 4.8 us)
Async XLA Ops:
  0.6 32.8 %copy-start.1 = (bf16[1,1024,1024]{2,1,0:T(8,128)(2,1)S(1)}, bf16[1,1024,1024]{2,1,0:T(8,128)(2,1)}, u32[]{:S(2)}) copy-start(bf16[1,1024,1024]{2,1,0:T(8,128)(2,1)} %param.17) | copy-start | bytes 6291460
  2.0 31.5 %copy-start = (bf16[1024,1024]{1,0:T(8,128)(2,1)S(1)}, bf16[1024,1024]{1,0:T(8,128)(2,1)}, u32[]{:S(2)}) copy-start(bf16[1024,1024]{1,0:T(8,128)(2,1)} %refs_2_.5) | copy-start | bytes 6291460
  2.0 13.8 %collective-permute-start = (bf16[1040,128]{1,0:T(8,128)(2,1)S(1)}, bf16[1040,128]{1,0:T(8,128)(2,1)S(1)}, u32[]{:S(2)}, u32[]{:S(2)}) collective-permute-start(bf16[1040,128]{1,0:T(8,128)(2,1)S(1)} %get-tuple-element.43), channel_id=1, source_target_pairs={{0,1},{1,0},{2,3},{3,2},{4,5},{5,4},{6,7},{7,6},{8,9},{9,8},{10,11... | collective-permute-start | bytes 798728 | tf_op jit(solution)/shard_map/ppermute | solution.py:269
  5.0 10.8 %collective-permute-start.1 = (bf16[1040,128]{1,0:T(8,128)(2,1)S(1)}, bf16[1040,128]{1,0:T(8,128)(2,1)S(1)}, u32[]{:S(2)}, u32[]{:S(2)}) collective-permute-start(bf16[1040,128]{1,0:T(8,128)(2,1)S(1)} %get-tuple-element.44), channel_id=1, source_target_pairs={{1,2},{3,4},{5,6},{7,8},{9,10},{11,12},{13,14},{2,1},{4,3},{6,5},{... | collective-permute-start | bytes 798728 | tf_op jit(solution)/shard_map/ppermute | solution.py:318
  6.9 16.9 %collective-permute-start.5 = (bf16[144,256]{1,0:T(8,128)(2,1)S(1)}, bf16[144,256]{1,0:T(8,128)(2,1)S(1)}, u32[]{:S(2)}, u32[]{:S(2)}) collective-permute-start(bf16[144,256]{1,0:T(8,128)(2,1)S(1)} %get-tuple-element.53), channel_id=1, source_target_pairs={{0,4},{1,5},{2,6},{3,7},{4,0},{5,1},{6,2},{7,3},{8,12},{9,13},{10,... | collective-permute-start | bytes 221192 | tf_op jit(solution)/shard_map/ppermute | solution.py:269
  11.3 13.6 %collective-permute-start.6 = (bf16[144,256]{1,0:T(8,128)(2,1)S(1)}, bf16[144,256]{1,0:T(8,128)(2,1)S(1)}, u32[]{:S(2)}, u32[]{:S(2)}) collective-permute-start(bf16[144,256]{1,0:T(8,128)(2,1)S(1)} %get-tuple-element.54), channel_id=1, source_target_pairs={{0,8},{1,9},{2,10},{3,11},{4,12},{5,13},{6,14},{7,15},{8,0},{9,1},... | collective-permute-start | bytes 221192 | tf_op jit(solution)/shard_map/ppermute | solution.py:269
  13.9 11.0 %collective-permute-start.7 = (bf16[144,256]{1,0:T(8,128)(2,1)S(1)}, bf16[144,256]{1,0:T(8,128)(2,1)S(1)}, u32[]{:S(2)}, u32[]{:S(2)}) collective-permute-start(bf16[144,256]{1,0:T(8,128)(2,1)S(1)} %get-tuple-element.55), channel_id=1, source_target_pairs={{0,12},{1,13},{2,14},{3,15},{4,8},{5,9},{6,10},{7,11},{8,4},{9,5},... | collective-permute-start | bytes 221192 | tf_op jit(solution)/shard_map/ppermute | solution.py:269
  17.2 9.2 %collective-permute-start.2 = (bf16[144,256]{1,0:T(8,128)(2,1)S(1)}, bf16[144,256]{1,0:T(8,128)(2,1)S(1)}, u32[]{:S(2)}, u32[]{:S(2)}) collective-permute-start(bf16[144,256]{1,0:T(8,128)(2,1)S(1)} %get-tuple-element.49), channel_id=1, source_target_pairs={{0,4},{1,5},{2,6},{3,7},{4,0},{5,1},{6,2},{7,3},{8,12},{9,13},{10,... | collective-permute-start | bytes 221192 | tf_op jit(solution)/shard_map/ppermute | solution.py:269
  21.0 6.1 %collective-permute-start.3 = (bf16[144,256]{1,0:T(8,128)(2,1)S(1)}, bf16[144,256]{1,0:T(8,128)(2,1)S(1)}, u32[]{:S(2)}, u32[]{:S(2)}) collective-permute-start(bf16[144,256]{1,0:T(8,128)(2,1)S(1)} %get-tuple-element.50), channel_id=1, source_target_pairs={{0,8},{1,9},{2,10},{3,11},{4,12},{5,13},{6,14},{7,15},{8,0},{9,1},... | collective-permute-start | bytes 221192 | tf_op jit(solution)/shard_map/ppermute | solution.py:269
  23.8 6.2 %collective-permute-start.4 = (bf16[144,256]{1,0:T(8,128)(2,1)S(1)}, bf16[144,256]{1,0:T(8,128)(2,1)S(1)}, u32[]{:S(2)}, u32[]{:S(2)}) collective-permute-start(bf16[144,256]{1,0:T(8,128)(2,1)S(1)} %get-tuple-element.51), channel_id=1, source_target_pairs={{0,12},{1,13},{2,14},{3,15},{4,8},{5,9},{6,10},{7,11},{8,4},{9,5},... | collective-permute-start | bytes 221192 | tf_op jit(solution)/shard_map/ppermute | solution.py:269
  24.9 6.9 %collective-permute-start.9 = (bf16[144,1024]{1,0:T(8,128)(2,1)S(1)}, bf16[144,1024]{1,0:T(8,128)(2,1)S(1)}, u32[]{:S(2)}, u32[]{:S(2)}) collective-permute-start(bf16[144,1024]{1,0:T(8,128)(2,1)S(1)} %shard_map.108.refs_4_), channel_id=1, source_target_pairs={{0,2},{1,3},{2,0},{3,1},{4,6},{5,7},{6,4},{7,5},{8,10},{9,11},{10,... | collective-permute-start | bytes 884744 | tf_op jit(solution)/shard_map/ppermute | solution.py:269
  25.0 8.4 %collective-permute-start.8 = (bf16[144,1024]{1,0:T(8,128)(2,1)S(1)}, bf16[144,1024]{1,0:T(8,128)(2,1)S(1)}, u32[]{:S(2)}, u32[]{:S(2)}) collective-permute-start(bf16[144,1024]{1,0:T(8,128)(2,1)S(1)} %shard_map.108.refs_4_), channel_id=1, source_target_pairs={{0,1},{1,0},{2,3},{3,2},{4,5},{5,4},{6,7},{7,6},{8,9},{9,8},{10,11... | collective-permute-start | bytes 884744 | tf_op jit(solution)/shard_map/ppermute | solution.py:269
  30.1 8.1 %collective-permute-start.10 = (bf16[144,1024]{1,0:T(8,128)(2,1)S(1)}, bf16[144,1024]{1,0:T(8,128)(2,1)S(1)}, u32[]{:S(2)}, u32[]{:S(2)}) collective-permute-start(bf16[144,1024]{1,0:T(8,128)(2,1)S(1)} %shard_map.107.refs_0_), channel_id=1, source_target_pairs={{0,1},{1,0},{2,3},{3,2},{4,5},{5,4},{6,7},{7,6},{8,9},{9,8},{10,11... | collective-permute-start | bytes 884744 | tf_op jit(solution)/shard_map/ppermute | solution.py:269
  31.7 8.5 %collective-permute-start.12 = (bf16[144,1024]{1,0:T(8,128)(2,1)S(1)}, bf16[144,1024]{1,0:T(8,128)(2,1)S(1)}, u32[]{:S(2)}, u32[]{:S(2)}) collective-permute-start(bf16[144,1024]{1,0:T(8,128)(2,1)S(1)} %shard_map.107.refs_0_), channel_id=1, source_target_pairs={{0,2},{1,3},{2,0},{3,1},{4,6},{5,7},{6,4},{7,5},{8,10},{9,11},{10,... | collective-permute-start | bytes 884744 | tf_op jit(solution)/shard_map/ppermute | solution.py:269
  38.1 8.1 %collective-permute-start.14 = (bf16[128,1024]{1,0:T(8,128)(2,1)S(1)}, bf16[128,1024]{1,0:T(8,128)(2,1)S(1)}, u32[]{:S(2)}, u32[]{:S(2)}) collective-permute-start(bf16[128,1024]{1,0:T(8,128)(2,1)S(1)} %shard_map.112), channel_id=1, source_target_pairs={{0,2},{1,3},{2,0},{3,1},{4,6},{5,7},{6,4},{7,5},{8,10},{9,11},{10,... | collective-permute-start | bytes 786440 | tf_op jit(solution)/shard_map/ppermute | solution.py:269
  40.2 9.8 %collective-permute-start.15 = (bf16[160,1024]{1,0:T(8,128)(2,1)S(1)}, bf16[160,1024]{1,0:T(8,128)(2,1)S(1)}, u32[]{:S(2)}, u32[]{:S(2)}) collective-permute-start(bf16[160,1024]{1,0:T(8,128)(2,1)S(1)} %shard_map.113), channel_id=1, source_target_pairs={{0,1},{1,0},{2,3},{3,2},{4,5},{5,4},{6,7},{7,6},{8,9},{9,8},{10,11... | collective-permute-start | bytes 983048 | tf_op jit(solution)/shard_map/ppermute | solution.py:269
  42.1 13.2 %collective-permute-start.11 = (bf16[144,1024]{1,0:T(8,128)(2,1)S(1)}, bf16[144,1024]{1,0:T(8,128)(2,1)S(1)}, u32[]{:S(2)}, u32[]{:S(2)}) collective-permute-start(bf16[144,1024]{1,0:T(8,128)(2,1)S(1)} %get-tuple-element.58), channel_id=1, source_target_pairs={{0,1},{1,0},{2,3},{3,2},{4,5},{5,4},{6,7},{7,6},{8,9},{9,8},{10,11... | collective-permute-start | bytes 884744 | tf_op jit(solution)/shard_map/ppermute | solution.py:269
  44.3 11.0 %collective-permute-start.13 = (bf16[144,1024]{1,0:T(8,128)(2,1)S(1)}, bf16[144,1024]{1,0:T(8,128)(2,1)S(1)}, u32[]{:S(2)}, u32[]{:S(2)}) collective-permute-start(bf16[144,1024]{1,0:T(8,128)(2,1)S(1)} %get-tuple-element.59), channel_id=1, source_target_pairs={{0,2},{1,3},{2,0},{3,1},{4,6},{5,7},{6,4},{7,5},{8,10},{9,11},{10,... | collective-permute-start | bytes 884744 | tf_op jit(solution)/shard_map/ppermute | solution.py:269
  44.5 1.2 %collective-permute-start.16 = (bf16[16,128]{1,0:T(8,128)(2,1)S(1)}, bf16[16,128]{1,0:T(8,128)(2,1)S(1)}, u32[]{:S(2)}, u32[]{:S(2)}) collective-permute-start(bf16[16,128]{1,0:T(8,128)(2,1)S(1)} %slice.3), channel_id=1, source_target_pairs={{0,16},{16,0},{1,17},{17,1},{2,18},{18,2},{3,19},{19,3},{4,20},{20... | collective-permute-start | bytes 12296 | tf_op jit(solution)/shard_map/ppermute | solution.py:285
  50.9 9.0 %collective-permute-start.17 = (bf16[144,1024]{1,0:T(8,128)(2,1)S(1)}, bf16[144,1024]{1,0:T(8,128)(2,1)S(1)}, u32[]{:S(2)}, u32[]{:S(2)}) collective-permute-start(bf16[144,1024]{1,0:T(8,128)(2,1)S(1)} %get-tuple-element.61), channel_id=1, source_target_pairs={{0,3},{1,2},{2,1},{3,0},{4,7},{5,6},{6,5},{7,4},{8,11},{9,10},{10,... | collective-permute-start | bytes 884744 | tf_op jit(solution)/shard_map/ppermute | solution.py:269
  56.3 5.8 %collective-permute-start.21 = (bf16[128,1024]{1,0:T(8,128)(2,1)S(1)}, bf16[128,1024]{1,0:T(8,128)(2,1)S(1)}, u32[]{:S(2)}, u32[]{:S(2)}) collective-permute-start(bf16[128,1024]{1,0:T(8,128)(2,1)S(1)} %get-tuple-element.68), channel_id=1, source_target_pairs={{0,16},{16,0},{1,17},{17,1},{2,18},{18,2},{3,19},{19,3},{4,20},{20... | collective-permute-start | bytes 786440 | tf_op jit(solution)/shard_map/ppermute | solution.py:373
  56.4 5.8 %collective-permute-start.22 = (bf16[128,1024]{1,0:T(8,128)(2,1)S(1)}, bf16[128,1024]{1,0:T(8,128)(2,1)S(1)}, u32[]{:S(2)}, u32[]{:S(2)}) collective-permute-start(bf16[128,1024]{1,0:T(8,128)(2,1)S(1)} %get-tuple-element.69), channel_id=1, source_target_pairs={{0,16},{16,0},{1,17},{17,1},{2,18},{18,2},{3,19},{19,3},{4,20},{20... | collective-permute-start | bytes 786440 | tf_op jit(solution)/shard_map/ppermute | solution.py:373
  56.9 7.6 %collective-permute-start.23 = (bf16[128,1024]{1,0:T(8,128)(2,1)S(1)}, bf16[128,1024]{1,0:T(8,128)(2,1)S(1)}, u32[]{:S(2)}, u32[]{:S(2)}) collective-permute-start(bf16[128,1024]{1,0:T(8,128)(2,1)S(1)} %get-tuple-element.70), channel_id=1, source_target_pairs={{0,16},{16,0},{1,17},{17,1},{2,18},{18,2},{3,19},{19,3},{4,20},{20... | collective-permute-start | bytes 786440 | tf_op jit(solution)/shard_map/ppermute | solution.py:373
  57.0 7.5 %collective-permute-start.24 = (bf16[128,1024]{1,0:T(8,128)(2,1)S(1)}, bf16[128,1024]{1,0:T(8,128)(2,1)S(1)}, u32[]{:S(2)}, u32[]{:S(2)}) collective-permute-start(bf16[128,1024]{1,0:T(8,128)(2,1)S(1)} %get-tuple-element.71), channel_id=1, source_target_pairs={{0,16},{16,0},{1,17},{17,1},{2,18},{18,2},{3,19},{19,3},{4,20},{20... | collective-permute-start | bytes 786440 | tf_op jit(solution)/shard_map/ppermute | solution.py:373
  60.1 6.5 %collective-permute-start.18 = (bf16[144,256]{1,0:T(8,128)(2,1)S(1)}, bf16[144,256]{1,0:T(8,128)(2,1)S(1)}, u32[]{:S(2)}, u32[]{:S(2)}) collective-permute-start(bf16[144,256]{1,0:T(8,128)(2,1)S(1)} %get-tuple-element.63), channel_id=1, source_target_pairs={{0,12},{1,13},{2,14},{3,15},{4,8},{5,9},{6,10},{7,11},{8,4},{9,5},... | collective-permute-start | bytes 221192 | tf_op jit(solution)/shard_map/ppermute | solution.py:269
  62.2 5.7 %collective-permute-start.19 = (bf16[144,256]{1,0:T(8,128)(2,1)S(1)}, bf16[144,256]{1,0:T(8,128)(2,1)S(1)}, u32[]{:S(2)}, u32[]{:S(2)}) collective-permute-start(bf16[144,256]{1,0:T(8,128)(2,1)S(1)} %get-tuple-element.64), channel_id=1, source_target_pairs={{0,8},{1,9},{2,10},{3,11},{4,12},{5,13},{6,14},{7,15},{8,0},{9,1},... | collective-permute-start | bytes 221192 | tf_op jit(solution)/shard_map/ppermute | solution.py:269
  62.2 5.7 %collective-permute-start.20 = (bf16[144,256]{1,0:T(8,128)(2,1)S(1)}, bf16[144,256]{1,0:T(8,128)(2,1)S(1)}, u32[]{:S(2)}, u32[]{:S(2)}) collective-permute-start(bf16[144,256]{1,0:T(8,128)(2,1)S(1)} %get-tuple-element.65), channel_id=1, source_target_pairs={{0,4},{1,5},{2,6},{3,7},{4,0},{5,1},{6,2},{7,3},{8,12},{9,13},{10,... | collective-permute-start | bytes 221192 | tf_op jit(solution)/shard_map/ppermute | solution.py:269

commit v8 on v7

--- a/solution.py
+++ b/solution.py
@@ -11,6 +11,7 @@
 SPLIT = 4
 HALO = 64
 NEG_FILL = -1e30
+LOG2_E = 1.4426950408889634
 PARTS = 4
 STEP = 256
 PIECES = 4
@@ -83,16 +84,19 @@
     rows = key_ref.shape[1]
     width = key_ref.shape[2] // HEADS
     odd = lax.axis_index("ep") % 2
-    for message, last in ((near_out, 1 - odd), (far_out, odd)):
-        mine = pl.ds(pl.multiple_of(last * (rows - HALO), HALO), HALO)
-        for head in range(HEADS):
-            columns = slice(head * width, (head + 1) * width)
-            message[head * HALO : (head + 1) * HALO, :] = key_ref[0, mine, columns]
-            start = (HEADS + head) * HALO
-            message[start : start + HALO, :] = value_ref[0, mine, columns]
-        mask = jnp.where(last == 1, mask_ref[:, rows - HALO :], mask_ref[:, :HALO]).astype(F32)
-        mask = jnp.concatenate([mask, jnp.zeros((1, width - HALO), F32)], axis=1)
-        message[2 * HEADS * HALO :, :] = jnp.broadcast_to(mask, (16, width)).astype(BF16)
+    for parity in (0, 1):
+
+        @pl.when(odd == parity)
+        def _():
+            for message, first in ((near_out, (1 - parity) * (rows - HALO)), (far_out, parity * (rows - HALO))):
+                for head in range(HEADS):
+                    columns = slice(head * width, (head + 1) * width)
+                    message[head * HALO : (head + 1) * HALO, :] = key_ref[0, first : first + HALO, columns]
+                    start = (HEADS + head) * HALO
+                    message[start : start + HALO, :] = value_ref[0, first : first + HALO, columns]
+                mask = mask_ref[:, first : first + HALO].astype(F32)
+                mask = jnp.concatenate([mask, jnp.zeros((1, width - HALO), F32)], axis=1)
+                message[2 * HEADS * HALO :, :] = jnp.broadcast_to(mask, (16, width)).astype(BF16)
 
 
 def routed(labels):
@@ -143,10 +147,11 @@
         c.wait()
 
 
-def gather_body(pitch, *refs):
+def gather_body(order, pitch, *refs):
     *message_refs, rows_ref = refs
     width = message_refs[0].shape[1]
-    for j, column in enumerate(from_messages(message_refs, pitch, rows_ref.shape[0])):
+    ordered = [message_refs[order.index(k)] for k in range(len(order))]
+    for j, column in enumerate(from_messages(ordered, pitch, rows_ref.shape[0])):
         rows_ref[:, j * width : (j + 1) * width] = column
 
 
@@ -182,26 +187,27 @@
     first = jnp.where(column < HALO, near_first, jnp.where(column < HALO + rows, -HALO, far_first))
     offset = column + first - iota((rows, count), 0)
     usable = (jnp.abs(offset) <= HALO) & ((mask > 0.5) | (offset == 0))
-    scale = width ** (-0.5)
+    factor = width ** (-0.5) * LOG2_E
+    scored, valued, weighted = [], [], []
     for head in range(HEADS):
         columns = slice(head * width, (head + 1) * width)
         at, value_at = head * HALO, (HEADS + head) * HALO
-        keys = jnp.concatenate(
-            [near_ref[at : at + HALO, :], key_ref[0, :, columns], far_ref[at : at + HALO, :]], axis=0
-        )
-        values = jnp.concatenate(
-            [
-                near_ref[value_at : value_at + HALO, :],
-                value_ref[0, :, columns],
-                far_ref[value_at : value_at + HALO, :],
-            ],
-            axis=0,
-        )
-        scores = dot(query_ref[0, :, columns], keys, (1, 1)) * scale
+        keys = [near_ref[at : at + HALO, :], key_ref[0, :, columns], far_ref[at : at + HALO, :]]
+        values = [
+            near_ref[value_at : value_at + HALO, :],
+            value_ref[0, :, columns],
+            far_ref[value_at : value_at + HALO, :],
+        ]
+        scored.append(dot(query_ref[0, :, columns], jnp.concatenate(keys, axis=0), (1, 1)))
+        valued.append(jnp.concatenate(values, axis=0))
+    for scores in scored:
         scores = jnp.where(usable, scores, NEG_FILL)
-        raised = jnp.exp(scores - jnp.max(scores, axis=1, keepdims=True))
-        soft = (raised * (1.0 / jnp.sum(raised, axis=1, keepdims=True))).astype(BF16)
-        mixed_ref[:, columns] = (token_ref[0, :, columns].astype(F32) + dot(soft, values)).astype(BF16)
+        raised = jnp.exp2((scores - jnp.max(scores, axis=1, keepdims=True)) * factor)
+        weighted.append((raised.astype(BF16), 1.0 / jnp.sum(raised, axis=1, keepdims=True)))
+    for head, (raised, share) in enumerate(weighted):
+        columns = slice(head * width, (head + 1) * width)
+        attended = dot(raised, valued[head]) * share
+        mixed_ref[:, columns] = (token_ref[0, :, columns].astype(F32) + attended).astype(BF16)
     pack(mixed_ref[...], place_ref, message_refs, pitch)
 
 
@@ -336,15 +342,18 @@
         flops=4 * rows_here * (rows_here + 2 * HALO) * features,
     )
 
+    order = [0, 2, 1, *range(3, experts)]
     (cot_rows,) = call(
-        functools.partial(gather_body, pitch),
+        functools.partial(gather_body, order, pitch),
         [out(plane_rows, features)],
-        vmem=cot_got,
+        vmem=[cot_got[k] for k in order],
         after=(mixed,),
         size=0,
     )
     cot_x, cot_y = permute(cot_rows, 1), permute(cot_rows, 2)
-    (rows,) = call(functools.partial(gather_body, pitch), [out(plane_rows, features)], vmem=along_line(sent))
+    (rows,) = call(
+        functools.partial(gather_body, range(experts), pitch), [out(plane_rows, features)], vmem=along_line(sent)
+    )
 
     row_x, row_y = permute(rows, 1), permute(rows, 2)
     part = plane_rows // 32 * 16

time: 69 us -> 68 us (0.986)
  waiting for transfers between devices: 23.2 us -> 20.6 us
  starting transfers between devices: 32.6 us -> 34.9 us
    ppermute x19, waiting for transfers between devices: 22.1 us -> 19.4 us  [permute(): lax.ppermute(value, 'ep', [(i, i ^ apart) for i in range(lax.axis_size('e...]
    ppermute x19, starting transfers between devices: 30.9 us -> 33.1 us  [permute(): lax.ppermute(value, 'ep', [(i, i ^ apart) for i in range(lax.axis_size('e...]
  transfers between devices with their start and end apart: 25 -> 25, of which waited for: 12 -> 11; matrix products, arithmetic and copies ran while one was open for 0% -> 0% of each run, Pallas kernels for 14% -> 14%
where the time goes in v8:
time: 68 us; the launch traced here: 67.8 us
  starting transfers between devices  34.9 us (51%)
  waiting for transfers between devices  20.6 us (30%)
  Pallas kernels  11.6 us (17%)
  between operations  0.78 us (1%)
    ppermute x19, starting transfers between devices, permute(): lax.ppermute(value, 'ep', [(i, i ^ apart) for i in range(lax.axis_size('e...  33.1 us
    ppermute x19, waiting for transfers between devices, permute(): lax.ppermute(value, 'ep', [(i, i ^ apart) for i in range(lax.axis_size('e...  19.4 us
    pallas_call x15, Pallas kernels, call(): pl.pallas_call(kernel, out_shape=outs, in_specs=[VMEM] * len(vmem) + [HBM...  11.6 us
  transfers between devices with their start and end apart: 25, of which 11 were waited for; matrix products, arithmetic and copies ran while one was open for 0% of the time, Pallas kernels for 14%

profile of v8, /device:TPU:0, one launch (start us, length us, event | category | flops | bytes accessed | tf_op | source)
XLA Modules:
  0.0 67.8 jit_solution(7448752474789679367)
XLA Ops:
  0.6 1.3 %shard_map.104 = (bf16[1040,128]{1,0:T(8,128)(2,1)S(1)}, bf16[1040,128]{1,0:T(8,128)(2,1)S(1)}, bf16[1,128,1024]{2,1,0:T(8,128)(2,1)S(1)}, bf16[1,128,1024]{2,1,0:T(8,128)(2,1)S(1)}, s32[1,128]{1,0:T(1,128)S(1)}) custom-call(bf16[1,128,1024]{2,1,0:T(8,128)(2,1)} %refs_0_.2, bf16[1,128,1024]{2,1,0:T(8,128)(2,1)} %refs_1_.4, s32[1,128]{1,0:T(1,128)} %refs_2_.3), custom_call_target="tpu_custom_call" | custom-call | bytes 1582080 | tf_op jit(solution)/shard_map/pallas_call | solution.py:35
  2.0 3.0 %collective-permute-start = (bf16[1040,128]{1,0:T(8,128)(2,1)S(1)}, bf16[1040,128]{1,0:T(8,128)(2,1)S(1)}, u32[]{:S(2)}, u32[]{:S(2)}) collective-permute-start(bf16[1040,128]{1,0:T(8,128)(2,1)S(1)} %get-tuple-element.43), channel_id=1, source_target_pairs={{0,1},{1,0},{2,3},{3,2},{4,5},{5,4},{6,7},{7,6},{8,9},{9,8},{10,11... | collective-permute-start | bytes 798728 | tf_op jit(solution)/shard_map/ppermute | solution.py:275
  5.7 1.2 %shard_map.105 = (bf16[144,128]{1,0:T(8,128)(2,1)S(1)}, bf16[128,144]{1,0:T(8,128)(2,1)S(1)}, bf16[1,128,1024]{2,1,0:T(8,128)(2,1)S(1)}, bf16[1,128,1024]{2,1,0:...) custom-call(bf16[1,128,1024]{2,1,0:T(8,128)(2,1)} %refs_0_.3, ...), custom_call_target="tpu_custom_call" | custom-call | tf_op jit(solution)/shard_map/pallas_call | solution.py:35
  7.0 5.3 %collective-permute-start.5 = (bf16[144,256]{1,0:T(8,128)(2,1)S(1)}, bf16[144,256]{1,0:T(8,128)(2,1)S(1)}, u32[]{:S(2)}, u32[]{:S(2)}) collective-permute-start(bf16[144,256]{1,0:T(8,128)(2,1)S(1)} %get-tuple-element.53), channel_id=1, source_target_pairs={{0,8},{1,9},{2,10},{3,11},{4,12},{5,13},{6,14},{7,15},{8,0},{9,1},... | collective-permute-start | bytes 221192 | tf_op jit(solution)/shard_map/ppermute | solution.py:275
  12.3 1.6 %collective-permute-start.6 = (bf16[144,256]{1,0:T(8,128)(2,1)S(1)}, bf16[144,256]{1,0:T(8,128)(2,1)S(1)}, u32[]{:S(2)}, u32[]{:S(2)}) collective-permute-start(bf16[144,256]{1,0:T(8,128)(2,1)S(1)} %get-tuple-element.54), channel_id=1, source_target_pairs={{0,4},{1,5},{2,6},{3,7},{4,0},{5,1},{6,2},{7,3},{8,12},{9,13},{10,... | collective-permute-start | bytes 221192 | tf_op jit(solution)/shard_map/ppermute | solution.py:275
  13.9 2.2 %collective-permute-done.refs_5_ = bf16[1040,128]{1,0:T(8,128)(2,1)S(1)} collective-permute-done((bf16[1040,128]{1,0:T(8,128)(2,1)S(1)}, bf16[1040,128]{1,0:T(8,128)(2,1)S(1)}, u32[]{:S(2)}, u32[]{:S(2)}) %collective-permute-start) | collective-permute-done | bytes 266272 | tf_op jit(solution)/shard_map/ppermute | solution.py:275
  16.9 3.6 %collective-permute-start.2 = (bf16[144,256]{1,0:T(8,128)(2,1)S(1)}, bf16[144,256]{1,0:T(8,128)(2,1)S(1)}, u32[]{:S(2)}, u32[]{:S(2)}) collective-permute-start(bf16[144,256]{1,0:T(8,128)(2,1)S(1)} %get-tuple-element.49), channel_id=1, source_target_pairs={{0,4},{1,5},{2,6},{3,7},{4,0},{5,1},{6,2},{7,3},{8,12},{9,13},{10,... | collective-permute-start | bytes 221192 | tf_op jit(solution)/shard_map/ppermute | solution.py:275
  20.5 3.5 %collective-permute-start.3 = (bf16[144,256]{1,0:T(8,128)(2,1)S(1)}, bf16[144,256]{1,0:T(8,128)(2,1)S(1)}, u32[]{:S(2)}, u32[]{:S(2)}) collective-permute-start(bf16[144,256]{1,0:T(8,128)(2,1)S(1)} %get-tuple-element.50), channel_id=1, source_target_pairs={{0,8},{1,9},{2,10},{3,11},{4,12},{5,13},{6,14},{7,15},{8,0},{9,1},... | collective-permute-start | bytes 221192 | tf_op jit(solution)/shard_map/ppermute | solution.py:275
  24.0 1.4 %collective-permute-start.4 = (bf16[144,256]{1,0:T(8,128)(2,1)S(1)}, bf16[144,256]{1,0:T(8,128)(2,1)S(1)}, u32[]{:S(2)}, u32[]{:S(2)}) collective-permute-start(bf16[144,256]{1,0:T(8,128)(2,1)S(1)} %get-tuple-element.51), channel_id=1, source_target_pairs={{0,12},{1,13},{2,14},{3,15},{4,8},{5,9},{6,10},{7,11},{8,4},{9,5},... | collective-permute-start | bytes 221192 | tf_op jit(solution)/shard_map/ppermute | solution.py:275
  25.5 3.3 %collective-permute-start.8 = (bf16[144,1024]{1,0:T(8,128)(2,1)S(1)}, bf16[144,1024]{1,0:T(8,128)(2,1)S(1)}, u32[]{:S(2)}, u32[]{:S(2)}) collective-permute-start(bf16[144,1024]{1,0:T(8,128)(2,1)S(1)} %shard_map.108.refs_4_), channel_id=1, source_target_pairs={{0,1},{1,0},{2,3},{3,2},{4,5},{5,4},{6,7},{7,6},{8,9},{9,8},{10,11... | collective-permute-start | bytes 884744 | tf_op jit(solution)/shard_map/ppermute | solution.py:275
  28.8 1.4 %collective-permute-done.4.refs_3_ = bf16[144,256]{1,0:T(8,128)(2,1)S(1)} collective-permute-done((bf16[144,256]{1,0:T(8,128)(2,1)S(1)}, bf16[144,256]{1,0:T(8,128)(2,1)S(1)}, u32[]{:S(2)}, u32[]{:S(2)}) %collective-permute-start.4) | collective-permute-done | bytes 73760 | tf_op jit(solution)/shard_map/ppermute | solution.py:275
  31.1 2.1 %collective-permute-done.9.refs_4_.refs_1_.refs_6_ = bf16[144,1024]{1,0:T(8,128)(2,1)S(1)} collective-permute-done((bf16[144,1024]{1,0:T(8,128)(2,1)S(1)}, bf16[144,1024]{1,0:T(8,128)(2,1)S(1)}, u32[]{:S(2)}, u32[]{:S(2)}) %collective-permute-start.9) | collective-permute-done | bytes 294944 | tf_op jit(solution)/shard_map/ppermute | solution.py:275
  33.3 2.6 %collective-permute-done.8.refs_3_.refs_1_.refs_5_ = bf16[144,1024]{1,0:T(8,128)(2,1)S(1)} collective-permute-done((bf16[144,1024]{1,0:T(8,128)(2,1)S(1)}, bf16[144,1024]{1,0:T(8,128)(2,1)S(1)}, u32[]{:S(2)}, u32[]{:S(2)}) %collective-permute-start.8) | collective-permute-done | bytes 294944 | tf_op jit(solution)/shard_map/ppermute | solution.py:275
  35.9 1.0 %shard_map.109 = (bf16[144,1024]{1,0:T(8,128)(2,1)S(1)}, bf16[144,1024]{1,0:T(8,128)(2,1)S(1)}) custom-call(bf16[144,1024]{1,0:T(8,128)(2,1)S(1)} %shard_map.107.refs_0_, bf16[1024,1024]{1,0:T(8,128)(2,1)S(1)} %copy-done, bf16[1024,1024]{1,0:T(8,128)(2,1)S(1)} %bitcast.2, bf16[144,1024]{1,0:T(8,128)(2,1)S(1)} %collective-permute-done.8.refs_3_.refs_1_.refs_5_, ...), custom_call_target="tpu_custom_call" | custom-call | flops 603979776 | bytes 5079040 | tf_op jit(solution)/shard_map/pallas_call | solution.py:35
  36.9 2.4 %collective-permute-done.10.refs_0_ = bf16[144,1024]{1,0:T(8,128)(2,1)S(1)} collective-permute-done((bf16[144,1024]{1,0:T(8,128)(2,1)S(1)}, bf16[144,1024]{1,0:T(8,128)(2,1)S(1)}, u32[]{:S(2)}, u32[]{:S(2)}) %collective-permute-start.10) | collective-permute-done | bytes 294944 | tf_op jit(solution)/shard_map/ppermute | solution.py:275
  39.9 1.7 %collective-permute-start.15 = (bf16[160,1024]{1,0:T(8,128)(2,1)S(1)}, bf16[160,1024]{1,0:T(8,128)(2,1)S(1)}, u32[]{:S(2)}, u32[]{:S(2)}) collective-permute-start(bf16[160,1024]{1,0:T(8,128)(2,1)S(1)} %shard_map.113), channel_id=1, source_target_pairs={{0,1},{1,0},{2,3},{3,2},{4,5},{5,4},{6,7},{7,6},{8,9},{9,8},{10,11... | collective-permute-start | bytes 983048 | tf_op jit(solution)/shard_map/ppermute | solution.py:275
  41.5 1.0 %shard_map.110 = (bf16[144,1024]{1,0:T(8,128)(2,1)S(1)}, bf16[144,1024]{1,0:T(8,128)(2,1)S(1)}) custom-call(bf16[144,1024]{1,0:T(8,128)(2,1)S(1)} %collective-permute-done.10.refs_0_, bf16[1024,1024]{1,0:T(8,128)(2,1)S(1)} %copy-done, bf16[1024,1024]{1,0:T(8,128)(2,1)S(1)} %bitcast.3, bf16[144,1024]{1,0:T(8,128)(2,1)S(1)} %get-tuple-element.57.refs_3_.refs_4_.refs_0_), custom_call_target="tpu_custom_call" | custom-call | flops 603979776 | bytes 5079040 | tf_op jit(solution)/shard_map/pallas_call | solution.py:35
  43.0 1.0 %shard_map.111 = (bf16[144,1024]{1,0:T(8,128)(2,1)S(1)}, bf16[144,1024]{1,0:T(8,128)(2,1)S(1)}) custom-call(bf16[144,1024]{1,0:T(8,128)(2,1)S(1)} %collective-permute-done.12.refs_0_, bf16[1024,1024]{1,0:T(8,128)(2,1)S(1)} %copy-done, bf16[1024,1024]{1,0:T(8,128)(2,1)S(1)} %bitcast.4, bf16[144,1024]{1,0:T(8,128)(2,1)S(1)} %get-tuple-element.57.refs_3_.refs_4_.refs_0_), custom_call_target="tpu_custom_call" | custom-call | flops 603979776 | bytes 5079040 | tf_op jit(solution)/shard_map/pallas_call | solution.py:35
  44.0 1.7 %collective-permute-start.13 = (bf16[144,1024]{1,0:T(8,128)(2,1)S(1)}, bf16[144,1024]{1,0:T(8,128)(2,1)S(1)}, u32[]{:S(2)}, u32[]{:S(2)}) collective-permute-start(bf16[144,1024]{1,0:T(8,128)(2,1)S(1)} %get-tuple-element.59), channel_id=1, source_target_pairs={{0,2},{1,3},{2,0},{3,1},{4,6},{5,7},{6,4},{7,5},{8,10},{9,11},{10,... | collective-permute-start | bytes 884744 | tf_op jit(solution)/shard_map/ppermute | solution.py:275
  45.7 1.2 %collective-permute-done.16.refs_5_ = bf16[16,128]{1,0:T(8,128)(2,1)S(1)} collective-permute-done((bf16[16,128]{1,0:T(8,128)(2,1)S(1)}, bf16[16,128]{1,0:T(8,128)(2,1)S(1)}, u32[]{:S(2)}, u32[]{:S(2)}) %collective-permute-start.16) | collective-permute-done | bytes 4128 | tf_op jit(solution)/shard_map/ppermute | solution.py:291
  46.8 1.5 %collective-permute-done.14.refs_0_.refs_7_ = bf16[128,1024]{1,0:T(8,128)(2,1)S(1)} collective-permute-done((bf16[128,1024]{1,0:T(8,128)(2,1)S(1)}, bf16[128,1024]{1,0:T(8,128)(2,1)S(1)}, u32[]{:S(2)}, u32[]{:S(2)}) %collective-permute-start.14) | collective-permute-done | bytes 262176 | tf_op jit(solution)/shard_map/ppermute | solution.py:275
  48.3 0.9 %collective-permute-done.15.refs_1_.refs_8_ = bf16[160,1024]{1,0:T(8,128)(2,1)S(1)} collective-permute-done((bf16[160,1024]{1,0:T(8,128)(2,1)S(1)}, bf16[160,1024]{1,0:T(8,128)(2,1)S(1)}, u32[]{:S(2)}, u32[]{:S(2)}) %collective-permute-start.15) | collective-permute-done | bytes 327712 | tf_op jit(solution)/shard_map/ppermute | solution.py:275
  49.2 1.0 %shard_map.114 = (bf16[144,1024]{1,0:T(8,128)(2,1)S(1)}, bf16[144,1024]{1,0:T(8,128)(2,1)S(1)}) custom-call(bf16[128,1024]{1,0:T(8,128)(2,1)S(1)} %collective-permute-done.14.refs_0_.refs_7_, bf16[160,1024]{1,0:T(8,128)(2,1)S(1)} %collective-permute-done.15.refs_1_.refs_8_, bf16[1024,1024]{1,0:T(8,128)(2,1)S(1)} %copy-done, bf16[1024,1024]{1,0:T(8,128)(2,1)S(1)} %bitcast.5, ...), custom_call_target="tpu_custom_call" | custom-call | flops 603979776 | bytes 5373952 | tf_op jit(solution)/shard_map/pallas_call | solution.py:35
  50.2 1.6 %collective-permute-start.17 = (bf16[144,1024]{1,0:T(8,128)(2,1)S(1)}, bf16[144,1024]{1,0:T(8,128)(2,1)S(1)}, u32[]{:S(2)}, u32[]{:S(2)}) collective-permute-start(bf16[144,1024]{1,0:T(8,128)(2,1)S(1)} %get-tuple-element.61), channel_id=1, source_target_pairs={{0,3},{1,2},{2,1},{3,0},{4,7},{5,6},{6,5},{7,4},{8,11},{9,10},{10,... | collective-permute-start | bytes 884744 | tf_op jit(solution)/shard_map/ppermute | solution.py:275
  51.8 1.9 %collective-permute-done.11.refs_1_.refs_9_ = bf16[144,1024]{1,0:T(8,128)(2,1)S(1)} collective-permute-done((bf16[144,1024]{1,0:T(8,128)(2,1)S(1)}, bf16[144,1024]{1,0:T(8,128)(2,1)S(1)}, u32[]{:S(2)}, u32[]{:S(2)}) %collective-permute-start.11) | collective-permute-done | bytes 294944 | tf_op jit(solution)/shard_map/ppermute | solution.py:275
  53.8 1.0 %shard_map.116 = (bf16[128,1024]{1,0:T(8,128)(2,1)S(1)}, bf16[128,1024]{1,0:T(8,128)(2,1)S(1)}, bf16[128,1024]{1,0:T(8,128)(2,1)S(1)}, bf16[128,1024]{1,0:T(8,128)(2,1)S(1)}) custom-call(bf16[144,1024]{1,0:T(8,128)(2,1)S(1)} %get-tuple-element.57.refs_3_.refs_4_.refs_0_, bf16[144,1024]{1,0:T(8,128)(2,1)S(1)} %get-tuple-element.66.refs_1_, ...), custom_call_target="tpu_custom_call" | custom-call | flops 603979776 | bytes 3702784 | tf_op jit(solution)/shard_map/pallas_call | solution.py:35
  55.9 3.0 %collective-permute-done.17.refs_3_ = bf16[144,1024]{1,0:T(8,128)(2,1)S(1)} collective-permute-done((bf16[144,1024]{1,0:T(8,128)(2,1)S(1)}, bf16[144,1024]{1,0:T(8,128)(2,1)S(1)}, u32[]{:S(2)}, u32[]{:S(2)}) %collective-permute-start.17) | collective-permute-done | bytes 294944 | tf_op jit(solution)/shard_map/ppermute | solution.py:275
  59.0 2.6 %collective-permute-start.18 = (bf16[144,256]{1,0:T(8,128)(2,1)S(1)}, bf16[144,256]{1,0:T(8,128)(2,1)S(1)}, u32[]{:S(2)}, u32[]{:S(2)}) collective-permute-start(bf16[144,256]{1,0:T(8,128)(2,1)S(1)} %get-tuple-element.63), channel_id=1, source_target_pairs={{0,12},{1,13},{2,14},{3,15},{4,8},{5,9},{6,10},{7,11},{8,4},{9,5},... | collective-permute-start | bytes 221192 | tf_op jit(solution)/shard_map/ppermute | solution.py:275
  61.7 1.8 %collective-permute-start.20 = (bf16[144,256]{1,0:T(8,128)(2,1)S(1)}, bf16[144,256]{1,0:T(8,128)(2,1)S(1)}, u32[]{:S(2)}, u32[]{:S(2)}) collective-permute-start(bf16[144,256]{1,0:T(8,128)(2,1)S(1)} %get-tuple-element.65), channel_id=1, source_target_pairs={{0,4},{1,5},{2,6},{3,7},{4,0},{5,1},{6,2},{7,3},{8,12},{9,13},{10,... | collective-permute-start | bytes 221192 | tf_op jit(solution)/shard_map/ppermute | solution.py:275
  63.5 2.0 %shard_map.117 = (bf16[1,512,1024]{2,1,0:T(8,128)(2,1)}, f32[8,128]{1,0:T(8,128)S(1)}) custom-call(bf16[144,1024]{1,0:T(8,128)(2,1)S(1)} %get-tuple-element.57.refs_3_.refs_4_.refs_0_, bf16[144,1024]{1,0:T(8,128)(2,1)S(1)} %get-tuple-element.66.refs_1_, bf16[144,1024]{1,0:T(8,128)(2,1)S(1)} %get-tuple-element.60.refs_2_, ...), custom_call_target="tpu_custom_call" | custom-call | flops 603979776 | bytes 4755456 | tf_op jit(solution)/shard_map/pallas_call | solution.py:35
  65.5 1.4 %collective-permute-done.19.refs_4_ = bf16[144,256]{1,0:T(8,128)(2,1)S(1)} collective-permute-done((bf16[144,256]{1,0:T(8,128)(2,1)S(1)}, bf16[144,256]{1,0:T(8,128)(2,1)S(1)}, u32[]{:S(2)}, u32[]{:S(2)}) %collective-permute-start.19) | collective-permute-done | bytes 73760 | tf_op jit(solution)/shard_map/ppermute | solution.py:275
  66.9 0.9 %shard_map.118 = bf16[1,128,1024]{2,1,0:T(8,128)(2,1)} custom-call(bf16[128,1024]{1,0:T(8,128)(2,1)S(1)} %get-tuple-element.46.refs_4_.refs_0_, bf16[128,144]{1,0:T(8,128)(2,1)S(1)} %get-tuple-element.47.refs_1_, bf16[144,256]{1,0:T(8,128)(2,1)S(1)} %get-tuple-element.62.refs_2_, bf16[144,256]{1,0:T(8,128)(2,1)S(1)} %collective-permute-done.18.refs_3_, ...), custom_call_target="tpu_custom_call" | custom-call | bytes 856064 | tf_op jit(solution)/shard_map/pallas_call | solution.py:35
  (38 shorter events, 5.0 us)
Async XLA Ops:
  0.6 35.2 %copy-start.1 = (bf16[1,1024,1024]{2,1,0:T(8,128)(2,1)S(1)}, bf16[1,1024,1024]{2,1,0:T(8,128)(2,1)}, u32[]{:S(2)}) copy-start(bf16[1,1024,1024]{2,1,0:T(8,128)(2,1)} %param.17) | copy-start | bytes 6291460
  2.0 33.9 %copy-start = (bf16[1024,1024]{1,0:T(8,128)(2,1)S(1)}, bf16[1024,1024]{1,0:T(8,128)(2,1)}, u32[]{:S(2)}) copy-start(bf16[1024,1024]{1,0:T(8,128)(2,1)} %refs_2_.5) | copy-start | bytes 6291460
  2.0 14.1 %collective-permute-start = (bf16[1040,128]{1,0:T(8,128)(2,1)S(1)}, bf16[1040,128]{1,0:T(8,128)(2,1)S(1)}, u32[]{:S(2)}, u32[]{:S(2)}) collective-permute-start(bf16[1040,128]{1,0:T(8,128)(2,1)S(1)} %get-tuple-element.43), channel_id=1, source_target_pairs={{0,1},{1,0},{2,3},{3,2},{4,5},{5,4},{6,7},{7,6},{8,9},{9,8},{10,11... | collective-permute-start | bytes 798728 | tf_op jit(solution)/shard_map/ppermute | solution.py:275
  5.0 11.0 %collective-permute-start.1 = (bf16[1040,128]{1,0:T(8,128)(2,1)S(1)}, bf16[1040,128]{1,0:T(8,128)(2,1)S(1)}, u32[]{:S(2)}, u32[]{:S(2)}) collective-permute-start(bf16[1040,128]{1,0:T(8,128)(2,1)S(1)} %get-tuple-element.44), channel_id=1, source_target_pairs={{1,2},{3,4},{5,6},{7,8},{9,10},{11,12},{13,14},{2,1},{4,3},{6,5},{... | collective-permute-start | bytes 798728 | tf_op jit(solution)/shard_map/ppermute | solution.py:324
  7.0 17.0 %collective-permute-start.5 = (bf16[144,256]{1,0:T(8,128)(2,1)S(1)}, bf16[144,256]{1,0:T(8,128)(2,1)S(1)}, u32[]{:S(2)}, u32[]{:S(2)}) collective-permute-start(bf16[144,256]{1,0:T(8,128)(2,1)S(1)} %get-tuple-element.53), channel_id=1, source_target_pairs={{0,8},{1,9},{2,10},{3,11},{4,12},{5,13},{6,14},{7,15},{8,0},{9,1},... | collective-permute-start | bytes 221192 | tf_op jit(solution)/shard_map/ppermute | solution.py:275
  12.3 13.1 %collective-permute-start.6 = (bf16[144,256]{1,0:T(8,128)(2,1)S(1)}, bf16[144,256]{1,0:T(8,128)(2,1)S(1)}, u32[]{:S(2)}, u32[]{:S(2)}) collective-permute-start(bf16[144,256]{1,0:T(8,128)(2,1)S(1)} %get-tuple-element.54), channel_id=1, source_target_pairs={{0,4},{1,5},{2,6},{3,7},{4,0},{5,1},{6,2},{7,3},{8,12},{9,13},{10,... | collective-permute-start | bytes 221192 | tf_op jit(solution)/shard_map/ppermute | solution.py:275
  13.9 11.5 %collective-permute-start.7 = (bf16[144,256]{1,0:T(8,128)(2,1)S(1)}, bf16[144,256]{1,0:T(8,128)(2,1)S(1)}, u32[]{:S(2)}, u32[]{:S(2)}) collective-permute-start(bf16[144,256]{1,0:T(8,128)(2,1)S(1)} %get-tuple-element.55), channel_id=1, source_target_pairs={{0,12},{1,13},{2,14},{3,15},{4,8},{5,9},{6,10},{7,11},{8,4},{9,5},... | collective-permute-start | bytes 221192 | tf_op jit(solution)/shard_map/ppermute | solution.py:275
  16.9 11.9 %collective-permute-start.2 = (bf16[144,256]{1,0:T(8,128)(2,1)S(1)}, bf16[144,256]{1,0:T(8,128)(2,1)S(1)}, u32[]{:S(2)}, u32[]{:S(2)}) collective-permute-start(bf16[144,256]{1,0:T(8,128)(2,1)S(1)} %get-tuple-element.49), channel_id=1, source_target_pairs={{0,4},{1,5},{2,6},{3,7},{4,0},{5,1},{6,2},{7,3},{8,12},{9,13},{10,... | collective-permute-start | bytes 221192 | tf_op jit(solution)/shard_map/ppermute | solution.py:275
  20.5 8.3 %collective-permute-start.3 = (bf16[144,256]{1,0:T(8,128)(2,1)S(1)}, bf16[144,256]{1,0:T(8,128)(2,1)S(1)}, u32[]{:S(2)}, u32[]{:S(2)}) collective-permute-start(bf16[144,256]{1,0:T(8,128)(2,1)S(1)} %get-tuple-element.50), channel_id=1, source_target_pairs={{0,8},{1,9},{2,10},{3,11},{4,12},{5,13},{6,14},{7,15},{8,0},{9,1},... | collective-permute-start | bytes 221192 | tf_op jit(solution)/shard_map/ppermute | solution.py:275
  24.0 6.3 %collective-permute-start.4 = (bf16[144,256]{1,0:T(8,128)(2,1)S(1)}, bf16[144,256]{1,0:T(8,128)(2,1)S(1)}, u32[]{:S(2)}, u32[]{:S(2)}) collective-permute-start(bf16[144,256]{1,0:T(8,128)(2,1)S(1)} %get-tuple-element.51), channel_id=1, source_target_pairs={{0,12},{1,13},{2,14},{3,15},{4,8},{5,9},{6,10},{7,11},{8,4},{9,5},... | collective-permute-start | bytes 221192 | tf_op jit(solution)/shard_map/ppermute | solution.py:275
  25.4 7.9 %collective-permute-start.9 = (bf16[144,1024]{1,0:T(8,128)(2,1)S(1)}, bf16[144,1024]{1,0:T(8,128)(2,1)S(1)}, u32[]{:S(2)}, u32[]{:S(2)}) collective-permute-start(bf16[144,1024]{1,0:T(8,128)(2,1)S(1)} %shard_map.108.refs_4_), channel_id=1, source_target_pairs={{0,2},{1,3},{2,0},{3,1},{4,6},{5,7},{6,4},{7,5},{8,10},{9,11},{10,... | collective-permute-start | bytes 884744 | tf_op jit(solution)/shard_map/ppermute | solution.py:275
  25.5 10.4 %collective-permute-start.8 = (bf16[144,1024]{1,0:T(8,128)(2,1)S(1)}, bf16[144,1024]{1,0:T(8,128)(2,1)S(1)}, u32[]{:S(2)}, u32[]{:S(2)}) collective-permute-start(bf16[144,1024]{1,0:T(8,128)(2,1)S(1)} %shard_map.108.refs_4_), channel_id=1, source_target_pairs={{0,1},{1,0},{2,3},{3,2},{4,5},{5,4},{6,7},{7,6},{8,9},{9,8},{10,11... | collective-permute-start | bytes 884744 | tf_op jit(solution)/shard_map/ppermute | solution.py:275
  30.3 9.0 %collective-permute-start.10 = (bf16[144,1024]{1,0:T(8,128)(2,1)S(1)}, bf16[144,1024]{1,0:T(8,128)(2,1)S(1)}, u32[]{:S(2)}, u32[]{:S(2)}) collective-permute-start(bf16[144,1024]{1,0:T(8,128)(2,1)S(1)} %shard_map.107.refs_0_), channel_id=1, source_target_pairs={{0,1},{1,0},{2,3},{3,2},{4,5},{5,4},{6,7},{7,6},{8,9},{9,8},{10,11... | collective-permute-start | bytes 884744 | tf_op jit(solution)/shard_map/ppermute | solution.py:275
  31.1 8.7 %collective-permute-start.12 = (bf16[144,1024]{1,0:T(8,128)(2,1)S(1)}, bf16[144,1024]{1,0:T(8,128)(2,1)S(1)}, u32[]{:S(2)}, u32[]{:S(2)}) collective-permute-start(bf16[144,1024]{1,0:T(8,128)(2,1)S(1)} %shard_map.107.refs_0_), channel_id=1, source_target_pairs={{0,2},{1,3},{2,0},{3,1},{4,6},{5,7},{6,4},{7,5},{8,10},{9,11},{10,... | collective-permute-start | bytes 884744 | tf_op jit(solution)/shard_map/ppermute | solution.py:275
  39.3 9.0 %collective-permute-start.14 = (bf16[128,1024]{1,0:T(8,128)(2,1)S(1)}, bf16[128,1024]{1,0:T(8,128)(2,1)S(1)}, u32[]{:S(2)}, u32[]{:S(2)}) collective-permute-start(bf16[128,1024]{1,0:T(8,128)(2,1)S(1)} %shard_map.112), channel_id=1, source_target_pairs={{0,2},{1,3},{2,0},{3,1},{4,6},{5,7},{6,4},{7,5},{8,10},{9,11},{10,... | collective-permute-start | bytes 786440 | tf_op jit(solution)/shard_map/ppermute | solution.py:275
  39.9 9.4 %collective-permute-start.15 = (bf16[160,1024]{1,0:T(8,128)(2,1)S(1)}, bf16[160,1024]{1,0:T(8,128)(2,1)S(1)}, u32[]{:S(2)}, u32[]{:S(2)}) collective-permute-start(bf16[160,1024]{1,0:T(8,128)(2,1)S(1)} %shard_map.113), channel_id=1, source_target_pairs={{0,1},{1,0},{2,3},{3,2},{4,5},{5,4},{6,7},{7,6},{8,9},{9,8},{10,11... | collective-permute-start | bytes 983048 | tf_op jit(solution)/shard_map/ppermute | solution.py:275
  42.5 11.2 %collective-permute-start.11 = (bf16[144,1024]{1,0:T(8,128)(2,1)S(1)}, bf16[144,1024]{1,0:T(8,128)(2,1)S(1)}, u32[]{:S(2)}, u32[]{:S(2)}) collective-permute-start(bf16[144,1024]{1,0:T(8,128)(2,1)S(1)} %get-tuple-element.58), channel_id=1, source_target_pairs={{0,1},{1,0},{2,3},{3,2},{4,5},{5,4},{6,7},{7,6},{8,9},{9,8},{10,11... | collective-permute-start | bytes 884744 | tf_op jit(solution)/shard_map/ppermute | solution.py:275
  44.0 9.8 %collective-permute-start.13 = (bf16[144,1024]{1,0:T(8,128)(2,1)S(1)}, bf16[144,1024]{1,0:T(8,128)(2,1)S(1)}, u32[]{:S(2)}, u32[]{:S(2)}) collective-permute-start(bf16[144,1024]{1,0:T(8,128)(2,1)S(1)} %get-tuple-element.59), channel_id=1, source_target_pairs={{0,2},{1,3},{2,0},{3,1},{4,6},{5,7},{6,4},{7,5},{8,10},{9,11},{10,... | collective-permute-start | bytes 884744 | tf_op jit(solution)/shard_map/ppermute | solution.py:275
  45.7 1.2 %collective-permute-start.16 = (bf16[16,128]{1,0:T(8,128)(2,1)S(1)}, bf16[16,128]{1,0:T(8,128)(2,1)S(1)}, u32[]{:S(2)}, u32[]{:S(2)}) collective-permute-start(bf16[16,128]{1,0:T(8,128)(2,1)S(1)} %slice.3), channel_id=1, source_target_pairs={{0,16},{16,0},{1,17},{17,1},{2,18},{18,2},{3,19},{19,3},{4,20},{20... | collective-permute-start | bytes 12296 | tf_op jit(solution)/shard_map/ppermute | solution.py:291
  50.2 8.6 %collective-permute-start.17 = (bf16[144,1024]{1,0:T(8,128)(2,1)S(1)}, bf16[144,1024]{1,0:T(8,128)(2,1)S(1)}, u32[]{:S(2)}, u32[]{:S(2)}) collective-permute-start(bf16[144,1024]{1,0:T(8,128)(2,1)S(1)} %get-tuple-element.61), channel_id=1, source_target_pairs={{0,3},{1,2},{2,1},{3,0},{4,7},{5,6},{6,5},{7,4},{8,11},{9,10},{10,... | collective-permute-start | bytes 884744 | tf_op jit(solution)/shard_map/ppermute | solution.py:275
  54.8 6.8 %collective-permute-start.21 = (bf16[128,1024]{1,0:T(8,128)(2,1)S(1)}, bf16[128,1024]{1,0:T(8,128)(2,1)S(1)}, u32[]{:S(2)}, u32[]{:S(2)}) collective-permute-start(bf16[128,1024]{1,0:T(8,128)(2,1)S(1)} %get-tuple-element.68), channel_id=1, source_target_pairs={{0,16},{16,0},{1,17},{17,1},{2,18},{18,2},{3,19},{19,3},{4,20},{20... | collective-permute-start | bytes 786440 | tf_op jit(solution)/shard_map/ppermute | solution.py:382
  54.9 6.8 %collective-permute-start.22 = (bf16[128,1024]{1,0:T(8,128)(2,1)S(1)}, bf16[128,1024]{1,0:T(8,128)(2,1)S(1)}, u32[]{:S(2)}, u32[]{:S(2)}) collective-permute-start(bf16[128,1024]{1,0:T(8,128)(2,1)S(1)} %get-tuple-element.69), channel_id=1, source_target_pairs={{0,16},{16,0},{1,17},{17,1},{2,18},{18,2},{3,19},{19,3},{4,20},{20... | collective-permute-start | bytes 786440 | tf_op jit(solution)/shard_map/ppermute | solution.py:382
  55.4 8.1 %collective-permute-start.23 = (bf16[128,1024]{1,0:T(8,128)(2,1)S(1)}, bf16[128,1024]{1,0:T(8,128)(2,1)S(1)}, u32[]{:S(2)}, u32[]{:S(2)}) collective-permute-start(bf16[128,1024]{1,0:T(8,128)(2,1)S(1)} %get-tuple-element.70), channel_id=1, source_target_pairs={{0,16},{16,0},{1,17},{17,1},{2,18},{18,2},{3,19},{19,3},{4,20},{20... | collective-permute-start | bytes 786440 | tf_op jit(solution)/shard_map/ppermute | solution.py:382
  55.5 8.0 %collective-permute-start.24 = (bf16[128,1024]{1,0:T(8,128)(2,1)S(1)}, bf16[128,1024]{1,0:T(8,128)(2,1)S(1)}, u32[]{:S(2)}, u32[]{:S(2)}) collective-permute-start(bf16[128,1024]{1,0:T(8,128)(2,1)S(1)} %get-tuple-element.71), channel_id=1, source_target_pairs={{0,16},{16,0},{1,17},{17,1},{2,18},{18,2},{3,19},{19,3},{4,20},{20... | collective-permute-start | bytes 786440 | tf_op jit(solution)/shard_map/ppermute | solution.py:382
  59.0 6.5 %collective-permute-start.18 = (bf16[144,256]{1,0:T(8,128)(2,1)S(1)}, bf16[144,256]{1,0:T(8,128)(2,1)S(1)}, u32[]{:S(2)}, u32[]{:S(2)}) collective-permute-start(bf16[144,256]{1,0:T(8,128)(2,1)S(1)} %get-tuple-element.63), channel_id=1, source_target_pairs={{0,12},{1,13},{2,14},{3,15},{4,8},{5,9},{6,10},{7,11},{8,4},{9,5},... | collective-permute-start | bytes 221192 | tf_op jit(solution)/shard_map/ppermute | solution.py:275
  61.6 5.3 %collective-permute-start.19 = (bf16[144,256]{1,0:T(8,128)(2,1)S(1)}, bf16[144,256]{1,0:T(8,128)(2,1)S(1)}, u32[]{:S(2)}, u32[]{:S(2)}) collective-permute-start(bf16[144,256]{1,0:T(8,128)(2,1)S(1)} %get-tuple-element.64), channel_id=1, source_target_pairs={{0,8},{1,9},{2,10},{3,11},{4,12},{5,13},{6,14},{7,15},{8,0},{9,1},... | collective-permute-start | bytes 221192 | tf_op jit(solution)/shard_map/ppermute | solution.py:275
  61.7 5.2 %collective-permute-start.20 = (bf16[144,256]{1,0:T(8,128)(2,1)S(1)}, bf16[144,256]{1,0:T(8,128)(2,1)S(1)}, u32[]{:S(2)}, u32[]{:S(2)}) collective-permute-start(bf16[144,256]{1,0:T(8,128)(2,1)S(1)} %get-tuple-element.65), channel_id=1, source_target_pairs={{0,4},{1,5},{2,6},{3,7},{4,0},{5,1},{6,2},{7,3},{8,12},{9,13},{10,... | collective-permute-start | bytes 221192 | tf_op jit(solution)/shard_map/ppermute | solution.py:275

commit v9 on v8

--- a/solution.py
+++ b/solution.py
@@ -230,10 +230,8 @@
     *message_refs, layer_ref = refs
     width = message_refs[0].shape[1]
     ordered = [message_refs[order.index(k)] for k in range(len(order))]
-    for j, column in enumerate(from_messages(ordered, pitch, back_ref.shape[1])):
-        columns = slice(j * width, (j + 1) * width)
-        taken = dot(back_ref[...], column)
-        layer_ref[0, :, columns] = (mixed_ref[:, columns].astype(F32) + taken).astype(BF16)
+    taken = dot(back_ref[...], jnp.concatenate(from_messages(ordered, pitch, back_ref.shape[1]), axis=1))
+    layer_ref[0, :, :] = (mixed_ref[...].astype(F32) + taken).astype(BF16)
 
 
 def half_terms(refs, side):

time: 68 us -> 68 us (level)
  no operation moved by 1% of the time
where the time goes in v9:
time: 68 us; the launch traced here: 67.8 us
  starting transfers between devices  34.9 us (51%)
  waiting for transfers between devices  20.6 us (30%)
  Pallas kernels  11.6 us (17%)
  between operations  0.78 us (1%)
    ppermute x19, starting transfers between devices, permute(): lax.ppermute(value, 'ep', [(i, i ^ apart) for i in range(lax.axis_size('e...  33.1 us
    ppermute x19, waiting for transfers between devices, permute(): lax.ppermute(value, 'ep', [(i, i ^ apart) for i in range(lax.axis_size('e...  19.4 us
    pallas_call x15, Pallas kernels, call(): pl.pallas_call(kernel, out_shape=outs, in_specs=[VMEM] * len(vmem) + [HBM...  11.6 us
  transfers between devices with their start and end apart: 25, of which 11 were waited for; matrix products, arithmetic and copies ran while one was open for 0% of the time, Pallas kernels for 14%

profile of v9, /device:TPU:0, one launch (start us, length us, event | category | flops | bytes accessed | tf_op | source)
XLA Modules:
  0.0 67.8 jit_solution(9987592901535880526)
XLA Ops:
  0.6 1.3 %shard_map.104 = (bf16[1040,128]{1,0:T(8,128)(2,1)S(1)}, bf16[1040,128]{1,0:T(8,128)(2,1)S(1)}, bf16[1,128,1024]{2,1,0:T(8,128)(2,1)S(1)}, bf16[1,128,1024]{2,1,0:T(8,128)(2,1)S(1)}, s32[1,128]{1,0:T(1,128)S(1)}) custom-call(bf16[1,128,1024]{2,1,0:T(8,128)(2,1)} %refs_0_.2, bf16[1,128,1024]{2,1,0:T(8,128)(2,1)} %refs_1_.4, s32[1,128]{1,0:T(1,128)} %refs_2_.3), custom_call_target="tpu_custom_call" | custom-call | bytes 1582080 | tf_op jit(solution)/shard_map/pallas_call | solution.py:35
  2.0 3.0 %collective-permute-start = (bf16[1040,128]{1,0:T(8,128)(2,1)S(1)}, bf16[1040,128]{1,0:T(8,128)(2,1)S(1)}, u32[]{:S(2)}, u32[]{:S(2)}) collective-permute-start(bf16[1040,128]{1,0:T(8,128)(2,1)S(1)} %get-tuple-element.43), channel_id=1, source_target_pairs={{0,1},{1,0},{2,3},{3,2},{4,5},{5,4},{6,7},{7,6},{8,9},{9,8},{10,11... | collective-permute-start | bytes 798728 | tf_op jit(solution)/shard_map/ppermute | solution.py:273
  5.7 1.2 %shard_map.105 = (bf16[144,128]{1,0:T(8,128)(2,1)S(1)}, bf16[128,144]{1,0:T(8,128)(2,1)S(1)}, bf16[1,128,1024]{2,1,0:T(8,128)(2,1)S(1)}, bf16[1,128,1024]{2,1,0:...) custom-call(bf16[1,128,1024]{2,1,0:T(8,128)(2,1)} %refs_0_.3, ...), custom_call_target="tpu_custom_call" | custom-call | tf_op jit(solution)/shard_map/pallas_call | solution.py:35
  7.0 5.3 %collective-permute-start.5 = (bf16[144,256]{1,0:T(8,128)(2,1)S(1)}, bf16[144,256]{1,0:T(8,128)(2,1)S(1)}, u32[]{:S(2)}, u32[]{:S(2)}) collective-permute-start(bf16[144,256]{1,0:T(8,128)(2,1)S(1)} %get-tuple-element.53), channel_id=1, source_target_pairs={{0,8},{1,9},{2,10},{3,11},{4,12},{5,13},{6,14},{7,15},{8,0},{9,1},... | collective-permute-start | bytes 221192 | tf_op jit(solution)/shard_map/ppermute | solution.py:273
  12.3 1.6 %collective-permute-start.6 = (bf16[144,256]{1,0:T(8,128)(2,1)S(1)}, bf16[144,256]{1,0:T(8,128)(2,1)S(1)}, u32[]{:S(2)}, u32[]{:S(2)}) collective-permute-start(bf16[144,256]{1,0:T(8,128)(2,1)S(1)} %get-tuple-element.54), channel_id=1, source_target_pairs={{0,4},{1,5},{2,6},{3,7},{4,0},{5,1},{6,2},{7,3},{8,12},{9,13},{10,... | collective-permute-start | bytes 221192 | tf_op jit(solution)/shard_map/ppermute | solution.py:273
  13.9 2.2 %collective-permute-done.refs_5_ = bf16[1040,128]{1,0:T(8,128)(2,1)S(1)} collective-permute-done((bf16[1040,128]{1,0:T(8,128)(2,1)S(1)}, bf16[1040,128]{1,0:T(8,128)(2,1)S(1)}, u32[]{:S(2)}, u32[]{:S(2)}) %collective-permute-start) | collective-permute-done | bytes 266272 | tf_op jit(solution)/shard_map/ppermute | solution.py:273
  16.9 3.6 %collective-permute-start.2 = (bf16[144,256]{1,0:T(8,128)(2,1)S(1)}, bf16[144,256]{1,0:T(8,128)(2,1)S(1)}, u32[]{:S(2)}, u32[]{:S(2)}) collective-permute-start(bf16[144,256]{1,0:T(8,128)(2,1)S(1)} %get-tuple-element.49), channel_id=1, source_target_pairs={{0,4},{1,5},{2,6},{3,7},{4,0},{5,1},{6,2},{7,3},{8,12},{9,13},{10,... | collective-permute-start | bytes 221192 | tf_op jit(solution)/shard_map/ppermute | solution.py:273
  20.5 3.5 %collective-permute-start.3 = (bf16[144,256]{1,0:T(8,128)(2,1)S(1)}, bf16[144,256]{1,0:T(8,128)(2,1)S(1)}, u32[]{:S(2)}, u32[]{:S(2)}) collective-permute-start(bf16[144,256]{1,0:T(8,128)(2,1)S(1)} %get-tuple-element.50), channel_id=1, source_target_pairs={{0,8},{1,9},{2,10},{3,11},{4,12},{5,13},{6,14},{7,15},{8,0},{9,1},... | collective-permute-start | bytes 221192 | tf_op jit(solution)/shard_map/ppermute | solution.py:273
  24.0 1.4 %collective-permute-start.4 = (bf16[144,256]{1,0:T(8,128)(2,1)S(1)}, bf16[144,256]{1,0:T(8,128)(2,1)S(1)}, u32[]{:S(2)}, u32[]{:S(2)}) collective-permute-start(bf16[144,256]{1,0:T(8,128)(2,1)S(1)} %get-tuple-element.51), channel_id=1, source_target_pairs={{0,12},{1,13},{2,14},{3,15},{4,8},{5,9},{6,10},{7,11},{8,4},{9,5},... | collective-permute-start | bytes 221192 | tf_op jit(solution)/shard_map/ppermute | solution.py:273
  25.5 3.3 %collective-permute-start.8 = (bf16[144,1024]{1,0:T(8,128)(2,1)S(1)}, bf16[144,1024]{1,0:T(8,128)(2,1)S(1)}, u32[]{:S(2)}, u32[]{:S(2)}) collective-permute-start(bf16[144,1024]{1,0:T(8,128)(2,1)S(1)} %shard_map.108.refs_4_), channel_id=1, source_target_pairs={{0,1},{1,0},{2,3},{3,2},{4,5},{5,4},{6,7},{7,6},{8,9},{9,8},{10,11... | collective-permute-start | bytes 884744 | tf_op jit(solution)/shard_map/ppermute | solution.py:273
  28.8 1.4 %collective-permute-done.4.refs_3_ = bf16[144,256]{1,0:T(8,128)(2,1)S(1)} collective-permute-done((bf16[144,256]{1,0:T(8,128)(2,1)S(1)}, bf16[144,256]{1,0:T(8,128)(2,1)S(1)}, u32[]{:S(2)}, u32[]{:S(2)}) %collective-permute-start.4) | collective-permute-done | bytes 73760 | tf_op jit(solution)/shard_map/ppermute | solution.py:273
  31.1 2.1 %collective-permute-done.9.refs_4_.refs_1_.refs_6_ = bf16[144,1024]{1,0:T(8,128)(2,1)S(1)} collective-permute-done((bf16[144,1024]{1,0:T(8,128)(2,1)S(1)}, bf16[144,1024]{1,0:T(8,128)(2,1)S(1)}, u32[]{:S(2)}, u32[]{:S(2)}) %collective-permute-start.9) | collective-permute-done | bytes 294944 | tf_op jit(solution)/shard_map/ppermute | solution.py:273
  33.3 2.6 %collective-permute-done.8.refs_3_.refs_1_.refs_5_ = bf16[144,1024]{1,0:T(8,128)(2,1)S(1)} collective-permute-done((bf16[144,1024]{1,0:T(8,128)(2,1)S(1)}, bf16[144,1024]{1,0:T(8,128)(2,1)S(1)}, u32[]{:S(2)}, u32[]{:S(2)}) %collective-permute-start.8) | collective-permute-done | bytes 294944 | tf_op jit(solution)/shard_map/ppermute | solution.py:273
  35.9 1.0 %shard_map.109 = (bf16[144,1024]{1,0:T(8,128)(2,1)S(1)}, bf16[144,1024]{1,0:T(8,128)(2,1)S(1)}) custom-call(bf16[144,1024]{1,0:T(8,128)(2,1)S(1)} %shard_map.107.refs_0_, bf16[1024,1024]{1,0:T(8,128)(2,1)S(1)} %copy-done, bf16[1024,1024]{1,0:T(8,128)(2,1)S(1)} %bitcast.2, bf16[144,1024]{1,0:T(8,128)(2,1)S(1)} %collective-permute-done.8.refs_3_.refs_1_.refs_5_, ...), custom_call_target="tpu_custom_call" | custom-call | flops 603979776 | bytes 5079040 | tf_op jit(solution)/shard_map/pallas_call | solution.py:35
  36.9 2.4 %collective-permute-done.10.refs_0_ = bf16[144,1024]{1,0:T(8,128)(2,1)S(1)} collective-permute-done((bf16[144,1024]{1,0:T(8,128)(2,1)S(1)}, bf16[144,1024]{1,0:T(8,128)(2,1)S(1)}, u32[]{:S(2)}, u32[]{:S(2)}) %collective-permute-start.10) | collective-permute-done | bytes 294944 | tf_op jit(solution)/shard_map/ppermute | solution.py:273
  39.9 1.7 %collective-permute-start.15 = (bf16[160,1024]{1,0:T(8,128)(2,1)S(1)}, bf16[160,1024]{1,0:T(8,128)(2,1)S(1)}, u32[]{:S(2)}, u32[]{:S(2)}) collective-permute-start(bf16[160,1024]{1,0:T(8,128)(2,1)S(1)} %shard_map.113), channel_id=1, source_target_pairs={{0,1},{1,0},{2,3},{3,2},{4,5},{5,4},{6,7},{7,6},{8,9},{9,8},{10,11... | collective-permute-start | bytes 983048 | tf_op jit(solution)/shard_map/ppermute | solution.py:273
  41.5 1.0 %shard_map.110 = (bf16[144,1024]{1,0:T(8,128)(2,1)S(1)}, bf16[144,1024]{1,0:T(8,128)(2,1)S(1)}) custom-call(bf16[144,1024]{1,0:T(8,128)(2,1)S(1)} %collective-permute-done.10.refs_0_, bf16[1024,1024]{1,0:T(8,128)(2,1)S(1)} %copy-done, bf16[1024,1024]{1,0:T(8,128)(2,1)S(1)} %bitcast.3, bf16[144,1024]{1,0:T(8,128)(2,1)S(1)} %get-tuple-element.57.refs_3_.refs_4_.refs_0_), custom_call_target="tpu_custom_call" | custom-call | flops 603979776 | bytes 5079040 | tf_op jit(solution)/shard_map/pallas_call | solution.py:35
  43.0 1.0 %shard_map.111 = (bf16[144,1024]{1,0:T(8,128)(2,1)S(1)}, bf16[144,1024]{1,0:T(8,128)(2,1)S(1)}) custom-call(bf16[144,1024]{1,0:T(8,128)(2,1)S(1)} %collective-permute-done.12.refs_0_, bf16[1024,1024]{1,0:T(8,128)(2,1)S(1)} %copy-done, bf16[1024,1024]{1,0:T(8,128)(2,1)S(1)} %bitcast.4, bf16[144,1024]{1,0:T(8,128)(2,1)S(1)} %get-tuple-element.57.refs_3_.refs_4_.refs_0_), custom_call_target="tpu_custom_call" | custom-call | flops 603979776 | bytes 5079040 | tf_op jit(solution)/shard_map/pallas_call | solution.py:35
  44.0 1.7 %collective-permute-start.13 = (bf16[144,1024]{1,0:T(8,128)(2,1)S(1)}, bf16[144,1024]{1,0:T(8,128)(2,1)S(1)}, u32[]{:S(2)}, u32[]{:S(2)}) collective-permute-start(bf16[144,1024]{1,0:T(8,128)(2,1)S(1)} %get-tuple-element.59), channel_id=1, source_target_pairs={{0,2},{1,3},{2,0},{3,1},{4,6},{5,7},{6,4},{7,5},{8,10},{9,11},{10,... | collective-permute-start | bytes 884744 | tf_op jit(solution)/shard_map/ppermute | solution.py:273
  45.7 1.2 %collective-permute-done.16.refs_5_ = bf16[16,128]{1,0:T(8,128)(2,1)S(1)} collective-permute-done((bf16[16,128]{1,0:T(8,128)(2,1)S(1)}, bf16[16,128]{1,0:T(8,128)(2,1)S(1)}, u32[]{:S(2)}, u32[]{:S(2)}) %collective-permute-start.16) | collective-permute-done | bytes 4128 | tf_op jit(solution)/shard_map/ppermute | solution.py:289
  46.8 1.5 %collective-permute-done.14.refs_0_.refs_7_ = bf16[128,1024]{1,0:T(8,128)(2,1)S(1)} collective-permute-done((bf16[128,1024]{1,0:T(8,128)(2,1)S(1)}, bf16[128,1024]{1,0:T(8,128)(2,1)S(1)}, u32[]{:S(2)}, u32[]{:S(2)}) %collective-permute-start.14) | collective-permute-done | bytes 262176 | tf_op jit(solution)/shard_map/ppermute | solution.py:273
  48.3 0.9 %collective-permute-done.15.refs_1_.refs_8_ = bf16[160,1024]{1,0:T(8,128)(2,1)S(1)} collective-permute-done((bf16[160,1024]{1,0:T(8,128)(2,1)S(1)}, bf16[160,1024]{1,0:T(8,128)(2,1)S(1)}, u32[]{:S(2)}, u32[]{:S(2)}) %collective-permute-start.15) | collective-permute-done | bytes 327712 | tf_op jit(solution)/shard_map/ppermute | solution.py:273
  49.2 1.0 %shard_map.114 = (bf16[144,1024]{1,0:T(8,128)(2,1)S(1)}, bf16[144,1024]{1,0:T(8,128)(2,1)S(1)}) custom-call(bf16[128,1024]{1,0:T(8,128)(2,1)S(1)} %collective-permute-done.14.refs_0_.refs_7_, bf16[160,1024]{1,0:T(8,128)(2,1)S(1)} %collective-permute-done.15.refs_1_.refs_8_, bf16[1024,1024]{1,0:T(8,128)(2,1)S(1)} %copy-done, bf16[1024,1024]{1,0:T(8,128)(2,1)S(1)} %bitcast.5, ...), custom_call_target="tpu_custom_call" | custom-call | flops 603979776 | bytes 5373952 | tf_op jit(solution)/shard_map/pallas_call | solution.py:35
  50.2 1.6 %collective-permute-start.17 = (bf16[144,1024]{1,0:T(8,128)(2,1)S(1)}, bf16[144,1024]{1,0:T(8,128)(2,1)S(1)}, u32[]{:S(2)}, u32[]{:S(2)}) collective-permute-start(bf16[144,1024]{1,0:T(8,128)(2,1)S(1)} %get-tuple-element.61), channel_id=1, source_target_pairs={{0,3},{1,2},{2,1},{3,0},{4,7},{5,6},{6,5},{7,4},{8,11},{9,10},{10,... | collective-permute-start | bytes 884744 | tf_op jit(solution)/shard_map/ppermute | solution.py:273
  51.8 1.9 %collective-permute-done.11.refs_1_.refs_9_ = bf16[144,1024]{1,0:T(8,128)(2,1)S(1)} collective-permute-done((bf16[144,1024]{1,0:T(8,128)(2,1)S(1)}, bf16[144,1024]{1,0:T(8,128)(2,1)S(1)}, u32[]{:S(2)}, u32[]{:S(2)}) %collective-permute-start.11) | collective-permute-done | bytes 294944 | tf_op jit(solution)/shard_map/ppermute | solution.py:273
  53.8 1.0 %shard_map.116 = (bf16[128,1024]{1,0:T(8,128)(2,1)S(1)}, bf16[128,1024]{1,0:T(8,128)(2,1)S(1)}, bf16[128,1024]{1,0:T(8,128)(2,1)S(1)}, bf16[128,1024]{1,0:T(8,128)(2,1)S(1)}) custom-call(bf16[144,1024]{1,0:T(8,128)(2,1)S(1)} %get-tuple-element.57.refs_3_.refs_4_.refs_0_, bf16[144,1024]{1,0:T(8,128)(2,1)S(1)} %get-tuple-element.66.refs_1_, ...), custom_call_target="tpu_custom_call" | custom-call | flops 603979776 | bytes 3702784 | tf_op jit(solution)/shard_map/pallas_call | solution.py:35
  55.9 3.0 %collective-permute-done.17.refs_3_ = bf16[144,1024]{1,0:T(8,128)(2,1)S(1)} collective-permute-done((bf16[144,1024]{1,0:T(8,128)(2,1)S(1)}, bf16[144,1024]{1,0:T(8,128)(2,1)S(1)}, u32[]{:S(2)}, u32[]{:S(2)}) %collective-permute-start.17) | collective-permute-done | bytes 294944 | tf_op jit(solution)/shard_map/ppermute | solution.py:273
  59.0 2.6 %collective-permute-start.18 = (bf16[144,256]{1,0:T(8,128)(2,1)S(1)}, bf16[144,256]{1,0:T(8,128)(2,1)S(1)}, u32[]{:S(2)}, u32[]{:S(2)}) collective-permute-start(bf16[144,256]{1,0:T(8,128)(2,1)S(1)} %get-tuple-element.63), channel_id=1, source_target_pairs={{0,12},{1,13},{2,14},{3,15},{4,8},{5,9},{6,10},{7,11},{8,4},{9,5},... | collective-permute-start | bytes 221192 | tf_op jit(solution)/shard_map/ppermute | solution.py:273
  61.7 1.8 %collective-permute-start.20 = (bf16[144,256]{1,0:T(8,128)(2,1)S(1)}, bf16[144,256]{1,0:T(8,128)(2,1)S(1)}, u32[]{:S(2)}, u32[]{:S(2)}) collective-permute-start(bf16[144,256]{1,0:T(8,128)(2,1)S(1)} %get-tuple-element.65), channel_id=1, source_target_pairs={{0,4},{1,5},{2,6},{3,7},{4,0},{5,1},{6,2},{7,3},{8,12},{9,13},{10,... | collective-permute-start | bytes 221192 | tf_op jit(solution)/shard_map/ppermute | solution.py:273
  63.5 2.0 %shard_map.117 = (bf16[1,512,1024]{2,1,0:T(8,128)(2,1)}, f32[8,128]{1,0:T(8,128)S(1)}) custom-call(bf16[144,1024]{1,0:T(8,128)(2,1)S(1)} %get-tuple-element.57.refs_3_.refs_4_.refs_0_, bf16[144,1024]{1,0:T(8,128)(2,1)S(1)} %get-tuple-element.66.refs_1_, bf16[144,1024]{1,0:T(8,128)(2,1)S(1)} %get-tuple-element.60.refs_2_, ...), custom_call_target="tpu_custom_call" | custom-call | flops 603979776 | bytes 4755456 | tf_op jit(solution)/shard_map/pallas_call | solution.py:35
  65.5 1.4 %collective-permute-done.19.refs_4_ = bf16[144,256]{1,0:T(8,128)(2,1)S(1)} collective-permute-done((bf16[144,256]{1,0:T(8,128)(2,1)S(1)}, bf16[144,256]{1,0:T(8,128)(2,1)S(1)}, u32[]{:S(2)}, u32[]{:S(2)}) %collective-permute-start.19) | collective-permute-done | bytes 73760 | tf_op jit(solution)/shard_map/ppermute | solution.py:273
  66.9 0.9 %shard_map.118 = bf16[1,128,1024]{2,1,0:T(8,128)(2,1)} custom-call(bf16[128,1024]{1,0:T(8,128)(2,1)S(1)} %get-tuple-element.46.refs_4_.refs_0_, bf16[128,144]{1,0:T(8,128)(2,1)S(1)} %get-tuple-element.47.refs_1_, bf16[144,256]{1,0:T(8,128)(2,1)S(1)} %get-tuple-element.62.refs_2_, bf16[144,256]{1,0:T(8,128)(2,1)S(1)} %collective-permute-done.18.refs_3_, ...), custom_call_target="tpu_custom_call" | custom-call | bytes 856064 | tf_op jit(solution)/shard_map/pallas_call | solution.py:35
  (38 shorter events, 5.0 us)
Async XLA Ops:
  0.6 35.2 %copy-start.1 = (bf16[1,1024,1024]{2,1,0:T(8,128)(2,1)S(1)}, bf16[1,1024,1024]{2,1,0:T(8,128)(2,1)}, u32[]{:S(2)}) copy-start(bf16[1,1024,1024]{2,1,0:T(8,128)(2,1)} %param.17) | copy-start | bytes 6291460
  2.0 33.9 %copy-start = (bf16[1024,1024]{1,0:T(8,128)(2,1)S(1)}, bf16[1024,1024]{1,0:T(8,128)(2,1)}, u32[]{:S(2)}) copy-start(bf16[1024,1024]{1,0:T(8,128)(2,1)} %refs_2_.5) | copy-start | bytes 6291460
  2.0 14.1 %collective-permute-start = (bf16[1040,128]{1,0:T(8,128)(2,1)S(1)}, bf16[1040,128]{1,0:T(8,128)(2,1)S(1)}, u32[]{:S(2)}, u32[]{:S(2)}) collective-permute-start(bf16[1040,128]{1,0:T(8,128)(2,1)S(1)} %get-tuple-element.43), channel_id=1, source_target_pairs={{0,1},{1,0},{2,3},{3,2},{4,5},{5,4},{6,7},{7,6},{8,9},{9,8},{10,11... | collective-permute-start | bytes 798728 | tf_op jit(solution)/shard_map/ppermute | solution.py:273
  5.0 11.0 %collective-permute-start.1 = (bf16[1040,128]{1,0:T(8,128)(2,1)S(1)}, bf16[1040,128]{1,0:T(8,128)(2,1)S(1)}, u32[]{:S(2)}, u32[]{:S(2)}) collective-permute-start(bf16[1040,128]{1,0:T(8,128)(2,1)S(1)} %get-tuple-element.44), channel_id=1, source_target_pairs={{1,2},{3,4},{5,6},{7,8},{9,10},{11,12},{13,14},{2,1},{4,3},{6,5},{... | collective-permute-start | bytes 798728 | tf_op jit(solution)/shard_map/ppermute | solution.py:322
  7.0 17.0 %collective-permute-start.5 = (bf16[144,256]{1,0:T(8,128)(2,1)S(1)}, bf16[144,256]{1,0:T(8,128)(2,1)S(1)}, u32[]{:S(2)}, u32[]{:S(2)}) collective-permute-start(bf16[144,256]{1,0:T(8,128)(2,1)S(1)} %get-tuple-element.53), channel_id=1, source_target_pairs={{0,8},{1,9},{2,10},{3,11},{4,12},{5,13},{6,14},{7,15},{8,0},{9,1},... | collective-permute-start | bytes 221192 | tf_op jit(solution)/shard_map/ppermute | solution.py:273
  12.3 13.1 %collective-permute-start.6 = (bf16[144,256]{1,0:T(8,128)(2,1)S(1)}, bf16[144,256]{1,0:T(8,128)(2,1)S(1)}, u32[]{:S(2)}, u32[]{:S(2)}) collective-permute-start(bf16[144,256]{1,0:T(8,128)(2,1)S(1)} %get-tuple-element.54), channel_id=1, source_target_pairs={{0,4},{1,5},{2,6},{3,7},{4,0},{5,1},{6,2},{7,3},{8,12},{9,13},{10,... | collective-permute-start | bytes 221192 | tf_op jit(solution)/shard_map/ppermute | solution.py:273
  13.9 11.5 %collective-permute-start.7 = (bf16[144,256]{1,0:T(8,128)(2,1)S(1)}, bf16[144,256]{1,0:T(8,128)(2,1)S(1)}, u32[]{:S(2)}, u32[]{:S(2)}) collective-permute-start(bf16[144,256]{1,0:T(8,128)(2,1)S(1)} %get-tuple-element.55), channel_id=1, source_target_pairs={{0,12},{1,13},{2,14},{3,15},{4,8},{5,9},{6,10},{7,11},{8,4},{9,5},... | collective-permute-start | bytes 221192 | tf_op jit(solution)/shard_map/ppermute | solution.py:273
  16.9 11.9 %collective-permute-start.2 = (bf16[144,256]{1,0:T(8,128)(2,1)S(1)}, bf16[144,256]{1,0:T(8,128)(2,1)S(1)}, u32[]{:S(2)}, u32[]{:S(2)}) collective-permute-start(bf16[144,256]{1,0:T(8,128)(2,1)S(1)} %get-tuple-element.49), channel_id=1, source_target_pairs={{0,4},{1,5},{2,6},{3,7},{4,0},{5,1},{6,2},{7,3},{8,12},{9,13},{10,... | collective-permute-start | bytes 221192 | tf_op jit(solution)/shard_map/ppermute | solution.py:273
  20.5 8.3 %collective-permute-start.3 = (bf16[144,256]{1,0:T(8,128)(2,1)S(1)}, bf16[144,256]{1,0:T(8,128)(2,1)S(1)}, u32[]{:S(2)}, u32[]{:S(2)}) collective-permute-start(bf16[144,256]{1,0:T(8,128)(2,1)S(1)} %get-tuple-element.50), channel_id=1, source_target_pairs={{0,8},{1,9},{2,10},{3,11},{4,12},{5,13},{6,14},{7,15},{8,0},{9,1},... | collective-permute-start | bytes 221192 | tf_op jit(solution)/shard_map/ppermute | solution.py:273
  24.0 6.3 %collective-permute-start.4 = (bf16[144,256]{1,0:T(8,128)(2,1)S(1)}, bf16[144,256]{1,0:T(8,128)(2,1)S(1)}, u32[]{:S(2)}, u32[]{:S(2)}) collective-permute-start(bf16[144,256]{1,0:T(8,128)(2,1)S(1)} %get-tuple-element.51), channel_id=1, source_target_pairs={{0,12},{1,13},{2,14},{3,15},{4,8},{5,9},{6,10},{7,11},{8,4},{9,5},... | collective-permute-start | bytes 221192 | tf_op jit(solution)/shard_map/ppermute | solution.py:273
  25.4 7.9 %collective-permute-start.9 = (bf16[144,1024]{1,0:T(8,128)(2,1)S(1)}, bf16[144,1024]{1,0:T(8,128)(2,1)S(1)}, u32[]{:S(2)}, u32[]{:S(2)}) collective-permute-start(bf16[144,1024]{1,0:T(8,128)(2,1)S(1)} %shard_map.108.refs_4_), channel_id=1, source_target_pairs={{0,2},{1,3},{2,0},{3,1},{4,6},{5,7},{6,4},{7,5},{8,10},{9,11},{10,... | collective-permute-start | bytes 884744 | tf_op jit(solution)/shard_map/ppermute | solution.py:273
  25.5 10.4 %collective-permute-start.8 = (bf16[144,1024]{1,0:T(8,128)(2,1)S(1)}, bf16[144,1024]{1,0:T(8,128)(2,1)S(1)}, u32[]{:S(2)}, u32[]{:S(2)}) collective-permute-start(bf16[144,1024]{1,0:T(8,128)(2,1)S(1)} %shard_map.108.refs_4_), channel_id=1, source_target_pairs={{0,1},{1,0},{2,3},{3,2},{4,5},{5,4},{6,7},{7,6},{8,9},{9,8},{10,11... | collective-permute-start | bytes 884744 | tf_op jit(solution)/shard_map/ppermute | solution.py:273
  30.3 9.0 %collective-permute-start.10 = (bf16[144,1024]{1,0:T(8,128)(2,1)S(1)}, bf16[144,1024]{1,0:T(8,128)(2,1)S(1)}, u32[]{:S(2)}, u32[]{:S(2)}) collective-permute-start(bf16[144,1024]{1,0:T(8,128)(2,1)S(1)} %shard_map.107.refs_0_), channel_id=1, source_target_pairs={{0,1},{1,0},{2,3},{3,2},{4,5},{5,4},{6,7},{7,6},{8,9},{9,8},{10,11... | collective-permute-start | bytes 884744 | tf_op jit(solution)/shard_map/ppermute | solution.py:273
  31.1 8.7 %collective-permute-start.12 = (bf16[144,1024]{1,0:T(8,128)(2,1)S(1)}, bf16[144,1024]{1,0:T(8,128)(2,1)S(1)}, u32[]{:S(2)}, u32[]{:S(2)}) collective-permute-start(bf16[144,1024]{1,0:T(8,128)(2,1)S(1)} %shard_map.107.refs_0_), channel_id=1, source_target_pairs={{0,2},{1,3},{2,0},{3,1},{4,6},{5,7},{6,4},{7,5},{8,10},{9,11},{10,... | collective-permute-start | bytes 884744 | tf_op jit(solution)/shard_map/ppermute | solution.py:273
  39.3 9.0 %collective-permute-start.14 = (bf16[128,1024]{1,0:T(8,128)(2,1)S(1)}, bf16[128,1024]{1,0:T(8,128)(2,1)S(1)}, u32[]{:S(2)}, u32[]{:S(2)}) collective-permute-start(bf16[128,1024]{1,0:T(8,128)(2,1)S(1)} %shard_map.112), channel_id=1, source_target_pairs={{0,2},{1,3},{2,0},{3,1},{4,6},{5,7},{6,4},{7,5},{8,10},{9,11},{10,... | collective-permute-start | bytes 786440 | tf_op jit(solution)/shard_map/ppermute | solution.py:273
  39.9 9.4 %collective-permute-start.15 = (bf16[160,1024]{1,0:T(8,128)(2,1)S(1)}, bf16[160,1024]{1,0:T(8,128)(2,1)S(1)}, u32[]{:S(2)}, u32[]{:S(2)}) collective-permute-start(bf16[160,1024]{1,0:T(8,128)(2,1)S(1)} %shard_map.113), channel_id=1, source_target_pairs={{0,1},{1,0},{2,3},{3,2},{4,5},{5,4},{6,7},{7,6},{8,9},{9,8},{10,11... | collective-permute-start | bytes 983048 | tf_op jit(solution)/shard_map/ppermute | solution.py:273
  42.5 11.2 %collective-permute-start.11 = (bf16[144,1024]{1,0:T(8,128)(2,1)S(1)}, bf16[144,1024]{1,0:T(8,128)(2,1)S(1)}, u32[]{:S(2)}, u32[]{:S(2)}) collective-permute-start(bf16[144,1024]{1,0:T(8,128)(2,1)S(1)} %get-tuple-element.58), channel_id=1, source_target_pairs={{0,1},{1,0},{2,3},{3,2},{4,5},{5,4},{6,7},{7,6},{8,9},{9,8},{10,11... | collective-permute-start | bytes 884744 | tf_op jit(solution)/shard_map/ppermute | solution.py:273
  44.0 9.8 %collective-permute-start.13 = (bf16[144,1024]{1,0:T(8,128)(2,1)S(1)}, bf16[144,1024]{1,0:T(8,128)(2,1)S(1)}, u32[]{:S(2)}, u32[]{:S(2)}) collective-permute-start(bf16[144,1024]{1,0:T(8,128)(2,1)S(1)} %get-tuple-element.59), channel_id=1, source_target_pairs={{0,2},{1,3},{2,0},{3,1},{4,6},{5,7},{6,4},{7,5},{8,10},{9,11},{10,... | collective-permute-start | bytes 884744 | tf_op jit(solution)/shard_map/ppermute | solution.py:273
  45.7 1.2 %collective-permute-start.16 = (bf16[16,128]{1,0:T(8,128)(2,1)S(1)}, bf16[16,128]{1,0:T(8,128)(2,1)S(1)}, u32[]{:S(2)}, u32[]{:S(2)}) collective-permute-start(bf16[16,128]{1,0:T(8,128)(2,1)S(1)} %slice.3), channel_id=1, source_target_pairs={{0,16},{16,0},{1,17},{17,1},{2,18},{18,2},{3,19},{19,3},{4,20},{20... | collective-permute-start | bytes 12296 | tf_op jit(solution)/shard_map/ppermute | solution.py:289
  50.2 8.6 %collective-permute-start.17 = (bf16[144,1024]{1,0:T(8,128)(2,1)S(1)}, bf16[144,1024]{1,0:T(8,128)(2,1)S(1)}, u32[]{:S(2)}, u32[]{:S(2)}) collective-permute-start(bf16[144,1024]{1,0:T(8,128)(2,1)S(1)} %get-tuple-element.61), channel_id=1, source_target_pairs={{0,3},{1,2},{2,1},{3,0},{4,7},{5,6},{6,5},{7,4},{8,11},{9,10},{10,... | collective-permute-start | bytes 884744 | tf_op jit(solution)/shard_map/ppermute | solution.py:273
  54.8 6.8 %collective-permute-start.21 = (bf16[128,1024]{1,0:T(8,128)(2,1)S(1)}, bf16[128,1024]{1,0:T(8,128)(2,1)S(1)}, u32[]{:S(2)}, u32[]{:S(2)}) collective-permute-start(bf16[128,1024]{1,0:T(8,128)(2,1)S(1)} %get-tuple-element.68), channel_id=1, source_target_pairs={{0,16},{16,0},{1,17},{17,1},{2,18},{18,2},{3,19},{19,3},{4,20},{20... | collective-permute-start | bytes 786440 | tf_op jit(solution)/shard_map/ppermute | solution.py:380
  54.9 6.8 %collective-permute-start.22 = (bf16[128,1024]{1,0:T(8,128)(2,1)S(1)}, bf16[128,1024]{1,0:T(8,128)(2,1)S(1)}, u32[]{:S(2)}, u32[]{:S(2)}) collective-permute-start(bf16[128,1024]{1,0:T(8,128)(2,1)S(1)} %get-tuple-element.69), channel_id=1, source_target_pairs={{0,16},{16,0},{1,17},{17,1},{2,18},{18,2},{3,19},{19,3},{4,20},{20... | collective-permute-start | bytes 786440 | tf_op jit(solution)/shard_map/ppermute | solution.py:380
  55.4 8.1 %collective-permute-start.23 = (bf16[128,1024]{1,0:T(8,128)(2,1)S(1)}, bf16[128,1024]{1,0:T(8,128)(2,1)S(1)}, u32[]{:S(2)}, u32[]{:S(2)}) collective-permute-start(bf16[128,1024]{1,0:T(8,128)(2,1)S(1)} %get-tuple-element.70), channel_id=1, source_target_pairs={{0,16},{16,0},{1,17},{17,1},{2,18},{18,2},{3,19},{19,3},{4,20},{20... | collective-permute-start | bytes 786440 | tf_op jit(solution)/shard_map/ppermute | solution.py:380
  55.5 8.0 %collective-permute-start.24 = (bf16[128,1024]{1,0:T(8,128)(2,1)S(1)}, bf16[128,1024]{1,0:T(8,128)(2,1)S(1)}, u32[]{:S(2)}, u32[]{:S(2)}) collective-permute-start(bf16[128,1024]{1,0:T(8,128)(2,1)S(1)} %get-tuple-element.71), channel_id=1, source_target_pairs={{0,16},{16,0},{1,17},{17,1},{2,18},{18,2},{3,19},{19,3},{4,20},{20... | collective-permute-start | bytes 786440 | tf_op jit(solution)/shard_map/ppermute | solution.py:380
  59.0 6.5 %collective-permute-start.18 = (bf16[144,256]{1,0:T(8,128)(2,1)S(1)}, bf16[144,256]{1,0:T(8,128)(2,1)S(1)}, u32[]{:S(2)}, u32[]{:S(2)}) collective-permute-start(bf16[144,256]{1,0:T(8,128)(2,1)S(1)} %get-tuple-element.63), channel_id=1, source_target_pairs={{0,12},{1,13},{2,14},{3,15},{4,8},{5,9},{6,10},{7,11},{8,4},{9,5},... | collective-permute-start | bytes 221192 | tf_op jit(solution)/shard_map/ppermute | solution.py:273
  61.6 5.3 %collective-permute-start.19 = (bf16[144,256]{1,0:T(8,128)(2,1)S(1)}, bf16[144,256]{1,0:T(8,128)(2,1)S(1)}, u32[]{:S(2)}, u32[]{:S(2)}) collective-permute-start(bf16[144,256]{1,0:T(8,128)(2,1)S(1)} %get-tuple-element.64), channel_id=1, source_target_pairs={{0,8},{1,9},{2,10},{3,11},{4,12},{5,13},{6,14},{7,15},{8,0},{9,1},... | collective-permute-start | bytes 221192 | tf_op jit(solution)/shard_map/ppermute | solution.py:273
  61.7 5.2 %collective-permute-start.20 = (bf16[144,256]{1,0:T(8,128)(2,1)S(1)}, bf16[144,256]{1,0:T(8,128)(2,1)S(1)}, u32[]{:S(2)}, u32[]{:S(2)}) collective-permute-start(bf16[144,256]{1,0:T(8,128)(2,1)S(1)} %get-tuple-element.65), channel_id=1, source_target_pairs={{0,4},{1,5},{2,6},{3,7},{4,0},{5,1},{6,2},{7,3},{8,12},{9,13},{10,... | collective-permute-start | bytes 221192 | tf_op jit(solution)/shard_map/ppermute | solution.py:273

commit v10 on v8

--- a/solution.py
+++ b/solution.py
@@ -364,7 +364,7 @@
             expert_body,
             [out(plane_rows, hidden_units), out(plane_rows, features)],
             vmem=(*pieces, in_here, out_here),
-            after=(*first, *hiddens[:1], *[of_other_core(h) for h in hiddens[2:]]),
+            after=(*first, *hiddens[:1], *[of_other_core(h) for h in hiddens[:1] if len(hiddens) > 2]),
             flops=4 * plane_rows * features * hidden_units,
         )
         hiddens.append(hidden)

time: 68 us -> 68 us (level)
  no operation moved by 1% of the time
where the time goes in v10:
time: 68 us; the launch traced here: 67.8 us
  starting transfers between devices  34.9 us (51%)
  waiting for transfers between devices  20.6 us (30%)
  Pallas kernels  11.5 us (17%)
  between operations  0.78 us (1%)
    ppermute x19, starting transfers between devices, permute(): lax.ppermute(value, 'ep', [(i, i ^ apart) for i in range(lax.axis_size('e...  33.1 us
    ppermute x19, waiting for transfers between devices, permute(): lax.ppermute(value, 'ep', [(i, i ^ apart) for i in range(lax.axis_size('e...  19.4 us
    pallas_call x15, Pallas kernels, call(): pl.pallas_call(kernel, out_shape=outs, in_specs=[VMEM] * len(vmem) + [HBM...  11.5 us
  transfers between devices with their start and end apart: 25, of which 11 were waited for; matrix products, arithmetic and copies ran while one was open for 0% of the time, Pallas kernels for 14%

profile of v10, /device:TPU:0, one launch (start us, length us, event | category | flops | bytes accessed | tf_op | source)
XLA Modules:
  0.0 67.8 jit_solution(18175508808666401451)
XLA Ops:
  0.6 1.3 %shard_map.104 = (bf16[1040,128]{1,0:T(8,128)(2,1)S(1)}, bf16[1040,128]{1,0:T(8,128)(2,1)S(1)}, bf16[1,128,1024]{2,1,0:T(8,128)(2,1)S(1)}, bf16[1,128,1024]{2,1,0:T(8,128)(2,1)S(1)}, s32[1,128]{1,0:T(1,128)S(1)}) custom-call(bf16[1,128,1024]{2,1,0:T(8,128)(2,1)} %refs_0_.2, bf16[1,128,1024]{2,1,0:T(8,128)(2,1)} %refs_1_.4, s32[1,128]{1,0:T(1,128)} %refs_2_.3), custom_call_target="tpu_custom_call" | custom-call | bytes 1582080 | tf_op jit(solution)/shard_map/pallas_call | solution.py:35
  2.0 3.0 %collective-permute-start = (bf16[1040,128]{1,0:T(8,128)(2,1)S(1)}, bf16[1040,128]{1,0:T(8,128)(2,1)S(1)}, u32[]{:S(2)}, u32[]{:S(2)}) collective-permute-start(bf16[1040,128]{1,0:T(8,128)(2,1)S(1)} %get-tuple-element.43), channel_id=1, source_target_pairs={{0,1},{1,0},{2,3},{3,2},{4,5},{5,4},{6,7},{7,6},{8,9},{9,8},{10,11... | collective-permute-start | bytes 798728 | tf_op jit(solution)/shard_map/ppermute | solution.py:275
  5.7 1.2 %shard_map.105 = (bf16[144,128]{1,0:T(8,128)(2,1)S(1)}, bf16[128,144]{1,0:T(8,128)(2,1)S(1)}, bf16[1,128,1024]{2,1,0:T(8,128)(2,1)S(1)}, bf16[1,128,1024]{2,1,0:...) custom-call(bf16[1,128,1024]{2,1,0:T(8,128)(2,1)} %refs_0_.3, ...), custom_call_target="tpu_custom_call" | custom-call | tf_op jit(solution)/shard_map/pallas_call | solution.py:35
  7.0 5.3 %collective-permute-start.5 = (bf16[144,256]{1,0:T(8,128)(2,1)S(1)}, bf16[144,256]{1,0:T(8,128)(2,1)S(1)}, u32[]{:S(2)}, u32[]{:S(2)}) collective-permute-start(bf16[144,256]{1,0:T(8,128)(2,1)S(1)} %get-tuple-element.53), channel_id=1, source_target_pairs={{0,8},{1,9},{2,10},{3,11},{4,12},{5,13},{6,14},{7,15},{8,0},{9,1},... | collective-permute-start | bytes 221192 | tf_op jit(solution)/shard_map/ppermute | solution.py:275
  12.3 1.6 %collective-permute-start.6 = (bf16[144,256]{1,0:T(8,128)(2,1)S(1)}, bf16[144,256]{1,0:T(8,128)(2,1)S(1)}, u32[]{:S(2)}, u32[]{:S(2)}) collective-permute-start(bf16[144,256]{1,0:T(8,128)(2,1)S(1)} %get-tuple-element.54), channel_id=1, source_target_pairs={{0,4},{1,5},{2,6},{3,7},{4,0},{5,1},{6,2},{7,3},{8,12},{9,13},{10,... | collective-permute-start | bytes 221192 | tf_op jit(solution)/shard_map/ppermute | solution.py:275
  13.9 2.2 %collective-permute-done.refs_5_ = bf16[1040,128]{1,0:T(8,128)(2,1)S(1)} collective-permute-done((bf16[1040,128]{1,0:T(8,128)(2,1)S(1)}, bf16[1040,128]{1,0:T(8,128)(2,1)S(1)}, u32[]{:S(2)}, u32[]{:S(2)}) %collective-permute-start) | collective-permute-done | bytes 266272 | tf_op jit(solution)/shard_map/ppermute | solution.py:275
  16.9 3.6 %collective-permute-start.2 = (bf16[144,256]{1,0:T(8,128)(2,1)S(1)}, bf16[144,256]{1,0:T(8,128)(2,1)S(1)}, u32[]{:S(2)}, u32[]{:S(2)}) collective-permute-start(bf16[144,256]{1,0:T(8,128)(2,1)S(1)} %get-tuple-element.49), channel_id=1, source_target_pairs={{0,4},{1,5},{2,6},{3,7},{4,0},{5,1},{6,2},{7,3},{8,12},{9,13},{10,... | collective-permute-start | bytes 221192 | tf_op jit(solution)/shard_map/ppermute | solution.py:275
  20.5 3.5 %collective-permute-start.3 = (bf16[144,256]{1,0:T(8,128)(2,1)S(1)}, bf16[144,256]{1,0:T(8,128)(2,1)S(1)}, u32[]{:S(2)}, u32[]{:S(2)}) collective-permute-start(bf16[144,256]{1,0:T(8,128)(2,1)S(1)} %get-tuple-element.50), channel_id=1, source_target_pairs={{0,8},{1,9},{2,10},{3,11},{4,12},{5,13},{6,14},{7,15},{8,0},{9,1},... | collective-permute-start | bytes 221192 | tf_op jit(solution)/shard_map/ppermute | solution.py:275
  24.0 1.4 %collective-permute-start.4 = (bf16[144,256]{1,0:T(8,128)(2,1)S(1)}, bf16[144,256]{1,0:T(8,128)(2,1)S(1)}, u32[]{:S(2)}, u32[]{:S(2)}) collective-permute-start(bf16[144,256]{1,0:T(8,128)(2,1)S(1)} %get-tuple-element.51), channel_id=1, source_target_pairs={{0,12},{1,13},{2,14},{3,15},{4,8},{5,9},{6,10},{7,11},{8,4},{9,5},... | collective-permute-start | bytes 221192 | tf_op jit(solution)/shard_map/ppermute | solution.py:275
  25.5 3.3 %collective-permute-start.8 = (bf16[144,1024]{1,0:T(8,128)(2,1)S(1)}, bf16[144,1024]{1,0:T(8,128)(2,1)S(1)}, u32[]{:S(2)}, u32[]{:S(2)}) collective-permute-start(bf16[144,1024]{1,0:T(8,128)(2,1)S(1)} %shard_map.108.refs_4_), channel_id=1, source_target_pairs={{0,1},{1,0},{2,3},{3,2},{4,5},{5,4},{6,7},{7,6},{8,9},{9,8},{10,11... | collective-permute-start | bytes 884744 | tf_op jit(solution)/shard_map/ppermute | solution.py:275
  28.8 1.4 %collective-permute-done.4.refs_3_ = bf16[144,256]{1,0:T(8,128)(2,1)S(1)} collective-permute-done((bf16[144,256]{1,0:T(8,128)(2,1)S(1)}, bf16[144,256]{1,0:T(8,128)(2,1)S(1)}, u32[]{:S(2)}, u32[]{:S(2)}) %collective-permute-start.4) | collective-permute-done | bytes 73760 | tf_op jit(solution)/shard_map/ppermute | solution.py:275
  31.1 2.1 %collective-permute-done.9.refs_4_.refs_1_.refs_6_ = bf16[144,1024]{1,0:T(8,128)(2,1)S(1)} collective-permute-done((bf16[144,1024]{1,0:T(8,128)(2,1)S(1)}, bf16[144,1024]{1,0:T(8,128)(2,1)S(1)}, u32[]{:S(2)}, u32[]{:S(2)}) %collective-permute-start.9) | collective-permute-done | bytes 294944 | tf_op jit(solution)/shard_map/ppermute | solution.py:275
  33.3 2.6 %collective-permute-done.8.refs_3_.refs_1_.refs_5_ = bf16[144,1024]{1,0:T(8,128)(2,1)S(1)} collective-permute-done((bf16[144,1024]{1,0:T(8,128)(2,1)S(1)}, bf16[144,1024]{1,0:T(8,128)(2,1)S(1)}, u32[]{:S(2)}, u32[]{:S(2)}) %collective-permute-start.8) | collective-permute-done | bytes 294944 | tf_op jit(solution)/shard_map/ppermute | solution.py:275
  35.9 1.0 %shard_map.109 = (bf16[144,1024]{1,0:T(8,128)(2,1)S(1)}, bf16[144,1024]{1,0:T(8,128)(2,1)S(1)}) custom-call(bf16[144,1024]{1,0:T(8,128)(2,1)S(1)} %shard_map.107.refs_0_, bf16[1024,1024]{1,0:T(8,128)(2,1)S(1)} %copy-done, bf16[1024,1024]{1,0:T(8,128)(2,1)S(1)} %bitcast.2, bf16[144,1024]{1,0:T(8,128)(2,1)S(1)} %collective-permute-done.8.refs_3_.refs_1_.refs_5_, ...), custom_call_target="tpu_custom_call" | custom-call | flops 603979776 | bytes 5079040 | tf_op jit(solution)/shard_map/pallas_call | solution.py:35
  36.9 2.4 %collective-permute-done.10.refs_0_ = bf16[144,1024]{1,0:T(8,128)(2,1)S(1)} collective-permute-done((bf16[144,1024]{1,0:T(8,128)(2,1)S(1)}, bf16[144,1024]{1,0:T(8,128)(2,1)S(1)}, u32[]{:S(2)}, u32[]{:S(2)}) %collective-permute-start.10) | collective-permute-done | bytes 294944 | tf_op jit(solution)/shard_map/ppermute | solution.py:275
  39.9 1.7 %collective-permute-start.15 = (bf16[160,1024]{1,0:T(8,128)(2,1)S(1)}, bf16[160,1024]{1,0:T(8,128)(2,1)S(1)}, u32[]{:S(2)}, u32[]{:S(2)}) collective-permute-start(bf16[160,1024]{1,0:T(8,128)(2,1)S(1)} %shard_map.113), channel_id=1, source_target_pairs={{0,1},{1,0},{2,3},{3,2},{4,5},{5,4},{6,7},{7,6},{8,9},{9,8},{10,11... | collective-permute-start | bytes 983048 | tf_op jit(solution)/shard_map/ppermute | solution.py:275
  41.5 1.0 %shard_map.110 = (bf16[144,1024]{1,0:T(8,128)(2,1)S(1)}, bf16[144,1024]{1,0:T(8,128)(2,1)S(1)}) custom-call(bf16[144,1024]{1,0:T(8,128)(2,1)S(1)} %collective-permute-done.10.refs_0_, bf16[1024,1024]{1,0:T(8,128)(2,1)S(1)} %copy-done, bf16[1024,1024]{1,0:T(8,128)(2,1)S(1)} %bitcast.3, bf16[144,1024]{1,0:T(8,128)(2,1)S(1)} %get-tuple-element.57.refs_3_.refs_4_.refs_0_), custom_call_target="tpu_custom_call" | custom-call | flops 603979776 | bytes 5079040 | tf_op jit(solution)/shard_map/pallas_call | solution.py:35
  43.0 1.0 %shard_map.111 = (bf16[144,1024]{1,0:T(8,128)(2,1)S(1)}, bf16[144,1024]{1,0:T(8,128)(2,1)S(1)}) custom-call(bf16[144,1024]{1,0:T(8,128)(2,1)S(1)} %collective-permute-done.12.refs_0_, bf16[1024,1024]{1,0:T(8,128)(2,1)S(1)} %copy-done, bf16[1024,1024]{1,0:T(8,128)(2,1)S(1)} %bitcast.4, bf16[144,1024]{1,0:T(8,128)(2,1)S(1)} %get-tuple-element.57.refs_3_.refs_4_.refs_0_), custom_call_target="tpu_custom_call" | custom-call | flops 603979776 | bytes 5079040 | tf_op jit(solution)/shard_map/pallas_call | solution.py:35
  44.0 1.7 %collective-permute-start.13 = (bf16[144,1024]{1,0:T(8,128)(2,1)S(1)}, bf16[144,1024]{1,0:T(8,128)(2,1)S(1)}, u32[]{:S(2)}, u32[]{:S(2)}) collective-permute-start(bf16[144,1024]{1,0:T(8,128)(2,1)S(1)} %get-tuple-element.59), channel_id=1, source_target_pairs={{0,2},{1,3},{2,0},{3,1},{4,6},{5,7},{6,4},{7,5},{8,10},{9,11},{10,... | collective-permute-start | bytes 884744 | tf_op jit(solution)/shard_map/ppermute | solution.py:275
  45.7 1.2 %collective-permute-done.16.refs_5_ = bf16[16,128]{1,0:T(8,128)(2,1)S(1)} collective-permute-done((bf16[16,128]{1,0:T(8,128)(2,1)S(1)}, bf16[16,128]{1,0:T(8,128)(2,1)S(1)}, u32[]{:S(2)}, u32[]{:S(2)}) %collective-permute-start.16) | collective-permute-done | bytes 4128 | tf_op jit(solution)/shard_map/ppermute | solution.py:291
  46.8 1.5 %collective-permute-done.14.refs_0_.refs_7_ = bf16[128,1024]{1,0:T(8,128)(2,1)S(1)} collective-permute-done((bf16[128,1024]{1,0:T(8,128)(2,1)S(1)}, bf16[128,1024]{1,0:T(8,128)(2,1)S(1)}, u32[]{:S(2)}, u32[]{:S(2)}) %collective-permute-start.14) | collective-permute-done | bytes 262176 | tf_op jit(solution)/shard_map/ppermute | solution.py:275
  48.3 0.9 %collective-permute-done.15.refs_1_.refs_8_ = bf16[160,1024]{1,0:T(8,128)(2,1)S(1)} collective-permute-done((bf16[160,1024]{1,0:T(8,128)(2,1)S(1)}, bf16[160,1024]{1,0:T(8,128)(2,1)S(1)}, u32[]{:S(2)}, u32[]{:S(2)}) %collective-permute-start.15) | collective-permute-done | bytes 327712 | tf_op jit(solution)/shard_map/ppermute | solution.py:275
  49.2 1.0 %shard_map.114 = (bf16[144,1024]{1,0:T(8,128)(2,1)S(1)}, bf16[144,1024]{1,0:T(8,128)(2,1)S(1)}) custom-call(bf16[128,1024]{1,0:T(8,128)(2,1)S(1)} %collective-permute-done.14.refs_0_.refs_7_, bf16[160,1024]{1,0:T(8,128)(2,1)S(1)} %collective-permute-done.15.refs_1_.refs_8_, bf16[1024,1024]{1,0:T(8,128)(2,1)S(1)} %copy-done, bf16[1024,1024]{1,0:T(8,128)(2,1)S(1)} %bitcast.5, ...), custom_call_target="tpu_custom_call" | custom-call | flops 603979776 | bytes 5373952 | tf_op jit(solution)/shard_map/pallas_call | solution.py:35
  50.2 1.6 %collective-permute-start.17 = (bf16[144,1024]{1,0:T(8,128)(2,1)S(1)}, bf16[144,1024]{1,0:T(8,128)(2,1)S(1)}, u32[]{:S(2)}, u32[]{:S(2)}) collective-permute-start(bf16[144,1024]{1,0:T(8,128)(2,1)S(1)} %get-tuple-element.60), channel_id=1, source_target_pairs={{0,3},{1,2},{2,1},{3,0},{4,7},{5,6},{6,5},{7,4},{8,11},{9,10},{10,... | collective-permute-start | bytes 884744 | tf_op jit(solution)/shard_map/ppermute | solution.py:275
  51.8 1.9 %collective-permute-done.11.refs_1_.refs_9_ = bf16[144,1024]{1,0:T(8,128)(2,1)S(1)} collective-permute-done((bf16[144,1024]{1,0:T(8,128)(2,1)S(1)}, bf16[144,1024]{1,0:T(8,128)(2,1)S(1)}, u32[]{:S(2)}, u32[]{:S(2)}) %collective-permute-start.11) | collective-permute-done | bytes 294944 | tf_op jit(solution)/shard_map/ppermute | solution.py:275
  53.8 1.0 %shard_map.116 = (bf16[128,1024]{1,0:T(8,128)(2,1)S(1)}, bf16[128,1024]{1,0:T(8,128)(2,1)S(1)}, bf16[128,1024]{1,0:T(8,128)(2,1)S(1)}, bf16[128,1024]{1,0:T(8,128)(2,1)S(1)}) custom-call(bf16[144,1024]{1,0:T(8,128)(2,1)S(1)} %get-tuple-element.57.refs_3_.refs_4_.refs_0_, bf16[144,1024]{1,0:T(8,128)(2,1)S(1)} %get-tuple-element.65.refs_1_, ...), custom_call_target="tpu_custom_call" | custom-call | flops 603979776 | bytes 3702784 | tf_op jit(solution)/shard_map/pallas_call | solution.py:35
  55.9 3.0 %collective-permute-done.17.refs_3_ = bf16[144,1024]{1,0:T(8,128)(2,1)S(1)} collective-permute-done((bf16[144,1024]{1,0:T(8,128)(2,1)S(1)}, bf16[144,1024]{1,0:T(8,128)(2,1)S(1)}, u32[]{:S(2)}, u32[]{:S(2)}) %collective-permute-start.17) | collective-permute-done | bytes 294944 | tf_op jit(solution)/shard_map/ppermute | solution.py:275
  59.0 2.6 %collective-permute-start.18 = (bf16[144,256]{1,0:T(8,128)(2,1)S(1)}, bf16[144,256]{1,0:T(8,128)(2,1)S(1)}, u32[]{:S(2)}, u32[]{:S(2)}) collective-permute-start(bf16[144,256]{1,0:T(8,128)(2,1)S(1)} %get-tuple-element.62), channel_id=1, source_target_pairs={{0,12},{1,13},{2,14},{3,15},{4,8},{5,9},{6,10},{7,11},{8,4},{9,5},... | collective-permute-start | bytes 221192 | tf_op jit(solution)/shard_map/ppermute | solution.py:275
  61.7 1.8 %collective-permute-start.20 = (bf16[144,256]{1,0:T(8,128)(2,1)S(1)}, bf16[144,256]{1,0:T(8,128)(2,1)S(1)}, u32[]{:S(2)}, u32[]{:S(2)}) collective-permute-start(bf16[144,256]{1,0:T(8,128)(2,1)S(1)} %get-tuple-element.64), channel_id=1, source_target_pairs={{0,4},{1,5},{2,6},{3,7},{4,0},{5,1},{6,2},{7,3},{8,12},{9,13},{10,... | collective-permute-start | bytes 221192 | tf_op jit(solution)/shard_map/ppermute | solution.py:275
  63.5 2.0 %shard_map.117 = (bf16[1,512,1024]{2,1,0:T(8,128)(2,1)}, f32[8,128]{1,0:T(8,128)S(1)}) custom-call(bf16[144,1024]{1,0:T(8,128)(2,1)S(1)} %get-tuple-element.57.refs_3_.refs_4_.refs_0_, bf16[144,1024]{1,0:T(8,128)(2,1)S(1)} %get-tuple-element.65.refs_1_, bf16[144,1024]{1,0:T(8,128)(2,1)S(1)} %get-tuple-element.66.refs_2_, ...), custom_call_target="tpu_custom_call" | custom-call | flops 603979776 | bytes 4755456 | tf_op jit(solution)/shard_map/pallas_call | solution.py:35
  65.5 1.4 %collective-permute-done.19.refs_4_ = bf16[144,256]{1,0:T(8,128)(2,1)S(1)} collective-permute-done((bf16[144,256]{1,0:T(8,128)(2,1)S(1)}, bf16[144,256]{1,0:T(8,128)(2,1)S(1)}, u32[]{:S(2)}, u32[]{:S(2)}) %collective-permute-start.19) | collective-permute-done | bytes 73760 | tf_op jit(solution)/shard_map/ppermute | solution.py:275
  66.9 0.9 %shard_map.118 = bf16[1,128,1024]{2,1,0:T(8,128)(2,1)} custom-call(bf16[128,1024]{1,0:T(8,128)(2,1)S(1)} %get-tuple-element.46.refs_4_.refs_0_, bf16[128,144]{1,0:T(8,128)(2,1)S(1)} %get-tuple-element.47.refs_1_, bf16[144,256]{1,0:T(8,128)(2,1)S(1)} %get-tuple-element.61.refs_2_, bf16[144,256]{1,0:T(8,128)(2,1)S(1)} %collective-permute-done.18.refs_3_, ...), custom_call_target="tpu_custom_call" | custom-call | bytes 856064 | tf_op jit(solution)/shard_map/pallas_call | solution.py:35
  (38 shorter events, 5.0 us)
Async XLA Ops:
  0.6 35.2 %copy-start.1 = (bf16[1,1024,1024]{2,1,0:T(8,128)(2,1)S(1)}, bf16[1,1024,1024]{2,1,0:T(8,128)(2,1)}, u32[]{:S(2)}) copy-start(bf16[1,1024,1024]{2,1,0:T(8,128)(2,1)} %param.17) | copy-start | bytes 6291460
  2.0 33.9 %copy-start = (bf16[1024,1024]{1,0:T(8,128)(2,1)S(1)}, bf16[1024,1024]{1,0:T(8,128)(2,1)}, u32[]{:S(2)}) copy-start(bf16[1024,1024]{1,0:T(8,128)(2,1)} %refs_2_.5) | copy-start | bytes 6291460
  2.0 14.1 %collective-permute-start = (bf16[1040,128]{1,0:T(8,128)(2,1)S(1)}, bf16[1040,128]{1,0:T(8,128)(2,1)S(1)}, u32[]{:S(2)}, u32[]{:S(2)}) collective-permute-start(bf16[1040,128]{1,0:T(8,128)(2,1)S(1)} %get-tuple-element.43), channel_id=1, source_target_pairs={{0,1},{1,0},{2,3},{3,2},{4,5},{5,4},{6,7},{7,6},{8,9},{9,8},{10,11... | collective-permute-start | bytes 798728 | tf_op jit(solution)/shard_map/ppermute | solution.py:275
  5.0 11.0 %collective-permute-start.1 = (bf16[1040,128]{1,0:T(8,128)(2,1)S(1)}, bf16[1040,128]{1,0:T(8,128)(2,1)S(1)}, u32[]{:S(2)}, u32[]{:S(2)}) collective-permute-start(bf16[1040,128]{1,0:T(8,128)(2,1)S(1)} %get-tuple-element.44), channel_id=1, source_target_pairs={{1,2},{3,4},{5,6},{7,8},{9,10},{11,12},{13,14},{2,1},{4,3},{6,5},{... | collective-permute-start | bytes 798728 | tf_op jit(solution)/shard_map/ppermute | solution.py:324
  7.0 17.0 %collective-permute-start.5 = (bf16[144,256]{1,0:T(8,128)(2,1)S(1)}, bf16[144,256]{1,0:T(8,128)(2,1)S(1)}, u32[]{:S(2)}, u32[]{:S(2)}) collective-permute-start(bf16[144,256]{1,0:T(8,128)(2,1)S(1)} %get-tuple-element.53), channel_id=1, source_target_pairs={{0,8},{1,9},{2,10},{3,11},{4,12},{5,13},{6,14},{7,15},{8,0},{9,1},... | collective-permute-start | bytes 221192 | tf_op jit(solution)/shard_map/ppermute | solution.py:275
  12.3 13.1 %collective-permute-start.6 = (bf16[144,256]{1,0:T(8,128)(2,1)S(1)}, bf16[144,256]{1,0:T(8,128)(2,1)S(1)}, u32[]{:S(2)}, u32[]{:S(2)}) collective-permute-start(bf16[144,256]{1,0:T(8,128)(2,1)S(1)} %get-tuple-element.54), channel_id=1, source_target_pairs={{0,4},{1,5},{2,6},{3,7},{4,0},{5,1},{6,2},{7,3},{8,12},{9,13},{10,... | collective-permute-start | bytes 221192 | tf_op jit(solution)/shard_map/ppermute | solution.py:275
  13.9 11.5 %collective-permute-start.7 = (bf16[144,256]{1,0:T(8,128)(2,1)S(1)}, bf16[144,256]{1,0:T(8,128)(2,1)S(1)}, u32[]{:S(2)}, u32[]{:S(2)}) collective-permute-start(bf16[144,256]{1,0:T(8,128)(2,1)S(1)} %get-tuple-element.55), channel_id=1, source_target_pairs={{0,12},{1,13},{2,14},{3,15},{4,8},{5,9},{6,10},{7,11},{8,4},{9,5},... | collective-permute-start | bytes 221192 | tf_op jit(solution)/shard_map/ppermute | solution.py:275
  16.9 11.9 %collective-permute-start.2 = (bf16[144,256]{1,0:T(8,128)(2,1)S(1)}, bf16[144,256]{1,0:T(8,128)(2,1)S(1)}, u32[]{:S(2)}, u32[]{:S(2)}) collective-permute-start(bf16[144,256]{1,0:T(8,128)(2,1)S(1)} %get-tuple-element.49), channel_id=1, source_target_pairs={{0,4},{1,5},{2,6},{3,7},{4,0},{5,1},{6,2},{7,3},{8,12},{9,13},{10,... | collective-permute-start | bytes 221192 | tf_op jit(solution)/shard_map/ppermute | solution.py:275
  20.5 8.3 %collective-permute-start.3 = (bf16[144,256]{1,0:T(8,128)(2,1)S(1)}, bf16[144,256]{1,0:T(8,128)(2,1)S(1)}, u32[]{:S(2)}, u32[]{:S(2)}) collective-permute-start(bf16[144,256]{1,0:T(8,128)(2,1)S(1)} %get-tuple-element.50), channel_id=1, source_target_pairs={{0,8},{1,9},{2,10},{3,11},{4,12},{5,13},{6,14},{7,15},{8,0},{9,1},... | collective-permute-start | bytes 221192 | tf_op jit(solution)/shard_map/ppermute | solution.py:275
  24.0 6.3 %collective-permute-start.4 = (bf16[144,256]{1,0:T(8,128)(2,1)S(1)}, bf16[144,256]{1,0:T(8,128)(2,1)S(1)}, u32[]{:S(2)}, u32[]{:S(2)}) collective-permute-start(bf16[144,256]{1,0:T(8,128)(2,1)S(1)} %get-tuple-element.51), channel_id=1, source_target_pairs={{0,12},{1,13},{2,14},{3,15},{4,8},{5,9},{6,10},{7,11},{8,4},{9,5},... | collective-permute-start | bytes 221192 | tf_op jit(solution)/shard_map/ppermute | solution.py:275
  25.4 7.9 %collective-permute-start.9 = (bf16[144,1024]{1,0:T(8,128)(2,1)S(1)}, bf16[144,1024]{1,0:T(8,128)(2,1)S(1)}, u32[]{:S(2)}, u32[]{:S(2)}) collective-permute-start(bf16[144,1024]{1,0:T(8,128)(2,1)S(1)} %shard_map.108.refs_4_), channel_id=1, source_target_pairs={{0,2},{1,3},{2,0},{3,1},{4,6},{5,7},{6,4},{7,5},{8,10},{9,11},{10,... | collective-permute-start | bytes 884744 | tf_op jit(solution)/shard_map/ppermute | solution.py:275
  25.5 10.4 %collective-permute-start.8 = (bf16[144,1024]{1,0:T(8,128)(2,1)S(1)}, bf16[144,1024]{1,0:T(8,128)(2,1)S(1)}, u32[]{:S(2)}, u32[]{:S(2)}) collective-permute-start(bf16[144,1024]{1,0:T(8,128)(2,1)S(1)} %shard_map.108.refs_4_), channel_id=1, source_target_pairs={{0,1},{1,0},{2,3},{3,2},{4,5},{5,4},{6,7},{7,6},{8,9},{9,8},{10,11... | collective-permute-start | bytes 884744 | tf_op jit(solution)/shard_map/ppermute | solution.py:275
  30.3 9.0 %collective-permute-start.10 = (bf16[144,1024]{1,0:T(8,128)(2,1)S(1)}, bf16[144,1024]{1,0:T(8,128)(2,1)S(1)}, u32[]{:S(2)}, u32[]{:S(2)}) collective-permute-start(bf16[144,1024]{1,0:T(8,128)(2,1)S(1)} %shard_map.107.refs_0_), channel_id=1, source_target_pairs={{0,1},{1,0},{2,3},{3,2},{4,5},{5,4},{6,7},{7,6},{8,9},{9,8},{10,11... | collective-permute-start | bytes 884744 | tf_op jit(solution)/shard_map/ppermute | solution.py:275
  31.1 8.7 %collective-permute-start.12 = (bf16[144,1024]{1,0:T(8,128)(2,1)S(1)}, bf16[144,1024]{1,0:T(8,128)(2,1)S(1)}, u32[]{:S(2)}, u32[]{:S(2)}) collective-permute-start(bf16[144,1024]{1,0:T(8,128)(2,1)S(1)} %shard_map.107.refs_0_), channel_id=1, source_target_pairs={{0,2},{1,3},{2,0},{3,1},{4,6},{5,7},{6,4},{7,5},{8,10},{9,11},{10,... | collective-permute-start | bytes 884744 | tf_op jit(solution)/shard_map/ppermute | solution.py:275
  39.3 9.0 %collective-permute-start.14 = (bf16[128,1024]{1,0:T(8,128)(2,1)S(1)}, bf16[128,1024]{1,0:T(8,128)(2,1)S(1)}, u32[]{:S(2)}, u32[]{:S(2)}) collective-permute-start(bf16[128,1024]{1,0:T(8,128)(2,1)S(1)} %shard_map.112), channel_id=1, source_target_pairs={{0,2},{1,3},{2,0},{3,1},{4,6},{5,7},{6,4},{7,5},{8,10},{9,11},{10,... | collective-permute-start | bytes 786440 | tf_op jit(solution)/shard_map/ppermute | solution.py:275
  39.9 9.4 %collective-permute-start.15 = (bf16[160,1024]{1,0:T(8,128)(2,1)S(1)}, bf16[160,1024]{1,0:T(8,128)(2,1)S(1)}, u32[]{:S(2)}, u32[]{:S(2)}) collective-permute-start(bf16[160,1024]{1,0:T(8,128)(2,1)S(1)} %shard_map.113), channel_id=1, source_target_pairs={{0,1},{1,0},{2,3},{3,2},{4,5},{5,4},{6,7},{7,6},{8,9},{9,8},{10,11... | collective-permute-start | bytes 983048 | tf_op jit(solution)/shard_map/ppermute | solution.py:275
  42.5 11.3 %collective-permute-start.11 = (bf16[144,1024]{1,0:T(8,128)(2,1)S(1)}, bf16[144,1024]{1,0:T(8,128)(2,1)S(1)}, u32[]{:S(2)}, u32[]{:S(2)}) collective-permute-start(bf16[144,1024]{1,0:T(8,128)(2,1)S(1)} %get-tuple-element.58), channel_id=1, source_target_pairs={{0,1},{1,0},{2,3},{3,2},{4,5},{5,4},{6,7},{7,6},{8,9},{9,8},{10,11... | collective-permute-start | bytes 884744 | tf_op jit(solution)/shard_map/ppermute | solution.py:275
  44.0 9.8 %collective-permute-start.13 = (bf16[144,1024]{1,0:T(8,128)(2,1)S(1)}, bf16[144,1024]{1,0:T(8,128)(2,1)S(1)}, u32[]{:S(2)}, u32[]{:S(2)}) collective-permute-start(bf16[144,1024]{1,0:T(8,128)(2,1)S(1)} %get-tuple-element.59), channel_id=1, source_target_pairs={{0,2},{1,3},{2,0},{3,1},{4,6},{5,7},{6,4},{7,5},{8,10},{9,11},{10,... | collective-permute-start | bytes 884744 | tf_op jit(solution)/shard_map/ppermute | solution.py:275
  45.7 1.2 %collective-permute-start.16 = (bf16[16,128]{1,0:T(8,128)(2,1)S(1)}, bf16[16,128]{1,0:T(8,128)(2,1)S(1)}, u32[]{:S(2)}, u32[]{:S(2)}) collective-permute-start(bf16[16,128]{1,0:T(8,128)(2,1)S(1)} %slice.3), channel_id=1, source_target_pairs={{0,16},{16,0},{1,17},{17,1},{2,18},{18,2},{3,19},{19,3},{4,20},{20... | collective-permute-start | bytes 12296 | tf_op jit(solution)/shard_map/ppermute | solution.py:291
  50.2 8.6 %collective-permute-start.17 = (bf16[144,1024]{1,0:T(8,128)(2,1)S(1)}, bf16[144,1024]{1,0:T(8,128)(2,1)S(1)}, u32[]{:S(2)}, u32[]{:S(2)}) collective-permute-start(bf16[144,1024]{1,0:T(8,128)(2,1)S(1)} %get-tuple-element.60), channel_id=1, source_target_pairs={{0,3},{1,2},{2,1},{3,0},{4,7},{5,6},{6,5},{7,4},{8,11},{9,10},{10,... | collective-permute-start | bytes 884744 | tf_op jit(solution)/shard_map/ppermute | solution.py:275
  54.8 6.8 %collective-permute-start.21 = (bf16[128,1024]{1,0:T(8,128)(2,1)S(1)}, bf16[128,1024]{1,0:T(8,128)(2,1)S(1)}, u32[]{:S(2)}, u32[]{:S(2)}) collective-permute-start(bf16[128,1024]{1,0:T(8,128)(2,1)S(1)} %get-tuple-element.68), channel_id=1, source_target_pairs={{0,16},{16,0},{1,17},{17,1},{2,18},{18,2},{3,19},{19,3},{4,20},{20... | collective-permute-start | bytes 786440 | tf_op jit(solution)/shard_map/ppermute | solution.py:382
  54.9 6.8 %collective-permute-start.22 = (bf16[128,1024]{1,0:T(8,128)(2,1)S(1)}, bf16[128,1024]{1,0:T(8,128)(2,1)S(1)}, u32[]{:S(2)}, u32[]{:S(2)}) collective-permute-start(bf16[128,1024]{1,0:T(8,128)(2,1)S(1)} %get-tuple-element.69), channel_id=1, source_target_pairs={{0,16},{16,0},{1,17},{17,1},{2,18},{18,2},{3,19},{19,3},{4,20},{20... | collective-permute-start | bytes 786440 | tf_op jit(solution)/shard_map/ppermute | solution.py:382
  55.4 8.1 %collective-permute-start.23 = (bf16[128,1024]{1,0:T(8,128)(2,1)S(1)}, bf16[128,1024]{1,0:T(8,128)(2,1)S(1)}, u32[]{:S(2)}, u32[]{:S(2)}) collective-permute-start(bf16[128,1024]{1,0:T(8,128)(2,1)S(1)} %get-tuple-element.70), channel_id=1, source_target_pairs={{0,16},{16,0},{1,17},{17,1},{2,18},{18,2},{3,19},{19,3},{4,20},{20... | collective-permute-start | bytes 786440 | tf_op jit(solution)/shard_map/ppermute | solution.py:382
  55.4 8.0 %collective-permute-start.24 = (bf16[128,1024]{1,0:T(8,128)(2,1)S(1)}, bf16[128,1024]{1,0:T(8,128)(2,1)S(1)}, u32[]{:S(2)}, u32[]{:S(2)}) collective-permute-start(bf16[128,1024]{1,0:T(8,128)(2,1)S(1)} %get-tuple-element.71), channel_id=1, source_target_pairs={{0,16},{16,0},{1,17},{17,1},{2,18},{18,2},{3,19},{19,3},{4,20},{20... | collective-permute-start | bytes 786440 | tf_op jit(solution)/shard_map/ppermute | solution.py:382
  59.0 6.5 %collective-permute-start.18 = (bf16[144,256]{1,0:T(8,128)(2,1)S(1)}, bf16[144,256]{1,0:T(8,128)(2,1)S(1)}, u32[]{:S(2)}, u32[]{:S(2)}) collective-permute-start(bf16[144,256]{1,0:T(8,128)(2,1)S(1)} %get-tuple-element.62), channel_id=1, source_target_pairs={{0,12},{1,13},{2,14},{3,15},{4,8},{5,9},{6,10},{7,11},{8,4},{9,5},... | collective-permute-start | bytes 221192 | tf_op jit(solution)/shard_map/ppermute | solution.py:275
  61.6 5.3 %collective-permute-start.19 = (bf16[144,256]{1,0:T(8,128)(2,1)S(1)}, bf16[144,256]{1,0:T(8,128)(2,1)S(1)}, u32[]{:S(2)}, u32[]{:S(2)}) collective-permute-start(bf16[144,256]{1,0:T(8,128)(2,1)S(1)} %get-tuple-element.63), channel_id=1, source_target_pairs={{0,8},{1,9},{2,10},{3,11},{4,12},{5,13},{6,14},{7,15},{8,0},{9,1},... | collective-permute-start | bytes 221192 | tf_op jit(solution)/shard_map/ppermute | solution.py:275
  61.7 5.2 %collective-permute-start.20 = (bf16[144,256]{1,0:T(8,128)(2,1)S(1)}, bf16[144,256]{1,0:T(8,128)(2,1)S(1)}, u32[]{:S(2)}, u32[]{:S(2)}) collective-permute-start(bf16[144,256]{1,0:T(8,128)(2,1)S(1)} %get-tuple-element.64), channel_id=1, source_target_pairs={{0,4},{1,5},{2,6},{3,7},{4,0},{5,1},{6,2},{7,3},{8,12},{9,13},{10,... | collective-permute-start | bytes 221192 | tf_op jit(solution)/shard_map/ppermute | solution.py:275
